TPU v7x, 32 devices: a whole 2x2x4 slice. The times are simulated.
32 devices in a mesh: row: 8 (over y, x, core), col: 4 (over z).
Axes of the slice: x: 2, y: 2, z: 4, core: 2. Of those that a mesh axis runs over, the one named last changes fastest.
Arguments:
- pair: bfloat16 [128, 128, 128], P('row', 'col'), may hold values from -6 to 6
- targets: int32 [128, 128], P('row', 'col'), may hold values from 0 to 63, as said below
- w_gate: bfloat16 [128, 512], replicated, may hold values from -0.5 to 0.5
- w_up: bfloat16 [128, 512], replicated, may hold values from -0.5 to 0.5
- w_out: bfloat16 [512, 128], replicated, may hold values from -0.25 to 0.25
- w_head: bfloat16 [128, 64], replicated, may hold values from -16 to 16
Outputs:
- d_pair: bfloat16 [128, 128, 128], P('row', 'col')
- grad_gate: float32 [128, 512], P('row', 'col')
- grad_up: float32 [128, 512], P('row', 'col')
- grad_out: float32 [512, 128], P('row', 'col')
- grad_head: float32 [128, 64], P('row', 'col')
Inputs may be any that keep to these rules, and one draw needn't show every extreme that they name: symmetric: targets[i, j] equals targets[j, i].
All inputs are finite; a program needn't handle non-finite values.
Results may differ from a plain program's by a relative error of at most 0.015.
Values may be sent and summed in bfloat16 or wider, within the bound.
No kernel may reach another device: no remote copies, remote signals or barrier semaphores. Data moves between devices by JAX's collectives and lax.ppermute only.
A program may use at most 64 MiB of HBM per device.

v0:
```python
import jax
import jax.numpy as jnp
from jax import lax
from jax.sharding import PartitionSpec as P

eps = 1e-05


def normalize(flat):
    values = flat.astype(jnp.float32)
    centre = values - jnp.mean(values, axis=-1, keepdims=True)
    scale_inv = lax.rsqrt(jnp.mean(centre * centre, axis=-1, keepdims=True) + eps)
    return (centre * scale_inv, scale_inv)


def forward_block(flat, w_gate, w_up, w_out, w_head):
    normed, scale_inv = normalize(flat)
    inputs = normed.astype(jnp.bfloat16)
    gate = jnp.dot(inputs, w_gate, preferred_element_type=jnp.float32)
    upper = jnp.dot(inputs, w_up, preferred_element_type=jnp.float32)
    hidden = (jax.nn.silu(gate) * upper).astype(jnp.bfloat16)
    updated = (
        flat.astype(jnp.float32) + jnp.dot(hidden, w_out, preferred_element_type=jnp.float32)
    ).astype(jnp.bfloat16)
    logits = jnp.dot(updated, w_head, preferred_element_type=jnp.float32).astype(jnp.bfloat16)
    return (updated, logits)


def backward_block(flat, updated, cotangent, w_gate, w_up, w_out, w_head):
    normed, scale_inv = normalize(flat)
    inputs = normed.astype(jnp.bfloat16)
    gate = jnp.dot(inputs, w_gate, preferred_element_type=jnp.float32)
    upper = jnp.dot(inputs, w_up, preferred_element_type=jnp.float32)
    sigma = jax.nn.sigmoid(gate)
    swish = jax.nn.silu(gate)
    hidden = (swish * upper).astype(jnp.bfloat16)
    d_updated = jnp.dot(cotangent, w_head.T, preferred_element_type=jnp.float32)
    d_upd_b = d_updated.astype(jnp.bfloat16)
    d_hidden = jnp.dot(d_upd_b, w_out.T, preferred_element_type=jnp.float32)
    d_gate = (d_hidden * upper * sigma * (1.0 + gate * (1.0 - sigma))).astype(jnp.bfloat16)
    d_up = (d_hidden * swish).astype(jnp.bfloat16)
    d_inputs = jnp.dot(d_gate, w_gate.T, preferred_element_type=jnp.float32) + jnp.dot(
        d_up, w_up.T, preferred_element_type=jnp.float32
    )
    d_norm = (
        d_inputs
        - jnp.mean(d_inputs, axis=-1, keepdims=True)
        - normed * jnp.mean(d_inputs * normed, axis=-1, keepdims=True)
    ) * scale_inv
    d_block = (d_updated + d_norm).astype(jnp.bfloat16)
    terms = (
        jnp.dot(inputs.T, d_gate, preferred_element_type=jnp.float32),
        jnp.dot(inputs.T, d_up, preferred_element_type=jnp.float32),
        jnp.dot(hidden.T, d_upd_b, preferred_element_type=jnp.float32),
        jnp.dot(updated.T, cotangent, preferred_element_type=jnp.float32),
    )
    return (terms, d_block)


def mirror(tile):
    rows, cols, bins = tile.shape
    ncol = lax.axis_size("col")
    nrow = lax.axis_size("row")
    part = rows // ncol
    first = tile.reshape(ncol, part, 2, rows * bins)
    got = lax.all_to_all(first, "col", split_axis=0, concat_axis=0, tiled=True)
    second = jnp.transpose(got, (0, 2, 1, 3)).reshape(nrow, part, rows * bins)
    got = lax.all_to_all(second, "row", split_axis=0, concat_axis=0, tiled=True)
    third = got.reshape(ncol, 2, part, rows * bins)
    got = lax.all_to_all(third, "col", split_axis=0, concat_axis=0, tiled=True)
    result = jnp.transpose(got.reshape(ncol, 2, part, rows, bins), (3, 1, 0, 2, 4))
    return result.reshape(rows, cols, bins)


def body(pair, targets, w_gate, w_up, w_out, w_head):
    rows, cols, width = pair.shape
    bins = w_head.shape[1]
    count = rows * cols
    nblocks = count // count
    blocks = pair.reshape(nblocks, count, width)
    updated, logits = lax.map(lambda blk: forward_block(blk, w_gate, w_up, w_out, w_head), blocks)
    tile = logits.reshape(rows, cols, bins)
    summed = tile.astype(jnp.float32) + mirror(tile).astype(jnp.float32)
    probs = jax.nn.softmax(summed, axis=-1)
    onehot = (targets[:, :, None] == jnp.arange(bins, dtype=jnp.int32)[None, None, :]).astype(
        jnp.float32
    )
    grad_sym = (probs - onehot).astype(jnp.bfloat16)
    cotangent = (grad_sym.astype(jnp.float32) * 2.0).astype(jnp.bfloat16)
    cotangent = cotangent.reshape(nblocks, count, bins)

    def accumulate(carry, items):
        flat, upd, cot = items
        terms, d_block = backward_block(flat, upd, cot, w_gate, w_up, w_out, w_head)
        return (tuple((c + t for c, t in zip(carry, terms))), d_block)

    start = (
        jnp.zeros(w_gate.shape, jnp.float32),
        jnp.zeros(w_up.shape, jnp.float32),
        jnp.zeros(w_out.shape, jnp.float32),
        jnp.zeros(w_head.shape, jnp.float32),
    )
    totals, d_blocks = lax.scan(accumulate, start, (blocks, updated, cotangent))
    d_pair = d_blocks.reshape(rows, cols, width)
    partial_sums = (
        lax.psum_scatter(
            totals[0].astype(jnp.bfloat16), "row", scatter_dimension=0, tiled=True
        ).astype(jnp.float32),
        lax.psum_scatter(
            totals[1].astype(jnp.bfloat16), "row", scatter_dimension=0, tiled=True
        ).astype(jnp.float32),
        lax.psum_scatter(
            totals[2].astype(jnp.bfloat16), "row", scatter_dimension=0, tiled=True
        ).astype(jnp.float32),
        lax.psum_scatter(
            totals[3].astype(jnp.bfloat16), "row", scatter_dimension=0, tiled=True
        ).astype(jnp.float32),
    )
    owned = (
        lax.psum_scatter(partial_sums[0], "col", scatter_dimension=1, tiled=True),
        lax.psum_scatter(partial_sums[1], "col", scatter_dimension=1, tiled=True),
        lax.psum_scatter(partial_sums[2], "col", scatter_dimension=1, tiled=True),
        lax.psum_scatter(partial_sums[3], "col", scatter_dimension=1, tiled=True),
    )
    factor = 1.0 / (rows * lax.axis_size("row"))
    return (d_pair, owned[0] * factor, owned[1] * factor, owned[2] * factor, owned[3] * factor)


def solution(mesh):
    placed = (P("row", "col", None), P("row", "col"), P(), P(), P(), P())
    return jax.shard_map(
        body,
        mesh=mesh,
        in_specs=placed,
        out_specs=(
            P("row", "col", None),
            P("row", "col"),
            P("row", "col"),
            P("row", "col"),
            P("row", "col"),
        ),
        check_vma=False,
    )
```

profile of v0, /device:TPU:0, one launch (start us, length us, event | category | flops | bytes accessed | tf_op | source)
XLA Modules:
  0.0 269.2 jit_solution(10372777390659000032)
XLA Ops:
  7.2 1.1 convert_reduce_fusion
  8.3 0.3 multiply_reduce_fusion.1
  8.6 0.1 div.40
  8.7 0.1 rsqrt.15
  8.8 0.2 fusion.3
  9.0 0.7 copy-done.2
  9.7 0.3 fusion.10
  10.0 1.3 multiply_convert_fusion.2
  11.3 0.3 fusion
  11.6 0.4 copy-done.4
  12.0 0.2 convolution_convert_fusion.3
  12.2 0.1 copy.17
  12.3 0.1 reshape_reshape.3
  12.5 11.8 %all_to_all.15 = bf16[4,4,2,1024]{3,2,1,0:T(2,128)(2,1)S(1)} all-to-all(bf16[4,4,2,1024]{3,2,1,0:T(2,128)(2,1)S(1)} %reshape_reshape.3), channel_id=1, replica_groups=mesh['row'=8,'col'=4] {'col'}, dimensions={0} | all-to-all | bytes 131072 | tf_op jit(solution)/shard_map/all_to_all | solution.py:66
  24.3 8.7 %all_to_all.16 = bf16[8,4,1024]{2,1,0:T(4,128)(2,1)} all-to-all(bf16[8,4,1024]{2,1,0:T(4,128)(2,1)S(1)} %bitcast.48), channel_id=1, replica_groups=mesh['row'=8,'col'=4] {'row'}, dimensions={0} | all-to-all | bytes 131072 | tf_op jit(solution)/shard_map/all_to_all | solution.py:68
  33.0 3.4 %all-to-all-start.2 = ((bf16[4,2,4,1024]{3,2,1,0:T(4,128)(2,1)}), bf16[4,2,4,1024]{3,2,1,0:T(4,128)(2,1)S(1)}, u32[]{:S(2)}, u32[]{:S(2)}) async-start(bf16[4,2,4,1024]{3,2,1,0:T(4,128)(2,1)} %bitcast.3), calls=%async_computation.2 | async-start | bytes 131072 | tf_op jit(solution)/shard_map/all_to_all | solution.py:70
  36.4 0.0 reduce-scatter.23.cloned.1.call-start
  36.5 0.1 eq.16
  36.5 5.6 %all-to-all-done.2 = bf16[4,2,4,1024]{3,2,1,0:T(4,128)(2,1)S(1)} async-done(((bf16[4,2,4,1024]{3,2,1,0:T(4,128)(2,1)}), bf16[4,2,4,1024]{3,2,1,0:T(4,128)(2,1)S(1)}, u32[]{:S(2)}, u32[]{:S(2)}) %all-to-all-start.2) | async-done | bytes 65568 | tf_op jit(solution)/shard_map/all_to_all | solution.py:70
  42.1 0.1 reshape.100
  42.2 0.1 copy.19
  42.4 0.1 copy.20
  42.5 0.1 fusion.4
  42.6 0.1 multiply_convert_fusion.3
  42.6 0.8 convolution_convert_fusion.4
  43.4 0.2 fusion.11
  43.7 0.0 reduce-scatter.23.cloned.1.call-update
  43.7 0.0 reduce-scatter.21.cloned.1.call-start
  43.7 1.0 convolution_convert_fusion
  44.7 1.8 multiply_convert_fusion
  46.6 0.3 fusion.12
  46.9 0.0 reduce-scatter.21.cloned.1.call-update
  46.9 0.0 reduce-scatter.27.cloned.1.call-start
  46.9 0.4 fusion.9
  47.4 24.4 %reduce-scatter.23.cloned.1.call-done = bf16[16,64]{1,0:T(8,128)(2,1)} async-done(((bf16[128,64]{1,0:T(8,128)(2,1)}), bf16[16,64]{1,0:T(8,128)(2,1)}) %reduce-scatter.23.cloned.1.call-update) | async-done | bytes 2064 | tf_op jit(solution)/shard_map/reduce_scatter | solution.py:115
  71.8 1.4 copy.24
  73.2 0.0 reduce-scatter.27.cloned.1.call-update
  73.2 0.0 reduce-scatter.17.cloned.1.call-start
  73.2 0.9 convolution_convert_fusion.1
  74.2 0.0 reduce-scatter.17.cloned.1.call-update
  74.2 0.0 reduce-scatter.13.cloned.1.call-start
  74.2 0.9 convolution_convert_fusion.2
  75.1 0.0 reduce-scatter.13.cloned.1.call-update
  75.1 0.0 reduce-scatter.25.cloned.1.call-start
  75.2 33.8 %reduce-scatter.21.cloned.1.call-done = bf16[64,128]{1,0:T(8,128)(2,1)} async-done(((bf16[512,128]{1,0:T(8,128)(2,1)}), bf16[64,128]{1,0:T(8,128)(2,1)}) %reduce-scatter.21.cloned.1.call-update) | async-done | bytes 16400 | tf_op jit(solution)/shard_map/reduce_scatter | solution.py:112
  109.1 1.4 copy.22
  110.5 0.0 reduce-scatter.25.cloned.1.call-update
  110.5 0.0 reduce-scatter.19.cloned.1.call-start
  110.6 1.0 add_convert_fusion
  111.6 18.7 %reduce-scatter.27.cloned.1.call-done = f32[16,16]{1,0:T(8,128)} async-done(((f32[64,16]{1,0:T(8,128)}), f32[16,16]{1,0:T(8,128)}) %reduce-scatter.27.cloned.1.call-update) | async-done | bytes 1040
  130.3 0.8 copy.25
  131.0 33.9 %reduce-scatter.17.cloned.1.call-done = bf16[16,512]{1,0:T(8,128)(2,1)} async-done(((bf16[128,512]{1,0:T(8,128)(2,1)}), bf16[16,512]{1,0:T(8,128)(2,1)}) %reduce-scatter.17.cloned.1.call-update) | async-done | bytes 16400 | tf_op jit(solution)/shard_map/reduce_scatter | solution.py:109
  164.9 1.3 convert_element_type.134
  166.2 0.0 reduce-scatter.15.cloned.1.call-start
  166.3 0.6 broadcast_multiply_fusion.1
  166.9 34.2 %reduce-scatter.13.cloned.1.call-done = bf16[16,512]{1,0:T(8,128)(2,1)} async-done(((bf16[128,512]{1,0:T(8,128)(2,1)}), bf16[16,512]{1,0:T(8,128)(2,1)}) %reduce-scatter.13.cloned.1.call-update) | async-done | bytes 16400 | tf_op jit(solution)/shard_map/reduce_scatter | solution.py:106
  201.1 1.3 convert_element_type.132
  202.5 19.8 %reduce-scatter.25.cloned.1.call-done = f32[32,64]{1,0:T(8,128)} async-done(((f32[128,64]{1,0:T(8,128)}), f32[32,64]{1,0:T(8,128)}) %reduce-scatter.25.cloned.1.call-update) | async-done | bytes 8208
  222.3 0.8 copy.23
  223.1 18.6 %reduce-scatter.19.cloned.1.call-done = f32[16,128]{1,0:T(8,128)} async-done(((f32[16,512]{1,0:T(8,128)}), f32[16,128]{1,0:T(8,128)}) %reduce-scatter.19.cloned.1.call-update) | async-done | bytes 8208 | tf_op jit(solution)/shard_map/reduce_scatter | solution.py:121
  241.7 1.3 broadcast_multiply_fusion.2
  243.0 0.7 copy.21
  243.7 17.4 %reduce-scatter.15.cloned.1.call-done = f32[16,128]{1,0:T(8,128)} async-done(((f32[16,512]{1,0:T(8,128)}), f32[16,128]{1,0:T(8,128)}) %reduce-scatter.15.cloned.1.call-update) | async-done | bytes 8208 | tf_op jit(solution)/shard_map/reduce_scatter | solution.py:120
  261.1 1.3 broadcast_multiply_fusion.3
  (18 shorter events, 0.1 us)
Async XLA Ops:
  7.2 2.8 %copy-start = (bf16[128,512]{1,0:T(8,128)(2,1)S(1)}, bf16[128,512]{1,0:T(8,128)(2,1)}, u32[]{:S(2)}) copy-start(bf16[128,512]{1,0:T(8,128)(2,1)} %param.9) | copy-start | bytes 393220
  7.2 1.1 copy-start.1
  8.8 0.9 copy-start.2
  10.0 1.3 copy-start.3
  11.3 0.7 copy-start.4
  33.0 3.5 %copy-start.5 = (s32[16,32]{1,0:T(8,128)S(1)}, s32[16,32]{1,0:T(8,128)}, u32[]{:S(2)}) copy-start(s32[16,32]{1,0:T(8,128)} %param.7) | copy-start | bytes 6148
  33.0 9.1 %all-to-all-start.2 = ((bf16[4,2,4,1024]{3,2,1,0:T(4,128)(2,1)}), bf16[4,2,4,1024]{3,2,1,0:T(4,128)(2,1)S(1)}, u32[]{:S(2)}, u32[]{:S(2)}) async-start(bf16[4,2,4,1024]{3,2,1,0:T(4,128)(2,1)} %bitcast.3), calls=%async_computation.2 | async-start | bytes 131072 | tf_op jit(solution)/shard_map/all_to_all | solution.py:70
  36.4 35.4 %reduce-scatter.23.cloned.1.call-start = ((), (), s32[]{:S(2)}) async-start(), calls=%async_computation.16 | async-start | bytes 36864 | tf_op jit(solution)/shard_map/reduce_scatter | solution.py:115
  43.7 65.4 %reduce-scatter.21.cloned.1.call-start = ((), (), s32[]{:S(2)}) async-start(), calls=%async_computation.15 | async-start | bytes 147456 | tf_op jit(solution)/shard_map/reduce_scatter | solution.py:112
  46.9 83.4 %reduce-scatter.27.cloned.1.call-start = ((), (), s32[]{:S(2)}) async-start(), calls=%async_computation.18 | async-start | bytes 40960
  73.2 91.7 %reduce-scatter.17.cloned.1.call-start = ((), (), s32[]{:S(2)}) async-start(), calls=%async_computation.13 | async-start | bytes 147456 | tf_op jit(solution)/shard_map/reduce_scatter | solution.py:109
  74.2 126.9 %reduce-scatter.13.cloned.1.call-start = ((), (), s32[]{:S(2)}) async-start(), calls=%async_computation.11 | async-start | bytes 147456 | tf_op jit(solution)/shard_map/reduce_scatter | solution.py:106
  75.1 147.1 %reduce-scatter.25.cloned.1.call-start = ((), (), s32[]{:S(2)}) async-start(), calls=%async_computation.17 | async-start | bytes 81920
  110.5 131.2 %reduce-scatter.19.cloned.1.call-start = ((), (), s32[]{:S(2)}) async-start(), calls=%async_computation.14 | async-start | bytes 40960 | tf_op jit(solution)/shard_map/reduce_scatter | solution.py:121
  166.2 94.8 %reduce-scatter.15.cloned.1.call-start = ((), (), s32[]{:S(2)}) async-start(), calls=%async_computation.12 | async-start | bytes 40960 | tf_op jit(solution)/shard_map/reduce_scatter | solution.py:120
Sparse Core Ops, SparseCore 0:
  43.8 27.9 reduce-scatter.22
  75.7 33.3 reduce-scatter.20
  111.3 18.9 reduce-scatter.26
  133.4 31.4 reduce-scatter.16
  167.7 33.3 reduce-scatter.12
  203.3 18.9 reduce-scatter.24
  224.5 17.1 reduce-scatter.18
  244.0 16.9 reduce-scatter.14
where the time goes:
time: 270 us; the launch traced here: 269 us
  waiting for transfers between devices  207 us (77%)
  blocking collectives  20.5 us (8%)
  between operations  14.3 us (5%)
  other arithmetic  8.56 us (3%)
  matrix products  8.46 us (3%)
  local copies, waits for them, and re-layouts  7.04 us (3%)
  starting transfers between devices  3.75 us (1%)
    unnamed x10, waiting for transfers between devices  38.7 us
    reduce_scatter x1, waiting for transfers between devices, body(): lax.psum_scatter(totals[0].astype(jnp.bfloat16), 'row', scatter_dimension...  34.2 us
    reduce_scatter x1, waiting for transfers between devices, body(): lax.psum_scatter(totals[1].astype(jnp.bfloat16), 'row', scatter_dimension...  33.9 us
    reduce_scatter x1, waiting for transfers between devices, body(): lax.psum_scatter(totals[2].astype(jnp.bfloat16), 'row', scatter_dimension...  33.8 us
    reduce_scatter x1, waiting for transfers between devices, body(): lax.psum_scatter(totals[3].astype(jnp.bfloat16), 'row', scatter_dimension...  24.4 us
    reduce_scatter x1, waiting for transfers between devices, body(): lax.psum_scatter(partial_sums[1], 'col', scatter_dimension=1, tiled=True)  18.6 us
    reduce_scatter x1, waiting for transfers between devices, body(): lax.psum_scatter(partial_sums[0], 'col', scatter_dimension=1, tiled=True)  17.4 us
    all_to_all x1, blocking collectives, mirror(): got = lax.all_to_all(first, 'col', split_axis=0, concat_axis=0, tiled=True)  11.8 us
  transfers between devices with their start and end apart: 9, of which 9 were waited for; matrix products, arithmetic and copies ran while one was open for 6% of the time, Pallas kernels for 0%

commit v1 on v0

v1 whole, which is shorter than its diff:
```python
import functools

import jax
import jax.numpy as jnp
from jax import lax
from jax.experimental import pallas as pl
from jax.experimental.pallas import tpu as pltpu
from jax.sharding import PartitionSpec as P

eps = 1e-05
f32 = jnp.float32
bf16 = jnp.bfloat16
SMEM = pl.BlockSpec(memory_space=pltpu.SMEM)
VMEM = pl.BlockSpec(memory_space=pltpu.VMEM)


def nn(a, b):
    return lax.dot_general(a, b, (((1,), (0,)), ((), ())), preferred_element_type=f32)


def nt(a, b):
    return lax.dot_general(a, b, (((1,), (1,)), ((), ())), preferred_element_type=f32)


def tn(a, b):
    return lax.dot_general(a, b, (((0,), (0,)), ((), ())), preferred_element_type=f32)


def normalize(flat):
    values = flat.astype(f32)
    centre = values - jnp.mean(values, axis=-1, keepdims=True)
    scale_inv = lax.rsqrt(jnp.mean(centre * centre, axis=-1, keepdims=True) + eps)
    return centre * scale_inv, scale_inv


def sigmoid(v):
    return 1.0 / (1.0 + jnp.exp(-v))


def chunks_of(size, most):
    step = most if size % most == 0 else size
    return [(at, step) for at in range(0, size, step)]


def forward_kernel(q, place, pair, w_gate, w_up, w_out, w_head, updated, logits, *rest):
    sends, halves = rest[:q], rest[q]
    count, width = pair.shape
    hidden_units = w_gate.shape[1]
    side = halves.shape[1]
    flat = pair[...]
    inputs = normalize(flat)[0].astype(bf16)
    total = flat.astype(f32)
    for at, step in chunks_of(hidden_units, 256):
        gate = nn(inputs, w_gate[:, at : at + step])
        upper = nn(inputs, w_up[:, at : at + step])
        hidden = (gate * sigmoid(gate) * upper).astype(bf16)
        total = total + nn(hidden, w_out[at : at + step, :])
    upd = total.astype(bf16)
    updated[...] = upd
    logit = nn(upd, w_head[...]).astype(bf16)
    logits[...] = logit
    edge = 1
    while edge * edge < side:
        edge *= 2
    out_row = lax.broadcasted_iota(jnp.int32, (side, side), 0)
    in_row = lax.broadcasted_iota(jnp.int32, (side, side), 1)
    shift = edge.bit_length() - 1
    wanted = ((out_row & (edge - 1)) << shift) | (out_row >> shift)
    swap = jnp.where(in_row == wanted, 1.0, 0.0).astype(bf16)
    blocks = logit.reshape(edge, q, edge, logit.shape[-1])
    for k in range(q):
        piece = blocks[:, k].reshape(side, logit.shape[-1])
        halves[k] = nn(swap, piece).astype(bf16)
    first = place[0]
    for p in range(q):
        sends[p][...] = halves[lax.rem(first + p, q)]


def backward_kernel(q, packed, place, pair, updated, logits, onehot, w_gate, w_up, w_out, w_head, *rest):
    got, rest = rest[:q], rest[q:]
    d_pair, rest = rest[0], rest[1:]
    mirrored, hot = rest[-2], rest[:-2]
    count, width = pair.shape
    units = w_gate.shape[1]
    bins = w_head.shape[1]
    edge = mirrored.shape[0]
    for p in range(q):
        h = lax.rem(place[0] + q - p, q)
        mirrored[:, h] = got[p][...].reshape(edge, edge, bins)
    summed = logits[...].astype(f32) + mirrored[...].reshape(count, bins).astype(f32)
    powers = jnp.exp(summed - jnp.max(summed, axis=-1, keepdims=True))
    probs = powers / jnp.sum(powers, axis=-1, keepdims=True)
    grad_sym = (probs - onehot[...].astype(f32)).astype(bf16)
    cotangent = (grad_sym.astype(f32) * 2.0).astype(bf16)
    d_updated = nt(cotangent, w_head[...])
    d_upd_b = d_updated.astype(bf16)
    normed, scale_inv = normalize(pair[...])
    inputs = normed.astype(bf16)
    head_term = tn(updated[...], cotangent)
    d_inputs = jnp.zeros((count, width), f32)
    gate_terms, up_terms, out_terms = [], [], []
    for at, step in chunks_of(units, 256):
        gate_w, up_w, out_w = w_gate[:, at : at + step], w_up[:, at : at + step], w_out[at : at + step, :]
        gate = nn(inputs, gate_w)
        upper = nn(inputs, up_w)
        sigma = sigmoid(gate)
        swish = gate * sigma
        hidden = (swish * upper).astype(bf16)
        d_hidden = nt(d_upd_b, out_w)
        d_gate = (d_hidden * upper * sigma * (1.0 + gate * (1.0 - sigma))).astype(bf16)
        d_up = (d_hidden * swish).astype(bf16)
        d_inputs = d_inputs + nt(d_gate, gate_w) + nt(d_up, up_w)
        gate_terms.append(tn(inputs, d_gate))
        up_terms.append(tn(inputs, d_up))
        out_terms.append(tn(hidden, d_upd_b))
    d_norm = (
        d_inputs
        - jnp.mean(d_inputs, axis=-1, keepdims=True)
        - normed * jnp.mean(d_inputs * normed, axis=-1, keepdims=True)
    ) * scale_inv
    d_pair[...] = (d_updated + d_norm).astype(bf16)
    terms = (
        jnp.concatenate(gate_terms, axis=1),
        jnp.concatenate(up_terms, axis=1),
        jnp.concatenate(out_terms, axis=0),
        head_term,
    )
    if not packed:
        for ref, term in zip(hot, terms):
            ref[...] = term.astype(bf16)
        return
    nrow, ncol = packed
    slots = rest[-1]
    lanes = units // ncol
    part, tall = width // nrow, units // nrow
    for d in range(nrow):
        for n in range(2):
            for c in range(ncol):
                at = (n * ncol + c) * part
                slots[d, at : at + part, :] = terms[n][d * part : (d + 1) * part, c * lanes : (c + 1) * lanes].astype(bf16)
        at = 2 * ncol * part
        slots[d, at : at + tall, :] = terms[2][d * tall : (d + 1) * tall, :].astype(bf16)
        piece = terms[3][d * part : (d + 1) * part, :]
        piece = jnp.concatenate([piece, jnp.zeros((part, lanes - bins), f32)], axis=1)
        slots[d, at + tall : at + tall + part, :] = piece.astype(bf16)
    for p in range(nrow):
        hot[p][...] = slots[lax.rem(place[1] + p, nrow)]


def row_sum_kernel(shapes, place, *rest):
    nrow, ncol, width, units, bins = shapes
    terms, hot, slots = rest[:nrow], rest[nrow:-1], rest[-1]
    lanes, part, tall = units // ncol, width // nrow, units // nrow
    total = terms[0][...].astype(f32)
    for term in terms[1:]:
        total = total + term[...].astype(f32)
    narrow, few = width // ncol, bins // ncol
    group = lanes // narrow
    at = 2 * ncol * part
    out = total[at : at + tall]
    head = total[at + tall : at + tall + part]
    deep = tall // group
    for c in range(ncol):
        slots[c, 0:part] = total[c * part : (c + 1) * part].astype(bf16)
        slots[c, part : 2 * part] = total[(ncol + c) * part : (ncol + c + 1) * part].astype(bf16)
        pieces = [out[k * deep : (k + 1) * deep, c * narrow : (c + 1) * narrow] for k in range(group)]
        slots[c, 2 * part : 2 * part + deep] = jnp.concatenate(pieces, axis=1).astype(bf16)
        piece = head[:, c * few : (c + 1) * few]
        piece = jnp.concatenate([piece, jnp.zeros((part, lanes - few), f32)], axis=1)
        slots[c, 2 * part + deep : 3 * part + deep] = piece.astype(bf16)
    for p in range(ncol):
        hot[p][...] = slots[lax.rem(place[2] + p, ncol)]


def col_sum_kernel(shapes, factor, *rest):
    nrow, ncol, width, units, bins = shapes
    terms, (gate, up, out, head) = rest[:ncol], rest[ncol:]
    lanes, part, tall = units // ncol, width // nrow, units // nrow
    total = terms[0][...].astype(f32)
    for term in terms[1:]:
        total = total + term[...].astype(f32)
    total = total * factor
    narrow, few = width // ncol, bins // ncol
    group = lanes // narrow
    deep = tall // group
    gate[...] = total[0:part]
    up[...] = total[part : 2 * part]
    for k in range(group):
        out[k * deep : (k + 1) * deep, :] = total[2 * part : 2 * part + deep, k * narrow : (k + 1) * narrow]
    head[...] = total[2 * part + deep : 3 * part + deep, 0:few]


def shaped(shape, kind):
    return jax.ShapeDtypeStruct(shape, kind)


def ring_permutes(values, axis, size):
    return [
        lax.ppermute(value, axis, [(s, (s + p) % size) for s in range(size)])
        for p, value in enumerate(values, start=1)
    ]


def body(pair, targets, w_gate, w_up, w_out, w_head):
    rows, cols, width = pair.shape
    units = w_gate.shape[1]
    bins = w_head.shape[1]
    count = rows * cols
    nrow, ncol = lax.axis_size("row"), lax.axis_size("col")
    q = nrow // ncol
    side = count // q
    row, col = lax.axis_index("row"), lax.axis_index("col")
    place = jnp.stack([lax.rem(row, q), row, col]).astype(jnp.int32)
    flat = pair.reshape(count, width)
    params = pltpu.CompilerParams(vmem_limit_bytes=40 * 1024 * 1024)

    updated, logits, *sends = pl.pallas_call(
        functools.partial(forward_kernel, q),
        out_shape=[shaped((count, width), bf16), shaped((count, bins), bf16)] + [shaped((side, bins), bf16)] * q,
        in_specs=[SMEM] + [VMEM] * 5,
        out_specs=[VMEM] * (2 + q),
        scratch_shapes=[pltpu.VMEM((q, side, bins), bf16)],
        compiler_params=params,
        name="forward",
    )(place, flat, w_gate, w_up, w_out, w_head)

    got = []
    for p in range(q):
        pairs = [
            (r * ncol + c, (q * c + (r % q + p) % q) * ncol + r // q) for r in range(nrow) for c in range(ncol)
        ]
        got.append(lax.ppermute(sends[p], ("row", "col"), pairs))
    onehot = (targets.reshape(count)[:, None] == jnp.arange(bins, dtype=jnp.int32)[None, :]).astype(bf16)

    part, tall = width // nrow, units // nrow
    lanes = units // ncol
    fits = (
        part % 16 == 0 and lanes == width and width % 128 == 0 and bins <= lanes
        and lanes % (width // ncol) == 0 and (tall // (lanes // (width // ncol))) % 16 == 0
    )
    height = 2 * ncol * part + tall + part
    if fits:
        hot_shapes = [shaped((height, lanes), bf16)] * nrow
        slots = pltpu.VMEM((nrow, height, lanes), bf16)
    else:
        hot_shapes = [shaped(w.shape, bf16) for w in (w_gate, w_up, w_out, w_head)]
        slots = pltpu.VMEM((16, 128), bf16)
    d_pair, *hot = pl.pallas_call(
        functools.partial(backward_kernel, q, (nrow, ncol) if fits else None),
        out_shape=[shaped((count, width), bf16)] + hot_shapes,
        in_specs=[SMEM] + [VMEM] * (8 + q),
        out_specs=[VMEM] * (1 + len(hot_shapes)),
        scratch_shapes=[pltpu.VMEM((rows, q, rows, bins), bf16), slots],
        compiler_params=params,
        name="backward",
    )(place, flat, updated, logits, onehot, w_gate, w_up, w_out, w_head, *got)
    d_pair = d_pair.reshape(rows, cols, width)
    factor = 1.0 / (rows * nrow)
    if not fits:
        owned = []
        for term in hot:
            mine = lax.psum_scatter(term, "row", scatter_dimension=0, tiled=True).astype(f32)
            owned.append(lax.psum_scatter(mine, "col", scatter_dimension=1, tiled=True) * factor)
        return (d_pair, *owned)

    shapes = (nrow, ncol, width, units, bins)
    short = 3 * part + tall // (lanes // (width // ncol))
    terms = [hot[0]] + ring_permutes(hot[1:], "row", nrow)
    hot = pl.pallas_call(
        functools.partial(row_sum_kernel, shapes),
        out_shape=[shaped((short, lanes), bf16)] * ncol,
        in_specs=[SMEM] + [VMEM] * nrow,
        out_specs=[VMEM] * ncol,
        scratch_shapes=[pltpu.VMEM((ncol, short, lanes), bf16)],
        compiler_params=params,
        name="row_sum",
    )(place, *terms)
    terms = [hot[0]] + ring_permutes(hot[1:], "col", ncol)
    owned = pl.pallas_call(
        functools.partial(col_sum_kernel, shapes, factor),
        out_shape=[
            shaped((part, lanes), f32),
            shaped((part, lanes), f32),
            shaped((tall, width // ncol), f32),
            shaped((part, bins // ncol), f32),
        ],
        in_specs=[VMEM] * ncol,
        out_specs=[VMEM] * 4,
        compiler_params=params,
        name="col_sum",
    )(*terms)
    return (d_pair, *owned)


def solution(mesh):
    placed = (P("row", "col", None), P("row", "col"), P(), P(), P(), P())
    return jax.shard_map(
        body,
        mesh=mesh,
        in_specs=placed,
        out_specs=(P("row", "col", None), P("row", "col"), P("row", "col"), P("row", "col"), P("row", "col")),
        check_vma=False,
    )
```

time: 270 us -> 45.5 us (0.17)
  waiting for transfers between devices: 207 us -> 6.35 us
  starting transfers between devices: 3.75 us -> 26.3 us
  blocking collectives: 20.5 us -> 0 us
  between operations: 14.3 us -> 0.71 us
  matrix products: 8.46 us -> 0 us
  other arithmetic: 8.56 us -> 0.22 us
  Pallas kernels: 0 us -> 6.39 us
    reduce_scatter x6 -> x0, waiting for transfers between devices: 162 us -> none  [the longest x1 34.2 us: body(): lax.psum_scatter(totals[0].astype(jnp.bfloat16), 'row', scatter_dimension...]
    unnamed x10 -> x0, waiting for transfers between devices: 38.7 us -> none
    ppermute x0 -> x12, starting transfers between devices: none -> 26.3 us  [the longest x10 25 us: ring_permutes(): lax.ppermute(value, axis, [(s, (s + p) % size) for s in range(size)])]
    all_to_all x2 -> x0, blocking collectives: 20.5 us -> none  [the longest x1 11.8 us: mirror(): got = lax.all_to_all(first, 'col', split_axis=0, concat_axis=0, tiled=True)]
    dot_general x12 -> x0, matrix products: 8.46 us -> none  [the longest x1 1.82 us: backward_block(): d_hidden = jnp.dot(d_upd_b, w_out.T, preferred_element_type=jnp.float32)]
    pallas_call x0 -> x4, Pallas kernels: none -> 6.39 us  [the longest x1 3.17 us: body(): pl.pallas_call(functools.partial(backward_kernel, q, (nrow, ncol) if fits...]
    ppermute x0 -> x12, waiting for transfers between devices: none -> 6.35 us  [the longest x10 5.68 us: ring_permutes(): lax.ppermute(value, axis, [(s, (s + p) % size) for s in range(size)])]
    all_to_all x1 -> x0, waiting for transfers between devices: 5.57 us -> none  [mirror(): got = lax.all_to_all(third, 'col', split_axis=0, concat_axis=0, tiled=True)]
  transfers between devices with their start and end apart: 9 -> 12, of which waited for: 9 -> 7; matrix products, arithmetic and copies ran while one was open for 6% -> 0% of each run, Pallas kernels for 0% -> 0%
where the time goes in v1:
time: 45.5 us; the launch traced here: 45.2 us
  starting transfers between devices  26.3 us (58%)
  Pallas kernels  6.39 us (14%)
  waiting for transfers between devices  6.35 us (14%)
  local copies, waits for them, and re-layouts  5.22 us (11%)
  between operations  0.71 us (2%)
    ppermute x10, starting transfers between devices, ring_permutes(): lax.ppermute(value, axis, [(s, (s + p) % size) for s in range(size)])  25 us
    ppermute x10, waiting for transfers between devices, ring_permutes(): lax.ppermute(value, axis, [(s, (s + p) % size) for s in range(size)])  5.68 us
    unnamed x22, local copies, waits for them, and re-layouts  5.14 us
    pallas_call x1, Pallas kernels, body(): pl.pallas_call(functools.partial(backward_kernel, q, (nrow, ncol) if fits...  3.17 us
    pallas_call x1, Pallas kernels, body(): pl.pallas_call(functools.partial(forward_kernel, q), out_shape=[shaped((c...  1.95 us
    ppermute x2, starting transfers between devices, body(): got.append(lax.ppermute(sends[p], ('row', 'col'), pairs))  1.32 us
  transfers between devices with their start and end apart: 12, of which 7 were waited for; matrix products, arithmetic and copies ran while one was open for 0% of the time, Pallas kernels for 0%

profile of v1, /device:TPU:0, one launch (start us, length us, event | category | flops | bytes accessed | tf_op | source)
XLA Modules:
  0.0 45.2 jit_solution(14928873796699916889)
XLA Ops:
  0.6 0.0 copy-start.8
  0.6 0.7 %copy-done.8 = bf16[128,64]{0,1:T(8,128)(2,1)S(1)} copy-done((bf16[128,64]{0,1:T(8,128)(2,1)S(1)}, bf16[128,64]{0,1:T(8,128)(2,1)}, u32[]{:S(2)}) %copy-start.8) | copy-done | bytes 16408
  1.3 0.1 copy.11.w_head
  1.5 0.1 pad_add_fusion.place
  1.5 0.0 copy-start
  1.5 0.9 %copy-done = bf16[16,32,128]{2,1,0:T(8,128)(2,1)S(1)} copy-done((bf16[16,32,128]{2,1,0:T(8,128)(2,1)S(1)}, bf16[16,32,128]{2,1,0:T(8,128)(2,1)}, u32[]{:S(2)}) %copy-start) | copy-done | bytes 131096
  2.5 0.0 copy-start.2
  2.5 0.9 %copy-done.2 = bf16[128,512]{1,0:T(8,128)(2,1)S(1)} copy-done((bf16[128,512]{1,0:T(8,128)(2,1)S(1)}, bf16[128,512]{1,0:T(8,128)(2,1)}, u32[]{:S(2)}) %copy-start.2) | copy-done | bytes 131096
  3.4 0.0 copy-start.4
  3.4 0.9 %copy-done.4 = bf16[128,512]{1,0:T(8,128)(2,1)S(1)} copy-done((bf16[128,512]{1,0:T(8,128)(2,1)S(1)}, bf16[128,512]{1,0:T(8,128)(2,1)}, u32[]{:S(2)}) %copy-start.4) | copy-done | bytes 131096
  4.3 0.0 copy-start.6
  4.3 0.9 %copy-done.6 = bf16[512,128]{1,0:T(8,128)(2,1)S(1)} copy-done((bf16[512,128]{1,0:T(8,128)(2,1)S(1)}, bf16[512,128]{1,0:T(8,128)(2,1)}, u32[]{:S(2)}) %copy-start.6) | copy-done | bytes 131096
  5.2 0.0 copy-start.9
  5.2 0.0 copy-start.3
  5.2 0.0 copy-start.5
  5.2 0.0 copy-start.7
  5.2 1.9 %forward.1 = (bf16[512,128]{1,0:T(8,128)(2,1)S(1)}, bf16[512,64]{1,0:T(8,128)(2,1)S(1)}, bf16[256,64]{1,0:T(8,128)(2,1)S(1)}, bf16[256,64]{1,0:T(8,128)(2,1)S(1)}) custom-call(s32[3]{0:T(128)S(1)} %pad_add_fusion.place, bf16[512,128]{1,0:T(8,128)(2,1)S(1)} %bitcast.5, bf16[128,512]{1,0:T(8,128)(2,1)S(1)} %copy-done.2, bf16[128,512]{1,0:T(8,128)(2,1)S(1)} %copy-done.4, ...), custom_call_target="tpu_custom_call" | custom-call | tf_op jit(solution)/shard_map/forward/pallas_call | solution.py:217
  7.1 0.0 copy-start.1
  7.1 0.8 %collective-permute-start = (bf16[256,64]{1,0:T(8,128)(2,1)S(1)}, bf16[256,64]{1,0:T(8,128)(2,1)S(1)}, u32[]{:S(2)}, u32[]{:S(2)}) collective-permute-start(bf16[256,64]{1,0:T(8,128)(2,1)S(1)} %get-tuple-element.28), channel_id=1, source_target_pairs={{0,0},{1,8},{2,16},{3,24},{4,4},{5,12},{6,20},{7,28},{8,1},{9,9},{... | collective-permute-start | bytes 98312 | tf_op jit(solution)/shard_map/ppermute | solution.py:232
  8.0 0.5 %collective-permute-start.1 = (bf16[256,64]{1,0:T(8,128)(2,1)S(1)}, bf16[256,64]{1,0:T(8,128)(2,1)S(1)}, u32[]{:S(2)}, u32[]{:S(2)}) collective-permute-start(bf16[256,64]{1,0:T(8,128)(2,1)S(1)} %get-tuple-element.29), channel_id=1, source_target_pairs={{0,4},{1,12},{2,20},{3,28},{4,0},{5,8},{6,16},{7,24},{8,5},{9,13},... | collective-permute-start | bytes 98312 | tf_op jit(solution)/shard_map/ppermute | solution.py:232
  8.5 0.0 copy-done.9
  8.5 0.1 eq.15
  8.6 0.1 fusion.onehot
  8.7 0.0 collective-permute-done.rest_0_
  8.7 0.7 %collective-permute-done.1.rest_1_ = bf16[256,64]{1,0:T(8,128)(2,1)S(1)} collective-permute-done((bf16[256,64]{1,0:T(8,128)(2,1)S(1)}, bf16[256,64]{1,0:T(8,128)(2,1)S(1)}, u32[]{:S(2)}, u32[]{:S(2)}) %collective-permute-start.1) | collective-permute-done | bytes 32800 | tf_op jit(solution)/shard_map/ppermute | solution.py:232
  9.4 0.0 copy-done.3
  9.4 0.0 copy-done.5
  9.4 0.0 copy-done.7
  9.4 0.0 copy-done.1
  9.4 3.2 %backward.1 = (bf16[512,128]{1,0:T(8,128)(2,1)}, bf16[208,128]{1,0:T(8,128)(2,1)S(1)}, bf16[208,128]{1,0:T(8,128)(2,1)S(1)}, bf16[208,128]{1,0:T(8,128)(2,1)S(1)...) custom-call(s32[3]{0:T(128)S(1)} %pad_add_fusion.place, ...), custom_call_target="tpu_custom_call" | custom-call | tf_op jit(solution)/shard_map/backward/pallas_call | solution.py:248
  12.6 0.4 collective-permute-start.2
  12.9 14.2 %collective-permute-start.3 = (bf16[208,128]{1,0:T(8,128)(2,1)S(1)}, bf16[208,128]{1,0:T(8,128)(2,1)S(1)}, u32[]{:S(2)}, u32[]{:S(2)}) collective-permute-start(bf16[208,128]{1,0:T(8,128)(2,1)S(1)} %get-tuple-element.33), channel_id=1, source_target_pairs={{0,8},{4,12},{8,16},{12,20},{16,24},{20,28},{24,0},{28,4},{1,9},{5... | collective-permute-start | bytes 159752 | tf_op jit(solution)/shard_map/ppermute | solution.py:199
  27.1 2.0 %collective-permute-start.4 = (bf16[208,128]{1,0:T(8,128)(2,1)S(1)}, bf16[208,128]{1,0:T(8,128)(2,1)S(1)}, u32[]{:S(2)}, u32[]{:S(2)}) collective-permute-start(bf16[208,128]{1,0:T(8,128)(2,1)S(1)} %get-tuple-element.34), channel_id=1, source_target_pairs={{0,12},{4,16},{8,20},{12,24},{16,28},{20,0},{24,4},{28,8},{1,13},{... | collective-permute-start | bytes 159752 | tf_op jit(solution)/shard_map/ppermute | solution.py:199
  29.2 0.8 %collective-permute-start.5 = (bf16[208,128]{1,0:T(8,128)(2,1)S(1)}, bf16[208,128]{1,0:T(8,128)(2,1)S(1)}, u32[]{:S(2)}, u32[]{:S(2)}) collective-permute-start(bf16[208,128]{1,0:T(8,128)(2,1)S(1)} %get-tuple-element.35), channel_id=1, source_target_pairs={{0,16},{4,20},{8,24},{12,28},{16,0},{20,4},{24,8},{28,12},{1,17},{... | collective-permute-start | bytes 159752 | tf_op jit(solution)/shard_map/ppermute | solution.py:199
  29.9 0.0 collective-permute-start.6
  30.0 0.0 collective-permute-done.2.rest_1_
  30.0 1.3 %collective-permute-start.7 = (bf16[208,128]{1,0:T(8,128)(2,1)S(1)}, bf16[208,128]{1,0:T(8,128)(2,1)S(1)}, u32[]{:S(2)}, u32[]{:S(2)}) collective-permute-start(bf16[208,128]{1,0:T(8,128)(2,1)S(1)} %get-tuple-element.37), channel_id=1, source_target_pairs={{0,24},{4,28},{8,0},{12,4},{16,8},{20,12},{24,16},{28,20},{1,25},{... | collective-permute-start | bytes 159752 | tf_op jit(solution)/shard_map/ppermute | solution.py:199
  31.3 0.0 collective-permute-done.3.rest_2_
  31.3 1.4 %collective-permute-start.8 = (bf16[208,128]{1,0:T(8,128)(2,1)S(1)}, bf16[208,128]{1,0:T(8,128)(2,1)S(1)}, u32[]{:S(2)}, u32[]{:S(2)}) collective-permute-start(bf16[208,128]{1,0:T(8,128)(2,1)S(1)} %get-tuple-element.38), channel_id=1, source_target_pairs={{0,28},{4,0},{8,4},{12,8},{16,12},{20,16},{24,20},{28,24},{1,29},{... | collective-permute-start | bytes 159752 | tf_op jit(solution)/shard_map/ppermute | solution.py:199
  32.6 0.0 collective-permute-done.4.rest_3_
  32.6 0.7 %collective-permute-done.5.rest_4_ = bf16[208,128]{1,0:T(8,128)(2,1)S(1)} collective-permute-done((bf16[208,128]{1,0:T(8,128)(2,1)S(1)}, bf16[208,128]{1,0:T(8,128)(2,1)S(1)}, u32[]{:S(2)}, u32[]{:S(2)}) %collective-permute-start.5) | collective-permute-done | bytes 53280 | tf_op jit(solution)/shard_map/ppermute | solution.py:199
  33.3 0.2 collective-permute-done.6.rest_5_
  33.5 1.1 %collective-permute-done.7.rest_6_ = bf16[208,128]{1,0:T(8,128)(2,1)S(1)} collective-permute-done((bf16[208,128]{1,0:T(8,128)(2,1)S(1)}, bf16[208,128]{1,0:T(8,128)(2,1)S(1)}, u32[]{:S(2)}, u32[]{:S(2)}) %collective-permute-start.7) | collective-permute-done | bytes 53280 | tf_op jit(solution)/shard_map/ppermute | solution.py:199
  34.6 0.0 collective-permute-done.8.rest_7_
  34.6 0.7 %row_sum.1 = (bf16[64,128]{1,0:T(8,128)(2,1)S(1)}, bf16[64,128]{1,0:T(8,128)(2,1)S(1)}, bf16[64,128]{1,0:T(8,128)(2,1)S(1)}, bf16[64,128]{1,0:T(8,128)(2,1)S(1)}) custom-call(s32[3]{0:T(128)S(1)} %pad_add_fusion.place, bf16[208,128]{1,0:T(8,128)(2,1)S(1)} %get-tuple-element.31.rest_0_, bf16[208,128]{1,0:T(8,128)(2,1)S(1)} %collective-permute-done.2.rest_1_, ...), custom_call_target="tpu_custom_call" | custom-call | tf_op jit(solution)/shard_map/row_sum/pallas_call | solution.py:269
  35.2 1.1 %collective-permute-start.9 = (bf16[64,128]{1,0:T(8,128)(2,1)S(1)}, bf16[64,128]{1,0:T(8,128)(2,1)S(1)}, u32[]{:S(2)}, u32[]{:S(2)}) collective-permute-start(bf16[64,128]{1,0:T(8,128)(2,1)S(1)} %get-tuple-element.40), channel_id=1, source_target_pairs={{0,1},{1,2},{2,3},{3,0},{4,5},{5,6},{6,7},{7,4},{8,9},{9,10},{10,1... | collective-permute-start | bytes 49160 | tf_op jit(solution)/shard_map/ppermute | solution.py:199
  36.4 3.8 %collective-permute-start.10 = (bf16[64,128]{1,0:T(8,128)(2,1)S(1)}, bf16[64,128]{1,0:T(8,128)(2,1)S(1)}, u32[]{:S(2)}, u32[]{:S(2)}) collective-permute-start(bf16[64,128]{1,0:T(8,128)(2,1)S(1)} %get-tuple-element.41), channel_id=1, source_target_pairs={{0,2},{1,3},{2,0},{3,1},{4,6},{5,7},{6,4},{7,5},{8,10},{9,11},{10,... | collective-permute-start | bytes 49160 | tf_op jit(solution)/shard_map/ppermute | solution.py:199
  40.2 0.0 collective-permute-start.11
  40.2 1.3 %collective-permute-done.9.rest_1_ = bf16[64,128]{1,0:T(8,128)(2,1)S(1)} collective-permute-done((bf16[64,128]{1,0:T(8,128)(2,1)S(1)}, bf16[64,128]{1,0:T(8,128)(2,1)S(1)}, u32[]{:S(2)}, u32[]{:S(2)}) %collective-permute-start.9) | collective-permute-done | bytes 16416 | tf_op jit(solution)/shard_map/ppermute | solution.py:199
  41.5 0.6 %collective-permute-done.10.rest_2_ = bf16[64,128]{1,0:T(8,128)(2,1)S(1)} collective-permute-done((bf16[64,128]{1,0:T(8,128)(2,1)S(1)}, bf16[64,128]{1,0:T(8,128)(2,1)S(1)}, u32[]{:S(2)}, u32[]{:S(2)}) %collective-permute-start.10) | collective-permute-done | bytes 16416 | tf_op jit(solution)/shard_map/ppermute | solution.py:199
  42.1 1.8 %collective-permute-done.11.rest_3_ = bf16[64,128]{1,0:T(8,128)(2,1)S(1)} collective-permute-done((bf16[64,128]{1,0:T(8,128)(2,1)S(1)}, bf16[64,128]{1,0:T(8,128)(2,1)S(1)}, u32[]{:S(2)}, u32[]{:S(2)}) %collective-permute-start.11) | collective-permute-done | bytes 16416 | tf_op jit(solution)/shard_map/ppermute | solution.py:199
  43.9 0.6 %col_sum.1 = (f32[16,128]{1,0:T(8,128)}, f32[16,128]{1,0:T(8,128)}, f32[64,32]{1,0:T(8,128)S(1)}, f32[16,16]{1,0:T(8,128)}) custom-call(bf16[64,128]{1,0:T(8,128)(2,1)S(1)} %get-tuple-element.39.rest_0_, bf16[64,128]{1,0:T(8,128)(2,1)S(1)} %collective-permute-done.9.rest_1_, bf16[64,128]{1,0:T(8,128)(2,1)S(1)} %collective-permute-done.10.rest_2_, ...), custom_call_target="tpu_custom_call" | custom-call | tf_op jit(solution)/shard_map/col_sum/pallas_call | solution.py:279
  44.5 0.7 %copy.13 = f32[64,32]{0,1:T(8,128)} copy(f32[64,32]{1,0:T(8,128)S(1)} %get-tuple-element.50) | data formatting | bytes 16384
Async XLA Ops:
  0.6 0.7 %copy-start.8 = (bf16[128,64]{0,1:T(8,128)(2,1)S(1)}, bf16[128,64]{0,1:T(8,128)(2,1)}, u32[]{:S(2)}) copy-start(bf16[128,64]{0,1:T(8,128)(2,1)} %param.11) | copy-start | bytes 49156
  1.5 0.9 %copy-start = (bf16[16,32,128]{2,1,0:T(8,128)(2,1)S(1)}, bf16[16,32,128]{2,1,0:T(8,128)(2,1)}, u32[]{:S(2)}) copy-start(bf16[16,32,128]{2,1,0:T(8,128)(2,1)} %param.6) | copy-start | bytes 393220
  2.5 0.9 %copy-start.2 = (bf16[128,512]{1,0:T(8,128)(2,1)S(1)}, bf16[128,512]{1,0:T(8,128)(2,1)}, u32[]{:S(2)}) copy-start(bf16[128,512]{1,0:T(8,128)(2,1)} %w_gate.3) | copy-start | bytes 393220
  3.4 0.9 %copy-start.4 = (bf16[128,512]{1,0:T(8,128)(2,1)S(1)}, bf16[128,512]{1,0:T(8,128)(2,1)}, u32[]{:S(2)}) copy-start(bf16[128,512]{1,0:T(8,128)(2,1)} %w_up.3) | copy-start | bytes 393220
  4.3 0.9 %copy-start.6 = (bf16[512,128]{1,0:T(8,128)(2,1)S(1)}, bf16[512,128]{1,0:T(8,128)(2,1)}, u32[]{:S(2)}) copy-start(bf16[512,128]{1,0:T(8,128)(2,1)} %w_out.3) | copy-start | bytes 393220
  5.2 3.3 %copy-start.9 = (s32[16,32]{1,0:T(8,128)S(1)}, s32[16,32]{1,0:T(8,128)}, u32[]{:S(2)}) copy-start(s32[16,32]{1,0:T(8,128)} %param.7) | copy-start | bytes 6148
  5.2 4.2 %copy-start.3 = (bf16[128,512]{1,0:T(8,128)(2,1)S(1)}, bf16[128,512]{1,0:T(8,128)(2,1)}, u32[]{:S(2)}) copy-start(bf16[128,512]{1,0:T(8,128)(2,1)} %w_gate.3) | copy-start | bytes 393220
  5.2 4.2 %copy-start.5 = (bf16[128,512]{1,0:T(8,128)(2,1)S(1)}, bf16[128,512]{1,0:T(8,128)(2,1)}, u32[]{:S(2)}) copy-start(bf16[128,512]{1,0:T(8,128)(2,1)} %w_up.3) | copy-start | bytes 393220
  5.2 4.2 %copy-start.7 = (bf16[512,128]{1,0:T(8,128)(2,1)S(1)}, bf16[512,128]{1,0:T(8,128)(2,1)}, u32[]{:S(2)}) copy-start(bf16[512,128]{1,0:T(8,128)(2,1)} %w_out.3) | copy-start | bytes 393220
  7.1 2.3 %copy-start.1 = (bf16[16,32,128]{2,1,0:T(8,128)(2,1)S(1)}, bf16[16,32,128]{2,1,0:T(8,128)(2,1)}, u32[]{:S(2)}) copy-start(bf16[16,32,128]{2,1,0:T(8,128)(2,1)} %param.6) | copy-start | bytes 393220
  7.1 1.6 %collective-permute-start = (bf16[256,64]{1,0:T(8,128)(2,1)S(1)}, bf16[256,64]{1,0:T(8,128)(2,1)S(1)}, u32[]{:S(2)}, u32[]{:S(2)}) collective-permute-start(bf16[256,64]{1,0:T(8,128)(2,1)S(1)} %get-tuple-element.28), channel_id=1, source_target_pairs={{0,0},{1,8},{2,16},{3,24},{4,4},{5,12},{6,20},{7,28},{8,1},{9,9},{... | collective-permute-start | bytes 98312 | tf_op jit(solution)/shard_map/ppermute | solution.py:232
  8.0 1.4 %collective-permute-start.1 = (bf16[256,64]{1,0:T(8,128)(2,1)S(1)}, bf16[256,64]{1,0:T(8,128)(2,1)S(1)}, u32[]{:S(2)}, u32[]{:S(2)}) collective-permute-start(bf16[256,64]{1,0:T(8,128)(2,1)S(1)} %get-tuple-element.29), channel_id=1, source_target_pairs={{0,4},{1,12},{2,20},{3,28},{4,0},{5,8},{6,16},{7,24},{8,5},{9,13},... | collective-permute-start | bytes 98312 | tf_op jit(solution)/shard_map/ppermute | solution.py:232
  12.6 17.4 %collective-permute-start.2 = (bf16[208,128]{1,0:T(8,128)(2,1)S(1)}, bf16[208,128]{1,0:T(8,128)(2,1)S(1)}, u32[]{:S(2)}, u32[]{:S(2)}) collective-permute-start(bf16[208,128]{1,0:T(8,128)(2,1)S(1)} %get-tuple-element.32), channel_id=1, source_target_pairs={{0,4},{4,8},{8,12},{12,16},{16,20},{20,24},{24,28},{28,0},{1,5},{5... | collective-permute-start | bytes 159752 | tf_op jit(solution)/shard_map/ppermute | solution.py:199
  12.9 18.3 %collective-permute-start.3 = (bf16[208,128]{1,0:T(8,128)(2,1)S(1)}, bf16[208,128]{1,0:T(8,128)(2,1)S(1)}, u32[]{:S(2)}, u32[]{:S(2)}) collective-permute-start(bf16[208,128]{1,0:T(8,128)(2,1)S(1)} %get-tuple-element.33), channel_id=1, source_target_pairs={{0,8},{4,12},{8,16},{12,20},{16,24},{20,28},{24,0},{28,4},{1,9},{5... | collective-permute-start | bytes 159752 | tf_op jit(solution)/shard_map/ppermute | solution.py:199
  27.1 5.5 %collective-permute-start.4 = (bf16[208,128]{1,0:T(8,128)(2,1)S(1)}, bf16[208,128]{1,0:T(8,128)(2,1)S(1)}, u32[]{:S(2)}, u32[]{:S(2)}) collective-permute-start(bf16[208,128]{1,0:T(8,128)(2,1)S(1)} %get-tuple-element.34), channel_id=1, source_target_pairs={{0,12},{4,16},{8,20},{12,24},{16,28},{20,0},{24,4},{28,8},{1,13},{... | collective-permute-start | bytes 159752 | tf_op jit(solution)/shard_map/ppermute | solution.py:199
  29.2 4.1 %collective-permute-start.5 = (bf16[208,128]{1,0:T(8,128)(2,1)S(1)}, bf16[208,128]{1,0:T(8,128)(2,1)S(1)}, u32[]{:S(2)}, u32[]{:S(2)}) collective-permute-start(bf16[208,128]{1,0:T(8,128)(2,1)S(1)} %get-tuple-element.35), channel_id=1, source_target_pairs={{0,16},{4,20},{8,24},{12,28},{16,0},{20,4},{24,8},{28,12},{1,17},{... | collective-permute-start | bytes 159752 | tf_op jit(solution)/shard_map/ppermute | solution.py:199
  29.9 3.6 %collective-permute-start.6 = (bf16[208,128]{1,0:T(8,128)(2,1)S(1)}, bf16[208,128]{1,0:T(8,128)(2,1)S(1)}, u32[]{:S(2)}, u32[]{:S(2)}) collective-permute-start(bf16[208,128]{1,0:T(8,128)(2,1)S(1)} %get-tuple-element.36), channel_id=1, source_target_pairs={{0,20},{4,24},{8,28},{12,0},{16,4},{20,8},{24,12},{28,16},{1,21},{... | collective-permute-start | bytes 159752 | tf_op jit(solution)/shard_map/ppermute | solution.py:199
  30.0 4.6 %collective-permute-start.7 = (bf16[208,128]{1,0:T(8,128)(2,1)S(1)}, bf16[208,128]{1,0:T(8,128)(2,1)S(1)}, u32[]{:S(2)}, u32[]{:S(2)}) collective-permute-start(bf16[208,128]{1,0:T(8,128)(2,1)S(1)} %get-tuple-element.37), channel_id=1, source_target_pairs={{0,24},{4,28},{8,0},{12,4},{16,8},{20,12},{24,16},{28,20},{1,25},{... | collective-permute-start | bytes 159752 | tf_op jit(solution)/shard_map/ppermute | solution.py:199
  31.3 3.3 %collective-permute-start.8 = (bf16[208,128]{1,0:T(8,128)(2,1)S(1)}, bf16[208,128]{1,0:T(8,128)(2,1)S(1)}, u32[]{:S(2)}, u32[]{:S(2)}) collective-permute-start(bf16[208,128]{1,0:T(8,128)(2,1)S(1)} %get-tuple-element.38), channel_id=1, source_target_pairs={{0,28},{4,0},{8,4},{12,8},{16,12},{20,16},{24,20},{28,24},{1,29},{... | collective-permute-start | bytes 159752 | tf_op jit(solution)/shard_map/ppermute | solution.py:199
  35.2 6.2 %collective-permute-start.9 = (bf16[64,128]{1,0:T(8,128)(2,1)S(1)}, bf16[64,128]{1,0:T(8,128)(2,1)S(1)}, u32[]{:S(2)}, u32[]{:S(2)}) collective-permute-start(bf16[64,128]{1,0:T(8,128)(2,1)S(1)} %get-tuple-element.40), channel_id=1, source_target_pairs={{0,1},{1,2},{2,3},{3,0},{4,5},{5,6},{6,7},{7,4},{8,9},{9,10},{10,1... | collective-permute-start | bytes 49160 | tf_op jit(solution)/shard_map/ppermute | solution.py:199
  36.4 5.7 %collective-permute-start.10 = (bf16[64,128]{1,0:T(8,128)(2,1)S(1)}, bf16[64,128]{1,0:T(8,128)(2,1)S(1)}, u32[]{:S(2)}, u32[]{:S(2)}) collective-permute-start(bf16[64,128]{1,0:T(8,128)(2,1)S(1)} %get-tuple-element.41), channel_id=1, source_target_pairs={{0,2},{1,3},{2,0},{3,1},{4,6},{5,7},{6,4},{7,5},{8,10},{9,11},{10,... | collective-permute-start | bytes 49160 | tf_op jit(solution)/shard_map/ppermute | solution.py:199
  40.2 3.7 %collective-permute-start.11 = (bf16[64,128]{1,0:T(8,128)(2,1)S(1)}, bf16[64,128]{1,0:T(8,128)(2,1)S(1)}, u32[]{:S(2)}, u32[]{:S(2)}) collective-permute-start(bf16[64,128]{1,0:T(8,128)(2,1)S(1)} %get-tuple-element.42), channel_id=1, source_target_pairs={{0,3},{1,0},{2,1},{3,2},{4,7},{5,4},{6,5},{7,6},{8,11},{9,8},{10,9... | collective-permute-start | bytes 49160 | tf_op jit(solution)/shard_map/ppermute | solution.py:199

commit v2 on v1

v2 whole, which is shorter than its diff:
```python
import functools

import jax
import jax.numpy as jnp
from jax import lax
from jax.experimental import pallas as pl
from jax.experimental.pallas import tpu as pltpu
from jax.sharding import PartitionSpec as P

eps = 1e-05
f32 = jnp.float32
bf16 = jnp.bfloat16
HBM = pl.BlockSpec(memory_space=pltpu.HBM)
VMEM = pl.BlockSpec(memory_space=pltpu.VMEM)
PARAMS = pltpu.CompilerParams(vmem_limit_bytes=24 * 1024 * 1024)


def nn(a, b):
    return lax.dot_general(a, b, (((1,), (0,)), ((), ())), preferred_element_type=f32)


def nt(a, b):
    return lax.dot_general(a, b, (((1,), (1,)), ((), ())), preferred_element_type=f32)


def tn(a, b):
    return lax.dot_general(a, b, (((0,), (0,)), ((), ())), preferred_element_type=f32)


def normalize(flat):
    values = flat.astype(f32)
    centre = values - jnp.mean(values, axis=-1, keepdims=True)
    scale_inv = lax.rsqrt(jnp.mean(centre * centre, axis=-1, keepdims=True) + eps)
    return centre * scale_inv, scale_inv


def sigmoid(v):
    return 0.5 * jnp.tanh(0.5 * v) + 0.5


def chunks_of(size, most):
    step = most if size % most == 0 else size
    return [(at, step) for at in range(0, size, step)]


def partner(s, p, n):
    if n & (n - 1) == 0:
        return s ^ p
    return (s + p) % n if isinstance(s, int) else lax.rem(s + p, n)


def lane_packs(bins, side):
    packs = max(1, 128 // bins)
    return packs if (side // packs) % 16 == 0 else 1


def forward_kernel(q, pair_hbm, gate_hbm, up_hbm, out_hbm, head_hbm, updated, logits, *rest):
    sends, (pair, w_gate, w_up, w_out, w_head, halves, sems) = rest[:q], rest[q:]
    copies = [
        pltpu.make_async_copy(source, target, sems.at[i])
        for i, (source, target) in enumerate(
            ((pair_hbm, pair), (gate_hbm, w_gate), (up_hbm, w_up), (out_hbm, w_out), (head_hbm, w_head))
        )
    ]
    for copy in copies:
        copy.start()
    count, width = pair.shape
    bins = w_head.shape[0]
    side = count // q
    edge = 1
    while edge * edge < side:
        edge *= 2
    shift = edge.bit_length() - 1
    out_row = lax.broadcasted_iota(jnp.int32, (side, side), 0)
    in_row = lax.broadcasted_iota(jnp.int32, (side, side), 1)
    wanted = ((out_row & (edge - 1)) << shift) | (out_row >> shift)
    swap = jnp.where(in_row == wanted, 1.0, 0.0).astype(bf16)
    copies[0].wait()
    flat = pair[...]
    inputs = normalize(flat)[0].astype(bf16)
    total = flat.astype(f32)
    copies[1].wait()
    copies[2].wait()
    copies[3].wait()
    for at, step in chunks_of(w_gate.shape[1], 256):
        gate = nn(inputs, w_gate[:, at : at + step])
        upper = nn(inputs, w_up[:, at : at + step])
        hidden = (gate * sigmoid(gate) * upper).astype(bf16)
        total = total + nn(hidden, w_out[at : at + step, :])
    upd = total.astype(bf16)
    updated[...] = upd
    copies[4].wait()
    logit = nt(upd, w_head[...]).astype(bf16)
    logits[...] = logit
    blocks = logit.reshape(edge, q, edge, bins)
    packs = lane_packs(bins, side)
    deep = side // packs
    for k in range(q):
        piece = nn(swap, blocks[:, k].reshape(side, bins))
        if packs > 1:
            piece = jnp.concatenate([piece[u * deep : (u + 1) * deep] for u in range(packs)], axis=1)
        halves[k] = piece.astype(bf16)
    first = lax.rem(lax.axis_index("row"), q)
    for p in range(q):
        sends[p][...] = halves[lax.rem(first + p, q)]


def prepare_kernel(pair, updated, w_gate, w_up, inputs_t, updated_t, hidden, slope, swish, normed, scale):
    normal, scale_inv = normalize(pair[...])
    normed[...] = normal
    scale[...] = jnp.broadcast_to(scale_inv, scale.shape)
    inputs = normal.astype(bf16)
    inputs_t[...] = inputs.T
    updated_t[...] = updated[...].T
    for at, step in chunks_of(w_gate.shape[1], 256):
        span = slice(at, at + step)
        gate = nn(inputs, w_gate[:, span])
        upper = nn(inputs, w_up[:, span])
        sigma = sigmoid(gate)
        swished = gate * sigma
        swish[:, span] = swished
        hidden[:, span] = (swished * upper).astype(bf16)
        slope[:, span] = upper * sigma * (1.0 + gate * (1.0 - sigma))


def backward_kernel(q, packed, inputs_t, updated_t, hidden, slope, swish, logits, onehot, w_out, w_head, *rest):
    got, (d_updated, d_gate, d_up, *hot), mirrored, slots = rest[:q], rest[q:-2], rest[-2], rest[-1]
    count, bins = logits.shape
    width, units = inputs_t.shape[0], hidden.shape[1]
    edge = mirrored.shape[0]
    side = count // q
    packs = lane_packs(bins, side)
    own = lax.rem(lax.axis_index("row"), q)
    for p in range(q):
        h = lax.rem(own + q - p, q)
        piece = got[p][...]
        for u in range(packs):
            mirrored[u * (edge // packs) : (u + 1) * (edge // packs), h] = (
                piece[:, u * bins : (u + 1) * bins].astype(f32).reshape(edge // packs, edge, bins)
            )
    summed = logits[...].astype(f32) + mirrored[...].reshape(count, bins)
    powers = jnp.exp(summed - jnp.max(summed, axis=-1, keepdims=True))
    probs = powers / jnp.sum(powers, axis=-1, keepdims=True)
    grad_sym = (probs - onehot[...].astype(f32)).astype(bf16)
    cotangent = (grad_sym.astype(f32) * 2.0).astype(bf16)
    d_upd = nn(cotangent, w_head[...])
    d_updated[...] = d_upd
    d_upd_b = d_upd.astype(bf16)
    d_upd_t = d_upd_b.T
    gate_terms, up_terms, out_terms = [], [], []
    for at, step in chunks_of(units, 256):
        span = slice(at, at + step)
        d_hidden = nt(d_upd_b, w_out[span, :])
        d_gate_part = (d_hidden * slope[:, span]).astype(bf16)
        d_up_part = (d_hidden * swish[:, span]).astype(bf16)
        d_gate[:, span] = d_gate_part
        d_up[:, span] = d_up_part
        gate_terms.append(nn(inputs_t[...], d_gate_part))
        up_terms.append(nn(inputs_t[...], d_up_part))
        out_terms.append(nn(d_upd_t, hidden[:, span]))
    gate_term, up_term, out_term = (jnp.concatenate(t, axis=1) for t in (gate_terms, up_terms, out_terms))
    head_term = nn(updated_t[...], cotangent)
    if not packed:
        for ref, term in zip(hot, (gate_term, up_term, out_term, head_term)):
            ref[...] = term.astype(bf16)
        return
    nrow, ncol = packed
    groups = nrow // q
    lanes, part, tall = units // ncol, width // nrow, units // nrow
    deep = width // q
    for k in range(q):
        for a in range(groups):
            r = a * q + k
            at = 0
            for term in (gate_term, up_term):
                for c in range(ncol):
                    piece = term[r * part : (r + 1) * part, c * lanes : (c + 1) * lanes]
                    slots[k, a, at : at + part] = piece.astype(bf16)
                    at += part
            pieces = [out_term[u * deep : (u + 1) * deep, r * tall : (r + 1) * tall] for u in range(q)]
            slots[k, a, at : at + deep] = jnp.concatenate(pieces, axis=1).astype(bf16)
            at += deep
            piece = head_term[r * part : (r + 1) * part, :]
            piece = jnp.concatenate([piece, jnp.zeros((part, lanes - bins), f32)], axis=1)
            slots[k, a, at : at + part] = piece.astype(bf16)
    for p in range(q):
        hot[p][...] = slots[partner(own, p, q)]


def input_kernel(d_gate, d_up, d_updated, normed, scale, w_gate, w_up, d_pair):
    d_inputs = nt(d_gate[...], w_gate[...]) + nt(d_up[...], w_up[...])
    normal = normed[...]
    d_norm = (
        d_inputs
        - jnp.mean(d_inputs, axis=-1, keepdims=True)
        - normal * jnp.mean(d_inputs * normal, axis=-1, keepdims=True)
    ) * scale[...]
    d_pair[...] = (d_updated[...] + d_norm).astype(bf16)


def core_sum_kernel(q, groups, *rest):
    terms, hot = rest[:q], rest[q:]
    mine = lax.axis_index("row") // q
    for p in range(groups):
        a = partner(mine, p, groups)
        total = terms[0][a].astype(f32)
        for term in terms[1:]:
            total = total + term[a].astype(f32)
        hot[p][...] = total.astype(bf16)


def chip_sum_kernel(q, groups, ncol, shapes, *rest):
    terms, hot, slots = rest[:groups], rest[groups:-1], rest[-1]
    part, lanes, deep, tall, few = shapes
    total = terms[0][...].astype(f32)
    for term in terms[1:]:
        total = total + term[...].astype(f32)
    at = 2 * ncol * part
    out = total[at : at + deep]
    head = total[at + deep : at + deep + part]
    narrow = deep * q // ncol
    fold = lanes // tall
    short = narrow // fold
    for c in range(ncol):
        slots[c, 0:part] = total[c * part : (c + 1) * part].astype(bf16)
        slots[c, part : 2 * part] = total[(ncol + c) * part : (ncol + c + 1) * part].astype(bf16)
        u, top = (c * narrow) // deep, (c * narrow) % deep
        block = out[top : top + narrow, u * tall : (u + 1) * tall]
        block = jnp.concatenate([block[v * short : (v + 1) * short] for v in range(fold)], axis=1)
        slots[c, 2 * part : 2 * part + short] = block.astype(bf16)
        piece = jnp.concatenate([head[:, c * few : (c + 1) * few], jnp.zeros((part, lanes - few), f32)], axis=1)
        slots[c, 2 * part + short : 3 * part + short] = piece.astype(bf16)
    for p in range(ncol):
        hot[p][...] = slots[partner(lax.axis_index("col"), p, ncol)]


def col_sum_kernel(shapes, factor, *rest):
    terms, (gate, up, out, head) = rest[:-4], rest[-4:]
    part, lanes, tall, few = shapes
    total = terms[0][...].astype(f32)
    for term in terms[1:]:
        total = total + term[...].astype(f32)
    total = total * factor
    fold = lanes // tall
    short = out.shape[0] // fold
    gate[...] = total[0:part]
    up[...] = total[part : 2 * part]
    for v in range(fold):
        out[v * short : (v + 1) * short, :] = total[2 * part : 2 * part + short, v * tall : (v + 1) * tall]
    head[...] = total[2 * part + short : 3 * part + short, 0:few]


def shaped(shape, kind):
    return jax.ShapeDtypeStruct(shape, kind)


def cost(flops, moved):
    return pl.CostEstimate(flops=flops, bytes_accessed=moved, transcendentals=0)


def body(pair, targets, w_gate, w_up, w_out, w_head):
    rows, cols, width = pair.shape
    units = w_gate.shape[1]
    bins = w_head.shape[1]
    count = rows * cols
    nrow, ncol = lax.axis_size("row"), lax.axis_size("col")
    q = nrow // ncol
    groups = nrow // q
    side = count // q
    packs = lane_packs(bins, side)
    flat = pair.reshape(count, width)
    head_t = w_head.T
    piece = (side // packs, bins * packs)

    updated, logits, *sends = pl.pallas_call(
        functools.partial(forward_kernel, q),
        out_shape=[shaped((count, width), bf16), shaped((count, bins), bf16)] + [shaped(piece, bf16)] * q,
        in_specs=[HBM] * 5,
        out_specs=[VMEM] * (2 + q),
        scratch_shapes=[
            pltpu.VMEM((count, width), bf16),
            pltpu.VMEM(w_gate.shape, bf16),
            pltpu.VMEM(w_up.shape, bf16),
            pltpu.VMEM(w_out.shape, bf16),
            pltpu.VMEM(head_t.shape, bf16),
            pltpu.VMEM((q, *piece), bf16),
            pltpu.SemaphoreType.DMA((5,)),
        ],
        compiler_params=PARAMS,
        name="forward",
    )(*(pltpu.with_memory_space_constraint(x, pltpu.HBM) for x in (flat, w_gate, w_up, w_out, head_t)))

    got = []
    for p in range(q):
        pairs = [
            (r * ncol + c, (q * c + (r % q + p) % q) * ncol + r // q) for r in range(nrow) for c in range(ncol)
        ]
        got.append(lax.ppermute(sends[p], ("row", "col"), pairs))
    onehot = (targets.reshape(count)[:, None] == jnp.arange(bins, dtype=jnp.int32)[None, :]).astype(bf16)
    inputs_t, updated_t, hidden, slope, swish, normed, scale = pl.pallas_call(
        prepare_kernel,
        out_shape=[
            shaped((width, count), bf16),
            shaped((width, count), bf16),
            shaped((count, units), bf16),
            shaped((count, units), f32),
            shaped((count, units), f32),
            shaped((count, width), f32),
            shaped((count, width), f32),
        ],
        in_specs=[VMEM] * 4,
        out_specs=[VMEM] * 7,
        compiler_params=PARAMS,
        cost_estimate=cost(4 * count * width * units, 4 * count * units),
        name="prepare",
    )(flat, updated, w_gate, w_up)

    part, tall, few = width // nrow, units // nrow, bins // ncol
    lanes, deep = units // ncol, width // q
    fits = (
        part % 16 == 0 and lanes == 128 and tall * q == lanes and bins <= lanes and deep % (width // ncol) == 0
        and (width // ncol * tall // lanes) % 16 == 0
    )
    height = 2 * ncol * part + deep + part
    if fits:
        hot_shapes = [shaped((groups, height, lanes), bf16)] * q
        slots = pltpu.VMEM((q, groups, height, lanes), bf16)
    else:
        hot_shapes = [shaped((width, n), bf16) for n in (units, units, units, bins)]
        slots = pltpu.VMEM((16, 128), bf16)
    d_updated, d_gate, d_up, *hot = pl.pallas_call(
        functools.partial(backward_kernel, q, (nrow, ncol) if fits else None),
        out_shape=[shaped((count, width), f32)] + [shaped((count, units), bf16)] * 2 + hot_shapes,
        in_specs=[VMEM] * (9 + q),
        out_specs=[VMEM] * (3 + len(hot_shapes)),
        scratch_shapes=[pltpu.VMEM((rows, q, cols // q, bins), f32), slots],
        compiler_params=PARAMS,
        cost_estimate=cost(8 * count * width * units, 4 * count * units),
        name="backward",
    )(inputs_t, updated_t, hidden, slope, swish, logits, onehot, w_out, head_t, *got)

    d_pair = pl.pallas_call(
        input_kernel,
        out_shape=shaped((count, width), bf16),
        in_specs=[VMEM] * 7,
        out_specs=VMEM,
        compiler_params=PARAMS,
        cost_estimate=cost(4 * count * width * units, 4 * count * units),
        name="d_inputs",
    )(d_gate, d_up, d_updated, normed, scale, w_gate, w_up)
    d_pair = d_pair.reshape(rows, cols, width)
    factor = 1.0 / (rows * nrow)
    if not fits:
        owned = []
        hot[2] = hot[2].T
        for term in hot:
            mine = lax.psum_scatter(term, "row", scatter_dimension=0, tiled=True).astype(f32)
            owned.append(lax.psum_scatter(mine, "col", scatter_dimension=1, tiled=True) * factor)
        return (d_pair, *owned)

    terms = [hot[0]]
    for p in range(1, q):
        terms.append(lax.ppermute(hot[p], "row", [(s, s - s % q + partner(s % q, p, q)) for s in range(nrow)]))
    hot = pl.pallas_call(
        functools.partial(core_sum_kernel, q, groups),
        out_shape=[shaped((height, lanes), bf16)] * groups,
        in_specs=[VMEM] * q,
        out_specs=[VMEM] * groups,
        compiler_params=PARAMS,
        name="core_sum",
    )(*terms)
    terms = [hot[0]]
    for p in range(1, groups):
        terms.append(lax.ppermute(hot[p], "row", [(s, partner(s // q, p, groups) * q + s % q) for s in range(nrow)]))
    short = 3 * part + width // ncol * tall // lanes
    hot = pl.pallas_call(
        functools.partial(chip_sum_kernel, q, groups, ncol, (part, lanes, deep, tall, few)),
        out_shape=[shaped((short, lanes), bf16)] * ncol,
        in_specs=[VMEM] * groups,
        out_specs=[VMEM] * ncol,
        scratch_shapes=[pltpu.VMEM((ncol, short, lanes), bf16)],
        compiler_params=PARAMS,
        name="chip_sum",
    )(*terms)
    terms = [hot[0]]
    for p in range(1, ncol):
        terms.append(lax.ppermute(hot[p], "col", [(s, partner(s, p, ncol)) for s in range(ncol)]))
    gate, up, out, head = pl.pallas_call(
        functools.partial(col_sum_kernel, (part, lanes, tall, few), factor),
        out_shape=[
            shaped((part, lanes), f32),
            shaped((part, lanes), f32),
            shaped((width // ncol, tall), f32),
            shaped((part, few), f32),
        ],
        in_specs=[VMEM] * ncol,
        out_specs=[VMEM] * 4,
        compiler_params=PARAMS,
        name="col_sum",
    )(*terms)
    return d_pair, gate, up, out.T, head


def solution(mesh):
    placed = (P("row", "col", None), P("row", "col"), P(), P(), P(), P())
    return jax.shard_map(
        body,
        mesh=mesh,
        in_specs=placed,
        out_specs=(P("row", "col", None), P("row", "col"), P("row", "col"), P("row", "col"), P("row", "col")),
        check_vma=False,
    )
```

time: 45.5 us -> 35.7 us (0.78)
  starting transfers between devices: 26.3 us -> 20.6 us
  local copies, waits for them, and re-layouts: 5.22 us -> 0.11 us
  waiting for transfers between devices: 6.35 us -> 7.15 us
    ppermute x10 -> x7, starting transfers between devices: 25 us -> 19.2 us  [the longest x3 14.7 us: body(): lax.ppermute(hot[p], 'row', [(s, partner(s // q, p, groups) * q + s % q)...]
    unnamed x22 -> x12, local copies, waits for them, and re-layouts: 5.14 us -> 0.03 us
    pallas_call x1, Pallas kernels: 3.17 us -> 1.41 us  [body(): pl.pallas_call(functools.partial(backward_kernel, q, (nrow, ncol) if fits...]
    pallas_call x2 -> x5, Pallas kernels: 1.27 us -> 2.86 us  [the longest x1 1.17 us: body(): pl.pallas_call(input_kernel, out_shape=shaped((count, width), bf16), in_s...]
    ppermute x10 -> x7, waiting for transfers between devices: 5.68 us -> 7.14 us  [the longest x3 5.03 us: body(): lax.ppermute(hot[p], 'row', [(s, partner(s // q, p, groups) * q + s % q)...]
    ppermute x2, waiting for transfers between devices: 0.67 us -> 0.01 us  [body(): got.append(lax.ppermute(sends[p], ('row', 'col'), pairs))]
    pallas_call x1, Pallas kernels: 1.95 us -> 2.5 us  [body(): pl.pallas_call(functools.partial(forward_kernel, q), out_shape=[shaped((c...]
  transfers between devices with their start and end apart: 12 -> 9, of which waited for: 7 -> 4; matrix products, arithmetic and copies ran while one was open for 0% -> 1% of each run, Pallas kernels for 0% -> 6%
where the time goes in v2:
time: 35.7 us; the launch traced here: 35.5 us
  starting transfers between devices  20.6 us (58%)
  waiting for transfers between devices  7.15 us (20%)
  Pallas kernels  6.77 us (19%)
  between operations  0.79 us (2%)
    ppermute x3, starting transfers between devices, body(): lax.ppermute(hot[p], 'row', [(s, partner(s // q, p, groups) * q + s % q)...  14.7 us
    ppermute x3, waiting for transfers between devices, body(): lax.ppermute(hot[p], 'row', [(s, partner(s // q, p, groups) * q + s % q)...  5.03 us
    ppermute x3, starting transfers between devices, body(): lax.ppermute(hot[p], 'col', [(s, partner(s, p, ncol)) for s in range(ncol)])  4.44 us
    pallas_call x1, Pallas kernels, body(): pl.pallas_call(functools.partial(forward_kernel, q), out_shape=[shaped((c...  2.5 us
    pallas_call x1, Pallas kernels, body(): pl.pallas_call(functools.partial(backward_kernel, q, (nrow, ncol) if fits...  1.41 us
    ppermute x1, waiting for transfers between devices, body(): lax.ppermute(hot[p], 'row', [(s, s - s % q + partner(s % q, p, q)) for s...  1.4 us
    ppermute x2, starting transfers between devices, body(): got.append(lax.ppermute(sends[p], ('row', 'col'), pairs))  1.32 us
    pallas_call x1, Pallas kernels, body(): pl.pallas_call(input_kernel, out_shape=shaped((count, width), bf16), in_s...  1.17 us
  transfers between devices with their start and end apart: 9, of which 4 were waited for; matrix products, arithmetic and copies ran while one was open for 1% of the time, Pallas kernels for 6%

profile of v2, /device:TPU:0, one launch (start us, length us, event | category | flops | bytes accessed | tf_op | source)
XLA Modules:
  0.0 35.5 jit_solution(5007343218599370894)
XLA Ops:
  0.6 0.0 copy-start.5
  0.6 0.0 copy-start.1
  0.7 0.0 copy-start.3
  0.7 2.5 %forward.1 = (bf16[512,128]{1,0:T(8,128)(2,1)S(1)}, bf16[512,64]{1,0:T(8,128)(2,1)S(1)}, bf16[128,128]{1,0:T(8,128)(2,1)S(1)}, bf16[128,128]{1,0:T(8,128)(2,1)S(1)}) custom-call(bf16[512,128]{1,0:T(8,128)(2,1)} %bitcast.4, bf16[128,512]{1,0:T(8,128)(2,1)} %w_gate.3, bf16[128,512]{1,0:T(8,128)(2,1)} %w_up.3, bf16[512,128]{1,0:T(8,128)(2,1)} %w_out.1, ...), custom_call_target="tpu_custom_call" | custom-call | tf_op jit(solution)/shard_map/forward/pallas_call | solution.py:275
  3.2 0.0 copy-start
  3.2 0.8 %collective-permute-start = (bf16[128,128]{1,0:T(8,128)(2,1)S(1)}, bf16[128,128]{1,0:T(8,128)(2,1)S(1)}, u32[]{:S(2)}, u32[]{:S(2)}) collective-permute-start(bf16[128,128]{1,0:T(8,128)(2,1)S(1)} %get-tuple-element.40), channel_id=1, source_target_pairs={{0,0},{1,8},{2,16},{3,24},{4,4},{5,12},{6,20},{7,28},{8,1},{9,9},{... | collective-permute-start | bytes 98312 | tf_op jit(solution)/shard_map/ppermute | solution.py:298
  4.0 0.5 %collective-permute-start.1 = (bf16[128,128]{1,0:T(8,128)(2,1)S(1)}, bf16[128,128]{1,0:T(8,128)(2,1)S(1)}, u32[]{:S(2)}, u32[]{:S(2)}) collective-permute-start(bf16[128,128]{1,0:T(8,128)(2,1)S(1)} %get-tuple-element.41), channel_id=1, source_target_pairs={{0,4},{1,12},{2,20},{3,28},{4,0},{5,8},{6,16},{7,24},{8,5},{9,13},... | collective-permute-start | bytes 98312 | tf_op jit(solution)/shard_map/ppermute | solution.py:298
  4.5 0.0 copy-done.5
  4.5 0.1 eq.15
  4.6 0.1 fusion.onehot
  4.7 0.0 copy-done.1
  4.7 0.0 copy-done.3
  4.8 0.0 copy-done
  4.8 0.0 copy-start.2
  4.8 0.0 copy-start.4
  4.8 0.9 %prepare.1 = (bf16[128,512]{1,0:T(8,128)(2,1)S(1)}, bf16[128,512]{1,0:T(8,128)(2,1)S(1)}, bf16[512,512]{1,0:T(8,128)(2,1)S(1)}, f32[512,512]{1,0:T(8,128)S(1)}, ...) custom-call(bf16[512,128]{1,0:T(8,128)(2,1)S(1)} %bitcast.5, ...), custom_call_target="tpu_custom_call" | custom-call | flops 134217728 | bytes 1048576 | tf_op jit(solution)/shard_map/prepare/pallas_call | solution.py:300
  5.7 0.0 collective-permute-done.rest_0_
  5.7 0.0 collective-permute-done.1.rest_1_
  5.7 0.0 copy-done.2
  5.7 0.0 copy-done.4
  5.7 1.4 %backward.1 = (f32[512,128]{1,0:T(8,128)S(1)}, bf16[512,512]{1,0:T(8,128)(2,1)S(1)}, bf16[512,512]{1,0:T(8,128)(2,1)S(1)}, bf16[4,208,128]{2,1,0:T(8,128)(2,1)S(1)}, bf16[4,208,128]{2,1,0:T(8,128)(2,1)S(1)}) custom-call(bf16[128,512]{1,0:T(8,128)(2,1)S(1)} %get-tuple-element.34.inputs_t, bf16[128,512]{1,0:T(8,128)(2,1)S(1)} %get-tuple-element.35.updated_t, ...), custom_call_target="tpu_custom_call" | custom-call | flops 268435456 | bytes 1048576 | tf_op jit(solution)/shard_map/backward/pallas_call | solution.py:331
  7.1 0.1 collective-permute-start.2
  7.3 1.4 %collective-permute-done.2.rest_1_ = bf16[4,208,128]{2,1,0:T(8,128)(2,1)S(1)} collective-permute-done((bf16[4,208,128]{2,1,0:T(8,128)(2,1)S(1)}, bf16[4,208,128]{2,1,0:T(8,128)(2,1)S(1)}, u32[]{:S(2)}, u32[]{:S(2)}) %collective-permute-start.2) | collective-permute-done | bytes 213024 | tf_op jit(solution)/shard_map/ppermute | solution.py:363
  8.6 0.1 core_sum.1
  8.7 9.2 %collective-permute-start.3 = (bf16[208,128]{1,0:T(8,128)(2,1)S(1)}, bf16[208,128]{1,0:T(8,128)(2,1)S(1)}, u32[]{:S(2)}, u32[]{:S(2)}) collective-permute-start(bf16[208,128]{1,0:T(8,128)(2,1)S(1)} %get-tuple-element.50), channel_id=1, source_target_pairs={{0,8},{4,12},{8,0},{12,4},{16,24},{20,28},{24,16},{28,20},{1,9},{5... | collective-permute-start | bytes 159752 | tf_op jit(solution)/shard_map/ppermute | solution.py:374
  17.9 5.5 %collective-permute-start.4 = (bf16[208,128]{1,0:T(8,128)(2,1)S(1)}, bf16[208,128]{1,0:T(8,128)(2,1)S(1)}, u32[]{:S(2)}, u32[]{:S(2)}) collective-permute-start(bf16[208,128]{1,0:T(8,128)(2,1)S(1)} %get-tuple-element.51), channel_id=1, source_target_pairs={{0,16},{4,20},{8,24},{12,28},{16,0},{20,4},{24,8},{28,12},{1,17},{... | collective-permute-start | bytes 159752 | tf_op jit(solution)/shard_map/ppermute | solution.py:374
  23.4 0.0 collective-permute-start.5
  23.4 0.0 collective-permute-done.3.rest_1_
  23.4 2.1 %collective-permute-done.4.rest_2_ = bf16[208,128]{1,0:T(8,128)(2,1)S(1)} collective-permute-done((bf16[208,128]{1,0:T(8,128)(2,1)S(1)}, bf16[208,128]{1,0:T(8,128)(2,1)S(1)}, u32[]{:S(2)}, u32[]{:S(2)}) %collective-permute-start.4) | collective-permute-done | bytes 53280 | tf_op jit(solution)/shard_map/ppermute | solution.py:374
  25.5 2.9 %collective-permute-done.5.rest_3_ = bf16[208,128]{1,0:T(8,128)(2,1)S(1)} collective-permute-done((bf16[208,128]{1,0:T(8,128)(2,1)S(1)}, bf16[208,128]{1,0:T(8,128)(2,1)S(1)}, u32[]{:S(2)}, u32[]{:S(2)}) %collective-permute-start.5) | collective-permute-done | bytes 53280 | tf_op jit(solution)/shard_map/ppermute | solution.py:374
  28.4 0.1 chip_sum.1
  28.5 0.1 collective-permute-start.6
  28.6 0.3 collective-permute-start.7
  28.9 4.1 %collective-permute-start.8 = (bf16[64,128]{1,0:T(8,128)(2,1)S(1)}, bf16[64,128]{1,0:T(8,128)(2,1)S(1)}, u32[]{:S(2)}, u32[]{:S(2)}) collective-permute-start(bf16[64,128]{1,0:T(8,128)(2,1)S(1)} %get-tuple-element.56), channel_id=1, source_target_pairs={{0,3},{1,2},{2,1},{3,0},{4,7},{5,6},{6,5},{7,4},{8,11},{9,10},{10,... | collective-permute-start | bytes 49160 | tf_op jit(solution)/shard_map/ppermute | solution.py:387
  33.0 1.2 %d_inputs.1 = bf16[512,128]{1,0:T(8,128)(2,1)} custom-call(bf16[512,512]{1,0:T(8,128)(2,1)S(1)} %get-tuple-element.42.d_gate, bf16[512,512]{1,0:T(8,128)(2,1)S(1)} %get-tuple-element.43.d_up, f32[512,128]{1,0:T(8,128)S(1)} %get-tuple-element.44.d_updated, f32[512,128]{1,0:T(8,128)S(1)} %get-tuple-element.45.normed, f32[512,128]{1,0:T(8,128)S(1)} %get-tuple-element.46.scale, ...), custom_call_target="tpu_custom_call" | custom-call | flops 134217728 | bytes 1048576 | tf_op jit(solution)/shard_map/d_inputs/pallas_call | solution.py:342
  34.1 0.0 collective-permute-done.6.rest_1_
  34.1 0.0 collective-permute-done.7.rest_2_
  34.1 0.7 %collective-permute-done.8.rest_3_ = bf16[64,128]{1,0:T(8,128)(2,1)S(1)} collective-permute-done((bf16[64,128]{1,0:T(8,128)(2,1)S(1)}, bf16[64,128]{1,0:T(8,128)(2,1)S(1)}, u32[]{:S(2)}, u32[]{:S(2)}) %collective-permute-start.8) | collective-permute-done | bytes 16416 | tf_op jit(solution)/shard_map/ppermute | solution.py:387
  34.8 0.7 %col_sum.1 = (f32[16,128]{1,0:T(8,128)}, f32[16,128]{1,0:T(8,128)}, f32[32,64]{1,0:T(8,128)}, f32[16,16]{1,0:T(8,128)}) custom-call(bf16[64,128]{1,0:T(8,128)(2,1)S(1)} %get-tuple-element.53.rest_0_, bf16[64,128]{1,0:T(8,128)(2,1)S(1)} %collective-permute-done.6.rest_1_, bf16[64,128]{1,0:T(8,128)(2,1)S(1)} %collective-permute-done.7.rest_2_, ...), custom_call_target="tpu_custom_call" | custom-call | tf_op jit(solution)/shard_map/col_sum/pallas_call | solution.py:388
Async XLA Ops:
  0.6 3.9 %copy-start.5 = (s32[16,32]{1,0:T(8,128)S(1)}, s32[16,32]{1,0:T(8,128)}, u32[]{:S(2)}) copy-start(s32[16,32]{1,0:T(8,128)} %param.7) | copy-start | bytes 6148
  0.6 4.1 %copy-start.1 = (bf16[128,512]{1,0:T(8,128)(2,1)S(1)}, bf16[128,512]{1,0:T(8,128)(2,1)}, u32[]{:S(2)}) copy-start(bf16[128,512]{1,0:T(8,128)(2,1)} %w_up.3) | copy-start | bytes 393220
  0.7 4.1 %copy-start.3 = (bf16[16,32,128]{2,1,0:T(8,128)(2,1)S(1)}, bf16[16,32,128]{2,1,0:T(8,128)(2,1)}, u32[]{:S(2)}) copy-start(bf16[16,32,128]{2,1,0:T(8,128)(2,1)} %param.6) | copy-start | bytes 393220
  3.2 1.6 %copy-start = (bf16[128,512]{1,0:T(8,128)(2,1)S(1)}, bf16[128,512]{1,0:T(8,128)(2,1)}, u32[]{:S(2)}) copy-start(bf16[128,512]{1,0:T(8,128)(2,1)} %w_gate.3) | copy-start | bytes 393220
  3.2 2.5 %collective-permute-start = (bf16[128,128]{1,0:T(8,128)(2,1)S(1)}, bf16[128,128]{1,0:T(8,128)(2,1)S(1)}, u32[]{:S(2)}, u32[]{:S(2)}) collective-permute-start(bf16[128,128]{1,0:T(8,128)(2,1)S(1)} %get-tuple-element.40), channel_id=1, source_target_pairs={{0,0},{1,8},{2,16},{3,24},{4,4},{5,12},{6,20},{7,28},{8,1},{9,9},{... | collective-permute-start | bytes 98312 | tf_op jit(solution)/shard_map/ppermute | solution.py:298
  4.0 1.7 %collective-permute-start.1 = (bf16[128,128]{1,0:T(8,128)(2,1)S(1)}, bf16[128,128]{1,0:T(8,128)(2,1)S(1)}, u32[]{:S(2)}, u32[]{:S(2)}) collective-permute-start(bf16[128,128]{1,0:T(8,128)(2,1)S(1)} %get-tuple-element.41), channel_id=1, source_target_pairs={{0,4},{1,12},{2,20},{3,28},{4,0},{5,8},{6,16},{7,24},{8,5},{9,13},... | collective-permute-start | bytes 98312 | tf_op jit(solution)/shard_map/ppermute | solution.py:298
  4.8 0.9 %copy-start.2 = (bf16[512,128]{1,0:T(8,128)(2,1)S(1)}, bf16[512,128]{1,0:T(8,128)(2,1)}, u32[]{:S(2)}) copy-start(bf16[512,128]{1,0:T(8,128)(2,1)} %w_out.1) | copy-start | bytes 393220
  4.8 0.9 %copy-start.4 = (bf16[128,64]{0,1:T(8,128)(2,1)S(1)}, bf16[128,64]{0,1:T(8,128)(2,1)}, u32[]{:S(2)}) copy-start(bf16[128,64]{0,1:T(8,128)(2,1)} %param.11) | copy-start | bytes 49156
  7.1 1.5 %collective-permute-start.2 = (bf16[4,208,128]{2,1,0:T(8,128)(2,1)S(1)}, bf16[4,208,128]{2,1,0:T(8,128)(2,1)S(1)}, u32[]{:S(2)}, u32[]{:S(2)}) collective-permute-start(bf16[4,208,128]{2,1,0:T(8,128)(2,1)S(1)} %get-tuple-element.48), channel_id=1, source_target_pairs={{0,4},{4,0},{8,12},{12,8},{16,20},{20,16},{24,28},{28,24},{1,5},{5... | collective-permute-start | bytes 638984 | tf_op jit(solution)/shard_map/ppermute | solution.py:363
  8.7 14.7 %collective-permute-start.3 = (bf16[208,128]{1,0:T(8,128)(2,1)S(1)}, bf16[208,128]{1,0:T(8,128)(2,1)S(1)}, u32[]{:S(2)}, u32[]{:S(2)}) collective-permute-start(bf16[208,128]{1,0:T(8,128)(2,1)S(1)} %get-tuple-element.50), channel_id=1, source_target_pairs={{0,8},{4,12},{8,0},{12,4},{16,24},{20,28},{24,16},{28,20},{1,9},{5... | collective-permute-start | bytes 159752 | tf_op jit(solution)/shard_map/ppermute | solution.py:374
  17.9 7.6 %collective-permute-start.4 = (bf16[208,128]{1,0:T(8,128)(2,1)S(1)}, bf16[208,128]{1,0:T(8,128)(2,1)S(1)}, u32[]{:S(2)}, u32[]{:S(2)}) collective-permute-start(bf16[208,128]{1,0:T(8,128)(2,1)S(1)} %get-tuple-element.51), channel_id=1, source_target_pairs={{0,16},{4,20},{8,24},{12,28},{16,0},{20,4},{24,8},{28,12},{1,17},{... | collective-permute-start | bytes 159752 | tf_op jit(solution)/shard_map/ppermute | solution.py:374
  23.4 5.0 %collective-permute-start.5 = (bf16[208,128]{1,0:T(8,128)(2,1)S(1)}, bf16[208,128]{1,0:T(8,128)(2,1)S(1)}, u32[]{:S(2)}, u32[]{:S(2)}) collective-permute-start(bf16[208,128]{1,0:T(8,128)(2,1)S(1)} %get-tuple-element.52), channel_id=1, source_target_pairs={{0,24},{4,28},{8,16},{12,20},{16,8},{20,12},{24,0},{28,4},{1,25},{... | collective-permute-start | bytes 159752 | tf_op jit(solution)/shard_map/ppermute | solution.py:374
  28.5 5.6 %collective-permute-start.6 = (bf16[64,128]{1,0:T(8,128)(2,1)S(1)}, bf16[64,128]{1,0:T(8,128)(2,1)S(1)}, u32[]{:S(2)}, u32[]{:S(2)}) collective-permute-start(bf16[64,128]{1,0:T(8,128)(2,1)S(1)} %get-tuple-element.54), channel_id=1, source_target_pairs={{0,1},{1,0},{2,3},{3,2},{4,5},{5,4},{6,7},{7,6},{8,9},{9,8},{10,11... | collective-permute-start | bytes 49160 | tf_op jit(solution)/shard_map/ppermute | solution.py:387
  28.6 5.6 %collective-permute-start.7 = (bf16[64,128]{1,0:T(8,128)(2,1)S(1)}, bf16[64,128]{1,0:T(8,128)(2,1)S(1)}, u32[]{:S(2)}, u32[]{:S(2)}) collective-permute-start(bf16[64,128]{1,0:T(8,128)(2,1)S(1)} %get-tuple-element.55), channel_id=1, source_target_pairs={{0,2},{1,3},{2,0},{3,1},{4,6},{5,7},{6,4},{7,5},{8,10},{9,11},{10,... | collective-permute-start | bytes 49160 | tf_op jit(solution)/shard_map/ppermute | solution.py:387
  28.9 6.0 %collective-permute-start.8 = (bf16[64,128]{1,0:T(8,128)(2,1)S(1)}, bf16[64,128]{1,0:T(8,128)(2,1)S(1)}, u32[]{:S(2)}, u32[]{:S(2)}) collective-permute-start(bf16[64,128]{1,0:T(8,128)(2,1)S(1)} %get-tuple-element.56), channel_id=1, source_target_pairs={{0,3},{1,2},{2,1},{3,0},{4,7},{5,6},{6,5},{7,4},{8,11},{9,10},{10,... | collective-permute-start | bytes 49160 | tf_op jit(solution)/shard_map/ppermute | solution.py:387

commit v3 on v2

--- a/solution.py
+++ b/solution.py
@@ -54,13 +54,12 @@
     return packs if (side // packs) % 16 == 0 else 1
 
 
-def forward_kernel(q, pair_hbm, gate_hbm, up_hbm, out_hbm, head_hbm, updated, logits, *rest):
-    sends, (pair, w_gate, w_up, w_out, w_head, halves, sems) = rest[:q], rest[q:]
+def forward_kernel(q, *refs):
+    sources, kept, (updated, logits) = refs[:6], refs[6:12], refs[12:14]
+    sends, (halves, sems) = refs[14 : 14 + q], refs[14 + q :]
+    pair, w_gate, w_up, w_out, w_head, _ = kept
     copies = [
-        pltpu.make_async_copy(source, target, sems.at[i])
-        for i, (source, target) in enumerate(
-            ((pair_hbm, pair), (gate_hbm, w_gate), (up_hbm, w_up), (out_hbm, w_out), (head_hbm, w_head))
-        )
+        pltpu.make_async_copy(source, target, sems.at[i]) for i, (source, target) in enumerate(zip(sources, kept))
     ]
     for copy in copies:
         copy.start()
@@ -103,6 +102,7 @@
     first = lax.rem(lax.axis_index("row"), q)
     for p in range(q):
         sends[p][...] = halves[lax.rem(first + p, q)]
+    copies[5].wait()
 
 
 def prepare_kernel(pair, updated, w_gate, w_up, inputs_t, updated_t, hidden, slope, swish, normed, scale):
@@ -272,23 +272,17 @@
     head_t = w_head.T
     piece = (side // packs, bins * packs)
 
-    updated, logits, *sends = pl.pallas_call(
+    sources = (flat, w_gate, w_up, w_out, head_t, targets)
+    kept = [shaped(x.shape, x.dtype) for x in sources]
+    flat, w_gate, w_up, w_out, head_t, targets, updated, logits, *sends = pl.pallas_call(
         functools.partial(forward_kernel, q),
-        out_shape=[shaped((count, width), bf16), shaped((count, bins), bf16)] + [shaped(piece, bf16)] * q,
-        in_specs=[HBM] * 5,
-        out_specs=[VMEM] * (2 + q),
-        scratch_shapes=[
-            pltpu.VMEM((count, width), bf16),
-            pltpu.VMEM(w_gate.shape, bf16),
-            pltpu.VMEM(w_up.shape, bf16),
-            pltpu.VMEM(w_out.shape, bf16),
-            pltpu.VMEM(head_t.shape, bf16),
-            pltpu.VMEM((q, *piece), bf16),
-            pltpu.SemaphoreType.DMA((5,)),
-        ],
+        out_shape=kept + [shaped((count, width), bf16), shaped((count, bins), bf16)] + [shaped(piece, bf16)] * q,
+        in_specs=[HBM] * 6,
+        out_specs=[VMEM] * (8 + q),
+        scratch_shapes=[pltpu.VMEM((q, *piece), bf16), pltpu.SemaphoreType.DMA((6,))],
         compiler_params=PARAMS,
         name="forward",
-    )(*(pltpu.with_memory_space_constraint(x, pltpu.HBM) for x in (flat, w_gate, w_up, w_out, head_t)))
+    )(*(pltpu.with_memory_space_constraint(x, pltpu.HBM) for x in sources))
 
     got = []
     for p in range(q):
@@ -370,7 +364,7 @@
         name="core_sum",
     )(*terms)
     terms = [hot[0]]
-    for p in range(1, groups):
+    for p in range(groups - 1, 0, -1):
         terms.append(lax.ppermute(hot[p], "row", [(s, partner(s // q, p, groups) * q + s % q) for s in range(nrow)]))
     short = 3 * part + width // ncol * tall // lanes
     hot = pl.pallas_call(
@@ -383,7 +377,7 @@
         name="chip_sum",
     )(*terms)
     terms = [hot[0]]
-    for p in range(1, ncol):
+    for p in range(ncol - 1, 0, -1):
         terms.append(lax.ppermute(hot[p], "col", [(s, partner(s, p, ncol)) for s in range(ncol)]))
     gate, up, out, head = pl.pallas_call(
         functools.partial(col_sum_kernel, (part, lanes, tall, few), factor),

time: 35.7 us -> 33.8 us (0.947)
  waiting for transfers between devices: 7.15 us -> 5.4 us
    ppermute x3, waiting for transfers between devices: 5.03 us -> 3.49 us  [body(): lax.ppermute(hot[p], 'row', [(s, partner(s // q, p, groups) * q + s % q)...]
  transfers between devices with their start and end apart: 9 -> 9, of which waited for: 4 -> 5; matrix products, arithmetic and copies ran while one was open for 1% -> 1% of each run, Pallas kernels for 6% -> 6%
where the time goes in v3:
time: 33.8 us; the launch traced here: 33.7 us
  starting transfers between devices  20.6 us (61%)
  Pallas kernels  6.73 us (20%)
  waiting for transfers between devices  5.4 us (16%)
  between operations  0.7 us (2%)
    ppermute x3, starting transfers between devices, body(): lax.ppermute(hot[p], 'row', [(s, partner(s // q, p, groups) * q + s % q)...  14.8 us
    ppermute x3, starting transfers between devices, body(): lax.ppermute(hot[p], 'col', [(s, partner(s, p, ncol)) for s in range(ncol)])  4.45 us
    ppermute x3, waiting for transfers between devices, body(): lax.ppermute(hot[p], 'row', [(s, partner(s // q, p, groups) * q + s % q)...  3.49 us
    pallas_call x1, Pallas kernels, body(): pl.pallas_call(functools.partial(forward_kernel, q), out_shape=kept + [sh...  2.45 us
    pallas_call x1, Pallas kernels, body(): pl.pallas_call(functools.partial(backward_kernel, q, (nrow, ncol) if fits...  1.41 us
    ppermute x1, waiting for transfers between devices, body(): lax.ppermute(hot[p], 'row', [(s, s - s % q + partner(s % q, p, q)) for s...  1.36 us
    ppermute x2, starting transfers between devices, body(): got.append(lax.ppermute(sends[p], ('row', 'col'), pairs))  1.19 us
    pallas_call x1, Pallas kernels, body(): pl.pallas_call(input_kernel, out_shape=shaped((count, width), bf16), in_s...  1.17 us
  transfers between devices with their start and end apart: 9, of which 5 were waited for; matrix products, arithmetic and copies ran while one was open for 1% of the time, Pallas kernels for 6%

profile of v3, /device:TPU:0, one launch (start us, length us, event | category | flops | bytes accessed | tf_op | source)
XLA Modules:
  0.0 33.7 jit_solution(2223489720226996941)
XLA Ops:
  0.6 2.5 %forward.1 = (bf16[512,128]{1,0:T(8,128)(2,1)S(1)}, bf16[128,512]{1,0:T(8,128)(2,1)S(1)}, bf16[128,512]{1,0:T(8,128)(2,1)S(1)}, bf16[512,128]{1,0:T(8,128)(2,1)S...) custom-call(bf16[512,128]{1,0:T(8,128)(2,1)} %bitcast.5, ...), custom_call_target="tpu_custom_call" | custom-call | tf_op jit(solution)/shard_map/forward/pallas_call | solution.py:277
  3.1 0.7 %collective-permute-start = (bf16[128,128]{1,0:T(8,128)(2,1)S(1)}, bf16[128,128]{1,0:T(8,128)(2,1)S(1)}, u32[]{:S(2)}, u32[]{:S(2)}) collective-permute-start(bf16[128,128]{1,0:T(8,128)(2,1)S(1)} %get-tuple-element.52), channel_id=1, source_target_pairs={{0,0},{1,8},{2,16},{3,24},{4,4},{5,12},{6,20},{7,28},{8,1},{9,9},{... | collective-permute-start | bytes 98312 | tf_op jit(solution)/shard_map/ppermute | solution.py:292
  3.8 0.5 %collective-permute-start.1 = (bf16[128,128]{1,0:T(8,128)(2,1)S(1)}, bf16[128,128]{1,0:T(8,128)(2,1)S(1)}, u32[]{:S(2)}, u32[]{:S(2)}) collective-permute-start(bf16[128,128]{1,0:T(8,128)(2,1)S(1)} %get-tuple-element.53), channel_id=1, source_target_pairs={{0,4},{1,12},{2,20},{3,28},{4,0},{5,8},{6,16},{7,24},{8,5},{9,13},... | collective-permute-start | bytes 98312 | tf_op jit(solution)/shard_map/ppermute | solution.py:292
  4.3 0.1 eq.15
  4.4 0.1 fusion.onehot
  4.5 0.9 %prepare.1 = (bf16[128,512]{1,0:T(8,128)(2,1)S(1)}, bf16[128,512]{1,0:T(8,128)(2,1)S(1)}, bf16[512,512]{1,0:T(8,128)(2,1)S(1)}, f32[512,512]{1,0:T(8,128)S(1)}, ...) custom-call(bf16[512,128]{1,0:T(8,128)(2,1)S(1)} %get-tuple-element.39.pair, ...), custom_call_target="tpu_custom_call" | custom-call | flops 134217728 | bytes 1048576 | tf_op jit(solution)/shard_map/prepare/pallas_call | solution.py:294
  5.4 0.0 collective-permute-done.rest_0_
  5.4 0.0 collective-permute-done.1.rest_1_
  5.4 1.4 %backward.1 = (f32[512,128]{1,0:T(8,128)S(1)}, bf16[512,512]{1,0:T(8,128)(2,1)S(1)}, bf16[512,512]{1,0:T(8,128)(2,1)S(1)}, bf16[4,208,128]{2,1,0:T(8,128)(2,1)S(1)}, bf16[4,208,128]{2,1,0:T(8,128)(2,1)S(1)}) custom-call(bf16[128,512]{1,0:T(8,128)(2,1)S(1)} %get-tuple-element.43.inputs_t, bf16[128,512]{1,0:T(8,128)(2,1)S(1)} %get-tuple-element.44.updated_t, ...), custom_call_target="tpu_custom_call" | custom-call | flops 268435456 | bytes 1048576 | tf_op jit(solution)/shard_map/backward/pallas_call | solution.py:325
  6.8 0.2 collective-permute-start.2
  7.0 1.4 %collective-permute-done.2.rest_1_ = bf16[4,208,128]{2,1,0:T(8,128)(2,1)S(1)} collective-permute-done((bf16[4,208,128]{2,1,0:T(8,128)(2,1)S(1)}, bf16[4,208,128]{2,1,0:T(8,128)(2,1)S(1)}, u32[]{:S(2)}, u32[]{:S(2)}) %collective-permute-start.2) | collective-permute-done | bytes 213024 | tf_op jit(solution)/shard_map/ppermute | solution.py:357
  8.3 0.1 core_sum.1
  8.4 14.2 %collective-permute-start.3 = (bf16[208,128]{1,0:T(8,128)(2,1)S(1)}, bf16[208,128]{1,0:T(8,128)(2,1)S(1)}, u32[]{:S(2)}, u32[]{:S(2)}) collective-permute-start(bf16[208,128]{1,0:T(8,128)(2,1)S(1)} %get-tuple-element.62), channel_id=1, source_target_pairs={{0,24},{4,28},{8,16},{12,20},{16,8},{20,12},{24,0},{28,4},{1,25},{... | collective-permute-start | bytes 159752 | tf_op jit(solution)/shard_map/ppermute | solution.py:368
  22.6 0.0 collective-permute-start.4
  22.6 0.6 %collective-permute-start.5 = (bf16[208,128]{1,0:T(8,128)(2,1)S(1)}, bf16[208,128]{1,0:T(8,128)(2,1)S(1)}, u32[]{:S(2)}, u32[]{:S(2)}) collective-permute-start(bf16[208,128]{1,0:T(8,128)(2,1)S(1)} %get-tuple-element.64), channel_id=1, source_target_pairs={{0,8},{4,12},{8,0},{12,4},{16,24},{20,28},{24,16},{28,20},{1,9},{5... | collective-permute-start | bytes 159752 | tf_op jit(solution)/shard_map/ppermute | solution.py:368
  23.2 1.5 %collective-permute-done.3.rest_1_ = bf16[208,128]{1,0:T(8,128)(2,1)S(1)} collective-permute-done((bf16[208,128]{1,0:T(8,128)(2,1)S(1)}, bf16[208,128]{1,0:T(8,128)(2,1)S(1)}, u32[]{:S(2)}, u32[]{:S(2)}) %collective-permute-start.3) | collective-permute-done | bytes 53280 | tf_op jit(solution)/shard_map/ppermute | solution.py:368
  24.7 2.0 %collective-permute-done.4.rest_2_ = bf16[208,128]{1,0:T(8,128)(2,1)S(1)} collective-permute-done((bf16[208,128]{1,0:T(8,128)(2,1)S(1)}, bf16[208,128]{1,0:T(8,128)(2,1)S(1)}, u32[]{:S(2)}, u32[]{:S(2)}) %collective-permute-start.4) | collective-permute-done | bytes 53280 | tf_op jit(solution)/shard_map/ppermute | solution.py:368
  26.7 0.0 collective-permute-done.5.rest_3_
  26.7 0.1 chip_sum.1
  26.8 1.3 %collective-permute-start.6 = (bf16[64,128]{1,0:T(8,128)(2,1)S(1)}, bf16[64,128]{1,0:T(8,128)(2,1)S(1)}, u32[]{:S(2)}, u32[]{:S(2)}) collective-permute-start(bf16[64,128]{1,0:T(8,128)(2,1)S(1)} %get-tuple-element.66), channel_id=1, source_target_pairs={{0,3},{1,2},{2,1},{3,0},{4,7},{5,6},{6,5},{7,4},{8,11},{9,10},{10,... | collective-permute-start | bytes 49160 | tf_op jit(solution)/shard_map/ppermute | solution.py:381
  28.1 0.0 collective-permute-start.7
  28.1 3.2 %collective-permute-start.8 = (bf16[64,128]{1,0:T(8,128)(2,1)S(1)}, bf16[64,128]{1,0:T(8,128)(2,1)S(1)}, u32[]{:S(2)}, u32[]{:S(2)}) collective-permute-start(bf16[64,128]{1,0:T(8,128)(2,1)S(1)} %get-tuple-element.68), channel_id=1, source_target_pairs={{0,1},{1,0},{2,3},{3,2},{4,5},{5,4},{6,7},{7,6},{8,9},{9,8},{10,11... | collective-permute-start | bytes 49160 | tf_op jit(solution)/shard_map/ppermute | solution.py:381
  31.3 1.2 %d_inputs.1 = bf16[512,128]{1,0:T(8,128)(2,1)} custom-call(bf16[512,512]{1,0:T(8,128)(2,1)S(1)} %get-tuple-element.54.d_gate, bf16[512,512]{1,0:T(8,128)(2,1)S(1)} %get-tuple-element.55.d_up, f32[512,128]{1,0:T(8,128)S(1)} %get-tuple-element.56.d_updated, f32[512,128]{1,0:T(8,128)S(1)} %get-tuple-element.57.normed, f32[512,128]{1,0:T(8,128)S(1)} %get-tuple-element.58.scale, ...), custom_call_target="tpu_custom_call" | custom-call | flops 134217728 | bytes 1048576 | tf_op jit(solution)/shard_map/d_inputs/pallas_call | solution.py:336
  32.4 0.0 collective-permute-done.6.rest_1_
  32.4 0.3 collective-permute-done.7.rest_2_
  32.8 0.2 collective-permute-done.8.rest_3_
  33.0 0.7 %col_sum.1 = (f32[16,128]{1,0:T(8,128)}, f32[16,128]{1,0:T(8,128)}, f32[32,64]{1,0:T(8,128)}, f32[16,16]{1,0:T(8,128)}) custom-call(bf16[64,128]{1,0:T(8,128)(2,1)S(1)} %get-tuple-element.65.rest_0_, bf16[64,128]{1,0:T(8,128)(2,1)S(1)} %collective-permute-done.6.rest_1_, bf16[64,128]{1,0:T(8,128)(2,1)S(1)} %collective-permute-done.7.rest_2_, ...), custom_call_target="tpu_custom_call" | custom-call | tf_op jit(solution)/shard_map/col_sum/pallas_call | solution.py:382
Async XLA Ops:
  3.1 2.3 %collective-permute-start = (bf16[128,128]{1,0:T(8,128)(2,1)S(1)}, bf16[128,128]{1,0:T(8,128)(2,1)S(1)}, u32[]{:S(2)}, u32[]{:S(2)}) collective-permute-start(bf16[128,128]{1,0:T(8,128)(2,1)S(1)} %get-tuple-element.52), channel_id=1, source_target_pairs={{0,0},{1,8},{2,16},{3,24},{4,4},{5,12},{6,20},{7,28},{8,1},{9,9},{... | collective-permute-start | bytes 98312 | tf_op jit(solution)/shard_map/ppermute | solution.py:292
  3.8 1.6 %collective-permute-start.1 = (bf16[128,128]{1,0:T(8,128)(2,1)S(1)}, bf16[128,128]{1,0:T(8,128)(2,1)S(1)}, u32[]{:S(2)}, u32[]{:S(2)}) collective-permute-start(bf16[128,128]{1,0:T(8,128)(2,1)S(1)} %get-tuple-element.53), channel_id=1, source_target_pairs={{0,4},{1,12},{2,20},{3,28},{4,0},{5,8},{6,16},{7,24},{8,5},{9,13},... | collective-permute-start | bytes 98312 | tf_op jit(solution)/shard_map/ppermute | solution.py:292
  6.8 1.5 %collective-permute-start.2 = (bf16[4,208,128]{2,1,0:T(8,128)(2,1)S(1)}, bf16[4,208,128]{2,1,0:T(8,128)(2,1)S(1)}, u32[]{:S(2)}, u32[]{:S(2)}) collective-permute-start(bf16[4,208,128]{2,1,0:T(8,128)(2,1)S(1)} %get-tuple-element.60), channel_id=1, source_target_pairs={{0,4},{4,0},{8,12},{12,8},{16,20},{20,16},{24,28},{28,24},{1,5},{5... | collective-permute-start | bytes 638984 | tf_op jit(solution)/shard_map/ppermute | solution.py:357
  8.4 16.3 %collective-permute-start.3 = (bf16[208,128]{1,0:T(8,128)(2,1)S(1)}, bf16[208,128]{1,0:T(8,128)(2,1)S(1)}, u32[]{:S(2)}, u32[]{:S(2)}) collective-permute-start(bf16[208,128]{1,0:T(8,128)(2,1)S(1)} %get-tuple-element.62), channel_id=1, source_target_pairs={{0,24},{4,28},{8,16},{12,20},{16,8},{20,12},{24,0},{28,4},{1,25},{... | collective-permute-start | bytes 159752 | tf_op jit(solution)/shard_map/ppermute | solution.py:368
  22.6 4.1 %collective-permute-start.4 = (bf16[208,128]{1,0:T(8,128)(2,1)S(1)}, bf16[208,128]{1,0:T(8,128)(2,1)S(1)}, u32[]{:S(2)}, u32[]{:S(2)}) collective-permute-start(bf16[208,128]{1,0:T(8,128)(2,1)S(1)} %get-tuple-element.63), channel_id=1, source_target_pairs={{0,16},{4,20},{8,24},{12,28},{16,0},{20,4},{24,8},{28,12},{1,17},{... | collective-permute-start | bytes 159752 | tf_op jit(solution)/shard_map/ppermute | solution.py:368
  22.6 4.1 %collective-permute-start.5 = (bf16[208,128]{1,0:T(8,128)(2,1)S(1)}, bf16[208,128]{1,0:T(8,128)(2,1)S(1)}, u32[]{:S(2)}, u32[]{:S(2)}) collective-permute-start(bf16[208,128]{1,0:T(8,128)(2,1)S(1)} %get-tuple-element.64), channel_id=1, source_target_pairs={{0,8},{4,12},{8,0},{12,4},{16,24},{20,28},{24,16},{28,20},{1,9},{5... | collective-permute-start | bytes 159752 | tf_op jit(solution)/shard_map/ppermute | solution.py:368
  26.8 5.6 %collective-permute-start.6 = (bf16[64,128]{1,0:T(8,128)(2,1)S(1)}, bf16[64,128]{1,0:T(8,128)(2,1)S(1)}, u32[]{:S(2)}, u32[]{:S(2)}) collective-permute-start(bf16[64,128]{1,0:T(8,128)(2,1)S(1)} %get-tuple-element.66), channel_id=1, source_target_pairs={{0,3},{1,2},{2,1},{3,0},{4,7},{5,6},{6,5},{7,4},{8,11},{9,10},{10,... | collective-permute-start | bytes 49160 | tf_op jit(solution)/shard_map/ppermute | solution.py:381
  28.1 4.7 %collective-permute-start.7 = (bf16[64,128]{1,0:T(8,128)(2,1)S(1)}, bf16[64,128]{1,0:T(8,128)(2,1)S(1)}, u32[]{:S(2)}, u32[]{:S(2)}) collective-permute-start(bf16[64,128]{1,0:T(8,128)(2,1)S(1)} %get-tuple-element.67), channel_id=1, source_target_pairs={{0,2},{1,3},{2,0},{3,1},{4,6},{5,7},{6,4},{7,5},{8,10},{9,11},{10,... | collective-permute-start | bytes 49160 | tf_op jit(solution)/shard_map/ppermute | solution.py:381
  28.1 4.9 %collective-permute-start.8 = (bf16[64,128]{1,0:T(8,128)(2,1)S(1)}, bf16[64,128]{1,0:T(8,128)(2,1)S(1)}, u32[]{:S(2)}, u32[]{:S(2)}) collective-permute-start(bf16[64,128]{1,0:T(8,128)(2,1)S(1)} %get-tuple-element.68), channel_id=1, source_target_pairs={{0,1},{1,0},{2,3},{3,2},{4,5},{5,4},{6,7},{7,6},{8,9},{9,8},{10,11... | collective-permute-start | bytes 49160 | tf_op jit(solution)/shard_map/ppermute | solution.py:381

commit v4 on v3

v4 whole, which is shorter than its diff:
```python
import functools

import jax
import jax.numpy as jnp
from jax import lax
from jax.experimental import pallas as pl
from jax.experimental.pallas import tpu as pltpu
from jax.sharding import PartitionSpec as P

eps = 1e-05
f32 = jnp.float32
bf16 = jnp.bfloat16
HBM = pl.BlockSpec(memory_space=pltpu.HBM)
VMEM = pl.BlockSpec(memory_space=pltpu.VMEM)
PARAMS = pltpu.CompilerParams(vmem_limit_bytes=24 * 1024 * 1024)


def nn(a, b):
    return lax.dot_general(a, b, (((1,), (0,)), ((), ())), preferred_element_type=f32)


def nt(a, b):
    return lax.dot_general(a, b, (((1,), (1,)), ((), ())), preferred_element_type=f32)


def tn(a, b):
    return lax.dot_general(a, b, (((0,), (0,)), ((), ())), preferred_element_type=f32)


def normalize(flat):
    values = flat.astype(f32)
    centre = values - jnp.mean(values, axis=-1, keepdims=True)
    scale_inv = lax.rsqrt(jnp.mean(centre * centre, axis=-1, keepdims=True) + eps)
    return centre * scale_inv, scale_inv


def sigmoid(v):
    return 0.5 * jnp.tanh(0.5 * v) + 0.5


def chunks_of(size, most):
    step = most if size % most == 0 else size
    return [(at, step) for at in range(0, size, step)]


def partner(s, p, n):
    if n & (n - 1) == 0:
        return s ^ p
    return (s + p) % n if isinstance(s, int) else lax.rem(s + p, n)


def lane_packs(bins, side):
    packs = max(1, 128 // bins)
    return packs if (side // packs) % 16 == 0 else 1


def forward_kernel(q, *refs):
    sources, kept, (updated, logits, sends, halves, sems) = refs[:6], refs[6:12], refs[12:]
    pair, w_gate, w_up, w_out, w_head, _ = kept
    _, side, width = pair.shape
    edge = sources[0].shape[0]
    bins = w_head.shape[0]
    copies = [
        pltpu.make_async_copy(source, target, sems.at[i]) for i, (source, target) in enumerate(zip(sources[1:], kept[1:]))
    ]
    pieces = [
        pltpu.make_async_copy(
            sources[0].at[:, h * edge : (h + 1) * edge, :], pair.reshape(q, edge, edge, width).at[h], sems.at[5 + h]
        )
        for h in range(q)
    ]
    for copy in pieces + copies:
        copy.start()
    shift = edge.bit_length() - 1
    out_row = lax.broadcasted_iota(jnp.int32, (side, side), 0)
    in_row = lax.broadcasted_iota(jnp.int32, (side, side), 1)
    wanted = ((out_row & (edge - 1)) << shift) | (out_row >> shift)
    swap = jnp.where(in_row == wanted, 1.0, 0.0).astype(bf16)
    for copy in pieces:
        copy.wait()
    flat = pair[...].reshape(q * side, width)
    inputs = normalize(flat)[0].astype(bf16)
    total = flat.astype(f32)
    for copy in copies[:4]:
        copy.wait()
    for at, step in chunks_of(w_gate.shape[1], 256):
        gate = nn(inputs, w_gate[:, at : at + step])
        upper = nn(inputs, w_up[:, at : at + step])
        hidden = (gate * sigmoid(gate) * upper).astype(bf16)
        total = total + nn(hidden, w_out[at : at + step, :])
    upd = total.astype(bf16)
    updated[...] = upd.reshape(updated.shape)
    logit = nt(upd, w_head[...]).astype(bf16)
    logits[...] = logit.reshape(logits.shape)
    packs = lane_packs(bins, side)
    deep = side // packs
    for h in range(q):
        piece = nn(swap, logit[h * side : (h + 1) * side])
        if packs > 1:
            piece = jnp.concatenate([piece[u * deep : (u + 1) * deep] for u in range(packs)], axis=1)
        halves[h] = piece.astype(bf16)
    own = lax.rem(lax.axis_index("row"), q)
    for p in range(q):
        sends[p] = halves[partner(own, p, q)]
    copies[4].wait()


def prepare_kernel(pair, updated, w_gate, w_up, inputs_t, updated_t, hidden, slope, swish, normed, scale):
    q, side, width = pair.shape
    units = w_gate.shape[1]
    normal, scale_inv = normalize(pair[...].reshape(q * side, width))
    normed[...] = normal.reshape(normed.shape)
    scale[...] = jnp.broadcast_to(scale_inv, normal.shape).reshape(scale.shape)
    inputs = normal.astype(bf16)
    for h in range(q):
        inputs_t[h] = inputs[h * side : (h + 1) * side].T
        updated_t[h] = updated[h].T
    for at, step in chunks_of(units, 256):
        span = slice(at, at + step)
        gate = nn(inputs, w_gate[:, span])
        upper = nn(inputs, w_up[:, span])
        sigma = sigmoid(gate)
        swished = gate * sigma
        swish[:, :, span] = swished.reshape(q, side, step)
        hidden[:, :, span] = (swished * upper).astype(bf16).reshape(q, side, step)
        slope[:, :, span] = (upper * sigma * (1.0 + gate * (1.0 - sigma))).reshape(q, side, step)


def backward_kernel(q, p, packed, inputs_t, updated_t, hidden, slope, swish, logits, onehot, w_out, w_head, *rest):
    piece, before, rest = rest[0], rest[1:5] if p else (), rest[5 if p else 1 :]
    d_updated, d_gate, d_up, *hot = rest
    _, side, bins = logits.shape
    width, units = inputs_t.shape[1], hidden.shape[2]
    packs = lane_packs(bins, side)
    own = lax.rem(lax.axis_index("row"), q)
    h = partner(own, p, q)
    mirrored = piece[...] if p else piece[0]
    if packs > 1:
        mirrored = jnp.concatenate([mirrored[:, u * bins : (u + 1) * bins] for u in range(packs)], axis=0)
    summed = logits[h].astype(f32) + mirrored.astype(f32)
    powers = jnp.exp(summed - jnp.max(summed, axis=-1, keepdims=True))
    probs = powers / jnp.sum(powers, axis=-1, keepdims=True)
    grad_sym = (probs - onehot[h].astype(f32)).astype(bf16)
    cotangent = (grad_sym.astype(f32) * 2.0).astype(bf16)
    d_upd = nn(cotangent, w_head[...])
    d_updated[...] = d_upd
    d_upd_b = d_upd.astype(bf16)
    d_upd_t = d_upd_b.T
    terms = [[], [], []]
    for at, step in chunks_of(units, 256):
        span = slice(at, at + step)
        d_hidden = nt(d_upd_b, w_out[span, :])
        d_gate_part = (d_hidden * slope[h, :, span]).astype(bf16)
        d_up_part = (d_hidden * swish[h, :, span]).astype(bf16)
        d_gate[:, span] = d_gate_part
        d_up[:, span] = d_up_part
        terms[0].append(nn(inputs_t[h], d_gate_part))
        terms[1].append(nn(inputs_t[h], d_up_part))
        terms[2].append(nn(d_upd_t, hidden[h, :, span]))
    terms = [jnp.concatenate(term, axis=1) for term in terms] + [nn(updated_t[h], cotangent)]
    if p:
        terms = [term + ref[...] for term, ref in zip(terms, before)]
    if p < q - 1 or not packed:
        for ref, term in zip(hot, terms):
            ref[...] = term.astype(ref.dtype)
        return
    gate_term, up_term, out_term, head_term = terms
    hot, slots = hot[:-1], hot[-1]
    nrow, ncol = packed
    groups = nrow // q
    lanes, part, tall = units // ncol, width // nrow, units // nrow
    deep = width // q
    for k in range(q):
        for a in range(groups):
            r = a * q + k
            at = 0
            for term in (gate_term, up_term):
                for c in range(ncol):
                    block = term[r * part : (r + 1) * part, c * lanes : (c + 1) * lanes]
                    slots[k, a, at : at + part] = block.astype(bf16)
                    at += part
            blocks = [out_term[u * deep : (u + 1) * deep, r * tall : (r + 1) * tall] for u in range(q)]
            slots[k, a, at : at + deep] = jnp.concatenate(blocks, axis=1).astype(bf16)
            at += deep
            block = head_term[r * part : (r + 1) * part, :]
            block = jnp.concatenate([block, jnp.zeros((part, lanes - bins), f32)], axis=1)
            slots[k, a, at : at + part] = block.astype(bf16)
    for n in range(q):
        hot[n][...] = slots[partner(own, n, q)]


def input_kernel(q, *refs):
    terms, (normed, scale, w_gate, w_up, d_pair) = refs[: 3 * q], refs[3 * q :]
    own = lax.rem(lax.axis_index("row"), q)
    for p in range(q):
        d_updated, d_gate, d_up = terms[3 * p : 3 * p + 3]
        h = partner(own, p, q)
        d_inputs = nt(d_gate[...], w_gate[...]) + nt(d_up[...], w_up[...])
        normal = normed[h]
        d_norm = (
            d_inputs
            - jnp.mean(d_inputs, axis=-1, keepdims=True)
            - normal * jnp.mean(d_inputs * normal, axis=-1, keepdims=True)
        ) * scale[h]
        result = (d_updated[...] + d_norm).astype(bf16)
        d_pair[:, h] = result.reshape(d_pair.shape[0], d_pair.shape[2], d_pair.shape[3])


def core_sum_kernel(q, groups, *rest):
    terms, hot = rest[:q], rest[q:]
    mine = lax.axis_index("row") // q
    for p in range(groups):
        a = partner(mine, p, groups)
        total = terms[0][a].astype(f32)
        for term in terms[1:]:
            total = total + term[a].astype(f32)
        hot[p][...] = total.astype(bf16)


def chip_sum_kernel(q, groups, ncol, shapes, *rest):
    terms, hot, slots = rest[:groups], rest[groups:-1], rest[-1]
    part, lanes, deep, tall, few = shapes
    total = terms[0][...].astype(f32)
    for term in terms[1:]:
        total = total + term[...].astype(f32)
    at = 2 * ncol * part
    out = total[at : at + deep]
    head = total[at + deep : at + deep + part]
    narrow = deep * q // ncol
    fold = lanes // tall
    short = narrow // fold
    for c in range(ncol):
        slots[c, 0:part] = total[c * part : (c + 1) * part].astype(bf16)
        slots[c, part : 2 * part] = total[(ncol + c) * part : (ncol + c + 1) * part].astype(bf16)
        u, top = (c * narrow) // deep, (c * narrow) % deep
        block = out[top : top + narrow, u * tall : (u + 1) * tall]
        block = jnp.concatenate([block[v * short : (v + 1) * short] for v in range(fold)], axis=1)
        slots[c, 2 * part : 2 * part + short] = block.astype(bf16)
        piece = jnp.concatenate([head[:, c * few : (c + 1) * few], jnp.zeros((part, lanes - few), f32)], axis=1)
        slots[c, 2 * part + short : 3 * part + short] = piece.astype(bf16)
    for p in range(ncol):
        hot[p][...] = slots[partner(lax.axis_index("col"), p, ncol)]


def col_sum_kernel(shapes, factor, *rest):
    terms, (gate, up, out, head) = rest[:-4], rest[-4:]
    part, lanes, tall, few = shapes
    total = terms[0][...].astype(f32)
    for term in terms[1:]:
        total = total + term[...].astype(f32)
    total = total * factor
    fold = lanes // tall
    short = out.shape[0] // fold
    gate[...] = total[0:part]
    up[...] = total[part : 2 * part]
    for v in range(fold):
        out[v * short : (v + 1) * short, :] = total[2 * part : 2 * part + short, v * tall : (v + 1) * tall]
    head[...] = total[2 * part + short : 3 * part + short, 0:few]


def core_pairs(nrow, q, p):
    return [(s, s - s % q + partner(s % q, p, q)) for s in range(nrow)]


def shaped(shape, kind):
    return jax.ShapeDtypeStruct(shape, kind)


def cost(flops, moved):
    return pl.CostEstimate(flops=flops, bytes_accessed=moved, transcendentals=0)


def body(pair, targets, w_gate, w_up, w_out, w_head):
    rows, cols, width = pair.shape
    units = w_gate.shape[1]
    bins = w_head.shape[1]
    nrow, ncol = lax.axis_size("row"), lax.axis_size("col")
    q = nrow // ncol
    groups = nrow // q
    side = rows * cols // q
    packs = lane_packs(bins, side)
    head_t = w_head.T
    piece = (side // packs, bins * packs)

    sources = (pair, w_gate, w_up, w_out, head_t, targets)
    kept = [shaped(x.shape, x.dtype) for x in sources]
    kept[0] = shaped((q, side, width), bf16)
    pair, w_gate, w_up, w_out, head_t, targets, updated, logits, sends = pl.pallas_call(
        functools.partial(forward_kernel, q),
        out_shape=kept + [shaped((q, side, width), bf16), shaped((q, side, bins), bf16), shaped((q, *piece), bf16)],
        in_specs=[HBM] * 6,
        out_specs=[VMEM] * 9,
        scratch_shapes=[pltpu.VMEM((q, *piece), bf16), pltpu.SemaphoreType.DMA((5 + q,))],
        compiler_params=PARAMS,
        name="forward",
    )(*(pltpu.with_memory_space_constraint(x, pltpu.HBM) for x in sources))

    pairs = [(r * ncol + c, (q * c + r % q) * ncol + r // q) for r in range(nrow) for c in range(ncol)]
    got = lax.ppermute(sends, ("row", "col"), pairs)
    targets = jnp.swapaxes(targets.reshape(rows, q, rows), 0, 1).reshape(q, side)
    onehot = (targets[:, :, None] == jnp.arange(bins, dtype=jnp.int32)[None, None, :]).astype(bf16)
    inputs_t, updated_t, hidden, slope, swish, normed, scale = pl.pallas_call(
        prepare_kernel,
        out_shape=[
            shaped((q, width, side), bf16),
            shaped((q, width, side), bf16),
            shaped((q, side, units), bf16),
            shaped((q, side, units), f32),
            shaped((q, side, units), f32),
            shaped((q, side, width), f32),
            shaped((q, side, width), f32),
        ],
        in_specs=[VMEM] * 4,
        out_specs=[VMEM] * 7,
        compiler_params=PARAMS,
        cost_estimate=cost(4 * q * side * width * units, 4 * q * side * units),
        name="prepare",
    )(pair, updated, w_gate, w_up)
    got, onehot, inputs_t = lax.optimization_barrier((got, onehot, inputs_t))
    got = [got] + [lax.ppermute(got[p], "row", core_pairs(nrow, q, p)) for p in range(1, q)]

    part, tall, few = width // nrow, units // nrow, bins // ncol
    lanes, deep = units // ncol, width // q
    fits = (
        part % 16 == 0 and lanes == 128 and tall * q == lanes and bins <= lanes and deep % (width // ncol) == 0
        and (width // ncol * tall // lanes) % 16 == 0
    )
    height = 2 * ncol * part + deep + part
    grads = [(width, n) for n in (units, units, units, bins)]
    hot, d_terms = [], []
    for p in range(q):
        scratch = []
        if p < q - 1 or not fits:
            hot_shapes = [shaped(shape, f32 if p < q - 1 else bf16) for shape in grads]
        else:
            hot_shapes = [shaped((groups, height, lanes), bf16)] * q
            scratch = [pltpu.VMEM((q, groups, height, lanes), bf16)]
        results = pl.pallas_call(
            functools.partial(backward_kernel, q, p, (nrow, ncol) if fits else None),
            out_shape=[shaped((side, width), f32)] + [shaped((side, units), bf16)] * 2 + hot_shapes,
            in_specs=[VMEM] * (10 + len(hot)),
            out_specs=[VMEM] * (3 + len(hot_shapes)),
            scratch_shapes=scratch,
            compiler_params=PARAMS,
            cost_estimate=cost(8 * side * width * units, 4 * side * units),
            name="backward",
        )(inputs_t, updated_t, hidden, slope, swish, logits, onehot, w_out, head_t, got[p], *hot)
        d_terms += results[:3]
        hot = list(results[3:])

    d_pair = pl.pallas_call(
        functools.partial(input_kernel, q),
        out_shape=shaped((rows, q, cols // q, width), bf16),
        in_specs=[VMEM] * (3 * q + 4),
        out_specs=VMEM,
        compiler_params=PARAMS,
        cost_estimate=cost(4 * q * side * width * units, 4 * q * side * units),
        name="d_inputs",
    )(*d_terms, normed, scale, w_gate, w_up)
    factor = 1.0 / (rows * nrow)
    if not fits:
        owned = []
        hot[2] = hot[2].T
        for term in hot:
            mine = lax.psum_scatter(term, "row", scatter_dimension=0, tiled=True).astype(f32)
            owned.append(lax.psum_scatter(mine, "col", scatter_dimension=1, tiled=True) * factor)
        return (d_pair.reshape(rows, cols, width), *owned)

    terms = [hot[0]]
    for p in range(1, q):
        terms.append(lax.ppermute(hot[p], "row", core_pairs(nrow, q, p)))
    hot = pl.pallas_call(
        functools.partial(core_sum_kernel, q, groups),
        out_shape=[shaped((height, lanes), bf16)] * groups,
        in_specs=[VMEM] * q,
        out_specs=[VMEM] * groups,
        compiler_params=PARAMS,
        name="core_sum",
    )(*terms)
    terms = [hot[0]]
    for p in range(groups - 1, 0, -1):
        terms.append(lax.ppermute(hot[p], "row", [(s, partner(s // q, p, groups) * q + s % q) for s in range(nrow)]))
    *terms, d_pair = lax.optimization_barrier((*terms, d_pair))
    short = 3 * part + width // ncol * tall // lanes
    hot = pl.pallas_call(
        functools.partial(chip_sum_kernel, q, groups, ncol, (part, lanes, deep, tall, few)),
        out_shape=[shaped((short, lanes), bf16)] * ncol,
        in_specs=[VMEM] * groups,
        out_specs=[VMEM] * ncol,
        scratch_shapes=[pltpu.VMEM((ncol, short, lanes), bf16)],
        compiler_params=PARAMS,
        name="chip_sum",
    )(*terms)
    terms = [hot[0]]
    for p in range(ncol - 1, 0, -1):
        terms.append(lax.ppermute(hot[p], "col", [(s, partner(s, p, ncol)) for s in range(ncol)]))
    gate, up, out, head = pl.pallas_call(
        functools.partial(col_sum_kernel, (part, lanes, tall, few), factor),
        out_shape=[
            shaped((part, lanes), f32),
            shaped((part, lanes), f32),
            shaped((width // ncol, tall), f32),
            shaped((part, few), f32),
        ],
        in_specs=[VMEM] * ncol,
        out_specs=[VMEM] * 4,
        compiler_params=PARAMS,
        name="col_sum",
    )(*terms)
    return d_pair.reshape(rows, cols, width), gate, up, out.T, head


def solution(mesh):
    placed = (P("row", "col", None), P("row", "col"), P(), P(), P(), P())
    return jax.shard_map(
        body,
        mesh=mesh,
        in_specs=placed,
        out_specs=(P("row", "col", None), P("row", "col"), P("row", "col"), P("row", "col"), P("row", "col")),
        check_vma=False,
    )
```

time: 33.8 us -> 33.8 us (level)
  starting transfers between devices: 20.6 us -> 18 us
  waiting for transfers between devices: 5.4 us -> 7.26 us
  Pallas kernels: 6.73 us -> 7.29 us
    ppermute x3, waiting for transfers between devices: 0.54 us -> 3.71 us  [body(): lax.ppermute(hot[p], 'col', [(s, partner(s, p, ncol)) for s in range(ncol)])]
    ppermute x3, starting transfers between devices: 14.8 us -> 12.1 us  [body(): lax.ppermute(hot[p], 'row', [(s, partner(s // q, p, groups) * q + s % q)...]
    ppermute x3, waiting for transfers between devices: 3.49 us -> 2.25 us  [body(): lax.ppermute(hot[p], 'row', [(s, partner(s // q, p, groups) * q + s % q)...]
    pallas_call x3 -> x4, Pallas kernels: 3.44 us -> 4.18 us  [the longest x2 2.08 us: body(): pl.pallas_call(functools.partial(backward_kernel, q, p, (nrow, ncol) if f...]
  transfers between devices with their start and end apart: 9 -> 9, of which waited for: 5 -> 5; matrix products, arithmetic and copies ran while one was open for 1% -> 1% of each run, Pallas kernels for 6% -> 9%
where the time goes in v4:
time: 33.8 us; the launch traced here: 33.6 us
  starting transfers between devices  18 us (53%)
  Pallas kernels  7.29 us (22%)
  waiting for transfers between devices  7.26 us (21%)
  between operations  0.72 us (2%)
    ppermute x3, starting transfers between devices, body(): lax.ppermute(hot[p], 'row', [(s, partner(s // q, p, groups) * q + s % q)...  12.1 us
    ppermute x3, starting transfers between devices, body(): lax.ppermute(hot[p], 'col', [(s, partner(s, p, ncol)) for s in range(ncol)])  4.45 us
    ppermute x3, waiting for transfers between devices, body(): lax.ppermute(hot[p], 'col', [(s, partner(s, p, ncol)) for s in range(ncol)])  3.71 us
    pallas_call x1, Pallas kernels, body(): pl.pallas_call(functools.partial(forward_kernel, q), out_shape=kept + [sh...  2.27 us
    ppermute x3, waiting for transfers between devices, body(): lax.ppermute(hot[p], 'row', [(s, partner(s // q, p, groups) * q + s % q)...  2.25 us
    pallas_call x2, Pallas kernels, body(): pl.pallas_call(functools.partial(backward_kernel, q, p, (nrow, ncol) if f...  2.08 us
    ppermute x1, waiting for transfers between devices, body(): terms.append(lax.ppermute(hot[p], 'row', core_pairs(nrow, q, p)))  1.28 us
    pallas_call x1, Pallas kernels, body(): pl.pallas_call(functools.partial(input_kernel, q), out_shape=shaped((rows...  1.24 us
  transfers between devices with their start and end apart: 9, of which 5 were waited for; matrix products, arithmetic and copies ran while one was open for 1% of the time, Pallas kernels for 9%

profile of v4, /device:TPU:0, one launch (start us, length us, event | category | flops | bytes accessed | tf_op | source)
XLA Modules:
  0.0 33.6 jit_solution(3990480266940522234)
XLA Ops:
  0.6 2.3 %forward.1 = (bf16[2,256,128]{2,1,0:T(8,128)(2,1)S(1)}, bf16[128,512]{1,0:T(8,128)(2,1)S(1)}, bf16[128,512]{1,0:T(8,128)(2,1)S(1)}, bf16[512,128]{1,0:T(8,128)(2...) custom-call(bf16[16,32,128]{2,1,0:T(8,128)(2,1)} %refs_0_.1, ...), custom_call_target="tpu_custom_call" | custom-call | tf_op jit(solution)/shard_map/forward/pallas_call | solution.py:288
  2.9 0.7 %collective-permute-start = (bf16[2,128,128]{2,1,0:T(8,128)(2,1)S(1)}, bf16[2,128,128]{2,1,0:T(8,128)(2,1)S(1)}, u32[]{:S(2)}, u32[]{:S(2)}) collective-permute-start(bf16[2,128,128]{2,1,0:T(8,128)(2,1)S(1)} %get-tuple-element.53), channel_id=1, source_target_pairs={{0,0},{1,8},{2,16},{3,24},{4,4},{5,12},{6,20},{7,28},{8,1},{9,9},{... | collective-permute-start | bytes 196616 | tf_op jit(solution)/shard_map/ppermute | solution.py:299
  3.6 0.1 reshape.17
  3.7 0.1 eq.15
  3.8 0.1 fusion.onehot
  3.9 0.9 %prepare.1 = (bf16[2,128,256]{2,1,0:T(8,128)(2,1)S(1)}, bf16[2,128,256]{2,1,0:T(8,128)(2,1)S(1)}, bf16[2,256,512]{2,1,0:T(8,128)(2,1)S(1)}, f32[2,256,512]{2,1,0...) custom-call(bf16[2,256,128]{2,1,0:T(8,128)(2,1)S(1)} %get-tuple-element.55.pair, ...), custom_call_target="tpu_custom_call" | custom-call | flops 134217728 | bytes 1048576 | tf_op jit(solution)/shard_map/prepare/pallas_call | solution.py:302
  4.8 0.0 collective-permute-done.rest_0_
  4.8 0.5 %collective-permute-start.1 = (bf16[128,128]{1,0:T(8,128)(2,1)S(1)}, bf16[128,128]{1,0:T(8,128)(2,1)S(1)}, u32[]{:S(2)}, u32[]{:S(2)}) collective-permute-start(bf16[128,128]{1,0:T(8,128)(2,1)S(1)} %slice_bitcast_fusion), channel_id=1, source_target_pairs={{0,4},{4,0},{8,12},{12,8},{16,20},{20,16},{24,28},{28,24},{1,5},{5... | collective-permute-start | bytes 98312 | tf_op jit(solution)/shard_map/ppermute | solution.py:320
  5.3 1.0 %backward.2 = (f32[256,128]{1,0:T(8,128)S(1)}, bf16[256,512]{1,0:T(8,128)(2,1)S(1)}, bf16[256,512]{1,0:T(8,128)(2,1)S(1)}, f32[128,512]{1,0:T(8,128)S(1)}, f32[1...) custom-call(bf16[2,128,256]{2,1,0:T(8,128)(2,1)S(1)} %get-tuple-element.60.inputs_t, ...), custom_call_target="tpu_custom_call" | custom-call | flops 134217728 | bytes 524288 | tf_op jit(solution)/shard_map/backward/pallas_call | solution.py:338
  6.4 0.0 collective-permute-done.1.rest_0_
  6.4 1.1 %backward.3 = (f32[256,128]{1,0:T(8,128)S(1)}, bf16[256,512]{1,0:T(8,128)(2,1)S(1)}, bf16[256,512]{1,0:T(8,128)(2,1)S(1)}, bf16[4,208,128]{2,1,0:T(8,128)(2,1)S(1)}, bf16[4,208,128]{2,1,0:T(8,128)(2,1)S(1)}) custom-call(bf16[2,128,256]{2,1,0:T(8,128)(2,1)S(1)} %get-tuple-element.60.inputs_t, bf16[2,128,256]{2,1,0:T(8,128)(2,1)S(1)} %get-tuple-element.61.updated_t, ...), custom_call_target="tpu_custom_call" | custom-call | flops 134217728 | bytes 524288 | tf_op jit(solution)/shard_map/backward/pallas_call | solution.py:338
  7.4 0.2 collective-permute-start.2
  7.7 1.3 %collective-permute-done.2.rest_1_ = bf16[4,208,128]{2,1,0:T(8,128)(2,1)S(1)} collective-permute-done((bf16[4,208,128]{2,1,0:T(8,128)(2,1)S(1)}, bf16[4,208,128]{2,1,0:T(8,128)(2,1)S(1)}, u32[]{:S(2)}, u32[]{:S(2)}) %collective-permute-start.2) | collective-permute-done | bytes 213024 | tf_op jit(solution)/shard_map/ppermute | solution.py:371
  9.0 0.1 core_sum.1
  9.0 11.5 %collective-permute-start.3 = (bf16[208,128]{1,0:T(8,128)(2,1)S(1)}, bf16[208,128]{1,0:T(8,128)(2,1)S(1)}, u32[]{:S(2)}, u32[]{:S(2)}) collective-permute-start(bf16[208,128]{1,0:T(8,128)(2,1)S(1)} %get-tuple-element.77), channel_id=1, source_target_pairs={{0,24},{4,28},{8,16},{12,20},{16,8},{20,12},{24,0},{28,4},{1,25},{... | collective-permute-start | bytes 159752 | tf_op jit(solution)/shard_map/ppermute | solution.py:382
  20.5 0.0 collective-permute-start.4
  20.5 0.6 %collective-permute-start.5 = (bf16[208,128]{1,0:T(8,128)(2,1)S(1)}, bf16[208,128]{1,0:T(8,128)(2,1)S(1)}, u32[]{:S(2)}, u32[]{:S(2)}) collective-permute-start(bf16[208,128]{1,0:T(8,128)(2,1)S(1)} %get-tuple-element.79), channel_id=1, source_target_pairs={{0,8},{4,12},{8,0},{12,4},{16,24},{20,28},{24,16},{28,20},{1,9},{5... | collective-permute-start | bytes 159752 | tf_op jit(solution)/shard_map/ppermute | solution.py:382
  21.2 1.2 %d_inputs.1 = bf16[16,2,16,128]{3,2,1,0:T(8,128)(2,1)} custom-call(f32[256,128]{1,0:T(8,128)S(1)} %get-tuple-element.80.refs_0_, bf16[256,512]{1,0:T(8,128)(2,1)S(1)} %get-tuple-element.81.refs_1_, bf16[256,512]{1,0:T(8,128)(2,1)S(1)} %get-tuple-element.82.refs_2_, f32[256,128]{1,0:T(8,128)S(1)} %get-tuple-element.83.refs_3_, ...), custom_call_target="tpu_custom_call" | custom-call | flops 134217728 | bytes 1048576 | tf_op jit(solution)/shard_map/d_inputs/pallas_call | solution.py:351
  22.4 0.5 %collective-permute-done.3.rest_1_ = bf16[208,128]{1,0:T(8,128)(2,1)S(1)} collective-permute-done((bf16[208,128]{1,0:T(8,128)(2,1)S(1)}, bf16[208,128]{1,0:T(8,128)(2,1)S(1)}, u32[]{:S(2)}, u32[]{:S(2)}) %collective-permute-start.3) | collective-permute-done | bytes 53280 | tf_op jit(solution)/shard_map/ppermute | solution.py:382
  22.9 1.8 %collective-permute-done.4.rest_2_ = bf16[208,128]{1,0:T(8,128)(2,1)S(1)} collective-permute-done((bf16[208,128]{1,0:T(8,128)(2,1)S(1)}, bf16[208,128]{1,0:T(8,128)(2,1)S(1)}, u32[]{:S(2)}, u32[]{:S(2)}) %collective-permute-start.4) | collective-permute-done | bytes 53280 | tf_op jit(solution)/shard_map/ppermute | solution.py:382
  24.6 0.0 collective-permute-done.5.rest_3_
  24.6 0.1 chip_sum.1
  24.7 3.5 %collective-permute-start.6 = (bf16[64,128]{1,0:T(8,128)(2,1)S(1)}, bf16[64,128]{1,0:T(8,128)(2,1)S(1)}, u32[]{:S(2)}, u32[]{:S(2)}) collective-permute-start(bf16[64,128]{1,0:T(8,128)(2,1)S(1)} %get-tuple-element.94), channel_id=1, source_target_pairs={{0,3},{1,2},{2,1},{3,0},{4,7},{5,6},{6,5},{7,4},{8,11},{9,10},{10,... | collective-permute-start | bytes 49160 | tf_op jit(solution)/shard_map/ppermute | solution.py:396
  28.3 0.0 collective-permute-start.7
  28.3 0.9 %collective-permute-start.8 = (bf16[64,128]{1,0:T(8,128)(2,1)S(1)}, bf16[64,128]{1,0:T(8,128)(2,1)S(1)}, u32[]{:S(2)}, u32[]{:S(2)}) collective-permute-start(bf16[64,128]{1,0:T(8,128)(2,1)S(1)} %get-tuple-element.96), channel_id=1, source_target_pairs={{0,1},{1,0},{2,3},{3,2},{4,5},{5,4},{6,7},{7,6},{8,9},{9,8},{10,11... | collective-permute-start | bytes 49160 | tf_op jit(solution)/shard_map/ppermute | solution.py:396
  29.2 1.1 %collective-permute-done.6.rest_1_ = bf16[64,128]{1,0:T(8,128)(2,1)S(1)} collective-permute-done((bf16[64,128]{1,0:T(8,128)(2,1)S(1)}, bf16[64,128]{1,0:T(8,128)(2,1)S(1)}, u32[]{:S(2)}, u32[]{:S(2)}) %collective-permute-start.6) | collective-permute-done | bytes 16416 | tf_op jit(solution)/shard_map/ppermute | solution.py:396
  30.3 2.6 %collective-permute-done.7.rest_2_ = bf16[64,128]{1,0:T(8,128)(2,1)S(1)} collective-permute-done((bf16[64,128]{1,0:T(8,128)(2,1)S(1)}, bf16[64,128]{1,0:T(8,128)(2,1)S(1)}, u32[]{:S(2)}, u32[]{:S(2)}) %collective-permute-start.7) | collective-permute-done | bytes 16416 | tf_op jit(solution)/shard_map/ppermute | solution.py:396
  32.9 0.0 collective-permute-done.8.rest_3_
  32.9 0.7 %col_sum.1 = (f32[16,128]{1,0:T(8,128)}, f32[16,128]{1,0:T(8,128)}, f32[32,64]{1,0:T(8,128)}, f32[16,16]{1,0:T(8,128)}) custom-call(bf16[64,128]{1,0:T(8,128)(2,1)S(1)} %get-tuple-element.93.rest_0_, bf16[64,128]{1,0:T(8,128)(2,1)S(1)} %collective-permute-done.6.rest_1_, bf16[64,128]{1,0:T(8,128)(2,1)S(1)} %collective-permute-done.7.rest_2_, ...), custom_call_target="tpu_custom_call" | custom-call | tf_op jit(solution)/shard_map/col_sum/pallas_call | solution.py:397
  (2 shorter events, 0.0 us)
Async XLA Ops:
  2.9 1.9 %collective-permute-start = (bf16[2,128,128]{2,1,0:T(8,128)(2,1)S(1)}, bf16[2,128,128]{2,1,0:T(8,128)(2,1)S(1)}, u32[]{:S(2)}, u32[]{:S(2)}) collective-permute-start(bf16[2,128,128]{2,1,0:T(8,128)(2,1)S(1)} %get-tuple-element.53), channel_id=1, source_target_pairs={{0,0},{1,8},{2,16},{3,24},{4,4},{5,12},{6,20},{7,28},{8,1},{9,9},{... | collective-permute-start | bytes 196616 | tf_op jit(solution)/shard_map/ppermute | solution.py:299
  4.8 1.6 %collective-permute-start.1 = (bf16[128,128]{1,0:T(8,128)(2,1)S(1)}, bf16[128,128]{1,0:T(8,128)(2,1)S(1)}, u32[]{:S(2)}, u32[]{:S(2)}) collective-permute-start(bf16[128,128]{1,0:T(8,128)(2,1)S(1)} %slice_bitcast_fusion), channel_id=1, source_target_pairs={{0,4},{4,0},{8,12},{12,8},{16,20},{20,16},{24,28},{28,24},{1,5},{5... | collective-permute-start | bytes 98312 | tf_op jit(solution)/shard_map/ppermute | solution.py:320
  7.4 1.5 %collective-permute-start.2 = (bf16[4,208,128]{2,1,0:T(8,128)(2,1)S(1)}, bf16[4,208,128]{2,1,0:T(8,128)(2,1)S(1)}, u32[]{:S(2)}, u32[]{:S(2)}) collective-permute-start(bf16[4,208,128]{2,1,0:T(8,128)(2,1)S(1)} %get-tuple-element.75), channel_id=1, source_target_pairs={{0,4},{4,0},{8,12},{12,8},{16,20},{20,16},{24,28},{28,24},{1,5},{5... | collective-permute-start | bytes 638984 | tf_op jit(solution)/shard_map/ppermute | solution.py:371
  9.0 13.8 %collective-permute-start.3 = (bf16[208,128]{1,0:T(8,128)(2,1)S(1)}, bf16[208,128]{1,0:T(8,128)(2,1)S(1)}, u32[]{:S(2)}, u32[]{:S(2)}) collective-permute-start(bf16[208,128]{1,0:T(8,128)(2,1)S(1)} %get-tuple-element.77), channel_id=1, source_target_pairs={{0,24},{4,28},{8,16},{12,20},{16,8},{20,12},{24,0},{28,4},{1,25},{... | collective-permute-start | bytes 159752 | tf_op jit(solution)/shard_map/ppermute | solution.py:382
  20.5 4.1 %collective-permute-start.4 = (bf16[208,128]{1,0:T(8,128)(2,1)S(1)}, bf16[208,128]{1,0:T(8,128)(2,1)S(1)}, u32[]{:S(2)}, u32[]{:S(2)}) collective-permute-start(bf16[208,128]{1,0:T(8,128)(2,1)S(1)} %get-tuple-element.78), channel_id=1, source_target_pairs={{0,16},{4,20},{8,24},{12,28},{16,0},{20,4},{24,8},{28,12},{1,17},{... | collective-permute-start | bytes 159752 | tf_op jit(solution)/shard_map/ppermute | solution.py:382
  20.5 4.1 %collective-permute-start.5 = (bf16[208,128]{1,0:T(8,128)(2,1)S(1)}, bf16[208,128]{1,0:T(8,128)(2,1)S(1)}, u32[]{:S(2)}, u32[]{:S(2)}) collective-permute-start(bf16[208,128]{1,0:T(8,128)(2,1)S(1)} %get-tuple-element.79), channel_id=1, source_target_pairs={{0,8},{4,12},{8,0},{12,4},{16,24},{20,28},{24,16},{28,20},{1,9},{5... | collective-permute-start | bytes 159752 | tf_op jit(solution)/shard_map/ppermute | solution.py:382
  24.7 5.6 %collective-permute-start.6 = (bf16[64,128]{1,0:T(8,128)(2,1)S(1)}, bf16[64,128]{1,0:T(8,128)(2,1)S(1)}, u32[]{:S(2)}, u32[]{:S(2)}) collective-permute-start(bf16[64,128]{1,0:T(8,128)(2,1)S(1)} %get-tuple-element.94), channel_id=1, source_target_pairs={{0,3},{1,2},{2,1},{3,0},{4,7},{5,6},{6,5},{7,4},{8,11},{9,10},{10,... | collective-permute-start | bytes 49160 | tf_op jit(solution)/shard_map/ppermute | solution.py:396
  28.3 4.6 %collective-permute-start.7 = (bf16[64,128]{1,0:T(8,128)(2,1)S(1)}, bf16[64,128]{1,0:T(8,128)(2,1)S(1)}, u32[]{:S(2)}, u32[]{:S(2)}) collective-permute-start(bf16[64,128]{1,0:T(8,128)(2,1)S(1)} %get-tuple-element.95), channel_id=1, source_target_pairs={{0,2},{1,3},{2,0},{3,1},{4,6},{5,7},{6,4},{7,5},{8,10},{9,11},{10,... | collective-permute-start | bytes 49160 | tf_op jit(solution)/shard_map/ppermute | solution.py:396
  28.3 4.6 %collective-permute-start.8 = (bf16[64,128]{1,0:T(8,128)(2,1)S(1)}, bf16[64,128]{1,0:T(8,128)(2,1)S(1)}, u32[]{:S(2)}, u32[]{:S(2)}) collective-permute-start(bf16[64,128]{1,0:T(8,128)(2,1)S(1)} %get-tuple-element.96), channel_id=1, source_target_pairs={{0,1},{1,0},{2,3},{3,2},{4,5},{5,4},{6,7},{7,6},{8,9},{9,8},{10,11... | collective-permute-start | bytes 49160 | tf_op jit(solution)/shard_map/ppermute | solution.py:396

commit v5 on v4

--- a/solution.py
+++ b/solution.py
@@ -209,16 +209,17 @@
 def core_sum_kernel(q, groups, *rest):
     terms, hot = rest[:q], rest[q:]
     mine = lax.axis_index("row") // q
-    for p in range(groups):
+    for n, p in enumerate([0] + [p for p, _ in stages(groups)]):
         a = partner(mine, p, groups)
         total = terms[0][a].astype(f32)
         for term in terms[1:]:
             total = total + term[a].astype(f32)
-        hot[p][...] = total.astype(bf16)
-
-
-def chip_sum_kernel(q, groups, ncol, shapes, *rest):
-    terms, hot, slots = rest[:groups], rest[groups:-1], rest[-1]
+        hot[n][...] = total.astype(bf16)
+
+
+def chip_sum_kernel(q, ncol, shapes, *rest):
+    steps = [0] + [p for p, _ in stages(ncol)]
+    terms, hot, slots = rest[: -1 - len(steps)], rest[-1 - len(steps) : -1], rest[-1]
     part, lanes, deep, tall, few = shapes
     total = terms[0][...].astype(f32)
     for term in terms[1:]:
@@ -238,8 +239,8 @@
         slots[c, 2 * part : 2 * part + short] = block.astype(bf16)
         piece = jnp.concatenate([head[:, c * few : (c + 1) * few], jnp.zeros((part, lanes - few), f32)], axis=1)
         slots[c, 2 * part + short : 3 * part + short] = piece.astype(bf16)
-    for p in range(ncol):
-        hot[p][...] = slots[partner(lax.axis_index("col"), p, ncol)]
+    for n, p in enumerate(steps):
+        hot[n][...] = slots[partner(lax.axis_index("col"), p, ncol)]
 
 
 def col_sum_kernel(shapes, factor, *rest):
@@ -260,6 +261,22 @@
 
 def core_pairs(nrow, q, p):
     return [(s, s - s % q + partner(s % q, p, q)) for s in range(nrow)]
+
+
+def stages(n):
+    if n & (n - 1) or n < 4:
+        return [(p, range(n)) for p in range(1, n)]
+    half = n // 2
+    across = range(half, n)
+    return [(p, range(n)) for p in range(1, half)] + [(p, across) for p in across] + [(p, range(half)) for p in across]
+
+
+def staged_permutes(values, axis, n, pairs):
+    moved = [
+        lax.ppermute(value, axis, [pair for s in members for pair in pairs(s, p)])
+        for value, (p, members) in zip(values[1:], stages(n))
+    ]
+    return [values[0]] + moved
 
 
 def shaped(shape, kind):
@@ -371,29 +388,25 @@
         terms.append(lax.ppermute(hot[p], "row", core_pairs(nrow, q, p)))
     hot = pl.pallas_call(
         functools.partial(core_sum_kernel, q, groups),
-        out_shape=[shaped((height, lanes), bf16)] * groups,
+        out_shape=[shaped((height, lanes), bf16)] * (1 + len(stages(groups))),
         in_specs=[VMEM] * q,
-        out_specs=[VMEM] * groups,
+        out_specs=[VMEM] * (1 + len(stages(groups))),
         compiler_params=PARAMS,
         name="core_sum",
     )(*terms)
-    terms = [hot[0]]
-    for p in range(groups - 1, 0, -1):
-        terms.append(lax.ppermute(hot[p], "row", [(s, partner(s // q, p, groups) * q + s % q) for s in range(nrow)]))
+    terms = staged_permutes(hot, "row", groups, lambda s, p: [(s * q + k, partner(s, p, groups) * q + k) for k in range(q)])
     *terms, d_pair = lax.optimization_barrier((*terms, d_pair))
     short = 3 * part + width // ncol * tall // lanes
     hot = pl.pallas_call(
-        functools.partial(chip_sum_kernel, q, groups, ncol, (part, lanes, deep, tall, few)),
-        out_shape=[shaped((short, lanes), bf16)] * ncol,
-        in_specs=[VMEM] * groups,
-        out_specs=[VMEM] * ncol,
+        functools.partial(chip_sum_kernel, q, ncol, (part, lanes, deep, tall, few)),
+        out_shape=[shaped((short, lanes), bf16)] * (1 + len(stages(ncol))),
+        in_specs=[VMEM] * len(terms),
+        out_specs=[VMEM] * (1 + len(stages(ncol))),
         scratch_shapes=[pltpu.VMEM((ncol, short, lanes), bf16)],
         compiler_params=PARAMS,
         name="chip_sum",
     )(*terms)
-    terms = [hot[0]]
-    for p in range(ncol - 1, 0, -1):
-        terms.append(lax.ppermute(hot[p], "col", [(s, partner(s, p, ncol)) for s in range(ncol)]))
+    terms = staged_permutes(hot, "col", ncol, lambda s, p: [(s, partner(s, p, ncol))])
     gate, up, out, head = pl.pallas_call(
         functools.partial(col_sum_kernel, (part, lanes, tall, few), factor),
         out_shape=[
@@ -402,7 +415,7 @@
             shaped((width // ncol, tall), f32),
             shaped((part, few), f32),
         ],
-        in_specs=[VMEM] * ncol,
+        in_specs=[VMEM] * len(terms),
         out_specs=[VMEM] * 4,
         compiler_params=PARAMS,
         name="col_sum",

time: 33.8 us -> 43.3 us (1.28)
  starting transfers between devices: 18 us -> 31.3 us
  waiting for transfers between devices: 7.26 us -> 3.19 us
    ppermute x6 -> x10, starting transfers between devices: 16.6 us -> 29.9 us  [staged_permutes(): lax.ppermute(value, axis, [pair for s in members for pair in pairs(s, p)])]
    ppermute x6 -> x10, waiting for transfers between devices: 5.97 us -> 1.9 us  [staged_permutes(): lax.ppermute(value, axis, [pair for s in members for pair in pairs(s, p)])]
  transfers between devices with their start and end apart: 9 -> 13, of which waited for: 5 -> 3; matrix products, arithmetic and copies ran while one was open for 1% -> 1% of each run, Pallas kernels for 9% -> 7%
where the time goes in v5:
time: 43.3 us; the launch traced here: 43 us
  starting transfers between devices  31.3 us (72%)
  Pallas kernels  7.31 us (17%)
  waiting for transfers between devices  3.19 us (7%)
  between operations  0.83 us (2%)
    ppermute x10, starting transfers between devices, staged_permutes(): lax.ppermute(value, axis, [pair for s in members for pair in pairs(s, p)])  29.9 us
    pallas_call x1, Pallas kernels, body(): pl.pallas_call(functools.partial(forward_kernel, q), out_shape=kept + [sh...  2.27 us
    pallas_call x2, Pallas kernels, body(): pl.pallas_call(functools.partial(backward_kernel, q, p, (nrow, ncol) if f...  2.08 us
    ppermute x10, waiting for transfers between devices, staged_permutes(): lax.ppermute(value, axis, [pair for s in members for pair in pairs(s, p)])  1.9 us
    ppermute x1, waiting for transfers between devices, body(): terms.append(lax.ppermute(hot[p], 'row', core_pairs(nrow, q, p)))  1.28 us
    pallas_call x1, Pallas kernels, body(): pl.pallas_call(functools.partial(input_kernel, q), out_shape=shaped((rows...  1.25 us
  transfers between devices with their start and end apart: 13, of which 3 were waited for; matrix products, arithmetic and copies ran while one was open for 1% of the time, Pallas kernels for 7%

profile of v5, /device:TPU:0, one launch (start us, length us, event | category | flops | bytes accessed | tf_op | source)
XLA Modules:
  0.0 43.0 jit_solution(18356718144572505996)
XLA Ops:
  0.6 2.3 %forward.1 = (bf16[2,256,128]{2,1,0:T(8,128)(2,1)S(1)}, bf16[128,512]{1,0:T(8,128)(2,1)S(1)}, bf16[128,512]{1,0:T(8,128)(2,1)S(1)}, bf16[512,128]{1,0:T(8,128)(2...) custom-call(bf16[16,32,128]{2,1,0:T(8,128)(2,1)} %refs_0_.1, ...), custom_call_target="tpu_custom_call" | custom-call | tf_op jit(solution)/shard_map/forward/pallas_call | solution.py:305
  2.9 0.7 %collective-permute-start = (bf16[2,128,128]{2,1,0:T(8,128)(2,1)S(1)}, bf16[2,128,128]{2,1,0:T(8,128)(2,1)S(1)}, u32[]{:S(2)}, u32[]{:S(2)}) collective-permute-start(bf16[2,128,128]{2,1,0:T(8,128)(2,1)S(1)} %get-tuple-element.59), channel_id=1, source_target_pairs={{0,0},{1,8},{2,16},{3,24},{4,4},{5,12},{6,20},{7,28},{8,1},{9,9},{... | collective-permute-start | bytes 196616 | tf_op jit(solution)/shard_map/ppermute | solution.py:316
  3.6 0.1 reshape.17
  3.7 0.1 eq.15
  3.8 0.1 fusion.onehot
  3.9 0.9 %prepare.1 = (bf16[2,128,256]{2,1,0:T(8,128)(2,1)S(1)}, bf16[2,128,256]{2,1,0:T(8,128)(2,1)S(1)}, bf16[2,256,512]{2,1,0:T(8,128)(2,1)S(1)}, f32[2,256,512]{2,1,0...) custom-call(bf16[2,256,128]{2,1,0:T(8,128)(2,1)S(1)} %get-tuple-element.61.pair, ...), custom_call_target="tpu_custom_call" | custom-call | flops 134217728 | bytes 1048576 | tf_op jit(solution)/shard_map/prepare/pallas_call | solution.py:319
  4.8 0.0 collective-permute-done.rest_0_
  4.8 0.5 %collective-permute-start.1 = (bf16[128,128]{1,0:T(8,128)(2,1)S(1)}, bf16[128,128]{1,0:T(8,128)(2,1)S(1)}, u32[]{:S(2)}, u32[]{:S(2)}) collective-permute-start(bf16[128,128]{1,0:T(8,128)(2,1)S(1)} %slice_bitcast_fusion), channel_id=1, source_target_pairs={{0,4},{4,0},{8,12},{12,8},{16,20},{20,16},{24,28},{28,24},{1,5},{5... | collective-permute-start | bytes 98312 | tf_op jit(solution)/shard_map/ppermute | solution.py:337
  5.3 1.0 %backward.2 = (f32[256,128]{1,0:T(8,128)S(1)}, bf16[256,512]{1,0:T(8,128)(2,1)S(1)}, bf16[256,512]{1,0:T(8,128)(2,1)S(1)}, f32[128,512]{1,0:T(8,128)S(1)}, f32[1...) custom-call(bf16[2,128,256]{2,1,0:T(8,128)(2,1)S(1)} %get-tuple-element.66.inputs_t, ...), custom_call_target="tpu_custom_call" | custom-call | flops 134217728 | bytes 524288 | tf_op jit(solution)/shard_map/backward/pallas_call | solution.py:355
  6.4 0.0 collective-permute-done.1.rest_0_
  6.4 1.1 %backward.3 = (f32[256,128]{1,0:T(8,128)S(1)}, bf16[256,512]{1,0:T(8,128)(2,1)S(1)}, bf16[256,512]{1,0:T(8,128)(2,1)S(1)}, bf16[4,208,128]{2,1,0:T(8,128)(2,1)S(1)}, bf16[4,208,128]{2,1,0:T(8,128)(2,1)S(1)}) custom-call(bf16[2,128,256]{2,1,0:T(8,128)(2,1)S(1)} %get-tuple-element.66.inputs_t, bf16[2,128,256]{2,1,0:T(8,128)(2,1)S(1)} %get-tuple-element.67.updated_t, ...), custom_call_target="tpu_custom_call" | custom-call | flops 134217728 | bytes 524288 | tf_op jit(solution)/shard_map/backward/pallas_call | solution.py:355
  7.4 0.2 collective-permute-start.2
  7.7 1.3 %collective-permute-done.2.rest_1_ = bf16[4,208,128]{2,1,0:T(8,128)(2,1)S(1)} collective-permute-done((bf16[4,208,128]{2,1,0:T(8,128)(2,1)S(1)}, bf16[4,208,128]{2,1,0:T(8,128)(2,1)S(1)}, u32[]{:S(2)}, u32[]{:S(2)}) %collective-permute-start.2) | collective-permute-done | bytes 213024 | tf_op jit(solution)/shard_map/ppermute | solution.py:388
  9.0 0.1 core_sum.1
  9.0 9.7 %collective-permute-start.3 = (bf16[208,128]{1,0:T(8,128)(2,1)S(1)}, bf16[208,128]{1,0:T(8,128)(2,1)S(1)}, u32[]{:S(2)}, u32[]{:S(2)}) collective-permute-start(bf16[208,128]{1,0:T(8,128)(2,1)S(1)} %get-tuple-element.83), channel_id=1, source_target_pairs={{0,8},{4,12},{8,0},{12,4},{16,24},{20,28},{24,16},{28,20},{1,9},{5... | collective-permute-start | bytes 159752 | tf_op jit(solution)/shard_map/ppermute | solution.py:276
  18.8 1.3 %collective-permute-start.4 = (bf16[208,128]{1,0:T(8,128)(2,1)S(1)}, bf16[208,128]{1,0:T(8,128)(2,1)S(1)}, u32[]{:S(2)}, u32[]{:S(2)}) collective-permute-start(bf16[208,128]{1,0:T(8,128)(2,1)S(1)} %get-tuple-element.84), channel_id=1, source_target_pairs={{16,0},{20,4},{24,8},{28,12},{17,1},{21,5},{25,9},{29,13},{18,2},{... | collective-permute-start | bytes 159752 | tf_op jit(solution)/shard_map/ppermute | solution.py:276
  20.1 1.3 %collective-permute-start.5 = (bf16[208,128]{1,0:T(8,128)(2,1)S(1)}, bf16[208,128]{1,0:T(8,128)(2,1)S(1)}, u32[]{:S(2)}, u32[]{:S(2)}) collective-permute-start(bf16[208,128]{1,0:T(8,128)(2,1)S(1)} %get-tuple-element.85), channel_id=1, source_target_pairs={{16,8},{20,12},{24,0},{28,4},{17,9},{21,13},{25,1},{29,5},{18,10},... | collective-permute-start | bytes 159752 | tf_op jit(solution)/shard_map/ppermute | solution.py:276
  21.4 4.5 %collective-permute-start.6 = (bf16[208,128]{1,0:T(8,128)(2,1)S(1)}, bf16[208,128]{1,0:T(8,128)(2,1)S(1)}, u32[]{:S(2)}, u32[]{:S(2)}) collective-permute-start(bf16[208,128]{1,0:T(8,128)(2,1)S(1)} %get-tuple-element.86), channel_id=1, source_target_pairs={{0,16},{4,20},{8,24},{12,28},{1,17},{5,21},{9,25},{13,29},{2,18},{... | collective-permute-start | bytes 159752 | tf_op jit(solution)/shard_map/ppermute | solution.py:276
  25.9 2.2 %collective-permute-start.7 = (bf16[208,128]{1,0:T(8,128)(2,1)S(1)}, bf16[208,128]{1,0:T(8,128)(2,1)S(1)}, u32[]{:S(2)}, u32[]{:S(2)}) collective-permute-start(bf16[208,128]{1,0:T(8,128)(2,1)S(1)} %get-tuple-element.87), channel_id=1, source_target_pairs={{0,24},{4,28},{8,16},{12,20},{1,25},{5,29},{9,17},{13,21},{2,26},{... | collective-permute-start | bytes 159752 | tf_op jit(solution)/shard_map/ppermute | solution.py:276
  28.1 1.2 %d_inputs.1 = bf16[16,2,16,128]{3,2,1,0:T(8,128)(2,1)} custom-call(f32[256,128]{1,0:T(8,128)S(1)} %get-tuple-element.88.refs_0_, bf16[256,512]{1,0:T(8,128)(2,1)S(1)} %get-tuple-element.89.refs_1_, bf16[256,512]{1,0:T(8,128)(2,1)S(1)} %get-tuple-element.90.refs_2_, f32[256,128]{1,0:T(8,128)S(1)} %get-tuple-element.91.refs_3_, ...), custom_call_target="tpu_custom_call" | custom-call | flops 134217728 | bytes 1048576 | tf_op jit(solution)/shard_map/d_inputs/pallas_call | solution.py:368
  29.4 0.0 collective-permute-done.3.rest_1_
  29.4 0.0 collective-permute-done.4.rest_2_
  29.4 0.0 collective-permute-done.5.rest_3_
  29.4 0.0 collective-permute-done.6.rest_4_
  29.4 0.5 %collective-permute-done.7.rest_5_ = bf16[208,128]{1,0:T(8,128)(2,1)S(1)} collective-permute-done((bf16[208,128]{1,0:T(8,128)(2,1)S(1)}, bf16[208,128]{1,0:T(8,128)(2,1)S(1)}, u32[]{:S(2)}, u32[]{:S(2)}) %collective-permute-start.7) | collective-permute-done | bytes 53280 | tf_op jit(solution)/shard_map/ppermute | solution.py:276
  29.9 0.1 chip_sum.1
  30.0 0.1 collective-permute-start.8
  30.1 1.3 %collective-permute-start.9 = (bf16[64,128]{1,0:T(8,128)(2,1)S(1)}, bf16[64,128]{1,0:T(8,128)(2,1)S(1)}, u32[]{:S(2)}, u32[]{:S(2)}) collective-permute-start(bf16[64,128]{1,0:T(8,128)(2,1)S(1)} %get-tuple-element.105), channel_id=1, source_target_pairs={{2,0},{3,1},{6,4},{7,5},{10,8},{11,9},{14,12},{15,13},{18,16},{19,... | collective-permute-start | bytes 49160 | tf_op jit(solution)/shard_map/ppermute | solution.py:276
  31.4 1.3 %collective-permute-start.10 = (bf16[64,128]{1,0:T(8,128)(2,1)S(1)}, bf16[64,128]{1,0:T(8,128)(2,1)S(1)}, u32[]{:S(2)}, u32[]{:S(2)}) collective-permute-start(bf16[64,128]{1,0:T(8,128)(2,1)S(1)} %get-tuple-element.106), channel_id=1, source_target_pairs={{2,1},{3,0},{6,5},{7,4},{10,9},{11,8},{14,13},{15,12},{18,17},{19,... | collective-permute-start | bytes 49160 | tf_op jit(solution)/shard_map/ppermute | solution.py:276
  32.7 6.2 %collective-permute-start.11 = (bf16[64,128]{1,0:T(8,128)(2,1)S(1)}, bf16[64,128]{1,0:T(8,128)(2,1)S(1)}, u32[]{:S(2)}, u32[]{:S(2)}) collective-permute-start(bf16[64,128]{1,0:T(8,128)(2,1)S(1)} %get-tuple-element.107), channel_id=1, source_target_pairs={{0,2},{1,3},{4,6},{5,7},{8,10},{9,11},{12,14},{13,15},{16,18},{17,... | collective-permute-start | bytes 49160 | tf_op jit(solution)/shard_map/ppermute | solution.py:276
  38.9 2.0 %collective-permute-start.12 = (bf16[64,128]{1,0:T(8,128)(2,1)S(1)}, bf16[64,128]{1,0:T(8,128)(2,1)S(1)}, u32[]{:S(2)}, u32[]{:S(2)}) collective-permute-start(bf16[64,128]{1,0:T(8,128)(2,1)S(1)} %get-tuple-element.108), channel_id=1, source_target_pairs={{0,3},{1,2},{4,7},{5,6},{8,11},{9,10},{12,15},{13,14},{16,19},{17,... | collective-permute-start | bytes 49160 | tf_op jit(solution)/shard_map/ppermute | solution.py:276
  40.9 0.0 collective-permute-done.8.rest_1_
  40.9 0.0 collective-permute-done.9.rest_2_
  40.9 0.0 collective-permute-done.10.rest_3_
  40.9 0.0 collective-permute-done.11.rest_4_
  40.9 1.4 %collective-permute-done.12.rest_5_ = bf16[64,128]{1,0:T(8,128)(2,1)S(1)} collective-permute-done((bf16[64,128]{1,0:T(8,128)(2,1)S(1)}, bf16[64,128]{1,0:T(8,128)(2,1)S(1)}, u32[]{:S(2)}, u32[]{:S(2)}) %collective-permute-start.12) | collective-permute-done | bytes 16416 | tf_op jit(solution)/shard_map/ppermute | solution.py:276
  42.3 0.7 %col_sum.1 = (f32[16,128]{1,0:T(8,128)}, f32[16,128]{1,0:T(8,128)}, f32[32,64]{1,0:T(8,128)}, f32[16,16]{1,0:T(8,128)}) custom-call(bf16[64,128]{1,0:T(8,128)(2,1)S(1)} %get-tuple-element.103.rest_0_, bf16[64,128]{1,0:T(8,128)(2,1)S(1)} %collective-permute-done.8.rest_1_, bf16[64,128]{1,0:T(8,128)(2,1)S(1)} %collective-permute-done.9.rest_2_, ...), custom_call_target="tpu_custom_call" | custom-call | tf_op jit(solution)/shard_map/col_sum/pallas_call | solution.py:410
  (2 shorter events, 0.0 us)
Async XLA Ops:
  2.9 1.9 %collective-permute-start = (bf16[2,128,128]{2,1,0:T(8,128)(2,1)S(1)}, bf16[2,128,128]{2,1,0:T(8,128)(2,1)S(1)}, u32[]{:S(2)}, u32[]{:S(2)}) collective-permute-start(bf16[2,128,128]{2,1,0:T(8,128)(2,1)S(1)} %get-tuple-element.59), channel_id=1, source_target_pairs={{0,0},{1,8},{2,16},{3,24},{4,4},{5,12},{6,20},{7,28},{8,1},{9,9},{... | collective-permute-start | bytes 196616 | tf_op jit(solution)/shard_map/ppermute | solution.py:316
  4.8 1.6 %collective-permute-start.1 = (bf16[128,128]{1,0:T(8,128)(2,1)S(1)}, bf16[128,128]{1,0:T(8,128)(2,1)S(1)}, u32[]{:S(2)}, u32[]{:S(2)}) collective-permute-start(bf16[128,128]{1,0:T(8,128)(2,1)S(1)} %slice_bitcast_fusion), channel_id=1, source_target_pairs={{0,4},{4,0},{8,12},{12,8},{16,20},{20,16},{24,28},{28,24},{1,5},{5... | collective-permute-start | bytes 98312 | tf_op jit(solution)/shard_map/ppermute | solution.py:337
  7.4 1.5 %collective-permute-start.2 = (bf16[4,208,128]{2,1,0:T(8,128)(2,1)S(1)}, bf16[4,208,128]{2,1,0:T(8,128)(2,1)S(1)}, u32[]{:S(2)}, u32[]{:S(2)}) collective-permute-start(bf16[4,208,128]{2,1,0:T(8,128)(2,1)S(1)} %get-tuple-element.81), channel_id=1, source_target_pairs={{0,4},{4,0},{8,12},{12,8},{16,20},{20,16},{24,28},{28,24},{1,5},{5... | collective-permute-start | bytes 638984 | tf_op jit(solution)/shard_map/ppermute | solution.py:388
  9.0 20.3 %collective-permute-start.3 = (bf16[208,128]{1,0:T(8,128)(2,1)S(1)}, bf16[208,128]{1,0:T(8,128)(2,1)S(1)}, u32[]{:S(2)}, u32[]{:S(2)}) collective-permute-start(bf16[208,128]{1,0:T(8,128)(2,1)S(1)} %get-tuple-element.83), channel_id=1, source_target_pairs={{0,8},{4,12},{8,0},{12,4},{16,24},{20,28},{24,16},{28,20},{1,9},{5... | collective-permute-start | bytes 159752 | tf_op jit(solution)/shard_map/ppermute | solution.py:276
  18.8 10.6 %collective-permute-start.4 = (bf16[208,128]{1,0:T(8,128)(2,1)S(1)}, bf16[208,128]{1,0:T(8,128)(2,1)S(1)}, u32[]{:S(2)}, u32[]{:S(2)}) collective-permute-start(bf16[208,128]{1,0:T(8,128)(2,1)S(1)} %get-tuple-element.84), channel_id=1, source_target_pairs={{16,0},{20,4},{24,8},{28,12},{17,1},{21,5},{25,9},{29,13},{18,2},{... | collective-permute-start | bytes 159752 | tf_op jit(solution)/shard_map/ppermute | solution.py:276
  20.1 9.3 %collective-permute-start.5 = (bf16[208,128]{1,0:T(8,128)(2,1)S(1)}, bf16[208,128]{1,0:T(8,128)(2,1)S(1)}, u32[]{:S(2)}, u32[]{:S(2)}) collective-permute-start(bf16[208,128]{1,0:T(8,128)(2,1)S(1)} %get-tuple-element.85), channel_id=1, source_target_pairs={{16,8},{20,12},{24,0},{28,4},{17,9},{21,13},{25,1},{29,5},{18,10},... | collective-permute-start | bytes 159752 | tf_op jit(solution)/shard_map/ppermute | solution.py:276
  21.4 8.0 %collective-permute-start.6 = (bf16[208,128]{1,0:T(8,128)(2,1)S(1)}, bf16[208,128]{1,0:T(8,128)(2,1)S(1)}, u32[]{:S(2)}, u32[]{:S(2)}) collective-permute-start(bf16[208,128]{1,0:T(8,128)(2,1)S(1)} %get-tuple-element.86), channel_id=1, source_target_pairs={{0,16},{4,20},{8,24},{12,28},{1,17},{5,21},{9,25},{13,29},{2,18},{... | collective-permute-start | bytes 159752 | tf_op jit(solution)/shard_map/ppermute | solution.py:276
  25.9 4.0 %collective-permute-start.7 = (bf16[208,128]{1,0:T(8,128)(2,1)S(1)}, bf16[208,128]{1,0:T(8,128)(2,1)S(1)}, u32[]{:S(2)}, u32[]{:S(2)}) collective-permute-start(bf16[208,128]{1,0:T(8,128)(2,1)S(1)} %get-tuple-element.87), channel_id=1, source_target_pairs={{0,24},{4,28},{8,16},{12,20},{1,25},{5,29},{9,17},{13,21},{2,26},{... | collective-permute-start | bytes 159752 | tf_op jit(solution)/shard_map/ppermute | solution.py:276
  30.0 10.9 %collective-permute-start.8 = (bf16[64,128]{1,0:T(8,128)(2,1)S(1)}, bf16[64,128]{1,0:T(8,128)(2,1)S(1)}, u32[]{:S(2)}, u32[]{:S(2)}) collective-permute-start(bf16[64,128]{1,0:T(8,128)(2,1)S(1)} %get-tuple-element.104), channel_id=1, source_target_pairs={{0,1},{1,0},{2,3},{3,2},{4,5},{5,4},{6,7},{7,6},{8,9},{9,8},{10,11... | collective-permute-start | bytes 49160 | tf_op jit(solution)/shard_map/ppermute | solution.py:276
  30.1 10.8 %collective-permute-start.9 = (bf16[64,128]{1,0:T(8,128)(2,1)S(1)}, bf16[64,128]{1,0:T(8,128)(2,1)S(1)}, u32[]{:S(2)}, u32[]{:S(2)}) collective-permute-start(bf16[64,128]{1,0:T(8,128)(2,1)S(1)} %get-tuple-element.105), channel_id=1, source_target_pairs={{2,0},{3,1},{6,4},{7,5},{10,8},{11,9},{14,12},{15,13},{18,16},{19,... | collective-permute-start | bytes 49160 | tf_op jit(solution)/shard_map/ppermute | solution.py:276
  31.4 9.5 %collective-permute-start.10 = (bf16[64,128]{1,0:T(8,128)(2,1)S(1)}, bf16[64,128]{1,0:T(8,128)(2,1)S(1)}, u32[]{:S(2)}, u32[]{:S(2)}) collective-permute-start(bf16[64,128]{1,0:T(8,128)(2,1)S(1)} %get-tuple-element.106), channel_id=1, source_target_pairs={{2,1},{3,0},{6,5},{7,4},{10,9},{11,8},{14,13},{15,12},{18,17},{19,... | collective-permute-start | bytes 49160 | tf_op jit(solution)/shard_map/ppermute | solution.py:276
  32.7 8.2 %collective-permute-start.11 = (bf16[64,128]{1,0:T(8,128)(2,1)S(1)}, bf16[64,128]{1,0:T(8,128)(2,1)S(1)}, u32[]{:S(2)}, u32[]{:S(2)}) collective-permute-start(bf16[64,128]{1,0:T(8,128)(2,1)S(1)} %get-tuple-element.107), channel_id=1, source_target_pairs={{0,2},{1,3},{4,6},{5,7},{8,10},{9,11},{12,14},{13,15},{16,18},{17,... | collective-permute-start | bytes 49160 | tf_op jit(solution)/shard_map/ppermute | solution.py:276
  38.9 3.4 %collective-permute-start.12 = (bf16[64,128]{1,0:T(8,128)(2,1)S(1)}, bf16[64,128]{1,0:T(8,128)(2,1)S(1)}, u32[]{:S(2)}, u32[]{:S(2)}) collective-permute-start(bf16[64,128]{1,0:T(8,128)(2,1)S(1)} %get-tuple-element.108), channel_id=1, source_target_pairs={{0,3},{1,2},{4,7},{5,6},{8,11},{9,10},{12,15},{13,14},{16,19},{17,... | collective-permute-start | bytes 49160 | tf_op jit(solution)/shard_map/ppermute | solution.py:276

commit v6 on v4

--- a/solution.py
+++ b/solution.py
@@ -127,14 +127,24 @@
 
 
 def backward_kernel(q, p, packed, inputs_t, updated_t, hidden, slope, swish, logits, onehot, w_out, w_head, *rest):
-    piece, before, rest = rest[0], rest[1:5] if p else (), rest[5 if p else 1 :]
-    d_updated, d_gate, d_up, *hot = rest
+    (piece, near), before, rest = rest[:2], rest[2:6] if p else (), rest[6 if p else 2 :]
+    d_updated, d_gate, d_up, *hot, mirrored = rest
     _, side, bins = logits.shape
     width, units = inputs_t.shape[1], hidden.shape[2]
     packs = lane_packs(bins, side)
     own = lax.rem(lax.axis_index("row"), q)
     h = partner(own, p, q)
-    mirrored = piece[...] if p else piece[0]
+    inside = lax.axis_index("row") // q == lax.axis_index("col")
+
+    @pl.when(inside)
+    def _():
+        mirrored[...] = near[p]
+
+    @pl.when(jnp.logical_not(inside))
+    def _():
+        mirrored[...] = piece[...] if p else piece[0]
+
+    mirrored = mirrored[...]
     if packs > 1:
         mirrored = jnp.concatenate([mirrored[:, u * bins : (u + 1) * bins] for u in range(packs)], axis=0)
     summed = logits[h].astype(f32) + mirrored.astype(f32)
@@ -295,7 +305,11 @@
         name="forward",
     )(*(pltpu.with_memory_space_constraint(x, pltpu.HBM) for x in sources))
 
-    pairs = [(r * ncol + c, (q * c + r % q) * ncol + r // q) for r in range(nrow) for c in range(ncol)]
+    pairs = [
+        (r * ncol + c, (q * c + (partner(r % q, 1, q) if q == 2 and r // q == c else r % q)) * ncol + r // q)
+        for r in range(nrow)
+        for c in range(ncol)
+    ]
     got = lax.ppermute(sends, ("row", "col"), pairs)
     targets = jnp.swapaxes(targets.reshape(rows, q, rows), 0, 1).reshape(q, side)
     onehot = (targets[:, :, None] == jnp.arange(bins, dtype=jnp.int32)[None, None, :]).astype(bf16)
@@ -317,6 +331,7 @@
         name="prepare",
     )(pair, updated, w_gate, w_up)
     got, onehot, inputs_t = lax.optimization_barrier((got, onehot, inputs_t))
+    near = [sends, got] if q == 2 else [got] * q
     got = [got] + [lax.ppermute(got[p], "row", core_pairs(nrow, q, p)) for p in range(1, q)]
 
     part, tall, few = width // nrow, units // nrow, bins // ncol
@@ -329,22 +344,22 @@
     grads = [(width, n) for n in (units, units, units, bins)]
     hot, d_terms = [], []
     for p in range(q):
-        scratch = []
+        scratch = [pltpu.VMEM(piece, bf16)]
         if p < q - 1 or not fits:
             hot_shapes = [shaped(shape, f32 if p < q - 1 else bf16) for shape in grads]
         else:
             hot_shapes = [shaped((groups, height, lanes), bf16)] * q
-            scratch = [pltpu.VMEM((q, groups, height, lanes), bf16)]
+            scratch.insert(0, pltpu.VMEM((q, groups, height, lanes), bf16))
         results = pl.pallas_call(
             functools.partial(backward_kernel, q, p, (nrow, ncol) if fits else None),
             out_shape=[shaped((side, width), f32)] + [shaped((side, units), bf16)] * 2 + hot_shapes,
-            in_specs=[VMEM] * (10 + len(hot)),
+            in_specs=[VMEM] * (11 + len(hot)),
             out_specs=[VMEM] * (3 + len(hot_shapes)),
             scratch_shapes=scratch,
             compiler_params=PARAMS,
             cost_estimate=cost(8 * side * width * units, 4 * side * units),
             name="backward",
-        )(inputs_t, updated_t, hidden, slope, swish, logits, onehot, w_out, head_t, got[p], *hot)
+        )(inputs_t, updated_t, hidden, slope, swish, logits, onehot, w_out, head_t, got[p], near[p], *hot)
         d_terms += results[:3]
         hot = list(results[3:])
 

time: 33.8 us -> 31.9 us (0.944)
  starting transfers between devices: 18 us -> 16.3 us
    ppermute x3, starting transfers between devices: 12.1 us -> 10.7 us  [body(): lax.ppermute(hot[p], 'row', [(s, partner(s // q, p, groups) * q + s % q)...]
    ppermute x1, starting transfers between devices: 0.53 us -> 0.11 us  [body(): lax.ppermute(got[p], 'row', core_pairs(nrow, q, p))]
  transfers between devices with their start and end apart: 9 -> 9, of which waited for: 5 -> 6; matrix products, arithmetic and copies ran while one was open for 1% -> 1% of each run, Pallas kernels for 9% -> 10%
where the time goes in v6:
time: 31.9 us; the launch traced here: 31.8 us
  starting transfers between devices  16.3 us (51%)
  Pallas kernels  7.28 us (23%)
  waiting for transfers between devices  7.18 us (23%)
  between operations  0.7 us (2%)
    ppermute x3, starting transfers between devices, body(): lax.ppermute(hot[p], 'row', [(s, partner(s // q, p, groups) * q + s % q)...  10.7 us
    ppermute x3, starting transfers between devices, body(): lax.ppermute(hot[p], 'col', [(s, partner(s, p, ncol)) for s in range(ncol)])  4.45 us
    ppermute x3, waiting for transfers between devices, body(): lax.ppermute(hot[p], 'col', [(s, partner(s, p, ncol)) for s in range(ncol)])  3.71 us
    pallas_call x1, Pallas kernels, body(): pl.pallas_call(functools.partial(forward_kernel, q), out_shape=kept + [sh...  2.27 us
    ppermute x3, waiting for transfers between devices, body(): lax.ppermute(hot[p], 'row', [(s, partner(s // q, p, groups) * q + s % q)...  2.25 us
    pallas_call x2, Pallas kernels, body(): pl.pallas_call(functools.partial(backward_kernel, q, p, (nrow, ncol) if f...  2.07 us
    pallas_call x1, Pallas kernels, body(): pl.pallas_call(functools.partial(input_kernel, q), out_shape=shaped((rows...  1.24 us
    ppermute x1, waiting for transfers between devices, body(): terms.append(lax.ppermute(hot[p], 'row', core_pairs(nrow, q, p)))  1.09 us
  transfers between devices with their start and end apart: 9, of which 6 were waited for; matrix products, arithmetic and copies ran while one was open for 1% of the time, Pallas kernels for 10%

profile of v6, /device:TPU:0, one launch (start us, length us, event | category | flops | bytes accessed | tf_op | source)
XLA Modules:
  0.0 31.8 jit_solution(6958213137687435464)
XLA Ops:
  0.6 2.3 %forward.1 = (bf16[2,256,128]{2,1,0:T(8,128)(2,1)S(1)}, bf16[128,512]{1,0:T(8,128)(2,1)S(1)}, bf16[128,512]{1,0:T(8,128)(2,1)S(1)}, bf16[512,128]{1,0:T(8,128)(2...) custom-call(bf16[16,32,128]{2,1,0:T(8,128)(2,1)} %refs_0_.1, ...), custom_call_target="tpu_custom_call" | custom-call | tf_op jit(solution)/shard_map/forward/pallas_call | solution.py:298
  2.9 0.5 %collective-permute-start = (bf16[2,128,128]{2,1,0:T(8,128)(2,1)S(1)}, bf16[2,128,128]{2,1,0:T(8,128)(2,1)S(1)}, u32[]{:S(2)}, u32[]{:S(2)}) collective-permute-start(bf16[2,128,128]{2,1,0:T(8,128)(2,1)S(1)} %get-tuple-element.53.rest_1_), channel_id=1, source_target_pairs={{0,4},{1,8},{2,16},{3,24},{4,0},{5,12},{6,20},{7,28},{8,1},{9,13},... | collective-permute-start | bytes 196616 | tf_op jit(solution)/shard_map/ppermute | solution.py:313
  3.4 0.1 reshape.17
  3.5 0.1 eq.15
  3.6 0.1 fusion.onehot
  3.8 0.9 %prepare.1 = (bf16[2,128,256]{2,1,0:T(8,128)(2,1)S(1)}, bf16[2,128,256]{2,1,0:T(8,128)(2,1)S(1)}, bf16[2,256,512]{2,1,0:T(8,128)(2,1)S(1)}, f32[2,256,512]{2,1,0...) custom-call(bf16[2,256,128]{2,1,0:T(8,128)(2,1)S(1)} %get-tuple-element.55.pair, ...), custom_call_target="tpu_custom_call" | custom-call | flops 134217728 | bytes 1048576 | tf_op jit(solution)/shard_map/prepare/pallas_call | solution.py:316
  4.6 0.0 collective-permute-done.rest_0_.rest_1_
  4.7 0.1 collective-permute-start.1
  4.8 1.0 %backward.2 = (f32[256,128]{1,0:T(8,128)S(1)}, bf16[256,512]{1,0:T(8,128)(2,1)S(1)}, bf16[256,512]{1,0:T(8,128)(2,1)S(1)}, f32[128,512]{1,0:T(8,128)S(1)}, f32[1...) custom-call(bf16[2,128,256]{2,1,0:T(8,128)(2,1)S(1)} %get-tuple-element.60.inputs_t, ...), custom_call_target="tpu_custom_call" | custom-call | flops 134217728 | bytes 524288 | tf_op jit(solution)/shard_map/backward/pallas_call | solution.py:353
  5.8 0.1 collective-permute-done.1.rest_0_
  5.9 1.0 %backward.3 = (f32[256,128]{1,0:T(8,128)S(1)}, bf16[256,512]{1,0:T(8,128)(2,1)S(1)}, bf16[256,512]{1,0:T(8,128)(2,1)S(1)}, bf16[4,208,128]{2,1,0:T(8,128)(2,1)S(1)}, bf16[4,208,128]{2,1,0:T(8,128)(2,1)S(1)}) custom-call(bf16[2,128,256]{2,1,0:T(8,128)(2,1)S(1)} %get-tuple-element.60.inputs_t, bf16[2,128,256]{2,1,0:T(8,128)(2,1)S(1)} %get-tuple-element.61.updated_t, ...), custom_call_target="tpu_custom_call" | custom-call | flops 134217728 | bytes 524288 | tf_op jit(solution)/shard_map/backward/pallas_call | solution.py:353
  7.0 0.5 %collective-permute-start.2 = (bf16[4,208,128]{2,1,0:T(8,128)(2,1)S(1)}, bf16[4,208,128]{2,1,0:T(8,128)(2,1)S(1)}, u32[]{:S(2)}, u32[]{:S(2)}) collective-permute-start(bf16[4,208,128]{2,1,0:T(8,128)(2,1)S(1)} %get-tuple-element.75), channel_id=1, source_target_pairs={{0,4},{4,0},{8,12},{12,8},{16,20},{20,16},{24,28},{28,24},{1,5},{5... | collective-permute-start | bytes 638984 | tf_op jit(solution)/shard_map/ppermute | solution.py:386
  7.4 1.1 %collective-permute-done.2.rest_1_ = bf16[4,208,128]{2,1,0:T(8,128)(2,1)S(1)} collective-permute-done((bf16[4,208,128]{2,1,0:T(8,128)(2,1)S(1)}, bf16[4,208,128]{2,1,0:T(8,128)(2,1)S(1)}, u32[]{:S(2)}, u32[]{:S(2)}) %collective-permute-start.2) | collective-permute-done | bytes 213024 | tf_op jit(solution)/shard_map/ppermute | solution.py:386
  8.5 0.1 core_sum.1
  8.6 10.1 %collective-permute-start.3 = (bf16[208,128]{1,0:T(8,128)(2,1)S(1)}, bf16[208,128]{1,0:T(8,128)(2,1)S(1)}, u32[]{:S(2)}, u32[]{:S(2)}) collective-permute-start(bf16[208,128]{1,0:T(8,128)(2,1)S(1)} %get-tuple-element.77), channel_id=1, source_target_pairs={{0,24},{4,28},{8,16},{12,20},{16,8},{20,12},{24,0},{28,4},{1,25},{... | collective-permute-start | bytes 159752 | tf_op jit(solution)/shard_map/ppermute | solution.py:397
  18.7 0.0 collective-permute-start.4
  18.7 0.6 %collective-permute-start.5 = (bf16[208,128]{1,0:T(8,128)(2,1)S(1)}, bf16[208,128]{1,0:T(8,128)(2,1)S(1)}, u32[]{:S(2)}, u32[]{:S(2)}) collective-permute-start(bf16[208,128]{1,0:T(8,128)(2,1)S(1)} %get-tuple-element.79), channel_id=1, source_target_pairs={{0,8},{4,12},{8,0},{12,4},{16,24},{20,28},{24,16},{28,20},{1,9},{5... | collective-permute-start | bytes 159752 | tf_op jit(solution)/shard_map/ppermute | solution.py:397
  19.3 1.2 %d_inputs.1 = bf16[16,2,16,128]{3,2,1,0:T(8,128)(2,1)} custom-call(f32[256,128]{1,0:T(8,128)S(1)} %get-tuple-element.80.refs_0_, bf16[256,512]{1,0:T(8,128)(2,1)S(1)} %get-tuple-element.81.refs_1_, bf16[256,512]{1,0:T(8,128)(2,1)S(1)} %get-tuple-element.82.refs_2_, f32[256,128]{1,0:T(8,128)S(1)} %get-tuple-element.83.refs_3_, ...), custom_call_target="tpu_custom_call" | custom-call | flops 134217728 | bytes 1048576 | tf_op jit(solution)/shard_map/d_inputs/pallas_call | solution.py:366
  20.6 0.5 %collective-permute-done.3.rest_1_ = bf16[208,128]{1,0:T(8,128)(2,1)S(1)} collective-permute-done((bf16[208,128]{1,0:T(8,128)(2,1)S(1)}, bf16[208,128]{1,0:T(8,128)(2,1)S(1)}, u32[]{:S(2)}, u32[]{:S(2)}) %collective-permute-start.3) | collective-permute-done | bytes 53280 | tf_op jit(solution)/shard_map/ppermute | solution.py:397
  21.0 1.8 %collective-permute-done.4.rest_2_ = bf16[208,128]{1,0:T(8,128)(2,1)S(1)} collective-permute-done((bf16[208,128]{1,0:T(8,128)(2,1)S(1)}, bf16[208,128]{1,0:T(8,128)(2,1)S(1)}, u32[]{:S(2)}, u32[]{:S(2)}) %collective-permute-start.4) | collective-permute-done | bytes 53280 | tf_op jit(solution)/shard_map/ppermute | solution.py:397
  22.8 0.0 collective-permute-done.5.rest_3_
  22.8 0.1 chip_sum.1
  22.9 3.5 %collective-permute-start.6 = (bf16[64,128]{1,0:T(8,128)(2,1)S(1)}, bf16[64,128]{1,0:T(8,128)(2,1)S(1)}, u32[]{:S(2)}, u32[]{:S(2)}) collective-permute-start(bf16[64,128]{1,0:T(8,128)(2,1)S(1)} %get-tuple-element.94), channel_id=1, source_target_pairs={{0,3},{1,2},{2,1},{3,0},{4,7},{5,6},{6,5},{7,4},{8,11},{9,10},{10,... | collective-permute-start | bytes 49160 | tf_op jit(solution)/shard_map/ppermute | solution.py:411
  26.5 0.0 collective-permute-start.7
  26.5 0.9 %collective-permute-start.8 = (bf16[64,128]{1,0:T(8,128)(2,1)S(1)}, bf16[64,128]{1,0:T(8,128)(2,1)S(1)}, u32[]{:S(2)}, u32[]{:S(2)}) collective-permute-start(bf16[64,128]{1,0:T(8,128)(2,1)S(1)} %get-tuple-element.96), channel_id=1, source_target_pairs={{0,1},{1,0},{2,3},{3,2},{4,5},{5,4},{6,7},{7,6},{8,9},{9,8},{10,11... | collective-permute-start | bytes 49160 | tf_op jit(solution)/shard_map/ppermute | solution.py:411
  27.4 1.1 %collective-permute-done.6.rest_1_ = bf16[64,128]{1,0:T(8,128)(2,1)S(1)} collective-permute-done((bf16[64,128]{1,0:T(8,128)(2,1)S(1)}, bf16[64,128]{1,0:T(8,128)(2,1)S(1)}, u32[]{:S(2)}, u32[]{:S(2)}) %collective-permute-start.6) | collective-permute-done | bytes 16416 | tf_op jit(solution)/shard_map/ppermute | solution.py:411
  28.5 2.6 %collective-permute-done.7.rest_2_ = bf16[64,128]{1,0:T(8,128)(2,1)S(1)} collective-permute-done((bf16[64,128]{1,0:T(8,128)(2,1)S(1)}, bf16[64,128]{1,0:T(8,128)(2,1)S(1)}, u32[]{:S(2)}, u32[]{:S(2)}) %collective-permute-start.7) | collective-permute-done | bytes 16416 | tf_op jit(solution)/shard_map/ppermute | solution.py:411
  31.1 0.0 collective-permute-done.8.rest_3_
  31.1 0.7 %col_sum.1 = (f32[16,128]{1,0:T(8,128)}, f32[16,128]{1,0:T(8,128)}, f32[32,64]{1,0:T(8,128)}, f32[16,16]{1,0:T(8,128)}) custom-call(bf16[64,128]{1,0:T(8,128)(2,1)S(1)} %get-tuple-element.93.rest_0_, bf16[64,128]{1,0:T(8,128)(2,1)S(1)} %collective-permute-done.6.rest_1_, bf16[64,128]{1,0:T(8,128)(2,1)S(1)} %collective-permute-done.7.rest_2_, ...), custom_call_target="tpu_custom_call" | custom-call | tf_op jit(solution)/shard_map/col_sum/pallas_call | solution.py:412
  (2 shorter events, 0.0 us)
Async XLA Ops:
  2.9 1.7 %collective-permute-start = (bf16[2,128,128]{2,1,0:T(8,128)(2,1)S(1)}, bf16[2,128,128]{2,1,0:T(8,128)(2,1)S(1)}, u32[]{:S(2)}, u32[]{:S(2)}) collective-permute-start(bf16[2,128,128]{2,1,0:T(8,128)(2,1)S(1)} %get-tuple-element.53.rest_1_), channel_id=1, source_target_pairs={{0,4},{1,8},{2,16},{3,24},{4,0},{5,12},{6,20},{7,28},{8,1},{9,13},... | collective-permute-start | bytes 196616 | tf_op jit(solution)/shard_map/ppermute | solution.py:313
  4.7 1.3 %collective-permute-start.1 = (bf16[128,128]{1,0:T(8,128)(2,1)S(1)}, bf16[128,128]{1,0:T(8,128)(2,1)S(1)}, u32[]{:S(2)}, u32[]{:S(2)}) collective-permute-start(bf16[128,128]{1,0:T(8,128)(2,1)S(1)} %slice_bitcast_fusion), channel_id=1, source_target_pairs={{0,4},{4,0},{8,12},{12,8},{16,20},{20,16},{24,28},{28,24},{1,5},{5... | collective-permute-start | bytes 98312 | tf_op jit(solution)/shard_map/ppermute | solution.py:335
  7.0 1.6 %collective-permute-start.2 = (bf16[4,208,128]{2,1,0:T(8,128)(2,1)S(1)}, bf16[4,208,128]{2,1,0:T(8,128)(2,1)S(1)}, u32[]{:S(2)}, u32[]{:S(2)}) collective-permute-start(bf16[4,208,128]{2,1,0:T(8,128)(2,1)S(1)} %get-tuple-element.75), channel_id=1, source_target_pairs={{0,4},{4,0},{8,12},{12,8},{16,20},{20,16},{24,28},{28,24},{1,5},{5... | collective-permute-start | bytes 638984 | tf_op jit(solution)/shard_map/ppermute | solution.py:386
  8.6 12.5 %collective-permute-start.3 = (bf16[208,128]{1,0:T(8,128)(2,1)S(1)}, bf16[208,128]{1,0:T(8,128)(2,1)S(1)}, u32[]{:S(2)}, u32[]{:S(2)}) collective-permute-start(bf16[208,128]{1,0:T(8,128)(2,1)S(1)} %get-tuple-element.77), channel_id=1, source_target_pairs={{0,24},{4,28},{8,16},{12,20},{16,8},{20,12},{24,0},{28,4},{1,25},{... | collective-permute-start | bytes 159752 | tf_op jit(solution)/shard_map/ppermute | solution.py:397
  18.7 4.1 %collective-permute-start.4 = (bf16[208,128]{1,0:T(8,128)(2,1)S(1)}, bf16[208,128]{1,0:T(8,128)(2,1)S(1)}, u32[]{:S(2)}, u32[]{:S(2)}) collective-permute-start(bf16[208,128]{1,0:T(8,128)(2,1)S(1)} %get-tuple-element.78), channel_id=1, source_target_pairs={{0,16},{4,20},{8,24},{12,28},{16,0},{20,4},{24,8},{28,12},{1,17},{... | collective-permute-start | bytes 159752 | tf_op jit(solution)/shard_map/ppermute | solution.py:397
  18.7 4.1 %collective-permute-start.5 = (bf16[208,128]{1,0:T(8,128)(2,1)S(1)}, bf16[208,128]{1,0:T(8,128)(2,1)S(1)}, u32[]{:S(2)}, u32[]{:S(2)}) collective-permute-start(bf16[208,128]{1,0:T(8,128)(2,1)S(1)} %get-tuple-element.79), channel_id=1, source_target_pairs={{0,8},{4,12},{8,0},{12,4},{16,24},{20,28},{24,16},{28,20},{1,9},{5... | collective-permute-start | bytes 159752 | tf_op jit(solution)/shard_map/ppermute | solution.py:397
  22.9 5.6 %collective-permute-start.6 = (bf16[64,128]{1,0:T(8,128)(2,1)S(1)}, bf16[64,128]{1,0:T(8,128)(2,1)S(1)}, u32[]{:S(2)}, u32[]{:S(2)}) collective-permute-start(bf16[64,128]{1,0:T(8,128)(2,1)S(1)} %get-tuple-element.94), channel_id=1, source_target_pairs={{0,3},{1,2},{2,1},{3,0},{4,7},{5,6},{6,5},{7,4},{8,11},{9,10},{10,... | collective-permute-start | bytes 49160 | tf_op jit(solution)/shard_map/ppermute | solution.py:411
  26.5 4.6 %collective-permute-start.7 = (bf16[64,128]{1,0:T(8,128)(2,1)S(1)}, bf16[64,128]{1,0:T(8,128)(2,1)S(1)}, u32[]{:S(2)}, u32[]{:S(2)}) collective-permute-start(bf16[64,128]{1,0:T(8,128)(2,1)S(1)} %get-tuple-element.95), channel_id=1, source_target_pairs={{0,2},{1,3},{2,0},{3,1},{4,6},{5,7},{6,4},{7,5},{8,10},{9,11},{10,... | collective-permute-start | bytes 49160 | tf_op jit(solution)/shard_map/ppermute | solution.py:411
  26.5 4.6 %collective-permute-start.8 = (bf16[64,128]{1,0:T(8,128)(2,1)S(1)}, bf16[64,128]{1,0:T(8,128)(2,1)S(1)}, u32[]{:S(2)}, u32[]{:S(2)}) collective-permute-start(bf16[64,128]{1,0:T(8,128)(2,1)S(1)} %get-tuple-element.96), channel_id=1, source_target_pairs={{0,1},{1,0},{2,3},{3,2},{4,5},{5,4},{6,7},{7,6},{8,9},{9,8},{10,11... | collective-permute-start | bytes 49160 | tf_op jit(solution)/shard_map/ppermute | solution.py:411

commit v7 on v6

v7 whole, which is shorter than its diff:
```python
import functools

import jax
import jax.numpy as jnp
from jax import lax
from jax.experimental import pallas as pl
from jax.experimental.pallas import tpu as pltpu
from jax.sharding import PartitionSpec as P

eps = 1e-05
f32 = jnp.float32
bf16 = jnp.bfloat16
HBM = pl.BlockSpec(memory_space=pltpu.HBM)
VMEM = pl.BlockSpec(memory_space=pltpu.VMEM)
PARAMS = pltpu.CompilerParams(vmem_limit_bytes=24 * 1024 * 1024)


def nn(a, b):
    return lax.dot_general(a, b, (((1,), (0,)), ((), ())), preferred_element_type=f32)


def nt(a, b):
    return lax.dot_general(a, b, (((1,), (1,)), ((), ())), preferred_element_type=f32)


def tn(a, b):
    return lax.dot_general(a, b, (((0,), (0,)), ((), ())), preferred_element_type=f32)


def normalize(flat):
    values = flat.astype(f32)
    centre = values - jnp.mean(values, axis=-1, keepdims=True)
    scale_inv = lax.rsqrt(jnp.mean(centre * centre, axis=-1, keepdims=True) + eps)
    return centre * scale_inv, scale_inv


def sigmoid(v):
    return 0.5 * jnp.tanh(0.5 * v) + 0.5


def chunks_of(size, most):
    step = most if size % most == 0 else size
    return [(at, step) for at in range(0, size, step)]


def partner(s, p, n):
    if n & (n - 1) == 0:
        return s ^ p
    return (s + p) % n if isinstance(s, int) else lax.rem(s + p, n)


def lane_packs(bins, side):
    packs = max(1, 128 // bins)
    return packs if (side // packs) % 16 == 0 else 1


def forward_kernel(q, *refs):
    sources, (pair, w_gate, w_up, w_out, w_head, marks, sends), (targets, halves, sems) = refs[:6], refs[6:13], refs[13:]
    _, side, width = pair.shape
    edge = sources[0].shape[0]
    bins = w_head.shape[0]
    copies = [
        pltpu.make_async_copy(source, target, sems.at[i])
        for i, (source, target) in enumerate(zip(sources[1:], (w_gate, w_up, w_out, w_head, targets)))
    ]
    pieces = [
        pltpu.make_async_copy(
            sources[0].at[:, h * edge : (h + 1) * edge, :], pair.reshape(q, edge, edge, width).at[h], sems.at[5 + h]
        )
        for h in range(q)
    ]
    for copy in pieces + copies:
        copy.start()
    shift = edge.bit_length() - 1
    out_row = lax.broadcasted_iota(jnp.int32, (side, side), 0)
    in_row = lax.broadcasted_iota(jnp.int32, (side, side), 1)
    wanted = ((out_row & (edge - 1)) << shift) | (out_row >> shift)
    swap = jnp.where(in_row == wanted, 1.0, 0.0).astype(bf16)
    own = lax.rem(lax.axis_index("row"), q)
    for copy in pieces:
        copy.wait()
    flat = pair[...].reshape(q * side, width)
    inputs = normalize(flat)[0].astype(bf16)
    total = flat.astype(f32)
    for copy in copies:
        copy.wait()
    for at, step in chunks_of(w_gate.shape[1], 256):
        gate = nn(inputs, w_gate[:, at : at + step])
        upper = nn(inputs, w_up[:, at : at + step])
        hidden = (gate * sigmoid(gate) * upper).astype(bf16)
        total = total + nn(hidden, w_out[at : at + step, :])
    logit = nt(total.astype(bf16), w_head[...]).astype(bf16)
    packs = lane_packs(bins, side)
    deep = side // packs
    for h in range(q):
        piece = nn(swap, logit[h * side : (h + 1) * side])
        if packs > 1:
            piece = jnp.concatenate([piece[u * deep : (u + 1) * deep] for u in range(packs)], axis=1)
        halves[h] = piece.astype(bf16)
        mark = targets[:, h * edge : (h + 1) * edge].astype(f32)
        marks[h] = jnp.concatenate([mark, jnp.zeros((edge, width - edge), f32)], axis=1).astype(bf16)
    for p in range(q):
        sends[p] = halves[partner(own, p, q)]


def lend_kernel(q, pair, marks, *lent):
    own = lax.rem(lax.axis_index("row"), q)
    side = pair.shape[1]
    for p in range(1, q):
        first, second = lent[2 * p - 2 : 2 * p]
        block = pair[partner(own, p, q)]
        first[...] = block[: side // 2]
        second[: side // 2] = block[side // 2 :]
        second[side // 2 :] = marks[partner(own, p, q)]


def prepare_kernel(q, p, *refs):
    if p:
        first, second, refs = refs[0], refs[1], refs[2:]
        side = 2 * first.shape[0]
        edge = second.shape[0] - first.shape[0]
        flat = jnp.concatenate([first[...], second[: side // 2]], axis=0)
        mark = second[side // 2 :]
    else:
        own = lax.rem(lax.axis_index("row"), q)
        side, edge = refs[0].shape[1], refs[1].shape[1]
        flat, mark, refs = refs[0][own], refs[1][own], refs[2:]
    w_gate, w_up, w_out, w_head, inputs_t, updated_t, hidden, slope, swish, logits, onehot, normed, scale = refs
    width, bins = flat.shape[1], w_head.shape[0]
    normal, scale_inv = normalize(flat)
    normed[...] = normal
    scale[...] = jnp.broadcast_to(scale_inv, normal.shape)
    inputs = normal.astype(bf16)
    inputs_t[...] = inputs.T
    total = flat.astype(f32)
    for at, step in chunks_of(w_gate.shape[1], 256):
        span = slice(at, at + step)
        gate = nn(inputs, w_gate[:, span])
        upper = nn(inputs, w_up[:, span])
        sigma = sigmoid(gate)
        swished = gate * sigma
        hidden_part = (swished * upper).astype(bf16)
        swish[:, span] = swished
        hidden[:, span] = hidden_part
        slope[:, span] = upper * sigma * (1.0 + gate * (1.0 - sigma))
        total = total + nn(hidden_part, w_out[span, :])
    upd = total.astype(bf16)
    updated_t[...] = upd.T
    logits[...] = nt(upd, w_head[...]).astype(bf16)
    shift = edge.bit_length() - 1
    rows = lax.broadcasted_iota(jnp.int32, (side, edge), 0) >> shift
    pick = jnp.where(rows == lax.broadcasted_iota(jnp.int32, (side, edge), 1), 1.0, 0.0).astype(bf16)
    columns = lax.broadcasted_iota(jnp.int32, (side, width), 0) & (edge - 1)
    mask = columns == lax.broadcasted_iota(jnp.int32, (side, width), 1)
    lanes = lax.broadcasted_iota(jnp.int32, (side, bins), 1).astype(f32)
    picked = jnp.where(mask, nn(pick, mark), 0.0).astype(bf16)
    wanted = nn(picked, jnp.ones((width, bins), bf16))
    onehot[...] = jnp.where(wanted == lanes, 1.0, 0.0)


def backward_kernel(q, packed, *refs):
    blocks, (w_out, w_head, far, near), rest = [refs[7 * p : 7 * p + 7] for p in range(q)], refs[7 * q : 7 * q + 4], refs[7 * q + 4 :]
    results, hot, mirrored = [rest[3 * p : 3 * p + 3] for p in range(q)], rest[3 * q : -1], rest[-1]
    (width, side), units, bins = blocks[0][0].shape, w_out.shape[0], w_head.shape[0]
    packs = lane_packs(bins, side)
    own = lax.rem(lax.axis_index("row"), q)
    inside = lax.axis_index("row") // q == lax.axis_index("col")

    @pl.when(inside)
    def _():
        mirrored[...] = near[...]

    @pl.when(jnp.logical_not(inside))
    def _():
        mirrored[...] = far[...]

    totals = None
    for p in range(q):
        inputs_t, updated_t, hidden, slope, swish, logits, onehot = blocks[p]
        d_updated, d_gate, d_up = results[p]
        pieces = [mirrored[p, :, u * bins : (u + 1) * bins] for u in range(packs)]
        summed = logits[...].astype(f32) + jnp.concatenate(pieces, axis=0).astype(f32)
        powers = jnp.exp(summed - jnp.max(summed, axis=-1, keepdims=True))
        probs = powers / jnp.sum(powers, axis=-1, keepdims=True)
        grad_sym = (probs - onehot[...]).astype(bf16)
        cotangent = (grad_sym.astype(f32) * 2.0).astype(bf16)
        d_upd = nn(cotangent, w_head[...])
        d_updated[...] = d_upd
        d_upd_b = d_upd.astype(bf16)
        d_upd_t = d_upd_b.T
        terms = [[], [], []]
        for at, step in chunks_of(units, 256):
            span = slice(at, at + step)
            d_hidden = nt(d_upd_b, w_out[span, :])
            d_gate_part = (d_hidden * slope[:, span]).astype(bf16)
            d_up_part = (d_hidden * swish[:, span]).astype(bf16)
            d_gate[:, span] = d_gate_part
            d_up[:, span] = d_up_part
            terms[0].append(nn(inputs_t[...], d_gate_part))
            terms[1].append(nn(inputs_t[...], d_up_part))
            terms[2].append(nn(d_upd_t, hidden[:, span]))
        terms = [jnp.concatenate(term, axis=1) for term in terms] + [nn(updated_t[...], cotangent)]
        totals = [a + b for a, b in zip(totals, terms)] if p else terms
    if not packed:
        for ref, term in zip(hot, totals):
            ref[...] = term.astype(ref.dtype)
        return
    gate_term, up_term, out_term, head_term = totals
    hot, slots = hot[:-1], hot[-1]
    nrow, ncol = packed
    groups = nrow // q
    lanes, part, tall = units // ncol, width // nrow, units // nrow
    deep = width // q
    for k in range(q):
        for a in range(groups):
            r = a * q + k
            at = 0
            for term in (gate_term, up_term):
                for c in range(ncol):
                    block = term[r * part : (r + 1) * part, c * lanes : (c + 1) * lanes]
                    slots[k, a, at : at + part] = block.astype(bf16)
                    at += part
            pieces = [out_term[u * deep : (u + 1) * deep, r * tall : (r + 1) * tall] for u in range(q)]
            slots[k, a, at : at + deep] = jnp.concatenate(pieces, axis=1).astype(bf16)
            at += deep
            block = head_term[r * part : (r + 1) * part, :]
            block = jnp.concatenate([block, jnp.zeros((part, lanes - bins), f32)], axis=1)
            slots[k, a, at : at + part] = block.astype(bf16)
    for n in range(q):
        hot[n][...] = slots[partner(own, n, q)]


def input_kernel(d_updated, d_gate, d_up, normed, scale, w_gate, w_up, result):
    d_inputs = nt(d_gate[...], w_gate[...]) + nt(d_up[...], w_up[...])
    normal = normed[...]
    d_norm = (
        d_inputs
        - jnp.mean(d_inputs, axis=-1, keepdims=True)
        - normal * jnp.mean(d_inputs * normal, axis=-1, keepdims=True)
    ) * scale[...]
    result[...] = (d_updated[...] + d_norm).astype(bf16)


def place_kernel(q, *refs):
    blocks, d_pair = refs[:-1], refs[-1]
    edge, _, _, width = d_pair.shape
    own = lax.rem(lax.axis_index("row"), q)
    d_pair[:, own] = blocks[0][...].reshape(edge, edge, width)
    for p in range(1, q):
        for n, half in enumerate((slice(0, edge // 2), slice(edge // 2, edge))):
            d_pair[half, partner(own, p, q)] = blocks[2 * p - 1 + n][...].reshape(edge // 2, edge, width)


def core_sum_kernel(q, groups, *rest):
    terms, blocks, hot, handed = rest[:q], rest[q : 2 * q - 1], rest[2 * q - 1 : 2 - 2 * q], rest[2 - 2 * q :]
    mine = lax.axis_index("row") // q
    for p in range(groups):
        a = partner(mine, p, groups)
        total = terms[0][a].astype(f32)
        for term in terms[1:]:
            total = total + term[a].astype(f32)
        hot[p][...] = total.astype(bf16)
    for p, block in enumerate(blocks):
        half = block.shape[0] // 2
        handed[2 * p][...] = block[:half]
        handed[2 * p + 1][...] = block[half:]


def chip_sum_kernel(q, groups, ncol, shapes, *rest):
    terms, hot, slots = rest[:groups], rest[groups:-1], rest[-1]
    part, lanes, deep, tall, few = shapes
    total = terms[0][...].astype(f32)
    for term in terms[1:]:
        total = total + term[...].astype(f32)
    at = 2 * ncol * part
    out = total[at : at + deep]
    head = total[at + deep : at + deep + part]
    narrow = deep * q // ncol
    fold = lanes // tall
    short = narrow // fold
    for c in range(ncol):
        slots[c, 0:part] = total[c * part : (c + 1) * part].astype(bf16)
        slots[c, part : 2 * part] = total[(ncol + c) * part : (ncol + c + 1) * part].astype(bf16)
        u, top = (c * narrow) // deep, (c * narrow) % deep
        block = out[top : top + narrow, u * tall : (u + 1) * tall]
        block = jnp.concatenate([block[v * short : (v + 1) * short] for v in range(fold)], axis=1)
        slots[c, 2 * part : 2 * part + short] = block.astype(bf16)
        piece = jnp.concatenate([head[:, c * few : (c + 1) * few], jnp.zeros((part, lanes - few), f32)], axis=1)
        slots[c, 2 * part + short : 3 * part + short] = piece.astype(bf16)
    for p in range(ncol):
        hot[p][...] = slots[partner(lax.axis_index("col"), p, ncol)]


def col_sum_kernel(shapes, factor, *rest):
    terms, (gate, up, out, head) = rest[:-4], rest[-4:]
    part, lanes, tall, few = shapes
    total = terms[0][...].astype(f32)
    for term in terms[1:]:
        total = total + term[...].astype(f32)
    total = total * factor
    fold = lanes // tall
    short = out.shape[0] // fold
    gate[...] = total[0:part]
    up[...] = total[part : 2 * part]
    for v in range(fold):
        out[v * short : (v + 1) * short, :] = total[2 * part : 2 * part + short, v * tall : (v + 1) * tall]
    head[...] = total[2 * part + short : 3 * part + short, 0:few]


def core_pairs(nrow, q, p):
    return [(s, s - s % q + partner(s % q, p, q)) for s in range(nrow)]


def shaped(shape, kind):
    return jax.ShapeDtypeStruct(shape, kind)


def cost(flops, moved):
    return pl.CostEstimate(flops=flops, bytes_accessed=moved, transcendentals=0)


def body(pair, targets, w_gate, w_up, w_out, w_head):
    rows, cols, width = pair.shape
    units = w_gate.shape[1]
    bins = w_head.shape[1]
    nrow, ncol = lax.axis_size("row"), lax.axis_size("col")
    q = nrow // ncol
    groups = nrow // q
    side = rows * cols // q
    packs = lane_packs(bins, side)
    head_t = w_head.T
    piece = (side // packs, bins * packs)

    sources = (pair, w_gate, w_up, w_out, head_t, targets)
    pair, w_gate, w_up, w_out, head_t, marks, sends = pl.pallas_call(
        functools.partial(forward_kernel, q),
        out_shape=[shaped((q, side, width), bf16)]
        + [shaped(x.shape, bf16) for x in sources[1:5]]
        + [shaped((q, rows, width), bf16), shaped((q, *piece), bf16)],
        in_specs=[HBM] * 6,
        out_specs=[VMEM] * 7,
        scratch_shapes=[
            pltpu.VMEM((rows, cols), jnp.int32),
            pltpu.VMEM((q, *piece), bf16),
            pltpu.SemaphoreType.DMA((5 + q,)),
        ],
        compiler_params=PARAMS,
        name="forward",
    )(*(pltpu.with_memory_space_constraint(x, pltpu.HBM) for x in sources))

    pairs = [
        (r * ncol + c, (q * c + (partner(r % q, 1, q) if q == 2 and r // q == c else r % q)) * ncol + r // q)
        for r in range(nrow)
        for c in range(ncol)
    ]
    far = lax.ppermute(sends, ("row", "col"), pairs)
    lent = pl.pallas_call(
        functools.partial(lend_kernel, q),
        out_shape=[shaped((side // 2, width), bf16), shaped((side // 2 + rows, width), bf16)] * (q - 1),
        in_specs=[VMEM] * 2,
        out_specs=[VMEM] * (2 * q - 2),
        compiler_params=PARAMS,
        name="lend",
    )(pair, marks)
    borrowed = [lax.ppermute(x, "row", core_pairs(nrow, q, n // 2 + 1)) for n, x in enumerate(lent)]
    prepared = []
    for p in range(q):
        source = borrowed[2 * p - 2 : 2 * p] if p else (pair, marks)
        prepared.append(
            pl.pallas_call(
                functools.partial(prepare_kernel, q, p),
                out_shape=[
                    shaped((width, side), bf16),
                    shaped((width, side), bf16),
                    shaped((side, units), bf16),
                    shaped((side, units), f32),
                    shaped((side, units), f32),
                    shaped((side, bins), bf16),
                    shaped((side, bins), f32),
                    shaped((side, width), f32),
                    shaped((side, width), f32),
                ],
                in_specs=[VMEM] * (len(source) + 4),
                out_specs=[VMEM] * 9,
                compiler_params=PARAMS,
                cost_estimate=cost(0, 0) if p else cost(6 * side * width * units, 8 * side * units),
                name="prepare",
            )(*source, w_gate, w_up, w_out, head_t)
        )

    part, tall, few = width // nrow, units // nrow, bins // ncol
    lanes, deep = units // ncol, width // q
    fits = (
        part % 16 == 0 and lanes == 128 and tall * q == lanes and bins <= lanes and deep % (width // ncol) == 0
        and (width // ncol * tall // lanes) % 16 == 0
    )
    height = 2 * ncol * part + deep + part
    if fits:
        hot_shapes = [shaped((groups, height, lanes), bf16)] * q
        scratch = [pltpu.VMEM((q, groups, height, lanes), bf16)]
    else:
        hot_shapes = [shaped((width, n), bf16) for n in (units, units, units, bins)]
        scratch = []
    results = pl.pallas_call(
        functools.partial(backward_kernel, q, (nrow, ncol) if fits else None),
        out_shape=([shaped((side, width), f32)] + [shaped((side, units), bf16)] * 2) * q + hot_shapes,
        in_specs=[VMEM] * (7 * q + 4),
        out_specs=[VMEM] * (3 * q + len(hot_shapes)),
        scratch_shapes=scratch + [pltpu.VMEM((q, *piece), bf16)],
        compiler_params=PARAMS,
        cost_estimate=cost(8 * q * side * width * units, 4 * q * side * units),
        name="backward",
    )(*(x for block in prepared for x in block[:7]), w_out, head_t, far, sends)
    hot = list(results[3 * q :])

    def d_inputs(p):
        return pl.pallas_call(
            input_kernel,
            out_shape=shaped((side, width), bf16),
            in_specs=[VMEM] * 7,
            out_specs=VMEM,
            compiler_params=PARAMS,
            cost_estimate=cost(4 * side * width * units, 4 * side * units),
            name="d_inputs",
        )(*results[3 * p : 3 * p + 3], *prepared[p][7:], w_gate, w_up)

    d_blocks = [d_inputs(p) for p in range(q)]

    def returned(blocks):
        moved = [lax.ppermute(x, "row", core_pairs(nrow, q, n // 2 + 1)) for n, x in enumerate(blocks[1:])]
        return blocks[:1] + moved

    def placed(blocks):
        return pl.pallas_call(
            functools.partial(place_kernel, q),
            out_shape=shaped((rows, q, cols // q, width), bf16),
            in_specs=[VMEM] * (2 * q - 1),
            out_specs=VMEM,
            compiler_params=PARAMS,
            name="place",
        )(*blocks).reshape(rows, cols, width)

    factor = 1.0 / (rows * nrow)
    if not fits:
        owned = []
        hot[2] = hot[2].T
        for term in hot:
            mine = lax.psum_scatter(term, "row", scatter_dimension=0, tiled=True).astype(f32)
            owned.append(lax.psum_scatter(mine, "col", scatter_dimension=1, tiled=True) * factor)
        d_blocks = d_blocks[:1] + [half for block in d_blocks[1:] for half in (block[: side // 2], block[side // 2 :])]
        return (placed(returned(d_blocks)), *owned)

    terms = [hot[0]]
    for p in range(1, q):
        terms.append(lax.ppermute(hot[p], "row", core_pairs(nrow, q, p)))
    terms, d_blocks = lax.optimization_barrier((terms, d_blocks))
    hot = pl.pallas_call(
        functools.partial(core_sum_kernel, q, groups),
        out_shape=[shaped((height, lanes), bf16)] * groups + [shaped((side // 2, width), bf16)] * (2 * q - 2),
        in_specs=[VMEM] * (2 * q - 1),
        out_specs=[VMEM] * (groups + 2 * q - 2),
        compiler_params=PARAMS,
        name="core_sum",
    )(*terms, *d_blocks[1:])
    hot, d_blocks = hot[:groups], d_blocks[:1] + list(hot[groups:])
    terms = [hot[0]]
    for p in range(groups - 1, 0, -1):
        terms.append(lax.ppermute(hot[p], "row", [(s, partner(s // q, p, groups) * q + s % q) for s in range(nrow)]))
    terms, d_blocks = lax.optimization_barrier((terms, returned(d_blocks)))
    short = 3 * part + width // ncol * tall // lanes
    hot = pl.pallas_call(
        functools.partial(chip_sum_kernel, q, groups, ncol, (part, lanes, deep, tall, few)),
        out_shape=[shaped((short, lanes), bf16)] * ncol,
        in_specs=[VMEM] * groups,
        out_specs=[VMEM] * ncol,
        scratch_shapes=[pltpu.VMEM((ncol, short, lanes), bf16)],
        compiler_params=PARAMS,
        name="chip_sum",
    )(*terms)
    terms = [hot[0]]
    for p in sorted(range(1, ncol), key=lambda p: (p != ncol // 2, -p)):
        terms.append(lax.ppermute(hot[p], "col", [(s, partner(s, p, ncol)) for s in range(ncol)]))
    *terms, d_pair = lax.optimization_barrier((*terms, placed(d_blocks)))
    gate, up, out, head = pl.pallas_call(
        functools.partial(col_sum_kernel, (part, lanes, tall, few), factor),
        out_shape=[
            shaped((part, lanes), f32),
            shaped((part, lanes), f32),
            shaped((width // ncol, tall), f32),
            shaped((part, few), f32),
        ],
        in_specs=[VMEM] * ncol,
        out_specs=[VMEM] * 4,
        compiler_params=PARAMS,
        name="col_sum",
    )(*terms)
    return d_pair, gate, up, out.T, head


def solution(mesh):
    placed = (P("row", "col", None), P("row", "col"), P(), P(), P(), P())
    return jax.shard_map(
        body,
        mesh=mesh,
        in_specs=placed,
        out_specs=(P("row", "col", None), P("row", "col"), P("row", "col"), P("row", "col"), P("row", "col")),
        check_vma=False,
    )
```

time: 31.9 us -> 31 us (0.972)
  waiting for transfers between devices: 7.18 us -> 6.55 us
  Pallas kernels: 7.28 us -> 7.9 us
  starting transfers between devices: 16.3 us -> 15.7 us
    ppermute x3, starting transfers between devices: 10.7 us -> 9.63 us  [body(): lax.ppermute(hot[p], 'row', [(s, partner(s // q, p, groups) * q + s % q)...]
    ppermute x2 -> x5, starting transfers between devices: 0.64 us -> 1.55 us  [the longest x1 0.53 us: body(): far = lax.ppermute(sends, ('row', 'col'), pairs)]
    ppermute x2 -> x5, waiting for transfers between devices: 0.13 us -> 0.87 us  [the longest x2 0.86 us: returned(): lax.ppermute(x, 'row', core_pairs(nrow, q, n // 2 + 1))]
    ppermute x1, waiting for transfers between devices: 1.09 us -> 0.38 us  [body(): terms.append(lax.ppermute(hot[p], 'row', core_pairs(nrow, q, p)))]
    pallas_call x5 -> x8, Pallas kernels: 6.45 us -> 7.06 us  [the longest x1 2.27 us: body(): pl.pallas_call(functools.partial(forward_kernel, q), out_shape=[shaped((q...]
    ppermute x3, waiting for transfers between devices: 3.71 us -> 3.18 us  [body(): lax.ppermute(hot[p], 'col', [(s, partner(s, p, ncol)) for s in range(ncol)])]
    ppermute x3, starting transfers between devices: 4.45 us -> 4.09 us  [body(): lax.ppermute(hot[p], 'col', [(s, partner(s, p, ncol)) for s in range(ncol)])]
  transfers between devices with their start and end apart: 9 -> 12, of which waited for: 6 -> 6; matrix products, arithmetic and copies ran while one was open for 1% -> 0% of each run, Pallas kernels for 10% -> 10%
where the time goes in v7:
time: 31 us; the launch traced here: 30.8 us
  starting transfers between devices  15.7 us (51%)
  Pallas kernels  7.9 us (25%)
  waiting for transfers between devices  6.55 us (21%)
  between operations  0.72 us (2%)
    ppermute x3, starting transfers between devices, body(): lax.ppermute(hot[p], 'row', [(s, partner(s // q, p, groups) * q + s % q)...  9.63 us
    ppermute x3, starting transfers between devices, body(): lax.ppermute(hot[p], 'col', [(s, partner(s, p, ncol)) for s in range(ncol)])  4.09 us
    ppermute x3, waiting for transfers between devices, body(): lax.ppermute(hot[p], 'col', [(s, partner(s, p, ncol)) for s in range(ncol)])  3.18 us
    pallas_call x1, Pallas kernels, body(): pl.pallas_call(functools.partial(forward_kernel, q), out_shape=[shaped((q...  2.27 us
    ppermute x3, waiting for transfers between devices, body(): lax.ppermute(hot[p], 'row', [(s, partner(s // q, p, groups) * q + s % q)...  2.12 us
    pallas_call x2, Pallas kernels, body(): pl.pallas_call(functools.partial(prepare_kernel, q, p), out_shape=[shaped...  1.77 us
    pallas_call x1, Pallas kernels, body(): pl.pallas_call(functools.partial(backward_kernel, q, (nrow, ncol) if fits...  1.58 us
    ppermute x2, waiting for transfers between devices, returned(): lax.ppermute(x, 'row', core_pairs(nrow, q, n // 2 + 1))  0.86 us
  transfers between devices with their start and end apart: 12, of which 6 were waited for; matrix products, arithmetic and copies ran while one was open for 0% of the time, Pallas kernels for 10%

profile of v7, /device:TPU:0, one launch (start us, length us, event | category | flops | bytes accessed | tf_op | source)
XLA Modules:
  0.0 30.8 jit_solution(1812925446654826367)
XLA Ops:
  0.6 2.3 %forward.1 = (bf16[2,256,128]{2,1,0:T(8,128)(2,1)S(1)}, bf16[128,512]{1,0:T(8,128)(2,1)S(1)}, bf16[128,512]{1,0:T(8,128)(2,1)S(1)}, bf16[512,128]{1,0:T(8,128)(2...) custom-call(bf16[16,32,128]{2,1,0:T(8,128)(2,1)} %refs_0_.1, ...), custom_call_target="tpu_custom_call" | custom-call | tf_op jit(solution)/shard_map/forward/pallas_call | solution.py:335
  2.9 0.5 %collective-permute-start.2 = (bf16[2,128,128]{2,1,0:T(8,128)(2,1)S(1)}, bf16[2,128,128]{2,1,0:T(8,128)(2,1)S(1)}, u32[]{:S(2)}, u32[]{:S(2)}) collective-permute-start(bf16[2,128,128]{2,1,0:T(8,128)(2,1)S(1)} %get-tuple-element.92.refs_17_), channel_id=1, source_target_pairs={{0,4},{1,8},{2,16},{3,24},{4,0},{5,12},{6,20},{7,28},{8,1},{9,13},... | collective-permute-start | bytes 196616 | tf_op jit(solution)/shard_map/ppermute | solution.py:356
  3.4 0.1 collective-permute-start.1
  3.5 0.4 %collective-permute-start = (bf16[128,128]{1,0:T(8,128)(2,1)S(1)}, bf16[128,128]{1,0:T(8,128)(2,1)S(1)}, u32[]{:S(2)}, u32[]{:S(2)}) collective-permute-start(bf16[128,128]{1,0:T(8,128)(2,1)S(1)} %get-tuple-element.83), channel_id=1, source_target_pairs={{0,4},{4,0},{8,12},{12,8},{16,20},{20,16},{24,28},{28,24},{1,5},{5... | collective-permute-start | bytes 98312 | tf_op jit(solution)/shard_map/ppermute | solution.py:365
  4.0 0.9 %prepare.2 = (bf16[128,256]{1,0:T(8,128)(2,1)S(1)}, bf16[128,256]{1,0:T(8,128)(2,1)S(1)}, bf16[256,512]{1,0:T(8,128)(2,1)S(1)}, f32[256,512]{1,0:T(8,128)S(1)}, ...) custom-call(bf16[2,256,128]{2,1,0:T(8,128)(2,1)S(1)} %get-tuple-elem, ...), custom_call_target="tpu_custom_call" | custom-call | flops 100663296 | bytes 1048576 | tf_op jit(solution)/shard_map/prepare/pallas_call | solution.py:370
  4.8 0.0 collective-permute-done.refs_0_
  4.9 0.0 collective-permute-done.1.refs_1_
  4.9 0.9 %prepare.3 = (bf16[128,256]{1,0:T(8,128)(2,1)S(1)}, bf16[128,256]{1,0:T(8,128)(2,1)S(1)}, bf16[256,512]{1,0:T(8,128)(2,1)S(1)}, f32[256,512]{1,0:T(8,128)S(1)}, ...) custom-call(bf16[128,128]{1,0:T(8,128)(2,1)S(1)} %collective-permute, ...), custom_call_target="tpu_custom_call" | custom-call | tf_op jit(solution)/shard_map/prepare/pallas_call | solution.py:370
  5.8 0.0 collective-permute-done.2.refs_16_
  5.8 1.6 %backward.1 = (f32[256,128]{1,0:T(8,128)S(1)}, bf16[256,512]{1,0:T(8,128)(2,1)S(1)}, bf16[256,512]{1,0:T(8,128)(2,1)S(1)}, f32[256,128]{1,0:T(8,128)S(1)}, bf16[...) custom-call(bf16[128,256]{1,0:T(8,128)(2,1)S(1)} %get-tuple-element., ...), custom_call_target="tpu_custom_call" | custom-call | flops 268435456 | bytes 1048576 | tf_op jit(solution)/shard_map/backward/pallas_call | solution.py:404
  7.4 0.4 %collective-permute-start.3 = (bf16[4,208,128]{2,1,0:T(8,128)(2,1)S(1)}, bf16[4,208,128]{2,1,0:T(8,128)(2,1)S(1)}, u32[]{:S(2)}, u32[]{:S(2)}) collective-permute-start(bf16[4,208,128]{2,1,0:T(8,128)(2,1)S(1)} %get-tuple-element.94), channel_id=1, source_target_pairs={{0,4},{4,0},{8,12},{12,8},{16,20},{20,16},{24,28},{28,24},{1,5},{5... | collective-permute-start | bytes 638984 | tf_op jit(solution)/shard_map/ppermute | solution.py:455
  7.7 0.4 %d_inputs.3.rest_2_ = bf16[256,128]{1,0:T(8,128)(2,1)S(1)} custom-call(f32[256,128]{1,0:T(8,128)S(1)} %get-tuple-element.100.d_updated, bf16[256,512]{1,0:T(8,128)(2,1)S(1)} %get-tuple-element.101.d_gate, bf16[256,512]{1,0:T(8,128)(2,1)S(1)} %get-tuple-element.102.d_up, f32[256,128]{1,0:T(8,128)S(1)} %get-tuple-element.103.normed, ...), custom_call_target="tpu_custom_call" | custom-call | flops 67108864 | bytes 524288 | tf_op jit(solution)/shard_map/d_inputs/pallas_call | solution.py:417
  8.1 0.4 %d_inputs.2.refs_0_ = bf16[256,128]{1,0:T(8,128)(2,1)S(1)} custom-call(f32[256,128]{1,0:T(8,128)S(1)} %get-tuple-element.95.d_updated, bf16[256,512]{1,0:T(8,128)(2,1)S(1)} %get-tuple-element.96.d_gate, bf16[256,512]{1,0:T(8,128)(2,1)S(1)} %get-tuple-element.97.d_up, f32[256,128]{1,0:T(8,128)S(1)} %get-tuple-element.98.normed, ...), custom_call_target="tpu_custom_call" | custom-call | flops 67108864 | bytes 524288 | tf_op jit(solution)/shard_map/d_inputs/pallas_call | solution.py:417
  8.5 0.4 %collective-permute-done.3.rest_1_ = bf16[4,208,128]{2,1,0:T(8,128)(2,1)S(1)} collective-permute-done((bf16[4,208,128]{2,1,0:T(8,128)(2,1)S(1)}, bf16[4,208,128]{2,1,0:T(8,128)(2,1)S(1)}, u32[]{:S(2)}, u32[]{:S(2)}) %collective-permute-start.3) | collective-permute-done | bytes 213024 | tf_op jit(solution)/shard_map/ppermute | solution.py:455
  8.9 0.1 core_sum.1
  9.0 9.0 %collective-permute-start.4 = (bf16[208,128]{1,0:T(8,128)(2,1)S(1)}, bf16[208,128]{1,0:T(8,128)(2,1)S(1)}, u32[]{:S(2)}, u32[]{:S(2)}) collective-permute-start(bf16[208,128]{1,0:T(8,128)(2,1)S(1)} %get-tuple-element.109), channel_id=1, source_target_pairs={{0,24},{4,28},{8,16},{12,20},{16,8},{20,12},{24,0},{28,4},{1,25},{... | collective-permute-start | bytes 159752 | tf_op jit(solution)/shard_map/ppermute | solution.py:468
  18.0 0.0 collective-permute-start.5
  18.0 0.6 %collective-permute-start.6 = (bf16[208,128]{1,0:T(8,128)(2,1)S(1)}, bf16[208,128]{1,0:T(8,128)(2,1)S(1)}, u32[]{:S(2)}, u32[]{:S(2)}) collective-permute-start(bf16[208,128]{1,0:T(8,128)(2,1)S(1)} %get-tuple-element.111), channel_id=1, source_target_pairs={{0,8},{4,12},{8,0},{12,4},{16,24},{20,28},{24,16},{28,20},{1,9},{5... | collective-permute-start | bytes 159752 | tf_op jit(solution)/shard_map/ppermute | solution.py:468
  18.6 0.0 collective-permute-start.7
  18.6 0.5 %collective-permute-start.8 = (bf16[128,128]{1,0:T(8,128)(2,1)S(1)}, bf16[128,128]{1,0:T(8,128)(2,1)S(1)}, u32[]{:S(2)}, u32[]{:S(2)}) collective-permute-start(bf16[128,128]{1,0:T(8,128)(2,1)S(1)} %get-tuple-element.114), channel_id=1, source_target_pairs={{0,4},{4,0},{8,12},{12,8},{16,20},{20,16},{24,28},{28,24},{1,5},{5... | collective-permute-start | bytes 98312 | tf_op jit(solution)/shard_map/ppermute | solution.py:430
  19.1 0.7 %collective-permute-done.7.refs_1_ = bf16[128,128]{1,0:T(8,128)(2,1)S(1)} collective-permute-done((bf16[128,128]{1,0:T(8,128)(2,1)S(1)}, bf16[128,128]{1,0:T(8,128)(2,1)S(1)}, u32[]{:S(2)}, u32[]{:S(2)}) %collective-permute-start.7) | collective-permute-done | bytes 32800 | tf_op jit(solution)/shard_map/ppermute | solution.py:430
  19.8 0.2 collective-permute-done.8.refs_2_
  20.0 0.1 collective-permute-done.4.rest_1_
  20.1 2.0 %collective-permute-done.5.rest_2_ = bf16[208,128]{1,0:T(8,128)(2,1)S(1)} collective-permute-done((bf16[208,128]{1,0:T(8,128)(2,1)S(1)}, bf16[208,128]{1,0:T(8,128)(2,1)S(1)}, u32[]{:S(2)}, u32[]{:S(2)}) %collective-permute-start.5) | collective-permute-done | bytes 53280 | tf_op jit(solution)/shard_map/ppermute | solution.py:468
  22.1 0.0 collective-permute-done.6.rest_3_
  22.1 0.1 chip_sum.1
  22.2 2.4 %collective-permute-start.9 = (bf16[64,128]{1,0:T(8,128)(2,1)S(1)}, bf16[64,128]{1,0:T(8,128)(2,1)S(1)}, u32[]{:S(2)}, u32[]{:S(2)}) collective-permute-start(bf16[64,128]{1,0:T(8,128)(2,1)S(1)} %get-tuple-element.120), channel_id=1, source_target_pairs={{0,2},{1,3},{2,0},{3,1},{4,6},{5,7},{6,4},{7,5},{8,10},{9,11},{10,... | collective-permute-start | bytes 49160 | tf_op jit(solution)/shard_map/ppermute | solution.py:482
  24.6 1.2 %collective-permute-start.10 = (bf16[64,128]{1,0:T(8,128)(2,1)S(1)}, bf16[64,128]{1,0:T(8,128)(2,1)S(1)}, u32[]{:S(2)}, u32[]{:S(2)}) collective-permute-start(bf16[64,128]{1,0:T(8,128)(2,1)S(1)} %get-tuple-element.121), channel_id=1, source_target_pairs={{0,3},{1,2},{2,1},{3,0},{4,7},{5,6},{6,5},{7,4},{8,11},{9,10},{10,... | collective-permute-start | bytes 49160 | tf_op jit(solution)/shard_map/ppermute | solution.py:482
  25.8 0.5 %collective-permute-start.11 = (bf16[64,128]{1,0:T(8,128)(2,1)S(1)}, bf16[64,128]{1,0:T(8,128)(2,1)S(1)}, u32[]{:S(2)}, u32[]{:S(2)}) collective-permute-start(bf16[64,128]{1,0:T(8,128)(2,1)S(1)} %get-tuple-element.122), channel_id=1, source_target_pairs={{0,1},{1,0},{2,3},{3,2},{4,5},{5,4},{6,7},{7,6},{8,9},{9,8},{10,11... | collective-permute-start | bytes 49160 | tf_op jit(solution)/shard_map/ppermute | solution.py:482
  26.3 0.7 %place.1 = bf16[16,2,16,128]{3,2,1,0:T(8,128)(2,1)} custom-call(bf16[256,128]{1,0:T(8,128)(2,1)S(1)} %d_inputs.2.refs_0_, bf16[128,128]{1,0:T(8,128)(2,1)S(1)} %collective-permute-done.7.refs_1_, bf16[128,128]{1,0:T(8,128)(2,1)S(1)} %collective-permute-done.8.refs_2_), custom_call_target="tpu_custom_call" | custom-call | tf_op jit(solution)/shard_map/place/pallas_call | solution.py:434
  26.9 0.0 collective-permute-done.9.rest_1_
  27.0 3.2 %collective-permute-done.10.rest_2_ = bf16[64,128]{1,0:T(8,128)(2,1)S(1)} collective-permute-done((bf16[64,128]{1,0:T(8,128)(2,1)S(1)}, bf16[64,128]{1,0:T(8,128)(2,1)S(1)}, u32[]{:S(2)}, u32[]{:S(2)}) %collective-permute-start.10) | collective-permute-done | bytes 16416 | tf_op jit(solution)/shard_map/ppermute | solution.py:482
  30.1 0.0 collective-permute-done.11.rest_3_
  30.1 0.7 %col_sum.1 = (f32[16,128]{1,0:T(8,128)}, f32[16,128]{1,0:T(8,128)}, f32[32,64]{1,0:T(8,128)}, f32[16,16]{1,0:T(8,128)}) custom-call(bf16[64,128]{1,0:T(8,128)(2,1)S(1)} %get-tuple-element.127.rest_0_, bf16[64,128]{1,0:T(8,128)(2,1)S(1)} %collective-permute-done.9.rest_1_, bf16[64,128]{1,0:T(8,128)(2,1)S(1)} %collective-permute-done.10.rest_2_, ...), custom_call_target="tpu_custom_call" | custom-call | tf_op jit(solution)/shard_map/col_sum/pallas_call | solution.py:484
  (1 shorter events, 0.0 us)
Async XLA Ops:
  2.9 2.9 %collective-permute-start.2 = (bf16[2,128,128]{2,1,0:T(8,128)(2,1)S(1)}, bf16[2,128,128]{2,1,0:T(8,128)(2,1)S(1)}, u32[]{:S(2)}, u32[]{:S(2)}) collective-permute-start(bf16[2,128,128]{2,1,0:T(8,128)(2,1)S(1)} %get-tuple-element.92.refs_17_), channel_id=1, source_target_pairs={{0,4},{1,8},{2,16},{3,24},{4,0},{5,12},{6,20},{7,28},{8,1},{9,13},... | collective-permute-start | bytes 196616 | tf_op jit(solution)/shard_map/ppermute | solution.py:356
  3.4 1.4 %collective-permute-start.1 = (bf16[144,128]{1,0:T(8,128)(2,1)S(1)}, bf16[144,128]{1,0:T(8,128)(2,1)S(1)}, u32[]{:S(2)}, u32[]{:S(2)}) collective-permute-start(bf16[144,128]{1,0:T(8,128)(2,1)S(1)} %get-tuple-element.84), channel_id=1, source_target_pairs={{0,4},{4,0},{8,12},{12,8},{16,20},{20,16},{24,28},{28,24},{1,5},{5... | collective-permute-start | bytes 110600 | tf_op jit(solution)/shard_map/ppermute | solution.py:365
  3.5 1.3 %collective-permute-start = (bf16[128,128]{1,0:T(8,128)(2,1)S(1)}, bf16[128,128]{1,0:T(8,128)(2,1)S(1)}, u32[]{:S(2)}, u32[]{:S(2)}) collective-permute-start(bf16[128,128]{1,0:T(8,128)(2,1)S(1)} %get-tuple-element.83), channel_id=1, source_target_pairs={{0,4},{4,0},{8,12},{12,8},{16,20},{20,16},{24,28},{28,24},{1,5},{5... | collective-permute-start | bytes 98312 | tf_op jit(solution)/shard_map/ppermute | solution.py:365
  7.4 1.5 %collective-permute-start.3 = (bf16[4,208,128]{2,1,0:T(8,128)(2,1)S(1)}, bf16[4,208,128]{2,1,0:T(8,128)(2,1)S(1)}, u32[]{:S(2)}, u32[]{:S(2)}) collective-permute-start(bf16[4,208,128]{2,1,0:T(8,128)(2,1)S(1)} %get-tuple-element.94), channel_id=1, source_target_pairs={{0,4},{4,0},{8,12},{12,8},{16,20},{20,16},{24,28},{28,24},{1,5},{5... | collective-permute-start | bytes 638984 | tf_op jit(solution)/shard_map/ppermute | solution.py:455
  9.0 11.1 %collective-permute-start.4 = (bf16[208,128]{1,0:T(8,128)(2,1)S(1)}, bf16[208,128]{1,0:T(8,128)(2,1)S(1)}, u32[]{:S(2)}, u32[]{:S(2)}) collective-permute-start(bf16[208,128]{1,0:T(8,128)(2,1)S(1)} %get-tuple-element.109), channel_id=1, source_target_pairs={{0,24},{4,28},{8,16},{12,20},{16,8},{20,12},{24,0},{28,4},{1,25},{... | collective-permute-start | bytes 159752 | tf_op jit(solution)/shard_map/ppermute | solution.py:468
  18.0 4.1 %collective-permute-start.5 = (bf16[208,128]{1,0:T(8,128)(2,1)S(1)}, bf16[208,128]{1,0:T(8,128)(2,1)S(1)}, u32[]{:S(2)}, u32[]{:S(2)}) collective-permute-start(bf16[208,128]{1,0:T(8,128)(2,1)S(1)} %get-tuple-element.110), channel_id=1, source_target_pairs={{0,16},{4,20},{8,24},{12,28},{16,0},{20,4},{24,8},{28,12},{1,17},{... | collective-permute-start | bytes 159752 | tf_op jit(solution)/shard_map/ppermute | solution.py:468
  18.0 4.1 %collective-permute-start.6 = (bf16[208,128]{1,0:T(8,128)(2,1)S(1)}, bf16[208,128]{1,0:T(8,128)(2,1)S(1)}, u32[]{:S(2)}, u32[]{:S(2)}) collective-permute-start(bf16[208,128]{1,0:T(8,128)(2,1)S(1)} %get-tuple-element.111), channel_id=1, source_target_pairs={{0,8},{4,12},{8,0},{12,4},{16,24},{20,28},{24,16},{28,20},{1,9},{5... | collective-permute-start | bytes 159752 | tf_op jit(solution)/shard_map/ppermute | solution.py:468
  18.6 1.2 %collective-permute-start.7 = (bf16[128,128]{1,0:T(8,128)(2,1)S(1)}, bf16[128,128]{1,0:T(8,128)(2,1)S(1)}, u32[]{:S(2)}, u32[]{:S(2)}) collective-permute-start(bf16[128,128]{1,0:T(8,128)(2,1)S(1)} %get-tuple-element.113), channel_id=1, source_target_pairs={{0,4},{4,0},{8,12},{12,8},{16,20},{20,16},{24,28},{28,24},{1,5},{5... | collective-permute-start | bytes 98312 | tf_op jit(solution)/shard_map/ppermute | solution.py:430
  18.6 1.4 %collective-permute-start.8 = (bf16[128,128]{1,0:T(8,128)(2,1)S(1)}, bf16[128,128]{1,0:T(8,128)(2,1)S(1)}, u32[]{:S(2)}, u32[]{:S(2)}) collective-permute-start(bf16[128,128]{1,0:T(8,128)(2,1)S(1)} %get-tuple-element.114), channel_id=1, source_target_pairs={{0,4},{4,0},{8,12},{12,8},{16,20},{20,16},{24,28},{28,24},{1,5},{5... | collective-permute-start | bytes 98312 | tf_op jit(solution)/shard_map/ppermute | solution.py:430
  22.2 4.8 %collective-permute-start.9 = (bf16[64,128]{1,0:T(8,128)(2,1)S(1)}, bf16[64,128]{1,0:T(8,128)(2,1)S(1)}, u32[]{:S(2)}, u32[]{:S(2)}) collective-permute-start(bf16[64,128]{1,0:T(8,128)(2,1)S(1)} %get-tuple-element.120), channel_id=1, source_target_pairs={{0,2},{1,3},{2,0},{3,1},{4,6},{5,7},{6,4},{7,5},{8,10},{9,11},{10,... | collective-permute-start | bytes 49160 | tf_op jit(solution)/shard_map/ppermute | solution.py:482
  24.6 5.5 %collective-permute-start.10 = (bf16[64,128]{1,0:T(8,128)(2,1)S(1)}, bf16[64,128]{1,0:T(8,128)(2,1)S(1)}, u32[]{:S(2)}, u32[]{:S(2)}) collective-permute-start(bf16[64,128]{1,0:T(8,128)(2,1)S(1)} %get-tuple-element.121), channel_id=1, source_target_pairs={{0,3},{1,2},{2,1},{3,0},{4,7},{5,6},{6,5},{7,4},{8,11},{9,10},{10,... | collective-permute-start | bytes 49160 | tf_op jit(solution)/shard_map/ppermute | solution.py:482
  25.8 4.3 %collective-permute-start.11 = (bf16[64,128]{1,0:T(8,128)(2,1)S(1)}, bf16[64,128]{1,0:T(8,128)(2,1)S(1)}, u32[]{:S(2)}, u32[]{:S(2)}) collective-permute-start(bf16[64,128]{1,0:T(8,128)(2,1)S(1)} %get-tuple-element.122), channel_id=1, source_target_pairs={{0,1},{1,0},{2,3},{3,2},{4,5},{5,4},{6,7},{7,6},{8,9},{9,8},{10,11... | collective-permute-start | bytes 49160 | tf_op jit(solution)/shard_map/ppermute | solution.py:482

commit v8 on v7

--- a/solution.py
+++ b/solution.py
@@ -46,6 +46,10 @@
 def partner(s, p, n):
     if n & (n - 1) == 0:
         return s ^ p
+    return (s + p) % n if isinstance(s, int) else lax.rem(s + p, n)
+
+
+def following(s, p, n):
     return (s + p) % n if isinstance(s, int) else lax.rem(s + p, n)
 
 
@@ -255,7 +259,7 @@
     terms, blocks, hot, handed = rest[:q], rest[q : 2 * q - 1], rest[2 * q - 1 : 2 - 2 * q], rest[2 - 2 * q :]
     mine = lax.axis_index("row") // q
     for p in range(groups):
-        a = partner(mine, p, groups)
+        a = following(mine, p, groups)
         total = terms[0][a].astype(f32)
         for term in terms[1:]:
             total = total + term[a].astype(f32)
@@ -464,8 +468,8 @@
     )(*terms, *d_blocks[1:])
     hot, d_blocks = hot[:groups], d_blocks[:1] + list(hot[groups:])
     terms = [hot[0]]
-    for p in range(groups - 1, 0, -1):
-        terms.append(lax.ppermute(hot[p], "row", [(s, partner(s // q, p, groups) * q + s % q) for s in range(nrow)]))
+    for p in range(1, groups):
+        terms.append(lax.ppermute(hot[p], "row", [(s, following(s // q, p, groups) * q + s % q) for s in range(nrow)]))
     terms, d_blocks = lax.optimization_barrier((terms, returned(d_blocks)))
     short = 3 * part + width // ncol * tall // lanes
     hot = pl.pallas_call(

time: 31 us -> 30.1 us (0.971)
  starting transfers between devices: 15.7 us -> 15 us
    ppermute x3, waiting for transfers between devices: 3.18 us -> 2.29 us  [body(): lax.ppermute(hot[p], 'col', [(s, partner(s, p, ncol)) for s in range(ncol)])]
    ppermute x3, waiting for transfers between devices: 2.12 us -> 2.76 us  [body(): lax.ppermute(hot[p], 'row', [(s, following(s // q, p, groups) * q + s % q...]
    ppermute x3, starting transfers between devices: 4.09 us -> 3.55 us  [body(): lax.ppermute(hot[p], 'col', [(s, partner(s, p, ncol)) for s in range(ncol)])]
  transfers between devices with their start and end apart: 12 -> 12, of which waited for: 6 -> 8; matrix products, arithmetic and copies ran while one was open for 0% -> 0% of each run, Pallas kernels for 10% -> 11%
where the time goes in v8:
time: 30.1 us; the launch traced here: 29.9 us
  starting transfers between devices  15 us (50%)
  Pallas kernels  7.89 us (26%)
  waiting for transfers between devices  6.3 us (21%)
  between operations  0.71 us (2%)
    ppermute x3, starting transfers between devices, body(): lax.ppermute(hot[p], 'row', [(s, following(s // q, p, groups) * q + s % q...  9.54 us
    ppermute x3, starting transfers between devices, body(): lax.ppermute(hot[p], 'col', [(s, partner(s, p, ncol)) for s in range(ncol)])  3.55 us
    ppermute x3, waiting for transfers between devices, body(): lax.ppermute(hot[p], 'row', [(s, following(s // q, p, groups) * q + s % q...  2.76 us
    ppermute x3, waiting for transfers between devices, body(): lax.ppermute(hot[p], 'col', [(s, partner(s, p, ncol)) for s in range(ncol)])  2.29 us
    pallas_call x1, Pallas kernels, body(): pl.pallas_call(functools.partial(forward_kernel, q), out_shape=[shaped((q...  2.27 us
    pallas_call x2, Pallas kernels, body(): pl.pallas_call(functools.partial(prepare_kernel, q, p), out_shape=[shaped...  1.77 us
    pallas_call x1, Pallas kernels, body(): pl.pallas_call(functools.partial(backward_kernel, q, (nrow, ncol) if fits...  1.58 us
    ppermute x2, waiting for transfers between devices, returned(): lax.ppermute(x, 'row', core_pairs(nrow, q, n // 2 + 1))  0.86 us
  transfers between devices with their start and end apart: 12, of which 8 were waited for; matrix products, arithmetic and copies ran while one was open for 0% of the time, Pallas kernels for 11%

profile of v8, /device:TPU:0, one launch (start us, length us, event | category | flops | bytes accessed | tf_op | source)
XLA Modules:
  0.0 29.9 jit_solution(2832328596814266308)
XLA Ops:
  0.6 2.3 %forward.1 = (bf16[2,256,128]{2,1,0:T(8,128)(2,1)S(1)}, bf16[128,512]{1,0:T(8,128)(2,1)S(1)}, bf16[128,512]{1,0:T(8,128)(2,1)S(1)}, bf16[512,128]{1,0:T(8,128)(2...) custom-call(bf16[16,32,128]{2,1,0:T(8,128)(2,1)} %refs_0_.1, ...), custom_call_target="tpu_custom_call" | custom-call | tf_op jit(solution)/shard_map/forward/pallas_call | solution.py:339
  2.9 0.5 %collective-permute-start.2 = (bf16[2,128,128]{2,1,0:T(8,128)(2,1)S(1)}, bf16[2,128,128]{2,1,0:T(8,128)(2,1)S(1)}, u32[]{:S(2)}, u32[]{:S(2)}) collective-permute-start(bf16[2,128,128]{2,1,0:T(8,128)(2,1)S(1)} %get-tuple-element.92.refs_17_), channel_id=1, source_target_pairs={{0,4},{1,8},{2,16},{3,24},{4,0},{5,12},{6,20},{7,28},{8,1},{9,13},... | collective-permute-start | bytes 196616 | tf_op jit(solution)/shard_map/ppermute | solution.py:360
  3.4 0.1 collective-permute-start.1
  3.5 0.4 %collective-permute-start = (bf16[128,128]{1,0:T(8,128)(2,1)S(1)}, bf16[128,128]{1,0:T(8,128)(2,1)S(1)}, u32[]{:S(2)}, u32[]{:S(2)}) collective-permute-start(bf16[128,128]{1,0:T(8,128)(2,1)S(1)} %get-tuple-element.83), channel_id=1, source_target_pairs={{0,4},{4,0},{8,12},{12,8},{16,20},{20,16},{24,28},{28,24},{1,5},{5... | collective-permute-start | bytes 98312 | tf_op jit(solution)/shard_map/ppermute | solution.py:369
  4.0 0.9 %prepare.2 = (bf16[128,256]{1,0:T(8,128)(2,1)S(1)}, bf16[128,256]{1,0:T(8,128)(2,1)S(1)}, bf16[256,512]{1,0:T(8,128)(2,1)S(1)}, f32[256,512]{1,0:T(8,128)S(1)}, ...) custom-call(bf16[2,256,128]{2,1,0:T(8,128)(2,1)S(1)} %get-tuple-elem, ...), custom_call_target="tpu_custom_call" | custom-call | flops 100663296 | bytes 1048576 | tf_op jit(solution)/shard_map/prepare/pallas_call | solution.py:374
  4.8 0.0 collective-permute-done.refs_0_
  4.9 0.0 collective-permute-done.1.refs_1_
  4.9 0.9 %prepare.3 = (bf16[128,256]{1,0:T(8,128)(2,1)S(1)}, bf16[128,256]{1,0:T(8,128)(2,1)S(1)}, bf16[256,512]{1,0:T(8,128)(2,1)S(1)}, f32[256,512]{1,0:T(8,128)S(1)}, ...) custom-call(bf16[128,128]{1,0:T(8,128)(2,1)S(1)} %collective-permute, ...), custom_call_target="tpu_custom_call" | custom-call | tf_op jit(solution)/shard_map/prepare/pallas_call | solution.py:374
  5.8 0.0 collective-permute-done.2.refs_16_
  5.8 1.6 %backward.1 = (f32[256,128]{1,0:T(8,128)S(1)}, bf16[256,512]{1,0:T(8,128)(2,1)S(1)}, bf16[256,512]{1,0:T(8,128)(2,1)S(1)}, f32[256,128]{1,0:T(8,128)S(1)}, bf16[...) custom-call(bf16[128,256]{1,0:T(8,128)(2,1)S(1)} %get-tuple-element., ...), custom_call_target="tpu_custom_call" | custom-call | flops 268435456 | bytes 1048576 | tf_op jit(solution)/shard_map/backward/pallas_call | solution.py:408
  7.4 0.4 %collective-permute-start.3 = (bf16[4,208,128]{2,1,0:T(8,128)(2,1)S(1)}, bf16[4,208,128]{2,1,0:T(8,128)(2,1)S(1)}, u32[]{:S(2)}, u32[]{:S(2)}) collective-permute-start(bf16[4,208,128]{2,1,0:T(8,128)(2,1)S(1)} %get-tuple-element.94), channel_id=1, source_target_pairs={{0,4},{4,0},{8,12},{12,8},{16,20},{20,16},{24,28},{28,24},{1,5},{5... | collective-permute-start | bytes 638984 | tf_op jit(solution)/shard_map/ppermute | solution.py:459
  7.7 0.4 %d_inputs.3.rest_2_ = bf16[256,128]{1,0:T(8,128)(2,1)S(1)} custom-call(f32[256,128]{1,0:T(8,128)S(1)} %get-tuple-element.100.d_updated, bf16[256,512]{1,0:T(8,128)(2,1)S(1)} %get-tuple-element.101.d_gate, bf16[256,512]{1,0:T(8,128)(2,1)S(1)} %get-tuple-element.102.d_up, f32[256,128]{1,0:T(8,128)S(1)} %get-tuple-element.103.normed, ...), custom_call_target="tpu_custom_call" | custom-call | flops 67108864 | bytes 524288 | tf_op jit(solution)/shard_map/d_inputs/pallas_call | solution.py:421
  8.1 0.4 %d_inputs.2.refs_0_ = bf16[256,128]{1,0:T(8,128)(2,1)S(1)} custom-call(f32[256,128]{1,0:T(8,128)S(1)} %get-tuple-element.95.d_updated, bf16[256,512]{1,0:T(8,128)(2,1)S(1)} %get-tuple-element.96.d_gate, bf16[256,512]{1,0:T(8,128)(2,1)S(1)} %get-tuple-element.97.d_up, f32[256,128]{1,0:T(8,128)S(1)} %get-tuple-element.98.normed, ...), custom_call_target="tpu_custom_call" | custom-call | flops 67108864 | bytes 524288 | tf_op jit(solution)/shard_map/d_inputs/pallas_call | solution.py:421
  8.5 0.4 %collective-permute-done.3.rest_1_ = bf16[4,208,128]{2,1,0:T(8,128)(2,1)S(1)} collective-permute-done((bf16[4,208,128]{2,1,0:T(8,128)(2,1)S(1)}, bf16[4,208,128]{2,1,0:T(8,128)(2,1)S(1)}, u32[]{:S(2)}, u32[]{:S(2)}) %collective-permute-start.3) | collective-permute-done | bytes 213024 | tf_op jit(solution)/shard_map/ppermute | solution.py:459
  8.9 0.1 core_sum.1
  9.0 7.2 %collective-permute-start.4 = (bf16[208,128]{1,0:T(8,128)(2,1)S(1)}, bf16[208,128]{1,0:T(8,128)(2,1)S(1)}, u32[]{:S(2)}, u32[]{:S(2)}) collective-permute-start(bf16[208,128]{1,0:T(8,128)(2,1)S(1)} %get-tuple-element.109), channel_id=1, source_target_pairs={{0,8},{4,12},{8,16},{12,20},{16,24},{20,28},{24,0},{28,4},{1,9},{5... | collective-permute-start | bytes 159752 | tf_op jit(solution)/shard_map/ppermute | solution.py:472
  16.2 2.3 %collective-permute-start.5 = (bf16[208,128]{1,0:T(8,128)(2,1)S(1)}, bf16[208,128]{1,0:T(8,128)(2,1)S(1)}, u32[]{:S(2)}, u32[]{:S(2)}) collective-permute-start(bf16[208,128]{1,0:T(8,128)(2,1)S(1)} %get-tuple-element.110), channel_id=1, source_target_pairs={{0,16},{4,20},{8,24},{12,28},{16,0},{20,4},{24,8},{28,12},{1,17},{... | collective-permute-start | bytes 159752 | tf_op jit(solution)/shard_map/ppermute | solution.py:472
  18.5 0.0 collective-permute-start.6
  18.5 0.0 collective-permute-start.7
  18.5 0.5 %collective-permute-start.8 = (bf16[128,128]{1,0:T(8,128)(2,1)S(1)}, bf16[128,128]{1,0:T(8,128)(2,1)S(1)}, u32[]{:S(2)}, u32[]{:S(2)}) collective-permute-start(bf16[128,128]{1,0:T(8,128)(2,1)S(1)} %get-tuple-element.114), channel_id=1, source_target_pairs={{0,4},{4,0},{8,12},{12,8},{16,20},{20,16},{24,28},{28,24},{1,5},{5... | collective-permute-start | bytes 98312 | tf_op jit(solution)/shard_map/ppermute | solution.py:434
  19.0 0.7 %collective-permute-done.7.refs_1_ = bf16[128,128]{1,0:T(8,128)(2,1)S(1)} collective-permute-done((bf16[128,128]{1,0:T(8,128)(2,1)S(1)}, bf16[128,128]{1,0:T(8,128)(2,1)S(1)}, u32[]{:S(2)}, u32[]{:S(2)}) %collective-permute-start.7) | collective-permute-done | bytes 32800 | tf_op jit(solution)/shard_map/ppermute | solution.py:434
  19.7 0.2 collective-permute-done.8.refs_2_
  19.9 0.3 collective-permute-done.4.rest_1_
  20.2 1.0 %collective-permute-done.5.rest_2_ = bf16[208,128]{1,0:T(8,128)(2,1)S(1)} collective-permute-done((bf16[208,128]{1,0:T(8,128)(2,1)S(1)}, bf16[208,128]{1,0:T(8,128)(2,1)S(1)}, u32[]{:S(2)}, u32[]{:S(2)}) %collective-permute-start.5) | collective-permute-done | bytes 53280 | tf_op jit(solution)/shard_map/ppermute | solution.py:472
  21.2 1.4 %collective-permute-done.6.rest_3_ = bf16[208,128]{1,0:T(8,128)(2,1)S(1)} collective-permute-done((bf16[208,128]{1,0:T(8,128)(2,1)S(1)}, bf16[208,128]{1,0:T(8,128)(2,1)S(1)}, u32[]{:S(2)}, u32[]{:S(2)}) %collective-permute-start.6) | collective-permute-done | bytes 53280 | tf_op jit(solution)/shard_map/ppermute | solution.py:472
  22.6 0.1 chip_sum.1
  22.7 0.7 %collective-permute-start.9 = (bf16[64,128]{1,0:T(8,128)(2,1)S(1)}, bf16[64,128]{1,0:T(8,128)(2,1)S(1)}, u32[]{:S(2)}, u32[]{:S(2)}) collective-permute-start(bf16[64,128]{1,0:T(8,128)(2,1)S(1)} %get-tuple-element.120), channel_id=1, source_target_pairs={{0,2},{1,3},{2,0},{3,1},{4,6},{5,7},{6,4},{7,5},{8,10},{9,11},{10,... | collective-permute-start | bytes 49160 | tf_op jit(solution)/shard_map/ppermute | solution.py:486
  23.4 2.0 %collective-permute-start.10 = (bf16[64,128]{1,0:T(8,128)(2,1)S(1)}, bf16[64,128]{1,0:T(8,128)(2,1)S(1)}, u32[]{:S(2)}, u32[]{:S(2)}) collective-permute-start(bf16[64,128]{1,0:T(8,128)(2,1)S(1)} %get-tuple-element.121), channel_id=1, source_target_pairs={{0,3},{1,2},{2,1},{3,0},{4,7},{5,6},{6,5},{7,4},{8,11},{9,10},{10,... | collective-permute-start | bytes 49160 | tf_op jit(solution)/shard_map/ppermute | solution.py:486
  25.4 0.9 %collective-permute-start.11 = (bf16[64,128]{1,0:T(8,128)(2,1)S(1)}, bf16[64,128]{1,0:T(8,128)(2,1)S(1)}, u32[]{:S(2)}, u32[]{:S(2)}) collective-permute-start(bf16[64,128]{1,0:T(8,128)(2,1)S(1)} %get-tuple-element.122), channel_id=1, source_target_pairs={{0,1},{1,0},{2,3},{3,2},{4,5},{5,4},{6,7},{7,6},{8,9},{9,8},{10,11... | collective-permute-start | bytes 49160 | tf_op jit(solution)/shard_map/ppermute | solution.py:486
  26.3 0.7 %place.1 = bf16[16,2,16,128]{3,2,1,0:T(8,128)(2,1)} custom-call(bf16[256,128]{1,0:T(8,128)(2,1)S(1)} %d_inputs.2.refs_0_, bf16[128,128]{1,0:T(8,128)(2,1)S(1)} %collective-permute-done.7.refs_1_, bf16[128,128]{1,0:T(8,128)(2,1)S(1)} %collective-permute-done.8.refs_2_), custom_call_target="tpu_custom_call" | custom-call | tf_op jit(solution)/shard_map/place/pallas_call | solution.py:438
  27.0 0.5 %collective-permute-done.9.rest_1_ = bf16[64,128]{1,0:T(8,128)(2,1)S(1)} collective-permute-done((bf16[64,128]{1,0:T(8,128)(2,1)S(1)}, bf16[64,128]{1,0:T(8,128)(2,1)S(1)}, u32[]{:S(2)}, u32[]{:S(2)}) %collective-permute-start.9) | collective-permute-done | bytes 16416 | tf_op jit(solution)/shard_map/ppermute | solution.py:486
  27.4 1.8 %collective-permute-done.10.rest_2_ = bf16[64,128]{1,0:T(8,128)(2,1)S(1)} collective-permute-done((bf16[64,128]{1,0:T(8,128)(2,1)S(1)}, bf16[64,128]{1,0:T(8,128)(2,1)S(1)}, u32[]{:S(2)}, u32[]{:S(2)}) %collective-permute-start.10) | collective-permute-done | bytes 16416 | tf_op jit(solution)/shard_map/ppermute | solution.py:486
  29.2 0.0 collective-permute-done.11.rest_3_
  29.3 0.7 %col_sum.1 = (f32[16,128]{1,0:T(8,128)}, f32[16,128]{1,0:T(8,128)}, f32[32,64]{1,0:T(8,128)}, f32[16,16]{1,0:T(8,128)}) custom-call(bf16[64,128]{1,0:T(8,128)(2,1)S(1)} %get-tuple-element.127.rest_0_, bf16[64,128]{1,0:T(8,128)(2,1)S(1)} %collective-permute-done.9.rest_1_, bf16[64,128]{1,0:T(8,128)(2,1)S(1)} %collective-permute-done.10.rest_2_, ...), custom_call_target="tpu_custom_call" | custom-call | tf_op jit(solution)/shard_map/col_sum/pallas_call | solution.py:488
  (1 shorter events, 0.0 us)
Async XLA Ops:
  2.9 2.9 %collective-permute-start.2 = (bf16[2,128,128]{2,1,0:T(8,128)(2,1)S(1)}, bf16[2,128,128]{2,1,0:T(8,128)(2,1)S(1)}, u32[]{:S(2)}, u32[]{:S(2)}) collective-permute-start(bf16[2,128,128]{2,1,0:T(8,128)(2,1)S(1)} %get-tuple-element.92.refs_17_), channel_id=1, source_target_pairs={{0,4},{1,8},{2,16},{3,24},{4,0},{5,12},{6,20},{7,28},{8,1},{9,13},... | collective-permute-start | bytes 196616 | tf_op jit(solution)/shard_map/ppermute | solution.py:360
  3.4 1.4 %collective-permute-start.1 = (bf16[144,128]{1,0:T(8,128)(2,1)S(1)}, bf16[144,128]{1,0:T(8,128)(2,1)S(1)}, u32[]{:S(2)}, u32[]{:S(2)}) collective-permute-start(bf16[144,128]{1,0:T(8,128)(2,1)S(1)} %get-tuple-element.84), channel_id=1, source_target_pairs={{0,4},{4,0},{8,12},{12,8},{16,20},{20,16},{24,28},{28,24},{1,5},{5... | collective-permute-start | bytes 110600 | tf_op jit(solution)/shard_map/ppermute | solution.py:369
  3.5 1.3 %collective-permute-start = (bf16[128,128]{1,0:T(8,128)(2,1)S(1)}, bf16[128,128]{1,0:T(8,128)(2,1)S(1)}, u32[]{:S(2)}, u32[]{:S(2)}) collective-permute-start(bf16[128,128]{1,0:T(8,128)(2,1)S(1)} %get-tuple-element.83), channel_id=1, source_target_pairs={{0,4},{4,0},{8,12},{12,8},{16,20},{20,16},{24,28},{28,24},{1,5},{5... | collective-permute-start | bytes 98312 | tf_op jit(solution)/shard_map/ppermute | solution.py:369
  7.4 1.5 %collective-permute-start.3 = (bf16[4,208,128]{2,1,0:T(8,128)(2,1)S(1)}, bf16[4,208,128]{2,1,0:T(8,128)(2,1)S(1)}, u32[]{:S(2)}, u32[]{:S(2)}) collective-permute-start(bf16[4,208,128]{2,1,0:T(8,128)(2,1)S(1)} %get-tuple-element.94), channel_id=1, source_target_pairs={{0,4},{4,0},{8,12},{12,8},{16,20},{20,16},{24,28},{28,24},{1,5},{5... | collective-permute-start | bytes 638984 | tf_op jit(solution)/shard_map/ppermute | solution.py:459
  9.0 11.2 %collective-permute-start.4 = (bf16[208,128]{1,0:T(8,128)(2,1)S(1)}, bf16[208,128]{1,0:T(8,128)(2,1)S(1)}, u32[]{:S(2)}, u32[]{:S(2)}) collective-permute-start(bf16[208,128]{1,0:T(8,128)(2,1)S(1)} %get-tuple-element.109), channel_id=1, source_target_pairs={{0,8},{4,12},{8,16},{12,20},{16,24},{20,28},{24,0},{28,4},{1,9},{5... | collective-permute-start | bytes 159752 | tf_op jit(solution)/shard_map/ppermute | solution.py:472
  16.2 5.0 %collective-permute-start.5 = (bf16[208,128]{1,0:T(8,128)(2,1)S(1)}, bf16[208,128]{1,0:T(8,128)(2,1)S(1)}, u32[]{:S(2)}, u32[]{:S(2)}) collective-permute-start(bf16[208,128]{1,0:T(8,128)(2,1)S(1)} %get-tuple-element.110), channel_id=1, source_target_pairs={{0,16},{4,20},{8,24},{12,28},{16,0},{20,4},{24,8},{28,12},{1,17},{... | collective-permute-start | bytes 159752 | tf_op jit(solution)/shard_map/ppermute | solution.py:472
  18.5 4.1 %collective-permute-start.6 = (bf16[208,128]{1,0:T(8,128)(2,1)S(1)}, bf16[208,128]{1,0:T(8,128)(2,1)S(1)}, u32[]{:S(2)}, u32[]{:S(2)}) collective-permute-start(bf16[208,128]{1,0:T(8,128)(2,1)S(1)} %get-tuple-element.111), channel_id=1, source_target_pairs={{0,24},{4,28},{8,0},{12,4},{16,8},{20,12},{24,16},{28,20},{1,25},{... | collective-permute-start | bytes 159752 | tf_op jit(solution)/shard_map/ppermute | solution.py:472
  18.5 1.2 %collective-permute-start.7 = (bf16[128,128]{1,0:T(8,128)(2,1)S(1)}, bf16[128,128]{1,0:T(8,128)(2,1)S(1)}, u32[]{:S(2)}, u32[]{:S(2)}) collective-permute-start(bf16[128,128]{1,0:T(8,128)(2,1)S(1)} %get-tuple-element.113), channel_id=1, source_target_pairs={{0,4},{4,0},{8,12},{12,8},{16,20},{20,16},{24,28},{28,24},{1,5},{5... | collective-permute-start | bytes 98312 | tf_op jit(solution)/shard_map/ppermute | solution.py:434
  18.5 1.4 %collective-permute-start.8 = (bf16[128,128]{1,0:T(8,128)(2,1)S(1)}, bf16[128,128]{1,0:T(8,128)(2,1)S(1)}, u32[]{:S(2)}, u32[]{:S(2)}) collective-permute-start(bf16[128,128]{1,0:T(8,128)(2,1)S(1)} %get-tuple-element.114), channel_id=1, source_target_pairs={{0,4},{4,0},{8,12},{12,8},{16,20},{20,16},{24,28},{28,24},{1,5},{5... | collective-permute-start | bytes 98312 | tf_op jit(solution)/shard_map/ppermute | solution.py:434
  22.7 4.7 %collective-permute-start.9 = (bf16[64,128]{1,0:T(8,128)(2,1)S(1)}, bf16[64,128]{1,0:T(8,128)(2,1)S(1)}, u32[]{:S(2)}, u32[]{:S(2)}) collective-permute-start(bf16[64,128]{1,0:T(8,128)(2,1)S(1)} %get-tuple-element.120), channel_id=1, source_target_pairs={{0,2},{1,3},{2,0},{3,1},{4,6},{5,7},{6,4},{7,5},{8,10},{9,11},{10,... | collective-permute-start | bytes 49160 | tf_op jit(solution)/shard_map/ppermute | solution.py:486
  23.4 5.8 %collective-permute-start.10 = (bf16[64,128]{1,0:T(8,128)(2,1)S(1)}, bf16[64,128]{1,0:T(8,128)(2,1)S(1)}, u32[]{:S(2)}, u32[]{:S(2)}) collective-permute-start(bf16[64,128]{1,0:T(8,128)(2,1)S(1)} %get-tuple-element.121), channel_id=1, source_target_pairs={{0,3},{1,2},{2,1},{3,0},{4,7},{5,6},{6,5},{7,4},{8,11},{9,10},{10,... | collective-permute-start | bytes 49160 | tf_op jit(solution)/shard_map/ppermute | solution.py:486
  25.4 3.8 %collective-permute-start.11 = (bf16[64,128]{1,0:T(8,128)(2,1)S(1)}, bf16[64,128]{1,0:T(8,128)(2,1)S(1)}, u32[]{:S(2)}, u32[]{:S(2)}) collective-permute-start(bf16[64,128]{1,0:T(8,128)(2,1)S(1)} %get-tuple-element.122), channel_id=1, source_target_pairs={{0,1},{1,0},{2,3},{3,2},{4,5},{5,4},{6,7},{7,6},{8,9},{9,8},{10,11... | collective-permute-start | bytes 49160 | tf_op jit(solution)/shard_map/ppermute | solution.py:486

commit v9 on v8

--- a/solution.py
+++ b/solution.py
@@ -53,13 +53,18 @@
     return (s + p) % n if isinstance(s, int) else lax.rem(s + p, n)
 
 
+def joined(refs, axis):
+    return jnp.concatenate([ref[...] for ref in refs], axis=axis)
+
+
 def lane_packs(bins, side):
     packs = max(1, 128 // bins)
     return packs if (side // packs) % 16 == 0 else 1
 
 
 def forward_kernel(q, *refs):
-    sources, (pair, w_gate, w_up, w_out, w_head, marks, sends), (targets, halves, sems) = refs[:6], refs[6:13], refs[13:]
+    sources, (pair, w_gate, w_up, w_out, w_head, marks, sends), scratch = refs[:6], refs[6:13], refs[13:]
+    targets, halves, hidden, sems = scratch
     _, side, width = pair.shape
     edge = sources[0].shape[0]
     bins = w_head.shape[0]
@@ -85,14 +90,16 @@
         copy.wait()
     flat = pair[...].reshape(q * side, width)
     inputs = normalize(flat)[0].astype(bf16)
-    total = flat.astype(f32)
-    for copy in copies:
+    for copy in copies[:2]:
         copy.wait()
-    for at, step in chunks_of(w_gate.shape[1], 256):
-        gate = nn(inputs, w_gate[:, at : at + step])
-        upper = nn(inputs, w_up[:, at : at + step])
-        hidden = (gate * sigmoid(gate) * upper).astype(bf16)
-        total = total + nn(hidden, w_out[at : at + step, :])
+    for top, tall in chunks_of(q * side, 128):
+        for at, step in chunks_of(w_gate.shape[1], 256):
+            gate = nn(inputs[top : top + tall], w_gate[:, at : at + step])
+            upper = nn(inputs[top : top + tall], w_up[:, at : at + step])
+            hidden[top : top + tall, at : at + step] = (gate * sigmoid(gate) * upper).astype(bf16)
+    for copy in copies[2:]:
+        copy.wait()
+    total = flat.astype(f32) + nn(hidden[...], w_out[...])
     logit = nt(total.astype(bf16), w_head[...]).astype(bf16)
     packs = lane_packs(bins, side)
     deep = side // packs
@@ -164,7 +171,7 @@
 
 def backward_kernel(q, packed, *refs):
     blocks, (w_out, w_head, far, near), rest = [refs[7 * p : 7 * p + 7] for p in range(q)], refs[7 * q : 7 * q + 4], refs[7 * q + 4 :]
-    results, hot, mirrored = [rest[3 * p : 3 * p + 3] for p in range(q)], rest[3 * q : -1], rest[-1]
+    (d_updated, d_gate, d_up), hot, mirrored = rest[:3], rest[3:-1], rest[-1]
     (width, side), units, bins = blocks[0][0].shape, w_out.shape[0], w_head.shape[0]
     packs = lane_packs(bins, side)
     own = lax.rem(lax.axis_index("row"), q)
@@ -178,33 +185,31 @@
     def _():
         mirrored[...] = far[...]
 
-    totals = None
+    inputs_t, updated_t, hidden, slope, swish, logits, onehot = zip(*blocks)
+    mirror = jnp.concatenate([mirrored[p, :, u * bins : (u + 1) * bins] for p in range(q) for u in range(packs)], axis=0)
+    summed = joined(logits, 0).astype(f32) + mirror.astype(f32)
+    powers = jnp.exp(summed - jnp.max(summed, axis=-1, keepdims=True))
+    probs = powers / jnp.sum(powers, axis=-1, keepdims=True)
+    grad_sym = (probs - joined(onehot, 0)).astype(bf16)
+    cotangent = (grad_sym.astype(f32) * 2.0).astype(bf16)
+    d_upd = nn(cotangent, w_head[...])
+    d_updated[...] = d_upd
+    d_upd_b = d_upd.astype(bf16)
     for p in range(q):
-        inputs_t, updated_t, hidden, slope, swish, logits, onehot = blocks[p]
-        d_updated, d_gate, d_up = results[p]
-        pieces = [mirrored[p, :, u * bins : (u + 1) * bins] for u in range(packs)]
-        summed = logits[...].astype(f32) + jnp.concatenate(pieces, axis=0).astype(f32)
-        powers = jnp.exp(summed - jnp.max(summed, axis=-1, keepdims=True))
-        probs = powers / jnp.sum(powers, axis=-1, keepdims=True)
-        grad_sym = (probs - onehot[...]).astype(bf16)
-        cotangent = (grad_sym.astype(f32) * 2.0).astype(bf16)
-        d_upd = nn(cotangent, w_head[...])
-        d_updated[...] = d_upd
-        d_upd_b = d_upd.astype(bf16)
-        d_upd_t = d_upd_b.T
-        terms = [[], [], []]
-        for at, step in chunks_of(units, 256):
-            span = slice(at, at + step)
-            d_hidden = nt(d_upd_b, w_out[span, :])
-            d_gate_part = (d_hidden * slope[:, span]).astype(bf16)
-            d_up_part = (d_hidden * swish[:, span]).astype(bf16)
-            d_gate[:, span] = d_gate_part
-            d_up[:, span] = d_up_part
-            terms[0].append(nn(inputs_t[...], d_gate_part))
-            terms[1].append(nn(inputs_t[...], d_up_part))
-            terms[2].append(nn(d_upd_t, hidden[:, span]))
-        terms = [jnp.concatenate(term, axis=1) for term in terms] + [nn(updated_t[...], cotangent)]
-        totals = [a + b for a, b in zip(totals, terms)] if p else terms
+        for top, tall in chunks_of(side, 128):
+            row = slice(p * side + top, p * side + top + tall)
+            for at, step in chunks_of(units, 256):
+                span = slice(at, at + step)
+                d_hidden = nt(d_upd_b[row], w_out[span, :])
+                d_gate[row, span] = (d_hidden * slope[p][top : top + tall, span]).astype(bf16)
+                d_up[row, span] = (d_hidden * swish[p][top : top + tall, span]).astype(bf16)
+    depth = joined(inputs_t, 1)
+    totals = (
+        nn(depth, d_gate[...]),
+        nn(depth, d_up[...]),
+        nn(d_upd_b.T, joined(hidden, 0)),
+        nn(joined(updated_t, 1), cotangent),
+    )
     if not packed:
         for ref, term in zip(hot, totals):
             ref[...] = term.astype(ref.dtype)
@@ -234,15 +239,17 @@
         hot[n][...] = slots[partner(own, n, q)]
 
 
-def input_kernel(d_updated, d_gate, d_up, normed, scale, w_gate, w_up, result):
-    d_inputs = nt(d_gate[...], w_gate[...]) + nt(d_up[...], w_up[...])
+def input_kernel(p, d_updated, d_gate, d_up, normed, scale, w_gate, w_up, result):
+    side = result.shape[0]
+    row = slice(p * side, (p + 1) * side)
+    d_inputs = nt(d_gate[row], w_gate[...]) + nt(d_up[row], w_up[...])
     normal = normed[...]
     d_norm = (
         d_inputs
         - jnp.mean(d_inputs, axis=-1, keepdims=True)
         - normal * jnp.mean(d_inputs * normal, axis=-1, keepdims=True)
     ) * scale[...]
-    result[...] = (d_updated[...] + d_norm).astype(bf16)
+    result[...] = (d_updated[row] + d_norm).astype(bf16)
 
 
 def place_kernel(q, *refs):
@@ -346,6 +353,7 @@
         scratch_shapes=[
             pltpu.VMEM((rows, cols), jnp.int32),
             pltpu.VMEM((q, *piece), bf16),
+            pltpu.VMEM((q * side, units), bf16),
             pltpu.SemaphoreType.DMA((5 + q,)),
         ],
         compiler_params=PARAMS,
@@ -407,26 +415,26 @@
         scratch = []
     results = pl.pallas_call(
         functools.partial(backward_kernel, q, (nrow, ncol) if fits else None),
-        out_shape=([shaped((side, width), f32)] + [shaped((side, units), bf16)] * 2) * q + hot_shapes,
+        out_shape=[shaped((q * side, width), f32)] + [shaped((q * side, units), bf16)] * 2 + hot_shapes,
         in_specs=[VMEM] * (7 * q + 4),
-        out_specs=[VMEM] * (3 * q + len(hot_shapes)),
+        out_specs=[VMEM] * (3 + len(hot_shapes)),
         scratch_shapes=scratch + [pltpu.VMEM((q, *piece), bf16)],
         compiler_params=PARAMS,
         cost_estimate=cost(8 * q * side * width * units, 4 * q * side * units),
         name="backward",
     )(*(x for block in prepared for x in block[:7]), w_out, head_t, far, sends)
-    hot = list(results[3 * q :])
+    hot = list(results[3:])
 
     def d_inputs(p):
         return pl.pallas_call(
-            input_kernel,
+            functools.partial(input_kernel, p),
             out_shape=shaped((side, width), bf16),
             in_specs=[VMEM] * 7,
             out_specs=VMEM,
             compiler_params=PARAMS,
             cost_estimate=cost(4 * side * width * units, 4 * side * units),
             name="d_inputs",
-        )(*results[3 * p : 3 * p + 3], *prepared[p][7:], w_gate, w_up)
+        )(*results[:3], *prepared[p][7:], w_gate, w_up)
 
     d_blocks = [d_inputs(p) for p in range(q)]
 

time: 30.1 us -> 29.8 us (0.990)
    pallas_call x1, Pallas kernels: 1.58 us -> 1.23 us  [body(): pl.pallas_call(functools.partial(backward_kernel, q, (nrow, ncol) if fits...]
where the time goes in v9:
time: 29.8 us; the launch traced here: 29.6 us
  starting transfers between devices  15 us (50%)
  Pallas kernels  7.59 us (25%)
  waiting for transfers between devices  6.32 us (21%)
  between operations  0.71 us (2%)
    ppermute x3, starting transfers between devices, body(): lax.ppermute(hot[p], 'row', [(s, following(s // q, p, groups) * q + s % q...  9.54 us
    ppermute x3, starting transfers between devices, body(): lax.ppermute(hot[p], 'col', [(s, partner(s, p, ncol)) for s in range(ncol)])  3.55 us
    ppermute x3, waiting for transfers between devices, body(): lax.ppermute(hot[p], 'row', [(s, following(s // q, p, groups) * q + s % q...  2.76 us
    pallas_call x1, Pallas kernels, body(): pl.pallas_call(functools.partial(forward_kernel, q), out_shape=[shaped((q...  2.31 us
    ppermute x3, waiting for transfers between devices, body(): lax.ppermute(hot[p], 'col', [(s, partner(s, p, ncol)) for s in range(ncol)])  2.29 us
    pallas_call x2, Pallas kernels, body(): pl.pallas_call(functools.partial(prepare_kernel, q, p), out_shape=[shaped...  1.77 us
    pallas_call x1, Pallas kernels, body(): pl.pallas_call(functools.partial(backward_kernel, q, (nrow, ncol) if fits...  1.23 us
    ppermute x2, waiting for transfers between devices, returned(): lax.ppermute(x, 'row', core_pairs(nrow, q, n // 2 + 1))  0.86 us
  transfers between devices with their start and end apart: 12, of which 8 were waited for; matrix products, arithmetic and copies ran while one was open for 0% of the time, Pallas kernels for 11%

profile of v9, /device:TPU:0, one launch (start us, length us, event | category | flops | bytes accessed | tf_op | source)
XLA Modules:
  0.0 29.6 jit_solution(13024870984221850317)
XLA Ops:
  0.6 2.3 %forward.1 = (bf16[2,256,128]{2,1,0:T(8,128)(2,1)S(1)}, bf16[128,512]{1,0:T(8,128)(2,1)S(1)}, bf16[128,512]{1,0:T(8,128)(2,1)S(1)}, bf16[512,128]{1,0:T(8,128)(2...) custom-call(bf16[16,32,128]{2,1,0:T(8,128)(2,1)} %refs_0_.1, ...), custom_call_target="tpu_custom_call" | custom-call | tf_op jit(solution)/shard_map/forward/pallas_call | solution.py:346
  3.0 0.5 %collective-permute-start.2 = (bf16[2,128,128]{2,1,0:T(8,128)(2,1)S(1)}, bf16[2,128,128]{2,1,0:T(8,128)(2,1)S(1)}, u32[]{:S(2)}, u32[]{:S(2)}) collective-permute-start(bf16[2,128,128]{2,1,0:T(8,128)(2,1)S(1)} %get-tuple-element.89.refs_17_), channel_id=1, source_target_pairs={{0,4},{1,8},{2,16},{3,24},{4,0},{5,12},{6,20},{7,28},{8,1},{9,13},... | collective-permute-start | bytes 196616 | tf_op jit(solution)/shard_map/ppermute | solution.py:368
  3.5 0.1 collective-permute-start.1
  3.6 0.4 %collective-permute-start = (bf16[128,128]{1,0:T(8,128)(2,1)S(1)}, bf16[128,128]{1,0:T(8,128)(2,1)S(1)}, u32[]{:S(2)}, u32[]{:S(2)}) collective-permute-start(bf16[128,128]{1,0:T(8,128)(2,1)S(1)} %get-tuple-element.80), channel_id=1, source_target_pairs={{0,4},{4,0},{8,12},{12,8},{16,20},{20,16},{24,28},{28,24},{1,5},{5... | collective-permute-start | bytes 98312 | tf_op jit(solution)/shard_map/ppermute | solution.py:377
  4.0 0.9 %prepare.2 = (bf16[128,256]{1,0:T(8,128)(2,1)S(1)}, bf16[128,256]{1,0:T(8,128)(2,1)S(1)}, bf16[256,512]{1,0:T(8,128)(2,1)S(1)}, f32[256,512]{1,0:T(8,128)S(1)}, ...) custom-call(bf16[2,256,128]{2,1,0:T(8,128)(2,1)S(1)} %get-tuple-elem, ...), custom_call_target="tpu_custom_call" | custom-call | flops 100663296 | bytes 1048576 | tf_op jit(solution)/shard_map/prepare/pallas_call | solution.py:382
  4.9 0.0 collective-permute-done.refs_0_
  4.9 0.0 collective-permute-done.1.refs_1_
  4.9 0.9 %prepare.3 = (bf16[128,256]{1,0:T(8,128)(2,1)S(1)}, bf16[128,256]{1,0:T(8,128)(2,1)S(1)}, bf16[256,512]{1,0:T(8,128)(2,1)S(1)}, f32[256,512]{1,0:T(8,128)S(1)}, ...) custom-call(bf16[128,128]{1,0:T(8,128)(2,1)S(1)} %collective-permute, ...), custom_call_target="tpu_custom_call" | custom-call | tf_op jit(solution)/shard_map/prepare/pallas_call | solution.py:382
  5.8 0.0 collective-permute-done.2.refs_16_
  5.8 1.2 %backward.1 = (f32[512,128]{1,0:T(8,128)S(1)}, bf16[512,512]{1,0:T(8,128)(2,1)S(1)}, bf16[512,512]{1,0:T(8,128)(2,1)S(1)}, bf16[4,208,128]{2,1,0:T(8,128)(2,1)S(1)}, bf16[4,208,128]{2,1,0:T(8,128)(2,1)S(1)}) custom-call(bf16[128,256]{1,0:T(8,128)(2,1)S(1)} %get-tuple-element.73.refs_0_, bf16[128,256]{1,0:T(8,128)(2,1)S(1)} %get-tuple-element.74.refs_1_, ...), custom_call_target="tpu_custom_call" | custom-call | flops 268435456 | bytes 1048576 | tf_op jit(solution)/shard_map/backward/pallas_call | solution.py:416
  7.1 0.4 %collective-permute-start.3 = (bf16[4,208,128]{2,1,0:T(8,128)(2,1)S(1)}, bf16[4,208,128]{2,1,0:T(8,128)(2,1)S(1)}, u32[]{:S(2)}, u32[]{:S(2)}) collective-permute-start(bf16[4,208,128]{2,1,0:T(8,128)(2,1)S(1)} %get-tuple-element.91), channel_id=1, source_target_pairs={{0,4},{4,0},{8,12},{12,8},{16,20},{20,16},{24,28},{28,24},{1,5},{5... | collective-permute-start | bytes 638984 | tf_op jit(solution)/shard_map/ppermute | solution.py:467
  7.4 0.4 %d_inputs.3.rest_2_ = bf16[256,128]{1,0:T(8,128)(2,1)S(1)} custom-call(f32[512,128]{1,0:T(8,128)S(1)} %get-tuple-element.92.d_updated, bf16[512,512]{1,0:T(8,128)(2,1)S(1)} %get-tuple-element.93.d_gate, bf16[512,512]{1,0:T(8,128)(2,1)S(1)} %get-tuple-element.94.d_up, f32[256,128]{1,0:T(8,128)S(1)} %get-tuple-element.97.normed, ...), custom_call_target="tpu_custom_call" | custom-call | flops 67108864 | bytes 524288 | tf_op jit(solution)/shard_map/d_inputs/pallas_call | solution.py:429
  7.8 0.4 %d_inputs.2.refs_0_ = bf16[256,128]{1,0:T(8,128)(2,1)S(1)} custom-call(f32[512,128]{1,0:T(8,128)S(1)} %get-tuple-element.92.d_updated, bf16[512,512]{1,0:T(8,128)(2,1)S(1)} %get-tuple-element.93.d_gate, bf16[512,512]{1,0:T(8,128)(2,1)S(1)} %get-tuple-element.94.d_up, f32[256,128]{1,0:T(8,128)S(1)} %get-tuple-element.95.normed, ...), custom_call_target="tpu_custom_call" | custom-call | flops 67108864 | bytes 524288 | tf_op jit(solution)/shard_map/d_inputs/pallas_call | solution.py:429
  8.2 0.4 %collective-permute-done.3.rest_1_ = bf16[4,208,128]{2,1,0:T(8,128)(2,1)S(1)} collective-permute-done((bf16[4,208,128]{2,1,0:T(8,128)(2,1)S(1)}, bf16[4,208,128]{2,1,0:T(8,128)(2,1)S(1)}, u32[]{:S(2)}, u32[]{:S(2)}) %collective-permute-start.3) | collective-permute-done | bytes 213024 | tf_op jit(solution)/shard_map/ppermute | solution.py:467
  8.6 0.1 core_sum.1
  8.7 7.2 %collective-permute-start.4 = (bf16[208,128]{1,0:T(8,128)(2,1)S(1)}, bf16[208,128]{1,0:T(8,128)(2,1)S(1)}, u32[]{:S(2)}, u32[]{:S(2)}) collective-permute-start(bf16[208,128]{1,0:T(8,128)(2,1)S(1)} %get-tuple-element.103), channel_id=1, source_target_pairs={{0,8},{4,12},{8,16},{12,20},{16,24},{20,28},{24,0},{28,4},{1,9},{5... | collective-permute-start | bytes 159752 | tf_op jit(solution)/shard_map/ppermute | solution.py:480
  15.9 2.3 %collective-permute-start.5 = (bf16[208,128]{1,0:T(8,128)(2,1)S(1)}, bf16[208,128]{1,0:T(8,128)(2,1)S(1)}, u32[]{:S(2)}, u32[]{:S(2)}) collective-permute-start(bf16[208,128]{1,0:T(8,128)(2,1)S(1)} %get-tuple-element.104), channel_id=1, source_target_pairs={{0,16},{4,20},{8,24},{12,28},{16,0},{20,4},{24,8},{28,12},{1,17},{... | collective-permute-start | bytes 159752 | tf_op jit(solution)/shard_map/ppermute | solution.py:480
  18.2 0.0 collective-permute-start.6
  18.2 0.0 collective-permute-start.7
  18.2 0.5 %collective-permute-start.8 = (bf16[128,128]{1,0:T(8,128)(2,1)S(1)}, bf16[128,128]{1,0:T(8,128)(2,1)S(1)}, u32[]{:S(2)}, u32[]{:S(2)}) collective-permute-start(bf16[128,128]{1,0:T(8,128)(2,1)S(1)} %get-tuple-element.108), channel_id=1, source_target_pairs={{0,4},{4,0},{8,12},{12,8},{16,20},{20,16},{24,28},{28,24},{1,5},{5... | collective-permute-start | bytes 98312 | tf_op jit(solution)/shard_map/ppermute | solution.py:442
  18.7 0.7 %collective-permute-done.7.refs_1_ = bf16[128,128]{1,0:T(8,128)(2,1)S(1)} collective-permute-done((bf16[128,128]{1,0:T(8,128)(2,1)S(1)}, bf16[128,128]{1,0:T(8,128)(2,1)S(1)}, u32[]{:S(2)}, u32[]{:S(2)}) %collective-permute-start.7) | collective-permute-done | bytes 32800 | tf_op jit(solution)/shard_map/ppermute | solution.py:442
  19.4 0.2 collective-permute-done.8.refs_2_
  19.6 0.3 collective-permute-done.4.rest_1_
  19.9 1.0 %collective-permute-done.5.rest_2_ = bf16[208,128]{1,0:T(8,128)(2,1)S(1)} collective-permute-done((bf16[208,128]{1,0:T(8,128)(2,1)S(1)}, bf16[208,128]{1,0:T(8,128)(2,1)S(1)}, u32[]{:S(2)}, u32[]{:S(2)}) %collective-permute-start.5) | collective-permute-done | bytes 53280 | tf_op jit(solution)/shard_map/ppermute | solution.py:480
  20.9 1.4 %collective-permute-done.6.rest_3_ = bf16[208,128]{1,0:T(8,128)(2,1)S(1)} collective-permute-done((bf16[208,128]{1,0:T(8,128)(2,1)S(1)}, bf16[208,128]{1,0:T(8,128)(2,1)S(1)}, u32[]{:S(2)}, u32[]{:S(2)}) %collective-permute-start.6) | collective-permute-done | bytes 53280 | tf_op jit(solution)/shard_map/ppermute | solution.py:480
  22.3 0.1 chip_sum.1
  22.4 0.7 %collective-permute-start.9 = (bf16[64,128]{1,0:T(8,128)(2,1)S(1)}, bf16[64,128]{1,0:T(8,128)(2,1)S(1)}, u32[]{:S(2)}, u32[]{:S(2)}) collective-permute-start(bf16[64,128]{1,0:T(8,128)(2,1)S(1)} %get-tuple-element.114), channel_id=1, source_target_pairs={{0,2},{1,3},{2,0},{3,1},{4,6},{5,7},{6,4},{7,5},{8,10},{9,11},{10,... | collective-permute-start | bytes 49160 | tf_op jit(solution)/shard_map/ppermute | solution.py:494
  23.1 2.0 %collective-permute-start.10 = (bf16[64,128]{1,0:T(8,128)(2,1)S(1)}, bf16[64,128]{1,0:T(8,128)(2,1)S(1)}, u32[]{:S(2)}, u32[]{:S(2)}) collective-permute-start(bf16[64,128]{1,0:T(8,128)(2,1)S(1)} %get-tuple-element.115), channel_id=1, source_target_pairs={{0,3},{1,2},{2,1},{3,0},{4,7},{5,6},{6,5},{7,4},{8,11},{9,10},{10,... | collective-permute-start | bytes 49160 | tf_op jit(solution)/shard_map/ppermute | solution.py:494
  25.1 0.9 %collective-permute-start.11 = (bf16[64,128]{1,0:T(8,128)(2,1)S(1)}, bf16[64,128]{1,0:T(8,128)(2,1)S(1)}, u32[]{:S(2)}, u32[]{:S(2)}) collective-permute-start(bf16[64,128]{1,0:T(8,128)(2,1)S(1)} %get-tuple-element.116), channel_id=1, source_target_pairs={{0,1},{1,0},{2,3},{3,2},{4,5},{5,4},{6,7},{7,6},{8,9},{9,8},{10,11... | collective-permute-start | bytes 49160 | tf_op jit(solution)/shard_map/ppermute | solution.py:494
  26.0 0.7 %place.1 = bf16[16,2,16,128]{3,2,1,0:T(8,128)(2,1)} custom-call(bf16[256,128]{1,0:T(8,128)(2,1)S(1)} %d_inputs.2.refs_0_, bf16[128,128]{1,0:T(8,128)(2,1)S(1)} %collective-permute-done.7.refs_1_, bf16[128,128]{1,0:T(8,128)(2,1)S(1)} %collective-permute-done.8.refs_2_), custom_call_target="tpu_custom_call" | custom-call | tf_op jit(solution)/shard_map/place/pallas_call | solution.py:446
  26.7 0.5 %collective-permute-done.9.rest_1_ = bf16[64,128]{1,0:T(8,128)(2,1)S(1)} collective-permute-done((bf16[64,128]{1,0:T(8,128)(2,1)S(1)}, bf16[64,128]{1,0:T(8,128)(2,1)S(1)}, u32[]{:S(2)}, u32[]{:S(2)}) %collective-permute-start.9) | collective-permute-done | bytes 16416 | tf_op jit(solution)/shard_map/ppermute | solution.py:494
  27.1 1.8 %collective-permute-done.10.rest_2_ = bf16[64,128]{1,0:T(8,128)(2,1)S(1)} collective-permute-done((bf16[64,128]{1,0:T(8,128)(2,1)S(1)}, bf16[64,128]{1,0:T(8,128)(2,1)S(1)}, u32[]{:S(2)}, u32[]{:S(2)}) %collective-permute-start.10) | collective-permute-done | bytes 16416 | tf_op jit(solution)/shard_map/ppermute | solution.py:494
  28.9 0.0 collective-permute-done.11.rest_3_
  28.9 0.7 %col_sum.1 = (f32[16,128]{1,0:T(8,128)}, f32[16,128]{1,0:T(8,128)}, f32[32,64]{1,0:T(8,128)}, f32[16,16]{1,0:T(8,128)}) custom-call(bf16[64,128]{1,0:T(8,128)(2,1)S(1)} %get-tuple-element.121.rest_0_, bf16[64,128]{1,0:T(8,128)(2,1)S(1)} %collective-permute-done.9.rest_1_, bf16[64,128]{1,0:T(8,128)(2,1)S(1)} %collective-permute-done.10.rest_2_, ...), custom_call_target="tpu_custom_call" | custom-call | tf_op jit(solution)/shard_map/col_sum/pallas_call | solution.py:496
  (1 shorter events, 0.0 us)
Async XLA Ops:
  3.0 2.9 %collective-permute-start.2 = (bf16[2,128,128]{2,1,0:T(8,128)(2,1)S(1)}, bf16[2,128,128]{2,1,0:T(8,128)(2,1)S(1)}, u32[]{:S(2)}, u32[]{:S(2)}) collective-permute-start(bf16[2,128,128]{2,1,0:T(8,128)(2,1)S(1)} %get-tuple-element.89.refs_17_), channel_id=1, source_target_pairs={{0,4},{1,8},{2,16},{3,24},{4,0},{5,12},{6,20},{7,28},{8,1},{9,13},... | collective-permute-start | bytes 196616 | tf_op jit(solution)/shard_map/ppermute | solution.py:368
  3.5 1.4 %collective-permute-start.1 = (bf16[144,128]{1,0:T(8,128)(2,1)S(1)}, bf16[144,128]{1,0:T(8,128)(2,1)S(1)}, u32[]{:S(2)}, u32[]{:S(2)}) collective-permute-start(bf16[144,128]{1,0:T(8,128)(2,1)S(1)} %get-tuple-element.81), channel_id=1, source_target_pairs={{0,4},{4,0},{8,12},{12,8},{16,20},{20,16},{24,28},{28,24},{1,5},{5... | collective-permute-start | bytes 110600 | tf_op jit(solution)/shard_map/ppermute | solution.py:377
  3.6 1.3 %collective-permute-start = (bf16[128,128]{1,0:T(8,128)(2,1)S(1)}, bf16[128,128]{1,0:T(8,128)(2,1)S(1)}, u32[]{:S(2)}, u32[]{:S(2)}) collective-permute-start(bf16[128,128]{1,0:T(8,128)(2,1)S(1)} %get-tuple-element.80), channel_id=1, source_target_pairs={{0,4},{4,0},{8,12},{12,8},{16,20},{20,16},{24,28},{28,24},{1,5},{5... | collective-permute-start | bytes 98312 | tf_op jit(solution)/shard_map/ppermute | solution.py:377
  7.1 1.5 %collective-permute-start.3 = (bf16[4,208,128]{2,1,0:T(8,128)(2,1)S(1)}, bf16[4,208,128]{2,1,0:T(8,128)(2,1)S(1)}, u32[]{:S(2)}, u32[]{:S(2)}) collective-permute-start(bf16[4,208,128]{2,1,0:T(8,128)(2,1)S(1)} %get-tuple-element.91), channel_id=1, source_target_pairs={{0,4},{4,0},{8,12},{12,8},{16,20},{20,16},{24,28},{28,24},{1,5},{5... | collective-permute-start | bytes 638984 | tf_op jit(solution)/shard_map/ppermute | solution.py:467
  8.7 11.2 %collective-permute-start.4 = (bf16[208,128]{1,0:T(8,128)(2,1)S(1)}, bf16[208,128]{1,0:T(8,128)(2,1)S(1)}, u32[]{:S(2)}, u32[]{:S(2)}) collective-permute-start(bf16[208,128]{1,0:T(8,128)(2,1)S(1)} %get-tuple-element.103), channel_id=1, source_target_pairs={{0,8},{4,12},{8,16},{12,20},{16,24},{20,28},{24,0},{28,4},{1,9},{5... | collective-permute-start | bytes 159752 | tf_op jit(solution)/shard_map/ppermute | solution.py:480
  15.9 5.0 %collective-permute-start.5 = (bf16[208,128]{1,0:T(8,128)(2,1)S(1)}, bf16[208,128]{1,0:T(8,128)(2,1)S(1)}, u32[]{:S(2)}, u32[]{:S(2)}) collective-permute-start(bf16[208,128]{1,0:T(8,128)(2,1)S(1)} %get-tuple-element.104), channel_id=1, source_target_pairs={{0,16},{4,20},{8,24},{12,28},{16,0},{20,4},{24,8},{28,12},{1,17},{... | collective-permute-start | bytes 159752 | tf_op jit(solution)/shard_map/ppermute | solution.py:480
  18.2 4.1 %collective-permute-start.6 = (bf16[208,128]{1,0:T(8,128)(2,1)S(1)}, bf16[208,128]{1,0:T(8,128)(2,1)S(1)}, u32[]{:S(2)}, u32[]{:S(2)}) collective-permute-start(bf16[208,128]{1,0:T(8,128)(2,1)S(1)} %get-tuple-element.105), channel_id=1, source_target_pairs={{0,24},{4,28},{8,0},{12,4},{16,8},{20,12},{24,16},{28,20},{1,25},{... | collective-permute-start | bytes 159752 | tf_op jit(solution)/shard_map/ppermute | solution.py:480
  18.2 1.2 %collective-permute-start.7 = (bf16[128,128]{1,0:T(8,128)(2,1)S(1)}, bf16[128,128]{1,0:T(8,128)(2,1)S(1)}, u32[]{:S(2)}, u32[]{:S(2)}) collective-permute-start(bf16[128,128]{1,0:T(8,128)(2,1)S(1)} %get-tuple-element.107), channel_id=1, source_target_pairs={{0,4},{4,0},{8,12},{12,8},{16,20},{20,16},{24,28},{28,24},{1,5},{5... | collective-permute-start | bytes 98312 | tf_op jit(solution)/shard_map/ppermute | solution.py:442
  18.2 1.4 %collective-permute-start.8 = (bf16[128,128]{1,0:T(8,128)(2,1)S(1)}, bf16[128,128]{1,0:T(8,128)(2,1)S(1)}, u32[]{:S(2)}, u32[]{:S(2)}) collective-permute-start(bf16[128,128]{1,0:T(8,128)(2,1)S(1)} %get-tuple-element.108), channel_id=1, source_target_pairs={{0,4},{4,0},{8,12},{12,8},{16,20},{20,16},{24,28},{28,24},{1,5},{5... | collective-permute-start | bytes 98312 | tf_op jit(solution)/shard_map/ppermute | solution.py:442
  22.4 4.7 %collective-permute-start.9 = (bf16[64,128]{1,0:T(8,128)(2,1)S(1)}, bf16[64,128]{1,0:T(8,128)(2,1)S(1)}, u32[]{:S(2)}, u32[]{:S(2)}) collective-permute-start(bf16[64,128]{1,0:T(8,128)(2,1)S(1)} %get-tuple-element.114), channel_id=1, source_target_pairs={{0,2},{1,3},{2,0},{3,1},{4,6},{5,7},{6,4},{7,5},{8,10},{9,11},{10,... | collective-permute-start | bytes 49160 | tf_op jit(solution)/shard_map/ppermute | solution.py:494
  23.1 5.8 %collective-permute-start.10 = (bf16[64,128]{1,0:T(8,128)(2,1)S(1)}, bf16[64,128]{1,0:T(8,128)(2,1)S(1)}, u32[]{:S(2)}, u32[]{:S(2)}) collective-permute-start(bf16[64,128]{1,0:T(8,128)(2,1)S(1)} %get-tuple-element.115), channel_id=1, source_target_pairs={{0,3},{1,2},{2,1},{3,0},{4,7},{5,6},{6,5},{7,4},{8,11},{9,10},{10,... | collective-permute-start | bytes 49160 | tf_op jit(solution)/shard_map/ppermute | solution.py:494
  25.1 3.8 %collective-permute-start.11 = (bf16[64,128]{1,0:T(8,128)(2,1)S(1)}, bf16[64,128]{1,0:T(8,128)(2,1)S(1)}, u32[]{:S(2)}, u32[]{:S(2)}) collective-permute-start(bf16[64,128]{1,0:T(8,128)(2,1)S(1)} %get-tuple-element.116), channel_id=1, source_target_pairs={{0,1},{1,0},{2,3},{3,2},{4,5},{5,4},{6,7},{7,6},{8,9},{9,8},{10,11... | collective-permute-start | bytes 49160 | tf_op jit(solution)/shard_map/ppermute | solution.py:494

commit v10 on v9

--- a/solution.py
+++ b/solution.py
@@ -47,6 +47,10 @@
     if n & (n - 1) == 0:
         return s ^ p
     return (s + p) % n if isinstance(s, int) else lax.rem(s + p, n)
+
+
+def crossed(k, q):
+    return partner(k, 1, q) if q > 1 else k
 
 
 def following(s, p, n):
@@ -111,7 +115,7 @@
         mark = targets[:, h * edge : (h + 1) * edge].astype(f32)
         marks[h] = jnp.concatenate([mark, jnp.zeros((edge, width - edge), f32)], axis=1).astype(bf16)
     for p in range(q):
-        sends[p] = halves[partner(own, p, q)]
+        sends[p] = halves[partner(crossed(own, q), p, q)]
 
 
 def lend_kernel(q, pair, marks, *lent):
@@ -119,10 +123,11 @@
     side = pair.shape[1]
     for p in range(1, q):
         first, second = lent[2 * p - 2 : 2 * p]
-        block = pair[partner(own, p, q)]
+        lent_half = crossed(partner(own, p, q), q)
+        block = pair[lent_half]
         first[...] = block[: side // 2]
         second[: side // 2] = block[side // 2 :]
-        second[side // 2 :] = marks[partner(own, p, q)]
+        second[side // 2 :] = marks[lent_half]
 
 
 def prepare_kernel(q, p, *refs):
@@ -135,6 +140,7 @@
     else:
         own = lax.rem(lax.axis_index("row"), q)
         side, edge = refs[0].shape[1], refs[1].shape[1]
+        own = crossed(own, q)
         flat, mark, refs = refs[0][own], refs[1][own], refs[2:]
     w_gate, w_up, w_out, w_head, inputs_t, updated_t, hidden, slope, swish, logits, onehot, normed, scale = refs
     width, bins = flat.shape[1], w_head.shape[0]
@@ -170,23 +176,13 @@
 
 
 def backward_kernel(q, packed, *refs):
-    blocks, (w_out, w_head, far, near), rest = [refs[7 * p : 7 * p + 7] for p in range(q)], refs[7 * q : 7 * q + 4], refs[7 * q + 4 :]
-    (d_updated, d_gate, d_up), hot, mirrored = rest[:3], rest[3:-1], rest[-1]
+    blocks, (w_out, w_head, far), rest = [refs[7 * p : 7 * p + 7] for p in range(q)], refs[7 * q : 7 * q + 3], refs[7 * q + 3 :]
+    (d_updated, d_gate, d_up), hot = rest[:3], rest[3:]
     (width, side), units, bins = blocks[0][0].shape, w_out.shape[0], w_head.shape[0]
     packs = lane_packs(bins, side)
     own = lax.rem(lax.axis_index("row"), q)
-    inside = lax.axis_index("row") // q == lax.axis_index("col")
-
-    @pl.when(inside)
-    def _():
-        mirrored[...] = near[...]
-
-    @pl.when(jnp.logical_not(inside))
-    def _():
-        mirrored[...] = far[...]
-
     inputs_t, updated_t, hidden, slope, swish, logits, onehot = zip(*blocks)
-    mirror = jnp.concatenate([mirrored[p, :, u * bins : (u + 1) * bins] for p in range(q) for u in range(packs)], axis=0)
+    mirror = jnp.concatenate([far[p, :, u * bins : (u + 1) * bins] for p in range(q) for u in range(packs)], axis=0)
     summed = joined(logits, 0).astype(f32) + mirror.astype(f32)
     powers = jnp.exp(summed - jnp.max(summed, axis=-1, keepdims=True))
     probs = powers / jnp.sum(powers, axis=-1, keepdims=True)
@@ -235,8 +231,11 @@
             block = head_term[r * part : (r + 1) * part, :]
             block = jnp.concatenate([block, jnp.zeros((part, lanes - bins), f32)], axis=1)
             slots[k, a, at : at + part] = block.astype(bf16)
+    mine = lax.axis_index("row") // q
     for n in range(q):
-        hot[n][...] = slots[partner(own, n, q)]
+        core = partner(own, n, q)
+        for a in range(groups):
+            hot[n][a] = slots[jnp.where(mine == a, core, crossed(core, q)), a]
 
 
 def input_kernel(p, d_updated, d_gate, d_up, normed, scale, w_gate, w_up, result):
@@ -256,10 +255,10 @@
     blocks, d_pair = refs[:-1], refs[-1]
     edge, _, _, width = d_pair.shape
     own = lax.rem(lax.axis_index("row"), q)
-    d_pair[:, own] = blocks[0][...].reshape(edge, edge, width)
+    d_pair[:, crossed(own, q)] = blocks[0][...].reshape(edge, edge, width)
     for p in range(1, q):
         for n, half in enumerate((slice(0, edge // 2), slice(edge // 2, edge))):
-            d_pair[half, partner(own, p, q)] = blocks[2 * p - 1 + n][...].reshape(edge // 2, edge, width)
+            d_pair[half, crossed(partner(own, p, q), q)] = blocks[2 * p - 1 + n][...].reshape(edge // 2, edge, width)
 
 
 def core_sum_kernel(q, groups, *rest):
@@ -361,9 +360,7 @@
     )(*(pltpu.with_memory_space_constraint(x, pltpu.HBM) for x in sources))
 
     pairs = [
-        (r * ncol + c, (q * c + (partner(r % q, 1, q) if q == 2 and r // q == c else r % q)) * ncol + r // q)
-        for r in range(nrow)
-        for c in range(ncol)
+        (r * ncol + c, (q * c + crossed(r % q, q)) * ncol + r // q) for r in range(nrow) for c in range(ncol)
     ]
     far = lax.ppermute(sends, ("row", "col"), pairs)
     lent = pl.pallas_call(
@@ -416,13 +413,13 @@
     results = pl.pallas_call(
         functools.partial(backward_kernel, q, (nrow, ncol) if fits else None),
         out_shape=[shaped((q * side, width), f32)] + [shaped((q * side, units), bf16)] * 2 + hot_shapes,
-        in_specs=[VMEM] * (7 * q + 4),
+        in_specs=[VMEM] * (7 * q + 3),
         out_specs=[VMEM] * (3 + len(hot_shapes)),
-        scratch_shapes=scratch + [pltpu.VMEM((q, *piece), bf16)],
+        scratch_shapes=scratch,
         compiler_params=PARAMS,
         cost_estimate=cost(8 * q * side * width * units, 4 * q * side * units),
         name="backward",
-    )(*(x for block in prepared for x in block[:7]), w_out, head_t, far, sends)
+    )(*(x for block in prepared for x in block[:7]), w_out, head_t, far)
     hot = list(results[3:])
 
     def d_inputs(p):
@@ -477,7 +474,7 @@
     hot, d_blocks = hot[:groups], d_blocks[:1] + list(hot[groups:])
     terms = [hot[0]]
     for p in range(1, groups):
-        terms.append(lax.ppermute(hot[p], "row", [(s, following(s // q, p, groups) * q + s % q) for s in range(nrow)]))
+        terms.append(lax.ppermute(hot[p], "row", [(s, following(s // q, p, groups) * q + crossed(s % q, q)) for s in range(nrow)]))
     terms, d_blocks = lax.optimization_barrier((terms, returned(d_blocks)))
     short = 3 * part + width // ncol * tall // lanes
     hot = pl.pallas_call(

time: 29.8 us -> 29.7 us (level)
    ppermute x3, waiting for transfers between devices: 2.76 us -> 2.3 us  [body(): lax.ppermute(hot[p], 'row', [(s, following(s // q, p, groups) * q + cross...]
where the time goes in v10:
time: 29.7 us; the launch traced here: 29.6 us
  starting transfers between devices  15.1 us (51%)
  Pallas kernels  7.55 us (25%)
  waiting for transfers between devices  6.15 us (21%)
  between operations  0.71 us (2%)
    ppermute x3, starting transfers between devices, body(): lax.ppermute(hot[p], 'row', [(s, following(s // q, p, groups) * q + cross...  9.51 us
    ppermute x3, starting transfers between devices, body(): lax.ppermute(hot[p], 'col', [(s, partner(s, p, ncol)) for s in range(ncol)])  3.71 us
    ppermute x3, waiting for transfers between devices, body(): lax.ppermute(hot[p], 'col', [(s, partner(s, p, ncol)) for s in range(ncol)])  2.58 us
    pallas_call x1, Pallas kernels, body(): pl.pallas_call(functools.partial(forward_kernel, q), out_shape=[shaped((q...  2.31 us
    ppermute x3, waiting for transfers between devices, body(): lax.ppermute(hot[p], 'row', [(s, following(s // q, p, groups) * q + cross...  2.3 us
    pallas_call x2, Pallas kernels, body(): pl.pallas_call(functools.partial(prepare_kernel, q, p), out_shape=[shaped...  1.77 us
    pallas_call x1, Pallas kernels, body(): pl.pallas_call(functools.partial(backward_kernel, q, (nrow, ncol) if fits...  1.2 us
    ppermute x2, waiting for transfers between devices, returned(): lax.ppermute(x, 'row', core_pairs(nrow, q, n // 2 + 1))  0.86 us
  transfers between devices with their start and end apart: 12, of which 8 were waited for; matrix products, arithmetic and copies ran while one was open for 0% of the time, Pallas kernels for 11%

profile of v10, /device:TPU:0, one launch (start us, length us, event | category | flops | bytes accessed | tf_op | source)
XLA Modules:
  0.0 29.6 jit_solution(9229427400623385775)
XLA Ops:
  0.6 2.3 %forward.1 = (bf16[2,256,128]{2,1,0:T(8,128)(2,1)S(1)}, bf16[128,512]{1,0:T(8,128)(2,1)S(1)}, bf16[128,512]{1,0:T(8,128)(2,1)S(1)}, bf16[512,128]{1,0:T(8,128)(2...) custom-call(bf16[16,32,128]{2,1,0:T(8,128)(2,1)} %refs_0_.1, ...), custom_call_target="tpu_custom_call" | custom-call | tf_op jit(solution)/shard_map/forward/pallas_call | solution.py:345
  3.0 0.5 %collective-permute-start.2 = (bf16[2,128,128]{2,1,0:T(8,128)(2,1)S(1)}, bf16[2,128,128]{2,1,0:T(8,128)(2,1)S(1)}, u32[]{:S(2)}, u32[]{:S(2)}) collective-permute-start(bf16[2,128,128]{2,1,0:T(8,128)(2,1)S(1)} %get-tuple-element.89), channel_id=1, source_target_pairs={{0,4},{1,12},{2,20},{3,28},{4,0},{5,8},{6,16},{7,24},{8,5},{9,13},... | collective-permute-start | bytes 196616 | tf_op jit(solution)/shard_map/ppermute | solution.py:365
  3.5 0.1 collective-permute-start.1
  3.6 0.4 %collective-permute-start = (bf16[128,128]{1,0:T(8,128)(2,1)S(1)}, bf16[128,128]{1,0:T(8,128)(2,1)S(1)}, u32[]{:S(2)}, u32[]{:S(2)}) collective-permute-start(bf16[128,128]{1,0:T(8,128)(2,1)S(1)} %get-tuple-element.80), channel_id=1, source_target_pairs={{0,4},{4,0},{8,12},{12,8},{16,20},{20,16},{24,28},{28,24},{1,5},{5... | collective-permute-start | bytes 98312 | tf_op jit(solution)/shard_map/ppermute | solution.py:374
  4.0 0.9 %prepare.2 = (bf16[128,256]{1,0:T(8,128)(2,1)S(1)}, bf16[128,256]{1,0:T(8,128)(2,1)S(1)}, bf16[256,512]{1,0:T(8,128)(2,1)S(1)}, f32[256,512]{1,0:T(8,128)S(1)}, ...) custom-call(bf16[2,256,128]{2,1,0:T(8,128)(2,1)S(1)} %get-tuple-elem, ...), custom_call_target="tpu_custom_call" | custom-call | flops 100663296 | bytes 1048576 | tf_op jit(solution)/shard_map/prepare/pallas_call | solution.py:379
  4.9 0.0 collective-permute-done.refs_0_
  4.9 0.0 collective-permute-done.1.refs_1_
  4.9 0.9 %prepare.3 = (bf16[128,256]{1,0:T(8,128)(2,1)S(1)}, bf16[128,256]{1,0:T(8,128)(2,1)S(1)}, bf16[256,512]{1,0:T(8,128)(2,1)S(1)}, f32[256,512]{1,0:T(8,128)S(1)}, ...) custom-call(bf16[128,128]{1,0:T(8,128)(2,1)S(1)} %collective-permute, ...), custom_call_target="tpu_custom_call" | custom-call | tf_op jit(solution)/shard_map/prepare/pallas_call | solution.py:379
  5.8 0.0 collective-permute-done.2.refs_16_
  5.8 1.2 %backward.1 = (f32[512,128]{1,0:T(8,128)S(1)}, bf16[512,512]{1,0:T(8,128)(2,1)S(1)}, bf16[512,512]{1,0:T(8,128)(2,1)S(1)}, bf16[4,208,128]{2,1,0:T(8,128)(2,1)S(1)}, bf16[4,208,128]{2,1,0:T(8,128)(2,1)S(1)}) custom-call(bf16[128,256]{1,0:T(8,128)(2,1)S(1)} %get-tuple-element.73.refs_0_, bf16[128,256]{1,0:T(8,128)(2,1)S(1)} %get-tuple-element.74.refs_1_, ...), custom_call_target="tpu_custom_call" | custom-call | flops 268435456 | bytes 1048576 | tf_op jit(solution)/shard_map/backward/pallas_call | solution.py:413
  7.0 0.4 %collective-permute-start.3 = (bf16[4,208,128]{2,1,0:T(8,128)(2,1)S(1)}, bf16[4,208,128]{2,1,0:T(8,128)(2,1)S(1)}, u32[]{:S(2)}, u32[]{:S(2)}) collective-permute-start(bf16[4,208,128]{2,1,0:T(8,128)(2,1)S(1)} %get-tuple-element.91), channel_id=1, source_target_pairs={{0,4},{4,0},{8,12},{12,8},{16,20},{20,16},{24,28},{28,24},{1,5},{5... | collective-permute-start | bytes 638984 | tf_op jit(solution)/shard_map/ppermute | solution.py:464
  7.4 0.4 %d_inputs.3.rest_2_ = bf16[256,128]{1,0:T(8,128)(2,1)S(1)} custom-call(f32[512,128]{1,0:T(8,128)S(1)} %get-tuple-element.92.d_updated, bf16[512,512]{1,0:T(8,128)(2,1)S(1)} %get-tuple-element.93.d_gate, bf16[512,512]{1,0:T(8,128)(2,1)S(1)} %get-tuple-element.94.d_up, f32[256,128]{1,0:T(8,128)S(1)} %get-tuple-element.97.normed, ...), custom_call_target="tpu_custom_call" | custom-call | flops 67108864 | bytes 524288 | tf_op jit(solution)/shard_map/d_inputs/pallas_call | solution.py:426
  7.8 0.4 %d_inputs.2.refs_0_ = bf16[256,128]{1,0:T(8,128)(2,1)S(1)} custom-call(f32[512,128]{1,0:T(8,128)S(1)} %get-tuple-element.92.d_updated, bf16[512,512]{1,0:T(8,128)(2,1)S(1)} %get-tuple-element.93.d_gate, bf16[512,512]{1,0:T(8,128)(2,1)S(1)} %get-tuple-element.94.d_up, f32[256,128]{1,0:T(8,128)S(1)} %get-tuple-element.95.normed, ...), custom_call_target="tpu_custom_call" | custom-call | flops 67108864 | bytes 524288 | tf_op jit(solution)/shard_map/d_inputs/pallas_call | solution.py:426
  8.2 0.4 %collective-permute-done.3.rest_1_ = bf16[4,208,128]{2,1,0:T(8,128)(2,1)S(1)} collective-permute-done((bf16[4,208,128]{2,1,0:T(8,128)(2,1)S(1)}, bf16[4,208,128]{2,1,0:T(8,128)(2,1)S(1)}, u32[]{:S(2)}, u32[]{:S(2)}) %collective-permute-start.3) | collective-permute-done | bytes 213024 | tf_op jit(solution)/shard_map/ppermute | solution.py:464
  8.6 0.1 core_sum.1
  8.6 8.0 %collective-permute-start.4 = (bf16[208,128]{1,0:T(8,128)(2,1)S(1)}, bf16[208,128]{1,0:T(8,128)(2,1)S(1)}, u32[]{:S(2)}, u32[]{:S(2)}) collective-permute-start(bf16[208,128]{1,0:T(8,128)(2,1)S(1)} %get-tuple-element.103), channel_id=1, source_target_pairs={{0,12},{4,8},{8,20},{12,16},{16,28},{20,24},{24,4},{28,0},{1,13},{... | collective-permute-start | bytes 159752 | tf_op jit(solution)/shard_map/ppermute | solution.py:477
  16.6 1.4 %collective-permute-start.5 = (bf16[208,128]{1,0:T(8,128)(2,1)S(1)}, bf16[208,128]{1,0:T(8,128)(2,1)S(1)}, u32[]{:S(2)}, u32[]{:S(2)}) collective-permute-start(bf16[208,128]{1,0:T(8,128)(2,1)S(1)} %get-tuple-element.104), channel_id=1, source_target_pairs={{0,20},{4,16},{8,28},{12,24},{16,4},{20,0},{24,12},{28,8},{1,21},{... | collective-permute-start | bytes 159752 | tf_op jit(solution)/shard_map/ppermute | solution.py:477
  18.0 0.1 collective-permute-start.6
  18.1 0.2 collective-permute-start.7
  18.3 0.4 %collective-permute-start.8 = (bf16[128,128]{1,0:T(8,128)(2,1)S(1)}, bf16[128,128]{1,0:T(8,128)(2,1)S(1)}, u32[]{:S(2)}, u32[]{:S(2)}) collective-permute-start(bf16[128,128]{1,0:T(8,128)(2,1)S(1)} %get-tuple-element.108), channel_id=1, source_target_pairs={{0,4},{4,0},{8,12},{12,8},{16,20},{20,16},{24,28},{28,24},{1,5},{5... | collective-permute-start | bytes 98312 | tf_op jit(solution)/shard_map/ppermute | solution.py:439
  18.6 0.7 %collective-permute-done.7.refs_1_ = bf16[128,128]{1,0:T(8,128)(2,1)S(1)} collective-permute-done((bf16[128,128]{1,0:T(8,128)(2,1)S(1)}, bf16[128,128]{1,0:T(8,128)(2,1)S(1)}, u32[]{:S(2)}, u32[]{:S(2)}) %collective-permute-start.7) | collective-permute-done | bytes 32800 | tf_op jit(solution)/shard_map/ppermute | solution.py:439
  19.3 0.2 collective-permute-done.8.refs_2_
  19.5 0.0 collective-permute-done.4.rest_1_
  19.5 1.2 %collective-permute-done.5.rest_2_ = bf16[208,128]{1,0:T(8,128)(2,1)S(1)} collective-permute-done((bf16[208,128]{1,0:T(8,128)(2,1)S(1)}, bf16[208,128]{1,0:T(8,128)(2,1)S(1)}, u32[]{:S(2)}, u32[]{:S(2)}) %collective-permute-start.5) | collective-permute-done | bytes 53280 | tf_op jit(solution)/shard_map/ppermute | solution.py:477
  20.7 1.1 %collective-permute-done.6.rest_3_ = bf16[208,128]{1,0:T(8,128)(2,1)S(1)} collective-permute-done((bf16[208,128]{1,0:T(8,128)(2,1)S(1)}, bf16[208,128]{1,0:T(8,128)(2,1)S(1)}, u32[]{:S(2)}, u32[]{:S(2)}) %collective-permute-start.6) | collective-permute-done | bytes 53280 | tf_op jit(solution)/shard_map/ppermute | solution.py:477
  21.8 0.1 chip_sum.1
  21.9 1.0 %collective-permute-start.9 = (bf16[64,128]{1,0:T(8,128)(2,1)S(1)}, bf16[64,128]{1,0:T(8,128)(2,1)S(1)}, u32[]{:S(2)}, u32[]{:S(2)}) collective-permute-start(bf16[64,128]{1,0:T(8,128)(2,1)S(1)} %get-tuple-element.114), channel_id=1, source_target_pairs={{0,2},{1,3},{2,0},{3,1},{4,6},{5,7},{6,4},{7,5},{8,10},{9,11},{10,... | collective-permute-start | bytes 49160 | tf_op jit(solution)/shard_map/ppermute | solution.py:491
  22.9 2.2 %collective-permute-start.10 = (bf16[64,128]{1,0:T(8,128)(2,1)S(1)}, bf16[64,128]{1,0:T(8,128)(2,1)S(1)}, u32[]{:S(2)}, u32[]{:S(2)}) collective-permute-start(bf16[64,128]{1,0:T(8,128)(2,1)S(1)} %get-tuple-element.115), channel_id=1, source_target_pairs={{0,3},{1,2},{2,1},{3,0},{4,7},{5,6},{6,5},{7,4},{8,11},{9,10},{10,... | collective-permute-start | bytes 49160 | tf_op jit(solution)/shard_map/ppermute | solution.py:491
  25.1 0.5 %collective-permute-start.11 = (bf16[64,128]{1,0:T(8,128)(2,1)S(1)}, bf16[64,128]{1,0:T(8,128)(2,1)S(1)}, u32[]{:S(2)}, u32[]{:S(2)}) collective-permute-start(bf16[64,128]{1,0:T(8,128)(2,1)S(1)} %get-tuple-element.116), channel_id=1, source_target_pairs={{0,1},{1,0},{2,3},{3,2},{4,5},{5,4},{6,7},{7,6},{8,9},{9,8},{10,11... | collective-permute-start | bytes 49160 | tf_op jit(solution)/shard_map/ppermute | solution.py:491
  25.6 0.7 %place.1 = bf16[16,2,16,128]{3,2,1,0:T(8,128)(2,1)} custom-call(bf16[256,128]{1,0:T(8,128)(2,1)S(1)} %d_inputs.2.refs_0_, bf16[128,128]{1,0:T(8,128)(2,1)S(1)} %collective-permute-done.7.refs_1_, bf16[128,128]{1,0:T(8,128)(2,1)S(1)} %collective-permute-done.8.refs_2_), custom_call_target="tpu_custom_call" | custom-call | tf_op jit(solution)/shard_map/place/pallas_call | solution.py:443
  26.3 0.3 %collective-permute-done.9.rest_1_ = bf16[64,128]{1,0:T(8,128)(2,1)S(1)} collective-permute-done((bf16[64,128]{1,0:T(8,128)(2,1)S(1)}, bf16[64,128]{1,0:T(8,128)(2,1)S(1)}, u32[]{:S(2)}, u32[]{:S(2)}) %collective-permute-start.9) | collective-permute-done | bytes 16416 | tf_op jit(solution)/shard_map/ppermute | solution.py:491
  26.6 1.8 %collective-permute-done.10.rest_2_ = bf16[64,128]{1,0:T(8,128)(2,1)S(1)} collective-permute-done((bf16[64,128]{1,0:T(8,128)(2,1)S(1)}, bf16[64,128]{1,0:T(8,128)(2,1)S(1)}, u32[]{:S(2)}, u32[]{:S(2)}) %collective-permute-start.10) | collective-permute-done | bytes 16416 | tf_op jit(solution)/shard_map/ppermute | solution.py:491
  28.4 0.4 %collective-permute-done.11.rest_3_ = bf16[64,128]{1,0:T(8,128)(2,1)S(1)} collective-permute-done((bf16[64,128]{1,0:T(8,128)(2,1)S(1)}, bf16[64,128]{1,0:T(8,128)(2,1)S(1)}, u32[]{:S(2)}, u32[]{:S(2)}) %collective-permute-start.11) | collective-permute-done | bytes 16416 | tf_op jit(solution)/shard_map/ppermute | solution.py:491
  28.9 0.7 %col_sum.1 = (f32[16,128]{1,0:T(8,128)}, f32[16,128]{1,0:T(8,128)}, f32[32,64]{1,0:T(8,128)}, f32[16,16]{1,0:T(8,128)}) custom-call(bf16[64,128]{1,0:T(8,128)(2,1)S(1)} %get-tuple-element.121.rest_0_, bf16[64,128]{1,0:T(8,128)(2,1)S(1)} %collective-permute-done.9.rest_1_, bf16[64,128]{1,0:T(8,128)(2,1)S(1)} %collective-permute-done.10.rest_2_, ...), custom_call_target="tpu_custom_call" | custom-call | tf_op jit(solution)/shard_map/col_sum/pallas_call | solution.py:493
  (1 shorter events, 0.0 us)
Async XLA Ops:
  3.0 2.9 %collective-permute-start.2 = (bf16[2,128,128]{2,1,0:T(8,128)(2,1)S(1)}, bf16[2,128,128]{2,1,0:T(8,128)(2,1)S(1)}, u32[]{:S(2)}, u32[]{:S(2)}) collective-permute-start(bf16[2,128,128]{2,1,0:T(8,128)(2,1)S(1)} %get-tuple-element.89), channel_id=1, source_target_pairs={{0,4},{1,12},{2,20},{3,28},{4,0},{5,8},{6,16},{7,24},{8,5},{9,13},... | collective-permute-start | bytes 196616 | tf_op jit(solution)/shard_map/ppermute | solution.py:365
  3.5 1.4 %collective-permute-start.1 = (bf16[144,128]{1,0:T(8,128)(2,1)S(1)}, bf16[144,128]{1,0:T(8,128)(2,1)S(1)}, u32[]{:S(2)}, u32[]{:S(2)}) collective-permute-start(bf16[144,128]{1,0:T(8,128)(2,1)S(1)} %get-tuple-element.81), channel_id=1, source_target_pairs={{0,4},{4,0},{8,12},{12,8},{16,20},{20,16},{24,28},{28,24},{1,5},{5... | collective-permute-start | bytes 110600 | tf_op jit(solution)/shard_map/ppermute | solution.py:374
  3.6 1.3 %collective-permute-start = (bf16[128,128]{1,0:T(8,128)(2,1)S(1)}, bf16[128,128]{1,0:T(8,128)(2,1)S(1)}, u32[]{:S(2)}, u32[]{:S(2)}) collective-permute-start(bf16[128,128]{1,0:T(8,128)(2,1)S(1)} %get-tuple-element.80), channel_id=1, source_target_pairs={{0,4},{4,0},{8,12},{12,8},{16,20},{20,16},{24,28},{28,24},{1,5},{5... | collective-permute-start | bytes 98312 | tf_op jit(solution)/shard_map/ppermute | solution.py:374
  7.0 1.5 %collective-permute-start.3 = (bf16[4,208,128]{2,1,0:T(8,128)(2,1)S(1)}, bf16[4,208,128]{2,1,0:T(8,128)(2,1)S(1)}, u32[]{:S(2)}, u32[]{:S(2)}) collective-permute-start(bf16[4,208,128]{2,1,0:T(8,128)(2,1)S(1)} %get-tuple-element.91), channel_id=1, source_target_pairs={{0,4},{4,0},{8,12},{12,8},{16,20},{20,16},{24,28},{28,24},{1,5},{5... | collective-permute-start | bytes 638984 | tf_op jit(solution)/shard_map/ppermute | solution.py:464
  8.6 10.9 %collective-permute-start.4 = (bf16[208,128]{1,0:T(8,128)(2,1)S(1)}, bf16[208,128]{1,0:T(8,128)(2,1)S(1)}, u32[]{:S(2)}, u32[]{:S(2)}) collective-permute-start(bf16[208,128]{1,0:T(8,128)(2,1)S(1)} %get-tuple-element.103), channel_id=1, source_target_pairs={{0,12},{4,8},{8,20},{12,16},{16,28},{20,24},{24,4},{28,0},{1,13},{... | collective-permute-start | bytes 159752 | tf_op jit(solution)/shard_map/ppermute | solution.py:477
  16.6 4.1 %collective-permute-start.5 = (bf16[208,128]{1,0:T(8,128)(2,1)S(1)}, bf16[208,128]{1,0:T(8,128)(2,1)S(1)}, u32[]{:S(2)}, u32[]{:S(2)}) collective-permute-start(bf16[208,128]{1,0:T(8,128)(2,1)S(1)} %get-tuple-element.104), channel_id=1, source_target_pairs={{0,20},{4,16},{8,28},{12,24},{16,4},{20,0},{24,12},{28,8},{1,21},{... | collective-permute-start | bytes 159752 | tf_op jit(solution)/shard_map/ppermute | solution.py:477
  18.0 3.8 %collective-permute-start.6 = (bf16[208,128]{1,0:T(8,128)(2,1)S(1)}, bf16[208,128]{1,0:T(8,128)(2,1)S(1)}, u32[]{:S(2)}, u32[]{:S(2)}) collective-permute-start(bf16[208,128]{1,0:T(8,128)(2,1)S(1)} %get-tuple-element.105), channel_id=1, source_target_pairs={{0,28},{4,24},{8,4},{12,0},{16,12},{20,8},{24,20},{28,16},{1,29},{... | collective-permute-start | bytes 159752 | tf_op jit(solution)/shard_map/ppermute | solution.py:477
  18.1 1.2 %collective-permute-start.7 = (bf16[128,128]{1,0:T(8,128)(2,1)S(1)}, bf16[128,128]{1,0:T(8,128)(2,1)S(1)}, u32[]{:S(2)}, u32[]{:S(2)}) collective-permute-start(bf16[128,128]{1,0:T(8,128)(2,1)S(1)} %get-tuple-element.107), channel_id=1, source_target_pairs={{0,4},{4,0},{8,12},{12,8},{16,20},{20,16},{24,28},{28,24},{1,5},{5... | collective-permute-start | bytes 98312 | tf_op jit(solution)/shard_map/ppermute | solution.py:439
  18.3 1.2 %collective-permute-start.8 = (bf16[128,128]{1,0:T(8,128)(2,1)S(1)}, bf16[128,128]{1,0:T(8,128)(2,1)S(1)}, u32[]{:S(2)}, u32[]{:S(2)}) collective-permute-start(bf16[128,128]{1,0:T(8,128)(2,1)S(1)} %get-tuple-element.108), channel_id=1, source_target_pairs={{0,4},{4,0},{8,12},{12,8},{16,20},{20,16},{24,28},{28,24},{1,5},{5... | collective-permute-start | bytes 98312 | tf_op jit(solution)/shard_map/ppermute | solution.py:439
  21.9 4.7 %collective-permute-start.9 = (bf16[64,128]{1,0:T(8,128)(2,1)S(1)}, bf16[64,128]{1,0:T(8,128)(2,1)S(1)}, u32[]{:S(2)}, u32[]{:S(2)}) collective-permute-start(bf16[64,128]{1,0:T(8,128)(2,1)S(1)} %get-tuple-element.114), channel_id=1, source_target_pairs={{0,2},{1,3},{2,0},{3,1},{4,6},{5,7},{6,4},{7,5},{8,10},{9,11},{10,... | collective-permute-start | bytes 49160 | tf_op jit(solution)/shard_map/ppermute | solution.py:491
  22.9 5.5 %collective-permute-start.10 = (bf16[64,128]{1,0:T(8,128)(2,1)S(1)}, bf16[64,128]{1,0:T(8,128)(2,1)S(1)}, u32[]{:S(2)}, u32[]{:S(2)}) collective-permute-start(bf16[64,128]{1,0:T(8,128)(2,1)S(1)} %get-tuple-element.115), channel_id=1, source_target_pairs={{0,3},{1,2},{2,1},{3,0},{4,7},{5,6},{6,5},{7,4},{8,11},{9,10},{10,... | collective-permute-start | bytes 49160 | tf_op jit(solution)/shard_map/ppermute | solution.py:491
  25.1 3.7 %collective-permute-start.11 = (bf16[64,128]{1,0:T(8,128)(2,1)S(1)}, bf16[64,128]{1,0:T(8,128)(2,1)S(1)}, u32[]{:S(2)}, u32[]{:S(2)}) collective-permute-start(bf16[64,128]{1,0:T(8,128)(2,1)S(1)} %get-tuple-element.116), channel_id=1, source_target_pairs={{0,1},{1,0},{2,3},{3,2},{4,5},{5,4},{6,7},{7,6},{8,9},{9,8},{10,11... | collective-permute-start | bytes 49160 | tf_op jit(solution)/shard_map/ppermute | solution.py:491

commit v11 on v9

--- a/solution.py
+++ b/solution.py
@@ -47,6 +47,10 @@
     if n & (n - 1) == 0:
         return s ^ p
     return (s + p) % n if isinstance(s, int) else lax.rem(s + p, n)
+
+
+def crossed(k, q):
+    return partner(k, 1, q) if q > 1 else k
 
 
 def following(s, p, n):
@@ -219,24 +223,41 @@
     nrow, ncol = packed
     groups = nrow // q
     lanes, part, tall = units // ncol, width // nrow, units // nrow
-    deep = width // q
+    narrow = width // ncol
+    fold = lanes // tall
+    short = narrow // fold
     for k in range(q):
         for a in range(groups):
             r = a * q + k
-            at = 0
-            for term in (gate_term, up_term):
-                for c in range(ncol):
+            for c in range(ncol):
+                for n, term in enumerate((gate_term, up_term)):
                     block = term[r * part : (r + 1) * part, c * lanes : (c + 1) * lanes]
-                    slots[k, a, at : at + part] = block.astype(bf16)
-                    at += part
-            pieces = [out_term[u * deep : (u + 1) * deep, r * tall : (r + 1) * tall] for u in range(q)]
-            slots[k, a, at : at + deep] = jnp.concatenate(pieces, axis=1).astype(bf16)
-            at += deep
+                    slots[k, a, (n * ncol + c) * part : (n * ncol + c + 1) * part] = block.astype(bf16)
+                at = 2 * ncol * part + c * short
+                block = out_term[c * narrow : (c + 1) * narrow, r * tall : (r + 1) * tall]
+                block = jnp.concatenate([block[v * short : (v + 1) * short] for v in range(fold)], axis=1)
+                slots[k, a, at : at + short] = block.astype(bf16)
+            at = 2 * ncol * part + ncol * short
             block = head_term[r * part : (r + 1) * part, :]
             block = jnp.concatenate([block, jnp.zeros((part, lanes - bins), f32)], axis=1)
             slots[k, a, at : at + part] = block.astype(bf16)
+    mine, level = lax.axis_index("row") // q, lax.axis_index("col")
+    at = 2 * ncol * part + ncol * short
+    lane = lax.broadcasted_iota(jnp.int32, (part, lanes), 1)
+    here = (lane >= level * (bins // ncol)) & (lane < (level + 1) * (bins // ncol))
     for n in range(q):
-        hot[n][...] = slots[partner(own, n, q)]
+        core = partner(own, n, q)
+        for a in range(groups):
+            same = jnp.where(mine == a, crossed(core, q), core)
+            other = jnp.where(mine == a, core, crossed(core, q))
+            for c in range(ncol):
+                k = jnp.where(level == c, other, same)
+                for m in (c, ncol + c):
+                    hot[n][a, m * part : (m + 1) * part] = slots[k, a, m * part : (m + 1) * part]
+                row = slice(2 * ncol * part + c * short, 2 * ncol * part + (c + 1) * short)
+                hot[n][a, row] = slots[k, a, row]
+            head = jnp.where(here, slots[other, a, at : at + part].astype(f32), slots[same, a, at : at + part].astype(f32))
+            hot[n][a, at : at + part] = head.astype(bf16)
 
 
 def input_kernel(p, d_updated, d_gate, d_up, normed, scale, w_gate, w_up, result):
@@ -279,23 +300,16 @@
 
 def chip_sum_kernel(q, groups, ncol, shapes, *rest):
     terms, hot, slots = rest[:groups], rest[groups:-1], rest[-1]
-    part, lanes, deep, tall, few = shapes
+    part, lanes, short, tall, few = shapes
     total = terms[0][...].astype(f32)
     for term in terms[1:]:
         total = total + term[...].astype(f32)
     at = 2 * ncol * part
-    out = total[at : at + deep]
-    head = total[at + deep : at + deep + part]
-    narrow = deep * q // ncol
-    fold = lanes // tall
-    short = narrow // fold
+    head = total[at + ncol * short : at + ncol * short + part]
     for c in range(ncol):
         slots[c, 0:part] = total[c * part : (c + 1) * part].astype(bf16)
         slots[c, part : 2 * part] = total[(ncol + c) * part : (ncol + c + 1) * part].astype(bf16)
-        u, top = (c * narrow) // deep, (c * narrow) % deep
-        block = out[top : top + narrow, u * tall : (u + 1) * tall]
-        block = jnp.concatenate([block[v * short : (v + 1) * short] for v in range(fold)], axis=1)
-        slots[c, 2 * part : 2 * part + short] = block.astype(bf16)
+        slots[c, 2 * part : 2 * part + short] = total[at + c * short : at + (c + 1) * short].astype(bf16)
         piece = jnp.concatenate([head[:, c * few : (c + 1) * few], jnp.zeros((part, lanes - few), f32)], axis=1)
         slots[c, 2 * part + short : 3 * part + short] = piece.astype(bf16)
     for p in range(ncol):
@@ -401,12 +415,10 @@
         )
 
     part, tall, few = width // nrow, units // nrow, bins // ncol
-    lanes, deep = units // ncol, width // q
-    fits = (
-        part % 16 == 0 and lanes == 128 and tall * q == lanes and bins <= lanes and deep % (width // ncol) == 0
-        and (width // ncol * tall // lanes) % 16 == 0
-    )
-    height = 2 * ncol * part + deep + part
+    lanes = units // ncol
+    short = width // ncol * tall // lanes
+    fits = part % 16 == 0 and lanes == 128 and lanes % tall == 0 and bins <= lanes and short % 16 == 0
+    height = 2 * ncol * part + ncol * short + part
     if fits:
         hot_shapes = [shaped((groups, height, lanes), bf16)] * q
         scratch = [pltpu.VMEM((q, groups, height, lanes), bf16)]
@@ -477,21 +489,26 @@
     hot, d_blocks = hot[:groups], d_blocks[:1] + list(hot[groups:])
     terms = [hot[0]]
     for p in range(1, groups):
-        terms.append(lax.ppermute(hot[p], "row", [(s, following(s // q, p, groups) * q + s % q) for s in range(nrow)]))
+        terms.append(lax.ppermute(hot[p], "row", [(s, following(s // q, p, groups) * q + crossed(s % q, q)) for s in range(nrow)]))
     terms, d_blocks = lax.optimization_barrier((terms, returned(d_blocks)))
-    short = 3 * part + width // ncol * tall // lanes
+    low = 3 * part + short
     hot = pl.pallas_call(
-        functools.partial(chip_sum_kernel, q, groups, ncol, (part, lanes, deep, tall, few)),
-        out_shape=[shaped((short, lanes), bf16)] * ncol,
+        functools.partial(chip_sum_kernel, q, groups, ncol, (part, lanes, short, tall, few)),
+        out_shape=[shaped((low, lanes), bf16)] * ncol,
         in_specs=[VMEM] * groups,
         out_specs=[VMEM] * ncol,
-        scratch_shapes=[pltpu.VMEM((ncol, short, lanes), bf16)],
+        scratch_shapes=[pltpu.VMEM((ncol, low, lanes), bf16)],
         compiler_params=PARAMS,
         name="chip_sum",
     )(*terms)
     terms = [hot[0]]
     for p in sorted(range(1, ncol), key=lambda p: (p != ncol // 2, -p)):
-        terms.append(lax.ppermute(hot[p], "col", [(s, partner(s, p, ncol)) for s in range(ncol)]))
+        pairs = [
+            (r * ncol + c, (r - r % q + crossed(r % q, q)) * ncol + partner(c, p, ncol))
+            for r in range(nrow)
+            for c in range(ncol)
+        ]
+        terms.append(lax.ppermute(hot[p], ("row", "col"), pairs))
     *terms, d_pair = lax.optimization_barrier((*terms, placed(d_blocks)))
     gate, up, out, head = pl.pallas_call(
         functools.partial(col_sum_kernel, (part, lanes, tall, few), factor),

time: 29.8 us -> 28.7 us (0.963)
  starting transfers between devices: 15 us -> 14.3 us
  waiting for transfers between devices: 6.32 us -> 5.9 us
    ppermute x6, starting transfers between devices: 13.1 us -> 12.4 us  [the longest x3 9.26 us: body(): lax.ppermute(hot[p], 'row', [(s, following(s // q, p, groups) * q + cross...]
    ppermute x6, waiting for transfers between devices: 5.05 us -> 4.63 us  [the longest x3 2.42 us: body(): lax.ppermute(hot[p], 'row', [(s, following(s // q, p, groups) * q + cross...]
where the time goes in v11:
time: 28.7 us; the launch traced here: 28.6 us
  starting transfers between devices  14.3 us (50%)
  Pallas kernels  7.58 us (26%)
  waiting for transfers between devices  5.9 us (21%)
  between operations  0.71 us (2%)
    ppermute x3, starting transfers between devices, body(): lax.ppermute(hot[p], 'row', [(s, following(s // q, p, groups) * q + cross...  9.26 us
    ppermute x3, starting transfers between devices, body(): terms.append(lax.ppermute(hot[p], ('row', 'col'), pairs))  3.18 us
    ppermute x3, waiting for transfers between devices, body(): lax.ppermute(hot[p], 'row', [(s, following(s // q, p, groups) * q + cross...  2.42 us
    pallas_call x1, Pallas kernels, body(): pl.pallas_call(functools.partial(forward_kernel, q), out_shape=[shaped((q...  2.31 us
    ppermute x3, waiting for transfers between devices, body(): terms.append(lax.ppermute(hot[p], ('row', 'col'), pairs))  2.21 us
    pallas_call x2, Pallas kernels, body(): pl.pallas_call(functools.partial(prepare_kernel, q, p), out_shape=[shaped...  1.77 us
    pallas_call x1, Pallas kernels, body(): pl.pallas_call(functools.partial(backward_kernel, q, (nrow, ncol) if fits...  1.23 us
    ppermute x2, waiting for transfers between devices, returned(): lax.ppermute(x, 'row', core_pairs(nrow, q, n // 2 + 1))  0.86 us
  transfers between devices with their start and end apart: 12, of which 8 were waited for; matrix products, arithmetic and copies ran while one was open for 0% of the time, Pallas kernels for 11%

profile of v11, /device:TPU:0, one launch (start us, length us, event | category | flops | bytes accessed | tf_op | source)
XLA Modules:
  0.0 28.6 jit_solution(14489994899360139455)
XLA Ops:
  0.6 2.3 %forward.1 = (bf16[2,256,128]{2,1,0:T(8,128)(2,1)S(1)}, bf16[128,512]{1,0:T(8,128)(2,1)S(1)}, bf16[128,512]{1,0:T(8,128)(2,1)S(1)}, bf16[512,128]{1,0:T(8,128)(2...) custom-call(bf16[16,32,128]{2,1,0:T(8,128)(2,1)} %refs_0_.1, ...), custom_call_target="tpu_custom_call" | custom-call | tf_op jit(solution)/shard_map/forward/pallas_call | solution.py:360
  3.0 0.5 %collective-permute-start.2 = (bf16[2,128,128]{2,1,0:T(8,128)(2,1)S(1)}, bf16[2,128,128]{2,1,0:T(8,128)(2,1)S(1)}, u32[]{:S(2)}, u32[]{:S(2)}) collective-permute-start(bf16[2,128,128]{2,1,0:T(8,128)(2,1)S(1)} %get-tuple-element.89.refs_17_), channel_id=1, source_target_pairs={{0,4},{1,8},{2,16},{3,24},{4,0},{5,12},{6,20},{7,28},{8,1},{9,13},... | collective-permute-start | bytes 196616 | tf_op jit(solution)/shard_map/ppermute | solution.py:382
  3.5 0.1 collective-permute-start.1
  3.6 0.4 %collective-permute-start = (bf16[128,128]{1,0:T(8,128)(2,1)S(1)}, bf16[128,128]{1,0:T(8,128)(2,1)S(1)}, u32[]{:S(2)}, u32[]{:S(2)}) collective-permute-start(bf16[128,128]{1,0:T(8,128)(2,1)S(1)} %get-tuple-element.80), channel_id=1, source_target_pairs={{0,4},{4,0},{8,12},{12,8},{16,20},{20,16},{24,28},{28,24},{1,5},{5... | collective-permute-start | bytes 98312 | tf_op jit(solution)/shard_map/ppermute | solution.py:391
  4.0 0.9 %prepare.2 = (bf16[128,256]{1,0:T(8,128)(2,1)S(1)}, bf16[128,256]{1,0:T(8,128)(2,1)S(1)}, bf16[256,512]{1,0:T(8,128)(2,1)S(1)}, f32[256,512]{1,0:T(8,128)S(1)}, ...) custom-call(bf16[2,256,128]{2,1,0:T(8,128)(2,1)S(1)} %get-tuple-elem, ...), custom_call_target="tpu_custom_call" | custom-call | flops 100663296 | bytes 1048576 | tf_op jit(solution)/shard_map/prepare/pallas_call | solution.py:396
  4.9 0.0 collective-permute-done.refs_0_
  4.9 0.0 collective-permute-done.1.refs_1_
  4.9 0.9 %prepare.3 = (bf16[128,256]{1,0:T(8,128)(2,1)S(1)}, bf16[128,256]{1,0:T(8,128)(2,1)S(1)}, bf16[256,512]{1,0:T(8,128)(2,1)S(1)}, f32[256,512]{1,0:T(8,128)S(1)}, ...) custom-call(bf16[128,128]{1,0:T(8,128)(2,1)S(1)} %collective-permute, ...), custom_call_target="tpu_custom_call" | custom-call | tf_op jit(solution)/shard_map/prepare/pallas_call | solution.py:396
  5.8 0.0 collective-permute-done.2.refs_16_
  5.8 1.2 %backward.1 = (f32[512,128]{1,0:T(8,128)S(1)}, bf16[512,512]{1,0:T(8,128)(2,1)S(1)}, bf16[512,512]{1,0:T(8,128)(2,1)S(1)}, bf16[4,208,128]{2,1,0:T(8,128)(2,1)S(1)}, bf16[4,208,128]{2,1,0:T(8,128)(2,1)S(1)}) custom-call(bf16[128,256]{1,0:T(8,128)(2,1)S(1)} %get-tuple-element.73.refs_0_, bf16[128,256]{1,0:T(8,128)(2,1)S(1)} %get-tuple-element.74.refs_1_, ...), custom_call_target="tpu_custom_call" | custom-call | flops 268435456 | bytes 1048576 | tf_op jit(solution)/shard_map/backward/pallas_call | solution.py:428
  7.1 0.4 %collective-permute-start.3 = (bf16[4,208,128]{2,1,0:T(8,128)(2,1)S(1)}, bf16[4,208,128]{2,1,0:T(8,128)(2,1)S(1)}, u32[]{:S(2)}, u32[]{:S(2)}) collective-permute-start(bf16[4,208,128]{2,1,0:T(8,128)(2,1)S(1)} %get-tuple-element.91), channel_id=1, source_target_pairs={{0,4},{4,0},{8,12},{12,8},{16,20},{20,16},{24,28},{28,24},{1,5},{5... | collective-permute-start | bytes 638984 | tf_op jit(solution)/shard_map/ppermute | solution.py:479
  7.4 0.4 %d_inputs.3.rest_2_ = bf16[256,128]{1,0:T(8,128)(2,1)S(1)} custom-call(f32[512,128]{1,0:T(8,128)S(1)} %get-tuple-element.92.d_updated, bf16[512,512]{1,0:T(8,128)(2,1)S(1)} %get-tuple-element.93.d_gate, bf16[512,512]{1,0:T(8,128)(2,1)S(1)} %get-tuple-element.94.d_up, f32[256,128]{1,0:T(8,128)S(1)} %get-tuple-element.97.normed, ...), custom_call_target="tpu_custom_call" | custom-call | flops 67108864 | bytes 524288 | tf_op jit(solution)/shard_map/d_inputs/pallas_call | solution.py:441
  7.8 0.4 %d_inputs.2.refs_0_ = bf16[256,128]{1,0:T(8,128)(2,1)S(1)} custom-call(f32[512,128]{1,0:T(8,128)S(1)} %get-tuple-element.92.d_updated, bf16[512,512]{1,0:T(8,128)(2,1)S(1)} %get-tuple-element.93.d_gate, bf16[512,512]{1,0:T(8,128)(2,1)S(1)} %get-tuple-element.94.d_up, f32[256,128]{1,0:T(8,128)S(1)} %get-tuple-element.95.normed, ...), custom_call_target="tpu_custom_call" | custom-call | flops 67108864 | bytes 524288 | tf_op jit(solution)/shard_map/d_inputs/pallas_call | solution.py:441
  8.2 0.4 %collective-permute-done.3.rest_1_ = bf16[4,208,128]{2,1,0:T(8,128)(2,1)S(1)} collective-permute-done((bf16[4,208,128]{2,1,0:T(8,128)(2,1)S(1)}, bf16[4,208,128]{2,1,0:T(8,128)(2,1)S(1)}, u32[]{:S(2)}, u32[]{:S(2)}) %collective-permute-start.3) | collective-permute-done | bytes 213024 | tf_op jit(solution)/shard_map/ppermute | solution.py:479
  8.6 0.1 core_sum.1
  8.7 7.0 %collective-permute-start.4 = (bf16[208,128]{1,0:T(8,128)(2,1)S(1)}, bf16[208,128]{1,0:T(8,128)(2,1)S(1)}, u32[]{:S(2)}, u32[]{:S(2)}) collective-permute-start(bf16[208,128]{1,0:T(8,128)(2,1)S(1)} %get-tuple-element.103), channel_id=1, source_target_pairs={{0,12},{4,8},{8,20},{12,16},{16,28},{20,24},{24,4},{28,0},{1,13},{... | collective-permute-start | bytes 159752 | tf_op jit(solution)/shard_map/ppermute | solution.py:492
  15.6 2.3 %collective-permute-start.5 = (bf16[208,128]{1,0:T(8,128)(2,1)S(1)}, bf16[208,128]{1,0:T(8,128)(2,1)S(1)}, u32[]{:S(2)}, u32[]{:S(2)}) collective-permute-start(bf16[208,128]{1,0:T(8,128)(2,1)S(1)} %get-tuple-element.104), channel_id=1, source_target_pairs={{0,20},{4,16},{8,28},{12,24},{16,4},{20,0},{24,12},{28,8},{1,21},{... | collective-permute-start | bytes 159752 | tf_op jit(solution)/shard_map/ppermute | solution.py:492
  17.9 0.0 collective-permute-start.6
  17.9 0.2 collective-permute-start.7
  18.1 0.4 %collective-permute-start.8 = (bf16[128,128]{1,0:T(8,128)(2,1)S(1)}, bf16[128,128]{1,0:T(8,128)(2,1)S(1)}, u32[]{:S(2)}, u32[]{:S(2)}) collective-permute-start(bf16[128,128]{1,0:T(8,128)(2,1)S(1)} %get-tuple-element.108), channel_id=1, source_target_pairs={{0,4},{4,0},{8,12},{12,8},{16,20},{20,16},{24,28},{28,24},{1,5},{5... | collective-permute-start | bytes 98312 | tf_op jit(solution)/shard_map/ppermute | solution.py:454
  18.4 0.7 %collective-permute-done.7.refs_1_ = bf16[128,128]{1,0:T(8,128)(2,1)S(1)} collective-permute-done((bf16[128,128]{1,0:T(8,128)(2,1)S(1)}, bf16[128,128]{1,0:T(8,128)(2,1)S(1)}, u32[]{:S(2)}, u32[]{:S(2)}) %collective-permute-start.7) | collective-permute-done | bytes 32800 | tf_op jit(solution)/shard_map/ppermute | solution.py:454
  19.1 0.2 collective-permute-done.8.refs_2_
  19.3 0.0 collective-permute-done.4.rest_1_
  19.3 1.6 %collective-permute-done.5.rest_2_ = bf16[208,128]{1,0:T(8,128)(2,1)S(1)} collective-permute-done((bf16[208,128]{1,0:T(8,128)(2,1)S(1)}, bf16[208,128]{1,0:T(8,128)(2,1)S(1)}, u32[]{:S(2)}, u32[]{:S(2)}) %collective-permute-start.5) | collective-permute-done | bytes 53280 | tf_op jit(solution)/shard_map/ppermute | solution.py:492
  20.9 0.8 %collective-permute-done.6.rest_3_ = bf16[208,128]{1,0:T(8,128)(2,1)S(1)} collective-permute-done((bf16[208,128]{1,0:T(8,128)(2,1)S(1)}, bf16[208,128]{1,0:T(8,128)(2,1)S(1)}, u32[]{:S(2)}, u32[]{:S(2)}) %collective-permute-start.6) | collective-permute-done | bytes 53280 | tf_op jit(solution)/shard_map/ppermute | solution.py:492
  21.7 0.1 chip_sum.1
  21.8 0.5 %collective-permute-start.9 = (bf16[64,128]{1,0:T(8,128)(2,1)S(1)}, bf16[64,128]{1,0:T(8,128)(2,1)S(1)}, u32[]{:S(2)}, u32[]{:S(2)}) collective-permute-start(bf16[64,128]{1,0:T(8,128)(2,1)S(1)} %get-tuple-element.114), channel_id=1, source_target_pairs={{0,6},{1,7},{2,4},{3,5},{4,2},{5,3},{6,0},{7,1},{8,14},{9,15},{10,... | collective-permute-start | bytes 49160 | tf_op jit(solution)/shard_map/ppermute | solution.py:511
  22.3 2.3 %collective-permute-start.10 = (bf16[64,128]{1,0:T(8,128)(2,1)S(1)}, bf16[64,128]{1,0:T(8,128)(2,1)S(1)}, u32[]{:S(2)}, u32[]{:S(2)}) collective-permute-start(bf16[64,128]{1,0:T(8,128)(2,1)S(1)} %get-tuple-element.115), channel_id=1, source_target_pairs={{0,7},{1,6},{2,5},{3,4},{4,3},{5,2},{6,1},{7,0},{8,15},{9,14},{10,... | collective-permute-start | bytes 49160 | tf_op jit(solution)/shard_map/ppermute | solution.py:511
  24.5 0.5 %collective-permute-start.11 = (bf16[64,128]{1,0:T(8,128)(2,1)S(1)}, bf16[64,128]{1,0:T(8,128)(2,1)S(1)}, u32[]{:S(2)}, u32[]{:S(2)}) collective-permute-start(bf16[64,128]{1,0:T(8,128)(2,1)S(1)} %get-tuple-element.116), channel_id=1, source_target_pairs={{0,5},{1,4},{2,7},{3,6},{4,1},{5,0},{6,3},{7,2},{8,13},{9,12},{10,... | collective-permute-start | bytes 49160 | tf_op jit(solution)/shard_map/ppermute | solution.py:511
  25.0 0.7 %place.1 = bf16[16,2,16,128]{3,2,1,0:T(8,128)(2,1)} custom-call(bf16[256,128]{1,0:T(8,128)(2,1)S(1)} %d_inputs.2.refs_0_, bf16[128,128]{1,0:T(8,128)(2,1)S(1)} %collective-permute-done.7.refs_1_, bf16[128,128]{1,0:T(8,128)(2,1)S(1)} %collective-permute-done.8.refs_2_), custom_call_target="tpu_custom_call" | custom-call | tf_op jit(solution)/shard_map/place/pallas_call | solution.py:458
  25.7 0.4 %collective-permute-done.9.rest_1_ = bf16[64,128]{1,0:T(8,128)(2,1)S(1)} collective-permute-done((bf16[64,128]{1,0:T(8,128)(2,1)S(1)}, bf16[64,128]{1,0:T(8,128)(2,1)S(1)}, u32[]{:S(2)}, u32[]{:S(2)}) %collective-permute-start.9) | collective-permute-done | bytes 16416 | tf_op jit(solution)/shard_map/ppermute | solution.py:511
  26.0 1.2 %collective-permute-done.10.rest_2_ = bf16[64,128]{1,0:T(8,128)(2,1)S(1)} collective-permute-done((bf16[64,128]{1,0:T(8,128)(2,1)S(1)}, bf16[64,128]{1,0:T(8,128)(2,1)S(1)}, u32[]{:S(2)}, u32[]{:S(2)}) %collective-permute-start.10) | collective-permute-done | bytes 16416 | tf_op jit(solution)/shard_map/ppermute | solution.py:511
  27.2 0.6 %collective-permute-done.11.rest_3_ = bf16[64,128]{1,0:T(8,128)(2,1)S(1)} collective-permute-done((bf16[64,128]{1,0:T(8,128)(2,1)S(1)}, bf16[64,128]{1,0:T(8,128)(2,1)S(1)}, u32[]{:S(2)}, u32[]{:S(2)}) %collective-permute-start.11) | collective-permute-done | bytes 16416 | tf_op jit(solution)/shard_map/ppermute | solution.py:511
  27.9 0.7 %col_sum.1 = (f32[16,128]{1,0:T(8,128)}, f32[16,128]{1,0:T(8,128)}, f32[32,64]{1,0:T(8,128)}, f32[16,16]{1,0:T(8,128)}) custom-call(bf16[64,128]{1,0:T(8,128)(2,1)S(1)} %get-tuple-element.121.rest_0_, bf16[64,128]{1,0:T(8,128)(2,1)S(1)} %collective-permute-done.9.rest_1_, bf16[64,128]{1,0:T(8,128)(2,1)S(1)} %collective-permute-done.10.rest_2_, ...), custom_call_target="tpu_custom_call" | custom-call | tf_op jit(solution)/shard_map/col_sum/pallas_call | solution.py:513
  (1 shorter events, 0.0 us)
Async XLA Ops:
  3.0 2.9 %collective-permute-start.2 = (bf16[2,128,128]{2,1,0:T(8,128)(2,1)S(1)}, bf16[2,128,128]{2,1,0:T(8,128)(2,1)S(1)}, u32[]{:S(2)}, u32[]{:S(2)}) collective-permute-start(bf16[2,128,128]{2,1,0:T(8,128)(2,1)S(1)} %get-tuple-element.89.refs_17_), channel_id=1, source_target_pairs={{0,4},{1,8},{2,16},{3,24},{4,0},{5,12},{6,20},{7,28},{8,1},{9,13},... | collective-permute-start | bytes 196616 | tf_op jit(solution)/shard_map/ppermute | solution.py:382
  3.5 1.4 %collective-permute-start.1 = (bf16[144,128]{1,0:T(8,128)(2,1)S(1)}, bf16[144,128]{1,0:T(8,128)(2,1)S(1)}, u32[]{:S(2)}, u32[]{:S(2)}) collective-permute-start(bf16[144,128]{1,0:T(8,128)(2,1)S(1)} %get-tuple-element.81), channel_id=1, source_target_pairs={{0,4},{4,0},{8,12},{12,8},{16,20},{20,16},{24,28},{28,24},{1,5},{5... | collective-permute-start | bytes 110600 | tf_op jit(solution)/shard_map/ppermute | solution.py:391
  3.6 1.3 %collective-permute-start = (bf16[128,128]{1,0:T(8,128)(2,1)S(1)}, bf16[128,128]{1,0:T(8,128)(2,1)S(1)}, u32[]{:S(2)}, u32[]{:S(2)}) collective-permute-start(bf16[128,128]{1,0:T(8,128)(2,1)S(1)} %get-tuple-element.80), channel_id=1, source_target_pairs={{0,4},{4,0},{8,12},{12,8},{16,20},{20,16},{24,28},{28,24},{1,5},{5... | collective-permute-start | bytes 98312 | tf_op jit(solution)/shard_map/ppermute | solution.py:391
  7.1 1.5 %collective-permute-start.3 = (bf16[4,208,128]{2,1,0:T(8,128)(2,1)S(1)}, bf16[4,208,128]{2,1,0:T(8,128)(2,1)S(1)}, u32[]{:S(2)}, u32[]{:S(2)}) collective-permute-start(bf16[4,208,128]{2,1,0:T(8,128)(2,1)S(1)} %get-tuple-element.91), channel_id=1, source_target_pairs={{0,4},{4,0},{8,12},{12,8},{16,20},{20,16},{24,28},{28,24},{1,5},{5... | collective-permute-start | bytes 638984 | tf_op jit(solution)/shard_map/ppermute | solution.py:479
  8.7 10.6 %collective-permute-start.4 = (bf16[208,128]{1,0:T(8,128)(2,1)S(1)}, bf16[208,128]{1,0:T(8,128)(2,1)S(1)}, u32[]{:S(2)}, u32[]{:S(2)}) collective-permute-start(bf16[208,128]{1,0:T(8,128)(2,1)S(1)} %get-tuple-element.103), channel_id=1, source_target_pairs={{0,12},{4,8},{8,20},{12,16},{16,28},{20,24},{24,4},{28,0},{1,13},{... | collective-permute-start | bytes 159752 | tf_op jit(solution)/shard_map/ppermute | solution.py:492
  15.6 5.2 %collective-permute-start.5 = (bf16[208,128]{1,0:T(8,128)(2,1)S(1)}, bf16[208,128]{1,0:T(8,128)(2,1)S(1)}, u32[]{:S(2)}, u32[]{:S(2)}) collective-permute-start(bf16[208,128]{1,0:T(8,128)(2,1)S(1)} %get-tuple-element.104), channel_id=1, source_target_pairs={{0,20},{4,16},{8,28},{12,24},{16,4},{20,0},{24,12},{28,8},{1,21},{... | collective-permute-start | bytes 159752 | tf_op jit(solution)/shard_map/ppermute | solution.py:492
  17.9 3.8 %collective-permute-start.6 = (bf16[208,128]{1,0:T(8,128)(2,1)S(1)}, bf16[208,128]{1,0:T(8,128)(2,1)S(1)}, u32[]{:S(2)}, u32[]{:S(2)}) collective-permute-start(bf16[208,128]{1,0:T(8,128)(2,1)S(1)} %get-tuple-element.105), channel_id=1, source_target_pairs={{0,28},{4,24},{8,4},{12,0},{16,12},{20,8},{24,20},{28,16},{1,29},{... | collective-permute-start | bytes 159752 | tf_op jit(solution)/shard_map/ppermute | solution.py:492
  17.9 1.2 %collective-permute-start.7 = (bf16[128,128]{1,0:T(8,128)(2,1)S(1)}, bf16[128,128]{1,0:T(8,128)(2,1)S(1)}, u32[]{:S(2)}, u32[]{:S(2)}) collective-permute-start(bf16[128,128]{1,0:T(8,128)(2,1)S(1)} %get-tuple-element.107), channel_id=1, source_target_pairs={{0,4},{4,0},{8,12},{12,8},{16,20},{20,16},{24,28},{28,24},{1,5},{5... | collective-permute-start | bytes 98312 | tf_op jit(solution)/shard_map/ppermute | solution.py:454
  18.1 1.2 %collective-permute-start.8 = (bf16[128,128]{1,0:T(8,128)(2,1)S(1)}, bf16[128,128]{1,0:T(8,128)(2,1)S(1)}, u32[]{:S(2)}, u32[]{:S(2)}) collective-permute-start(bf16[128,128]{1,0:T(8,128)(2,1)S(1)} %get-tuple-element.108), channel_id=1, source_target_pairs={{0,4},{4,0},{8,12},{12,8},{16,20},{20,16},{24,28},{28,24},{1,5},{5... | collective-permute-start | bytes 98312 | tf_op jit(solution)/shard_map/ppermute | solution.py:454
  21.8 4.2 %collective-permute-start.9 = (bf16[64,128]{1,0:T(8,128)(2,1)S(1)}, bf16[64,128]{1,0:T(8,128)(2,1)S(1)}, u32[]{:S(2)}, u32[]{:S(2)}) collective-permute-start(bf16[64,128]{1,0:T(8,128)(2,1)S(1)} %get-tuple-element.114), channel_id=1, source_target_pairs={{0,6},{1,7},{2,4},{3,5},{4,2},{5,3},{6,0},{7,1},{8,14},{9,15},{10,... | collective-permute-start | bytes 49160 | tf_op jit(solution)/shard_map/ppermute | solution.py:511
  22.3 5.0 %collective-permute-start.10 = (bf16[64,128]{1,0:T(8,128)(2,1)S(1)}, bf16[64,128]{1,0:T(8,128)(2,1)S(1)}, u32[]{:S(2)}, u32[]{:S(2)}) collective-permute-start(bf16[64,128]{1,0:T(8,128)(2,1)S(1)} %get-tuple-element.115), channel_id=1, source_target_pairs={{0,7},{1,6},{2,5},{3,4},{4,3},{5,2},{6,1},{7,0},{8,15},{9,14},{10,... | collective-permute-start | bytes 49160 | tf_op jit(solution)/shard_map/ppermute | solution.py:511
  24.5 3.3 %collective-permute-start.11 = (bf16[64,128]{1,0:T(8,128)(2,1)S(1)}, bf16[64,128]{1,0:T(8,128)(2,1)S(1)}, u32[]{:S(2)}, u32[]{:S(2)}) collective-permute-start(bf16[64,128]{1,0:T(8,128)(2,1)S(1)} %get-tuple-element.116), channel_id=1, source_target_pairs={{0,5},{1,4},{2,7},{3,6},{4,1},{5,0},{6,3},{7,2},{8,13},{9,12},{10,... | collective-permute-start | bytes 49160 | tf_op jit(solution)/shard_map/ppermute | solution.py:511

commit v12 on v11

--- a/solution.py
+++ b/solution.py
@@ -67,20 +67,20 @@
 
 
 def forward_kernel(q, *refs):
-    sources, (pair, w_gate, w_up, w_out, w_head, marks, sends), scratch = refs[:6], refs[6:13], refs[13:]
-    targets, halves, hidden, sems = scratch
+    sources, kept, (sends, hidden, sems) = refs[:6], refs[6:12], refs[12:]
+    pair, w_gate, w_up, w_out, w_head, _ = kept
     _, side, width = pair.shape
     edge = sources[0].shape[0]
     bins = w_head.shape[0]
-    copies = [
-        pltpu.make_async_copy(source, target, sems.at[i])
-        for i, (source, target) in enumerate(zip(sources[1:], (w_gate, w_up, w_out, w_head, targets)))
-    ]
     pieces = [
         pltpu.make_async_copy(
             sources[0].at[:, h * edge : (h + 1) * edge, :], pair.reshape(q, edge, edge, width).at[h], sems.at[5 + h]
         )
         for h in range(q)
+    ]
+    copies = [
+        pltpu.make_async_copy(source, target, sems.at[i])
+        for i, (source, target) in enumerate(zip(sources[1:], kept[1:]))
     ]
     for copy in pieces + copies:
         copy.start()
@@ -92,35 +92,35 @@
     own = lax.rem(lax.axis_index("row"), q)
     for copy in pieces:
         copy.wait()
-    flat = pair[...].reshape(q * side, width)
-    inputs = normalize(flat)[0].astype(bf16)
+    flats = [nn(swap, pair[partner(own, p, q)]) for p in range(q)]
+    inputs = [normalize(flat)[0].astype(bf16) for flat in flats]
     for copy in copies[:2]:
         copy.wait()
-    for top, tall in chunks_of(q * side, 128):
-        for at, step in chunks_of(w_gate.shape[1], 256):
-            gate = nn(inputs[top : top + tall], w_gate[:, at : at + step])
-            upper = nn(inputs[top : top + tall], w_up[:, at : at + step])
-            hidden[top : top + tall, at : at + step] = (gate * sigmoid(gate) * upper).astype(bf16)
-    for copy in copies[2:]:
-        copy.wait()
-    total = flat.astype(f32) + nn(hidden[...], w_out[...])
-    logit = nt(total.astype(bf16), w_head[...]).astype(bf16)
     packs = lane_packs(bins, side)
     deep = side // packs
-    for h in range(q):
-        piece = nn(swap, logit[h * side : (h + 1) * side])
+    for p in range(q):
+        for top, tall in chunks_of(side, 128):
+            for at, step in chunks_of(w_gate.shape[1], 256):
+                gate = nn(inputs[p][top : top + tall], w_gate[:, at : at + step])
+                upper = nn(inputs[p][top : top + tall], w_up[:, at : at + step])
+                hidden[p, top : top + tall, at : at + step] = (gate * sigmoid(gate) * upper).astype(bf16)
+        if p == 0:
+            for copy in copies[2:]:
+                copy.wait()
+        total = flats[p] + nn(hidden[p], w_out[...])
+        piece = nt(total.astype(bf16), w_head[...])
         if packs > 1:
             piece = jnp.concatenate([piece[u * deep : (u + 1) * deep] for u in range(packs)], axis=1)
-        halves[h] = piece.astype(bf16)
+        sends[p] = piece.astype(bf16)
+
+
+def lend_kernel(q, pair, targets, marks, *lent):
+    own = lax.rem(lax.axis_index("row"), q)
+    _, side, width = pair.shape
+    edge = targets.shape[0]
+    for h in range(q):
         mark = targets[:, h * edge : (h + 1) * edge].astype(f32)
         marks[h] = jnp.concatenate([mark, jnp.zeros((edge, width - edge), f32)], axis=1).astype(bf16)
-    for p in range(q):
-        sends[p] = halves[partner(own, p, q)]
-
-
-def lend_kernel(q, pair, marks, *lent):
-    own = lax.rem(lax.axis_index("row"), q)
-    side = pair.shape[1]
     for p in range(1, q):
         first, second = lent[2 * p - 2 : 2 * p]
         block = pair[partner(own, p, q)]
@@ -357,19 +357,14 @@
     piece = (side // packs, bins * packs)
 
     sources = (pair, w_gate, w_up, w_out, head_t, targets)
-    pair, w_gate, w_up, w_out, head_t, marks, sends = pl.pallas_call(
+    pair, w_gate, w_up, w_out, head_t, targets, sends = pl.pallas_call(
         functools.partial(forward_kernel, q),
         out_shape=[shaped((q, side, width), bf16)]
-        + [shaped(x.shape, bf16) for x in sources[1:5]]
-        + [shaped((q, rows, width), bf16), shaped((q, *piece), bf16)],
+        + [shaped(x.shape, x.dtype) for x in sources[1:]]
+        + [shaped((q, *piece), bf16)],
         in_specs=[HBM] * 6,
         out_specs=[VMEM] * 7,
-        scratch_shapes=[
-            pltpu.VMEM((rows, cols), jnp.int32),
-            pltpu.VMEM((q, *piece), bf16),
-            pltpu.VMEM((q * side, units), bf16),
-            pltpu.SemaphoreType.DMA((5 + q,)),
-        ],
+        scratch_shapes=[pltpu.VMEM((q, side, units), bf16), pltpu.SemaphoreType.DMA((5 + q,))],
         compiler_params=PARAMS,
         name="forward",
     )(*(pltpu.with_memory_space_constraint(x, pltpu.HBM) for x in sources))
@@ -380,14 +375,14 @@
         for c in range(ncol)
     ]
     far = lax.ppermute(sends, ("row", "col"), pairs)
-    lent = pl.pallas_call(
+    marks, *lent = pl.pallas_call(
         functools.partial(lend_kernel, q),
-        out_shape=[shaped((side // 2, width), bf16), shaped((side // 2 + rows, width), bf16)] * (q - 1),
+        out_shape=[shaped((q, rows, width), bf16)] + [shaped((side // 2, width), bf16), shaped((side // 2 + rows, width), bf16)] * (q - 1),
         in_specs=[VMEM] * 2,
-        out_specs=[VMEM] * (2 * q - 2),
+        out_specs=[VMEM] * (2 * q - 1),
         compiler_params=PARAMS,
         name="lend",
-    )(pair, marks)
+    )(pair, targets)
     borrowed = [lax.ppermute(x, "row", core_pairs(nrow, q, n // 2 + 1)) for n, x in enumerate(lent)]
     prepared = []
     for p in range(q):

time: 28.7 us -> 28.8 us (level)
  no operation moved by 1% of the time
where the time goes in v12:
time: 28.8 us; the launch traced here: 28.6 us
  starting transfers between devices  14.3 us (50%)
  Pallas kernels  7.74 us (27%)
  waiting for transfers between devices  5.91 us (21%)
  between operations  0.71 us (2%)
    ppermute x3, starting transfers between devices, body(): lax.ppermute(hot[p], 'row', [(s, following(s // q, p, groups) * q + cross...  9.2 us
    ppermute x3, starting transfers between devices, body(): terms.append(lax.ppermute(hot[p], ('row', 'col'), pairs))  3.16 us
    ppermute x3, waiting for transfers between devices, body(): lax.ppermute(hot[p], 'row', [(s, following(s // q, p, groups) * q + cross...  2.42 us
    pallas_call x1, Pallas kernels, body(): pl.pallas_call(functools.partial(forward_kernel, q), out_shape=[shaped((q...  2.4 us
    ppermute x3, waiting for transfers between devices, body(): terms.append(lax.ppermute(hot[p], ('row', 'col'), pairs))  2.22 us
    pallas_call x2, Pallas kernels, body(): pl.pallas_call(functools.partial(prepare_kernel, q, p), out_shape=[shaped...  1.77 us
    pallas_call x1, Pallas kernels, body(): pl.pallas_call(functools.partial(backward_kernel, q, (nrow, ncol) if fits...  1.23 us
    ppermute x2, waiting for transfers between devices, returned(): lax.ppermute(x, 'row', core_pairs(nrow, q, n // 2 + 1))  0.86 us
  transfers between devices with their start and end apart: 12, of which 8 were waited for; matrix products, arithmetic and copies ran while one was open for 0% of the time, Pallas kernels for 11%

profile of v12, /device:TPU:0, one launch (start us, length us, event | category | flops | bytes accessed | tf_op | source)
XLA Modules:
  0.0 28.6 jit_solution(16414662405890206376)
XLA Ops:
  0.6 2.4 %forward.1 = (bf16[2,256,128]{2,1,0:T(8,128)(2,1)S(1)}, bf16[128,512]{1,0:T(8,128)(2,1)S(1)}, bf16[128,512]{1,0:T(8,128)(2,1)S(1)}, bf16[512,128]{1,0:T(8,128)(2...) custom-call(bf16[16,32,128]{2,1,0:T(8,128)(2,1)} %refs_0_.1, ...), custom_call_target="tpu_custom_call" | custom-call | tf_op jit(solution)/shard_map/forward/pallas_call | solution.py:360
  3.0 0.5 %collective-permute-start.2 = (bf16[2,128,128]{2,1,0:T(8,128)(2,1)S(1)}, bf16[2,128,128]{2,1,0:T(8,128)(2,1)S(1)}, u32[]{:S(2)}, u32[]{:S(2)}) collective-permute-start(bf16[2,128,128]{2,1,0:T(8,128)(2,1)S(1)} %get-tuple-element.91.refs_17_), channel_id=1, source_target_pairs={{0,4},{1,8},{2,16},{3,24},{4,0},{5,12},{6,20},{7,28},{8,1},{9,13},... | collective-permute-start | bytes 196616 | tf_op jit(solution)/shard_map/ppermute | solution.py:377
  3.6 0.1 lend.1
  3.6 0.1 collective-permute-start.1
  3.7 0.5 %collective-permute-start = (bf16[128,128]{1,0:T(8,128)(2,1)S(1)}, bf16[128,128]{1,0:T(8,128)(2,1)S(1)}, u32[]{:S(2)}, u32[]{:S(2)}) collective-permute-start(bf16[128,128]{1,0:T(8,128)(2,1)S(1)} %get-tuple-element.82), channel_id=1, source_target_pairs={{0,4},{4,0},{8,12},{12,8},{16,20},{20,16},{24,28},{28,24},{1,5},{5... | collective-permute-start | bytes 98312 | tf_op jit(solution)/shard_map/ppermute | solution.py:386
  4.2 0.9 %prepare.2 = (bf16[128,256]{1,0:T(8,128)(2,1)S(1)}, bf16[128,256]{1,0:T(8,128)(2,1)S(1)}, bf16[256,512]{1,0:T(8,128)(2,1)S(1)}, f32[256,512]{1,0:T(8,128)S(1)}, ...) custom-call(bf16[2,256,128]{2,1,0:T(8,128)(2,1)S(1)} %get-tuple-elem, ...), custom_call_target="tpu_custom_call" | custom-call | flops 100663296 | bytes 1048576 | tf_op jit(solution)/shard_map/prepare/pallas_call | solution.py:391
  5.0 0.0 collective-permute-done.refs_0_
  5.1 0.0 collective-permute-done.1.refs_1_
  5.1 0.9 %prepare.3 = (bf16[128,256]{1,0:T(8,128)(2,1)S(1)}, bf16[128,256]{1,0:T(8,128)(2,1)S(1)}, bf16[256,512]{1,0:T(8,128)(2,1)S(1)}, f32[256,512]{1,0:T(8,128)S(1)}, ...) custom-call(bf16[128,128]{1,0:T(8,128)(2,1)S(1)} %collective-permute, ...), custom_call_target="tpu_custom_call" | custom-call | tf_op jit(solution)/shard_map/prepare/pallas_call | solution.py:391
  6.0 0.0 collective-permute-done.2.refs_16_
  6.0 1.2 %backward.1 = (f32[512,128]{1,0:T(8,128)S(1)}, bf16[512,512]{1,0:T(8,128)(2,1)S(1)}, bf16[512,512]{1,0:T(8,128)(2,1)S(1)}, bf16[4,208,128]{2,1,0:T(8,128)(2,1)S(1)}, bf16[4,208,128]{2,1,0:T(8,128)(2,1)S(1)}) custom-call(bf16[128,256]{1,0:T(8,128)(2,1)S(1)} %get-tuple-element.75.refs_0_, bf16[128,256]{1,0:T(8,128)(2,1)S(1)} %get-tuple-element.76.refs_1_, ...), custom_call_target="tpu_custom_call" | custom-call | flops 268435456 | bytes 1048576 | tf_op jit(solution)/shard_map/backward/pallas_call | solution.py:423
  7.2 0.4 %collective-permute-start.3 = (bf16[4,208,128]{2,1,0:T(8,128)(2,1)S(1)}, bf16[4,208,128]{2,1,0:T(8,128)(2,1)S(1)}, u32[]{:S(2)}, u32[]{:S(2)}) collective-permute-start(bf16[4,208,128]{2,1,0:T(8,128)(2,1)S(1)} %get-tuple-element.93), channel_id=1, source_target_pairs={{0,4},{4,0},{8,12},{12,8},{16,20},{20,16},{24,28},{28,24},{1,5},{5... | collective-permute-start | bytes 638984 | tf_op jit(solution)/shard_map/ppermute | solution.py:474
  7.6 0.4 %d_inputs.3.rest_2_ = bf16[256,128]{1,0:T(8,128)(2,1)S(1)} custom-call(f32[512,128]{1,0:T(8,128)S(1)} %get-tuple-element.94.d_updated, bf16[512,512]{1,0:T(8,128)(2,1)S(1)} %get-tuple-element.95.d_gate, bf16[512,512]{1,0:T(8,128)(2,1)S(1)} %get-tuple-element.96.d_up, f32[256,128]{1,0:T(8,128)S(1)} %get-tuple-element.99.normed, ...), custom_call_target="tpu_custom_call" | custom-call | flops 67108864 | bytes 524288 | tf_op jit(solution)/shard_map/d_inputs/pallas_call | solution.py:436
  8.0 0.4 %d_inputs.2.refs_0_ = bf16[256,128]{1,0:T(8,128)(2,1)S(1)} custom-call(f32[512,128]{1,0:T(8,128)S(1)} %get-tuple-element.94.d_updated, bf16[512,512]{1,0:T(8,128)(2,1)S(1)} %get-tuple-element.95.d_gate, bf16[512,512]{1,0:T(8,128)(2,1)S(1)} %get-tuple-element.96.d_up, f32[256,128]{1,0:T(8,128)S(1)} %get-tuple-element.97.normed, ...), custom_call_target="tpu_custom_call" | custom-call | flops 67108864 | bytes 524288 | tf_op jit(solution)/shard_map/d_inputs/pallas_call | solution.py:436
  8.3 0.4 %collective-permute-done.3.rest_1_ = bf16[4,208,128]{2,1,0:T(8,128)(2,1)S(1)} collective-permute-done((bf16[4,208,128]{2,1,0:T(8,128)(2,1)S(1)}, bf16[4,208,128]{2,1,0:T(8,128)(2,1)S(1)}, u32[]{:S(2)}, u32[]{:S(2)}) %collective-permute-start.3) | collective-permute-done | bytes 213024 | tf_op jit(solution)/shard_map/ppermute | solution.py:474
  8.7 0.1 core_sum.1
  8.8 6.9 %collective-permute-start.4 = (bf16[208,128]{1,0:T(8,128)(2,1)S(1)}, bf16[208,128]{1,0:T(8,128)(2,1)S(1)}, u32[]{:S(2)}, u32[]{:S(2)}) collective-permute-start(bf16[208,128]{1,0:T(8,128)(2,1)S(1)} %get-tuple-element.105), channel_id=1, source_target_pairs={{0,12},{4,8},{8,20},{12,16},{16,28},{20,24},{24,4},{28,0},{1,13},{... | collective-permute-start | bytes 159752 | tf_op jit(solution)/shard_map/ppermute | solution.py:487
  15.7 2.3 %collective-permute-start.5 = (bf16[208,128]{1,0:T(8,128)(2,1)S(1)}, bf16[208,128]{1,0:T(8,128)(2,1)S(1)}, u32[]{:S(2)}, u32[]{:S(2)}) collective-permute-start(bf16[208,128]{1,0:T(8,128)(2,1)S(1)} %get-tuple-element.106), channel_id=1, source_target_pairs={{0,20},{4,16},{8,28},{12,24},{16,4},{20,0},{24,12},{28,8},{1,21},{... | collective-permute-start | bytes 159752 | tf_op jit(solution)/shard_map/ppermute | solution.py:487
  18.0 0.0 collective-permute-start.6
  18.0 0.2 collective-permute-start.7
  18.2 0.4 %collective-permute-start.8 = (bf16[128,128]{1,0:T(8,128)(2,1)S(1)}, bf16[128,128]{1,0:T(8,128)(2,1)S(1)}, u32[]{:S(2)}, u32[]{:S(2)}) collective-permute-start(bf16[128,128]{1,0:T(8,128)(2,1)S(1)} %get-tuple-element.110), channel_id=1, source_target_pairs={{0,4},{4,0},{8,12},{12,8},{16,20},{20,16},{24,28},{28,24},{1,5},{5... | collective-permute-start | bytes 98312 | tf_op jit(solution)/shard_map/ppermute | solution.py:449
  18.5 0.7 %collective-permute-done.7.refs_1_ = bf16[128,128]{1,0:T(8,128)(2,1)S(1)} collective-permute-done((bf16[128,128]{1,0:T(8,128)(2,1)S(1)}, bf16[128,128]{1,0:T(8,128)(2,1)S(1)}, u32[]{:S(2)}, u32[]{:S(2)}) %collective-permute-start.7) | collective-permute-done | bytes 32800 | tf_op jit(solution)/shard_map/ppermute | solution.py:449
  19.2 0.2 collective-permute-done.8.refs_2_
  19.4 0.0 collective-permute-done.4.rest_1_
  19.4 1.6 %collective-permute-done.5.rest_2_ = bf16[208,128]{1,0:T(8,128)(2,1)S(1)} collective-permute-done((bf16[208,128]{1,0:T(8,128)(2,1)S(1)}, bf16[208,128]{1,0:T(8,128)(2,1)S(1)}, u32[]{:S(2)}, u32[]{:S(2)}) %collective-permute-start.5) | collective-permute-done | bytes 53280 | tf_op jit(solution)/shard_map/ppermute | solution.py:487
  21.0 0.8 %collective-permute-done.6.rest_3_ = bf16[208,128]{1,0:T(8,128)(2,1)S(1)} collective-permute-done((bf16[208,128]{1,0:T(8,128)(2,1)S(1)}, bf16[208,128]{1,0:T(8,128)(2,1)S(1)}, u32[]{:S(2)}, u32[]{:S(2)}) %collective-permute-start.6) | collective-permute-done | bytes 53280 | tf_op jit(solution)/shard_map/ppermute | solution.py:487
  21.8 0.1 chip_sum.1
  21.9 0.4 %collective-permute-start.9 = (bf16[64,128]{1,0:T(8,128)(2,1)S(1)}, bf16[64,128]{1,0:T(8,128)(2,1)S(1)}, u32[]{:S(2)}, u32[]{:S(2)}) collective-permute-start(bf16[64,128]{1,0:T(8,128)(2,1)S(1)} %get-tuple-element.116), channel_id=1, source_target_pairs={{0,6},{1,7},{2,4},{3,5},{4,2},{5,3},{6,0},{7,1},{8,14},{9,15},{10,... | collective-permute-start | bytes 49160 | tf_op jit(solution)/shard_map/ppermute | solution.py:506
  22.3 2.3 %collective-permute-start.10 = (bf16[64,128]{1,0:T(8,128)(2,1)S(1)}, bf16[64,128]{1,0:T(8,128)(2,1)S(1)}, u32[]{:S(2)}, u32[]{:S(2)}) collective-permute-start(bf16[64,128]{1,0:T(8,128)(2,1)S(1)} %get-tuple-element.117), channel_id=1, source_target_pairs={{0,7},{1,6},{2,5},{3,4},{4,3},{5,2},{6,1},{7,0},{8,15},{9,14},{10,... | collective-permute-start | bytes 49160 | tf_op jit(solution)/shard_map/ppermute | solution.py:506
  24.6 0.5 %collective-permute-start.11 = (bf16[64,128]{1,0:T(8,128)(2,1)S(1)}, bf16[64,128]{1,0:T(8,128)(2,1)S(1)}, u32[]{:S(2)}, u32[]{:S(2)}) collective-permute-start(bf16[64,128]{1,0:T(8,128)(2,1)S(1)} %get-tuple-element.118), channel_id=1, source_target_pairs={{0,5},{1,4},{2,7},{3,6},{4,1},{5,0},{6,3},{7,2},{8,13},{9,12},{10,... | collective-permute-start | bytes 49160 | tf_op jit(solution)/shard_map/ppermute | solution.py:506
  25.0 0.7 %place.1 = bf16[16,2,16,128]{3,2,1,0:T(8,128)(2,1)} custom-call(bf16[256,128]{1,0:T(8,128)(2,1)S(1)} %d_inputs.2.refs_0_, bf16[128,128]{1,0:T(8,128)(2,1)S(1)} %collective-permute-done.7.refs_1_, bf16[128,128]{1,0:T(8,128)(2,1)S(1)} %collective-permute-done.8.refs_2_), custom_call_target="tpu_custom_call" | custom-call | tf_op jit(solution)/shard_map/place/pallas_call | solution.py:453
  25.7 0.4 %collective-permute-done.9.rest_1_ = bf16[64,128]{1,0:T(8,128)(2,1)S(1)} collective-permute-done((bf16[64,128]{1,0:T(8,128)(2,1)S(1)}, bf16[64,128]{1,0:T(8,128)(2,1)S(1)}, u32[]{:S(2)}, u32[]{:S(2)}) %collective-permute-start.9) | collective-permute-done | bytes 16416 | tf_op jit(solution)/shard_map/ppermute | solution.py:506
  26.1 1.2 %collective-permute-done.10.rest_2_ = bf16[64,128]{1,0:T(8,128)(2,1)S(1)} collective-permute-done((bf16[64,128]{1,0:T(8,128)(2,1)S(1)}, bf16[64,128]{1,0:T(8,128)(2,1)S(1)}, u32[]{:S(2)}, u32[]{:S(2)}) %collective-permute-start.10) | collective-permute-done | bytes 16416 | tf_op jit(solution)/shard_map/ppermute | solution.py:506
  27.3 0.6 %collective-permute-done.11.rest_3_ = bf16[64,128]{1,0:T(8,128)(2,1)S(1)} collective-permute-done((bf16[64,128]{1,0:T(8,128)(2,1)S(1)}, bf16[64,128]{1,0:T(8,128)(2,1)S(1)}, u32[]{:S(2)}, u32[]{:S(2)}) %collective-permute-start.11) | collective-permute-done | bytes 16416 | tf_op jit(solution)/shard_map/ppermute | solution.py:506
  27.9 0.7 %col_sum.1 = (f32[16,128]{1,0:T(8,128)}, f32[16,128]{1,0:T(8,128)}, f32[32,64]{1,0:T(8,128)}, f32[16,16]{1,0:T(8,128)}) custom-call(bf16[64,128]{1,0:T(8,128)(2,1)S(1)} %get-tuple-element.123.rest_0_, bf16[64,128]{1,0:T(8,128)(2,1)S(1)} %collective-permute-done.9.rest_1_, bf16[64,128]{1,0:T(8,128)(2,1)S(1)} %collective-permute-done.10.rest_2_, ...), custom_call_target="tpu_custom_call" | custom-call | tf_op jit(solution)/shard_map/col_sum/pallas_call | solution.py:508
Async XLA Ops:
  3.0 2.9 %collective-permute-start.2 = (bf16[2,128,128]{2,1,0:T(8,128)(2,1)S(1)}, bf16[2,128,128]{2,1,0:T(8,128)(2,1)S(1)}, u32[]{:S(2)}, u32[]{:S(2)}) collective-permute-start(bf16[2,128,128]{2,1,0:T(8,128)(2,1)S(1)} %get-tuple-element.91.refs_17_), channel_id=1, source_target_pairs={{0,4},{1,8},{2,16},{3,24},{4,0},{5,12},{6,20},{7,28},{8,1},{9,13},... | collective-permute-start | bytes 196616 | tf_op jit(solution)/shard_map/ppermute | solution.py:377
  3.6 1.4 %collective-permute-start.1 = (bf16[144,128]{1,0:T(8,128)(2,1)S(1)}, bf16[144,128]{1,0:T(8,128)(2,1)S(1)}, u32[]{:S(2)}, u32[]{:S(2)}) collective-permute-start(bf16[144,128]{1,0:T(8,128)(2,1)S(1)} %get-tuple-element.83), channel_id=1, source_target_pairs={{0,4},{4,0},{8,12},{12,8},{16,20},{20,16},{24,28},{28,24},{1,5},{5... | collective-permute-start | bytes 110600 | tf_op jit(solution)/shard_map/ppermute | solution.py:386
  3.7 1.3 %collective-permute-start = (bf16[128,128]{1,0:T(8,128)(2,1)S(1)}, bf16[128,128]{1,0:T(8,128)(2,1)S(1)}, u32[]{:S(2)}, u32[]{:S(2)}) collective-permute-start(bf16[128,128]{1,0:T(8,128)(2,1)S(1)} %get-tuple-element.82), channel_id=1, source_target_pairs={{0,4},{4,0},{8,12},{12,8},{16,20},{20,16},{24,28},{28,24},{1,5},{5... | collective-permute-start | bytes 98312 | tf_op jit(solution)/shard_map/ppermute | solution.py:386
  7.2 1.5 %collective-permute-start.3 = (bf16[4,208,128]{2,1,0:T(8,128)(2,1)S(1)}, bf16[4,208,128]{2,1,0:T(8,128)(2,1)S(1)}, u32[]{:S(2)}, u32[]{:S(2)}) collective-permute-start(bf16[4,208,128]{2,1,0:T(8,128)(2,1)S(1)} %get-tuple-element.93), channel_id=1, source_target_pairs={{0,4},{4,0},{8,12},{12,8},{16,20},{20,16},{24,28},{28,24},{1,5},{5... | collective-permute-start | bytes 638984 | tf_op jit(solution)/shard_map/ppermute | solution.py:474
  8.8 10.6 %collective-permute-start.4 = (bf16[208,128]{1,0:T(8,128)(2,1)S(1)}, bf16[208,128]{1,0:T(8,128)(2,1)S(1)}, u32[]{:S(2)}, u32[]{:S(2)}) collective-permute-start(bf16[208,128]{1,0:T(8,128)(2,1)S(1)} %get-tuple-element.105), channel_id=1, source_target_pairs={{0,12},{4,8},{8,20},{12,16},{16,28},{20,24},{24,4},{28,0},{1,13},{... | collective-permute-start | bytes 159752 | tf_op jit(solution)/shard_map/ppermute | solution.py:487
  15.7 5.2 %collective-permute-start.5 = (bf16[208,128]{1,0:T(8,128)(2,1)S(1)}, bf16[208,128]{1,0:T(8,128)(2,1)S(1)}, u32[]{:S(2)}, u32[]{:S(2)}) collective-permute-start(bf16[208,128]{1,0:T(8,128)(2,1)S(1)} %get-tuple-element.106), channel_id=1, source_target_pairs={{0,20},{4,16},{8,28},{12,24},{16,4},{20,0},{24,12},{28,8},{1,21},{... | collective-permute-start | bytes 159752 | tf_op jit(solution)/shard_map/ppermute | solution.py:487
  18.0 3.8 %collective-permute-start.6 = (bf16[208,128]{1,0:T(8,128)(2,1)S(1)}, bf16[208,128]{1,0:T(8,128)(2,1)S(1)}, u32[]{:S(2)}, u32[]{:S(2)}) collective-permute-start(bf16[208,128]{1,0:T(8,128)(2,1)S(1)} %get-tuple-element.107), channel_id=1, source_target_pairs={{0,28},{4,24},{8,4},{12,0},{16,12},{20,8},{24,20},{28,16},{1,29},{... | collective-permute-start | bytes 159752 | tf_op jit(solution)/shard_map/ppermute | solution.py:487
  18.0 1.2 %collective-permute-start.7 = (bf16[128,128]{1,0:T(8,128)(2,1)S(1)}, bf16[128,128]{1,0:T(8,128)(2,1)S(1)}, u32[]{:S(2)}, u32[]{:S(2)}) collective-permute-start(bf16[128,128]{1,0:T(8,128)(2,1)S(1)} %get-tuple-element.109), channel_id=1, source_target_pairs={{0,4},{4,0},{8,12},{12,8},{16,20},{20,16},{24,28},{28,24},{1,5},{5... | collective-permute-start | bytes 98312 | tf_op jit(solution)/shard_map/ppermute | solution.py:449
  18.2 1.2 %collective-permute-start.8 = (bf16[128,128]{1,0:T(8,128)(2,1)S(1)}, bf16[128,128]{1,0:T(8,128)(2,1)S(1)}, u32[]{:S(2)}, u32[]{:S(2)}) collective-permute-start(bf16[128,128]{1,0:T(8,128)(2,1)S(1)} %get-tuple-element.110), channel_id=1, source_target_pairs={{0,4},{4,0},{8,12},{12,8},{16,20},{20,16},{24,28},{28,24},{1,5},{5... | collective-permute-start | bytes 98312 | tf_op jit(solution)/shard_map/ppermute | solution.py:449
  21.9 4.2 %collective-permute-start.9 = (bf16[64,128]{1,0:T(8,128)(2,1)S(1)}, bf16[64,128]{1,0:T(8,128)(2,1)S(1)}, u32[]{:S(2)}, u32[]{:S(2)}) collective-permute-start(bf16[64,128]{1,0:T(8,128)(2,1)S(1)} %get-tuple-element.116), channel_id=1, source_target_pairs={{0,6},{1,7},{2,4},{3,5},{4,2},{5,3},{6,0},{7,1},{8,14},{9,15},{10,... | collective-permute-start | bytes 49160 | tf_op jit(solution)/shard_map/ppermute | solution.py:506
  22.3 5.0 %collective-permute-start.10 = (bf16[64,128]{1,0:T(8,128)(2,1)S(1)}, bf16[64,128]{1,0:T(8,128)(2,1)S(1)}, u32[]{:S(2)}, u32[]{:S(2)}) collective-permute-start(bf16[64,128]{1,0:T(8,128)(2,1)S(1)} %get-tuple-element.117), channel_id=1, source_target_pairs={{0,7},{1,6},{2,5},{3,4},{4,3},{5,2},{6,1},{7,0},{8,15},{9,14},{10,... | collective-permute-start | bytes 49160 | tf_op jit(solution)/shard_map/ppermute | solution.py:506
  24.6 3.4 %collective-permute-start.11 = (bf16[64,128]{1,0:T(8,128)(2,1)S(1)}, bf16[64,128]{1,0:T(8,128)(2,1)S(1)}, u32[]{:S(2)}, u32[]{:S(2)}) collective-permute-start(bf16[64,128]{1,0:T(8,128)(2,1)S(1)} %get-tuple-element.118), channel_id=1, source_target_pairs={{0,5},{1,4},{2,7},{3,6},{4,1},{5,0},{6,3},{7,2},{8,13},{9,12},{10,... | collective-permute-start | bytes 49160 | tf_op jit(solution)/shard_map/ppermute | solution.py:506

commit v13 on v11

--- a/solution.py
+++ b/solution.py
@@ -8,6 +8,7 @@
 from jax.sharding import PartitionSpec as P
 
 eps = 1e-05
+PARTS = 4
 f32 = jnp.float32
 bf16 = jnp.bfloat16
 HBM = pl.BlockSpec(memory_space=pltpu.HBM)
@@ -72,17 +73,20 @@
     _, side, width = pair.shape
     edge = sources[0].shape[0]
     bins = w_head.shape[0]
-    copies = [
-        pltpu.make_async_copy(source, target, sems.at[i])
-        for i, (source, target) in enumerate(zip(sources[1:], (w_gate, w_up, w_out, w_head, targets)))
-    ]
+    copies, n = [], q
+    for source, target in zip(sources[1:], (w_gate, w_up, w_out, w_head, targets)):
+        parts = PARTS if source.shape[0] % (PARTS * 16) == 0 else 1
+        tall = source.shape[0] // parts
+        rows = [slice(i * tall, (i + 1) * tall) for i in range(parts)]
+        copies.append([pltpu.make_async_copy(source.at[r], target.at[r], sems.at[n + i]) for i, r in enumerate(rows)])
+        n += parts
     pieces = [
         pltpu.make_async_copy(
-            sources[0].at[:, h * edge : (h + 1) * edge, :], pair.reshape(q, edge, edge, width).at[h], sems.at[5 + h]
+            sources[0].at[:, h * edge : (h + 1) * edge, :], pair.reshape(q, edge, edge, width).at[h], sems.at[h]
         )
         for h in range(q)
     ]
-    for copy in pieces + copies:
+    for copy in pieces + [copy for group in copies for copy in group]:
         copy.start()
     shift = edge.bit_length() - 1
     out_row = lax.broadcasted_iota(jnp.int32, (side, side), 0)
@@ -94,14 +98,14 @@
         copy.wait()
     flat = pair[...].reshape(q * side, width)
     inputs = normalize(flat)[0].astype(bf16)
-    for copy in copies[:2]:
+    for copy in copies[0] + copies[1]:
         copy.wait()
     for top, tall in chunks_of(q * side, 128):
         for at, step in chunks_of(w_gate.shape[1], 256):
             gate = nn(inputs[top : top + tall], w_gate[:, at : at + step])
             upper = nn(inputs[top : top + tall], w_up[:, at : at + step])
             hidden[top : top + tall, at : at + step] = (gate * sigmoid(gate) * upper).astype(bf16)
-    for copy in copies[2:]:
+    for copy in copies[2] + copies[3] + copies[4]:
         copy.wait()
     total = flat.astype(f32) + nn(hidden[...], w_out[...])
     logit = nt(total.astype(bf16), w_head[...]).astype(bf16)
@@ -368,7 +372,7 @@
             pltpu.VMEM((rows, cols), jnp.int32),
             pltpu.VMEM((q, *piece), bf16),
             pltpu.VMEM((q * side, units), bf16),
-            pltpu.SemaphoreType.DMA((5 + q,)),
+            pltpu.SemaphoreType.DMA((5 * PARTS + q,)),
         ],
         compiler_params=PARAMS,
         name="forward",

time: 28.7 us -> 28.9 us (level)
  no operation moved by 1% of the time
where the time goes in v13:
time: 28.9 us; the launch traced here: 28.7 us
  starting transfers between devices  14.4 us (50%)
  Pallas kernels  7.73 us (27%)
  waiting for transfers between devices  5.91 us (20%)
  between operations  0.71 us (2%)
    ppermute x3, starting transfers between devices, body(): lax.ppermute(hot[p], 'row', [(s, following(s // q, p, groups) * q + cross...  9.26 us
    ppermute x3, starting transfers between devices, body(): terms.append(lax.ppermute(hot[p], ('row', 'col'), pairs))  3.18 us
    pallas_call x1, Pallas kernels, body(): pl.pallas_call(functools.partial(forward_kernel, q), out_shape=[shaped((q...  2.47 us
    ppermute x3, waiting for transfers between devices, body(): lax.ppermute(hot[p], 'row', [(s, following(s // q, p, groups) * q + cross...  2.42 us
    ppermute x3, waiting for transfers between devices, body(): terms.append(lax.ppermute(hot[p], ('row', 'col'), pairs))  2.22 us
    pallas_call x2, Pallas kernels, body(): pl.pallas_call(functools.partial(prepare_kernel, q, p), out_shape=[shaped...  1.77 us
    pallas_call x1, Pallas kernels, body(): pl.pallas_call(functools.partial(backward_kernel, q, (nrow, ncol) if fits...  1.23 us
    ppermute x2, waiting for transfers between devices, returned(): lax.ppermute(x, 'row', core_pairs(nrow, q, n // 2 + 1))  0.86 us
  transfers between devices with their start and end apart: 12, of which 8 were waited for; matrix products, arithmetic and copies ran while one was open for 0% of the time, Pallas kernels for 11%

profile of v13, /device:TPU:0, one launch (start us, length us, event | category | flops | bytes accessed | tf_op | source)
XLA Modules:
  0.0 28.7 jit_solution(16238803854998588128)
XLA Ops:
  0.6 2.5 %forward.1 = (bf16[2,256,128]{2,1,0:T(8,128)(2,1)S(1)}, bf16[128,512]{1,0:T(8,128)(2,1)S(1)}, bf16[128,512]{1,0:T(8,128)(2,1)S(1)}, bf16[512,128]{1,0:T(8,128)(2...) custom-call(bf16[16,32,128]{2,1,0:T(8,128)(2,1)} %refs_0_.1, ...), custom_call_target="tpu_custom_call" | custom-call | tf_op jit(solution)/shard_map/forward/pallas_call | solution.py:364
  3.1 0.5 %collective-permute-start.2 = (bf16[2,128,128]{2,1,0:T(8,128)(2,1)S(1)}, bf16[2,128,128]{2,1,0:T(8,128)(2,1)S(1)}, u32[]{:S(2)}, u32[]{:S(2)}) collective-permute-start(bf16[2,128,128]{2,1,0:T(8,128)(2,1)S(1)} %get-tuple-element.89.refs_17_), channel_id=1, source_target_pairs={{0,4},{1,8},{2,16},{3,24},{4,0},{5,12},{6,20},{7,28},{8,1},{9,13},... | collective-permute-start | bytes 196616 | tf_op jit(solution)/shard_map/ppermute | solution.py:386
  3.6 0.1 collective-permute-start.1
  3.7 0.4 %collective-permute-start = (bf16[128,128]{1,0:T(8,128)(2,1)S(1)}, bf16[128,128]{1,0:T(8,128)(2,1)S(1)}, u32[]{:S(2)}, u32[]{:S(2)}) collective-permute-start(bf16[128,128]{1,0:T(8,128)(2,1)S(1)} %get-tuple-element.80), channel_id=1, source_target_pairs={{0,4},{4,0},{8,12},{12,8},{16,20},{20,16},{24,28},{28,24},{1,5},{5... | collective-permute-start | bytes 98312 | tf_op jit(solution)/shard_map/ppermute | solution.py:395
  4.2 0.9 %prepare.2 = (bf16[128,256]{1,0:T(8,128)(2,1)S(1)}, bf16[128,256]{1,0:T(8,128)(2,1)S(1)}, bf16[256,512]{1,0:T(8,128)(2,1)S(1)}, f32[256,512]{1,0:T(8,128)S(1)}, ...) custom-call(bf16[2,256,128]{2,1,0:T(8,128)(2,1)S(1)} %get-tuple-elem, ...), custom_call_target="tpu_custom_call" | custom-call | flops 100663296 | bytes 1048576 | tf_op jit(solution)/shard_map/prepare/pallas_call | solution.py:400
  5.0 0.0 collective-permute-done.refs_0_
  5.1 0.0 collective-permute-done.1.refs_1_
  5.1 0.9 %prepare.3 = (bf16[128,256]{1,0:T(8,128)(2,1)S(1)}, bf16[128,256]{1,0:T(8,128)(2,1)S(1)}, bf16[256,512]{1,0:T(8,128)(2,1)S(1)}, f32[256,512]{1,0:T(8,128)S(1)}, ...) custom-call(bf16[128,128]{1,0:T(8,128)(2,1)S(1)} %collective-permute, ...), custom_call_target="tpu_custom_call" | custom-call | tf_op jit(solution)/shard_map/prepare/pallas_call | solution.py:400
  6.0 0.0 collective-permute-done.2.refs_16_
  6.0 1.2 %backward.1 = (f32[512,128]{1,0:T(8,128)S(1)}, bf16[512,512]{1,0:T(8,128)(2,1)S(1)}, bf16[512,512]{1,0:T(8,128)(2,1)S(1)}, bf16[4,208,128]{2,1,0:T(8,128)(2,1)S(1)}, bf16[4,208,128]{2,1,0:T(8,128)(2,1)S(1)}) custom-call(bf16[128,256]{1,0:T(8,128)(2,1)S(1)} %get-tuple-element.73.refs_0_, bf16[128,256]{1,0:T(8,128)(2,1)S(1)} %get-tuple-element.74.refs_1_, ...), custom_call_target="tpu_custom_call" | custom-call | flops 268435456 | bytes 1048576 | tf_op jit(solution)/shard_map/backward/pallas_call | solution.py:432
  7.2 0.4 %collective-permute-start.3 = (bf16[4,208,128]{2,1,0:T(8,128)(2,1)S(1)}, bf16[4,208,128]{2,1,0:T(8,128)(2,1)S(1)}, u32[]{:S(2)}, u32[]{:S(2)}) collective-permute-start(bf16[4,208,128]{2,1,0:T(8,128)(2,1)S(1)} %get-tuple-element.91), channel_id=1, source_target_pairs={{0,4},{4,0},{8,12},{12,8},{16,20},{20,16},{24,28},{28,24},{1,5},{5... | collective-permute-start | bytes 638984 | tf_op jit(solution)/shard_map/ppermute | solution.py:483
  7.6 0.4 %d_inputs.3.rest_2_ = bf16[256,128]{1,0:T(8,128)(2,1)S(1)} custom-call(f32[512,128]{1,0:T(8,128)S(1)} %get-tuple-element.92.d_updated, bf16[512,512]{1,0:T(8,128)(2,1)S(1)} %get-tuple-element.93.d_gate, bf16[512,512]{1,0:T(8,128)(2,1)S(1)} %get-tuple-element.94.d_up, f32[256,128]{1,0:T(8,128)S(1)} %get-tuple-element.97.normed, ...), custom_call_target="tpu_custom_call" | custom-call | flops 67108864 | bytes 524288 | tf_op jit(solution)/shard_map/d_inputs/pallas_call | solution.py:445
  8.0 0.4 %d_inputs.2.refs_0_ = bf16[256,128]{1,0:T(8,128)(2,1)S(1)} custom-call(f32[512,128]{1,0:T(8,128)S(1)} %get-tuple-element.92.d_updated, bf16[512,512]{1,0:T(8,128)(2,1)S(1)} %get-tuple-element.93.d_gate, bf16[512,512]{1,0:T(8,128)(2,1)S(1)} %get-tuple-element.94.d_up, f32[256,128]{1,0:T(8,128)S(1)} %get-tuple-element.95.normed, ...), custom_call_target="tpu_custom_call" | custom-call | flops 67108864 | bytes 524288 | tf_op jit(solution)/shard_map/d_inputs/pallas_call | solution.py:445
  8.3 0.4 %collective-permute-done.3.rest_1_ = bf16[4,208,128]{2,1,0:T(8,128)(2,1)S(1)} collective-permute-done((bf16[4,208,128]{2,1,0:T(8,128)(2,1)S(1)}, bf16[4,208,128]{2,1,0:T(8,128)(2,1)S(1)}, u32[]{:S(2)}, u32[]{:S(2)}) %collective-permute-start.3) | collective-permute-done | bytes 213024 | tf_op jit(solution)/shard_map/ppermute | solution.py:483
  8.8 0.1 core_sum.1
  8.8 7.0 %collective-permute-start.4 = (bf16[208,128]{1,0:T(8,128)(2,1)S(1)}, bf16[208,128]{1,0:T(8,128)(2,1)S(1)}, u32[]{:S(2)}, u32[]{:S(2)}) collective-permute-start(bf16[208,128]{1,0:T(8,128)(2,1)S(1)} %get-tuple-element.103), channel_id=1, source_target_pairs={{0,12},{4,8},{8,20},{12,16},{16,28},{20,24},{24,4},{28,0},{1,13},{... | collective-permute-start | bytes 159752 | tf_op jit(solution)/shard_map/ppermute | solution.py:496
  15.8 2.3 %collective-permute-start.5 = (bf16[208,128]{1,0:T(8,128)(2,1)S(1)}, bf16[208,128]{1,0:T(8,128)(2,1)S(1)}, u32[]{:S(2)}, u32[]{:S(2)}) collective-permute-start(bf16[208,128]{1,0:T(8,128)(2,1)S(1)} %get-tuple-element.104), channel_id=1, source_target_pairs={{0,20},{4,16},{8,28},{12,24},{16,4},{20,0},{24,12},{28,8},{1,21},{... | collective-permute-start | bytes 159752 | tf_op jit(solution)/shard_map/ppermute | solution.py:496
  18.1 0.0 collective-permute-start.6
  18.1 0.2 collective-permute-start.7
  18.2 0.4 %collective-permute-start.8 = (bf16[128,128]{1,0:T(8,128)(2,1)S(1)}, bf16[128,128]{1,0:T(8,128)(2,1)S(1)}, u32[]{:S(2)}, u32[]{:S(2)}) collective-permute-start(bf16[128,128]{1,0:T(8,128)(2,1)S(1)} %get-tuple-element.108), channel_id=1, source_target_pairs={{0,4},{4,0},{8,12},{12,8},{16,20},{20,16},{24,28},{28,24},{1,5},{5... | collective-permute-start | bytes 98312 | tf_op jit(solution)/shard_map/ppermute | solution.py:458
  18.6 0.7 %collective-permute-done.7.refs_1_ = bf16[128,128]{1,0:T(8,128)(2,1)S(1)} collective-permute-done((bf16[128,128]{1,0:T(8,128)(2,1)S(1)}, bf16[128,128]{1,0:T(8,128)(2,1)S(1)}, u32[]{:S(2)}, u32[]{:S(2)}) %collective-permute-start.7) | collective-permute-done | bytes 32800 | tf_op jit(solution)/shard_map/ppermute | solution.py:458
  19.3 0.2 collective-permute-done.8.refs_2_
  19.4 0.0 collective-permute-done.4.rest_1_
  19.4 1.6 %collective-permute-done.5.rest_2_ = bf16[208,128]{1,0:T(8,128)(2,1)S(1)} collective-permute-done((bf16[208,128]{1,0:T(8,128)(2,1)S(1)}, bf16[208,128]{1,0:T(8,128)(2,1)S(1)}, u32[]{:S(2)}, u32[]{:S(2)}) %collective-permute-start.5) | collective-permute-done | bytes 53280 | tf_op jit(solution)/shard_map/ppermute | solution.py:496
  21.0 0.8 %collective-permute-done.6.rest_3_ = bf16[208,128]{1,0:T(8,128)(2,1)S(1)} collective-permute-done((bf16[208,128]{1,0:T(8,128)(2,1)S(1)}, bf16[208,128]{1,0:T(8,128)(2,1)S(1)}, u32[]{:S(2)}, u32[]{:S(2)}) %collective-permute-start.6) | collective-permute-done | bytes 53280 | tf_op jit(solution)/shard_map/ppermute | solution.py:496
  21.9 0.1 chip_sum.1
  22.0 0.5 %collective-permute-start.9 = (bf16[64,128]{1,0:T(8,128)(2,1)S(1)}, bf16[64,128]{1,0:T(8,128)(2,1)S(1)}, u32[]{:S(2)}, u32[]{:S(2)}) collective-permute-start(bf16[64,128]{1,0:T(8,128)(2,1)S(1)} %get-tuple-element.114), channel_id=1, source_target_pairs={{0,6},{1,7},{2,4},{3,5},{4,2},{5,3},{6,0},{7,1},{8,14},{9,15},{10,... | collective-permute-start | bytes 49160 | tf_op jit(solution)/shard_map/ppermute | solution.py:515
  22.4 2.3 %collective-permute-start.10 = (bf16[64,128]{1,0:T(8,128)(2,1)S(1)}, bf16[64,128]{1,0:T(8,128)(2,1)S(1)}, u32[]{:S(2)}, u32[]{:S(2)}) collective-permute-start(bf16[64,128]{1,0:T(8,128)(2,1)S(1)} %get-tuple-element.115), channel_id=1, source_target_pairs={{0,7},{1,6},{2,5},{3,4},{4,3},{5,2},{6,1},{7,0},{8,15},{9,14},{10,... | collective-permute-start | bytes 49160 | tf_op jit(solution)/shard_map/ppermute | solution.py:515
  24.7 0.5 %collective-permute-start.11 = (bf16[64,128]{1,0:T(8,128)(2,1)S(1)}, bf16[64,128]{1,0:T(8,128)(2,1)S(1)}, u32[]{:S(2)}, u32[]{:S(2)}) collective-permute-start(bf16[64,128]{1,0:T(8,128)(2,1)S(1)} %get-tuple-element.116), channel_id=1, source_target_pairs={{0,5},{1,4},{2,7},{3,6},{4,1},{5,0},{6,3},{7,2},{8,13},{9,12},{10,... | collective-permute-start | bytes 49160 | tf_op jit(solution)/shard_map/ppermute | solution.py:515
  25.1 0.7 %place.1 = bf16[16,2,16,128]{3,2,1,0:T(8,128)(2,1)} custom-call(bf16[256,128]{1,0:T(8,128)(2,1)S(1)} %d_inputs.2.refs_0_, bf16[128,128]{1,0:T(8,128)(2,1)S(1)} %collective-permute-done.7.refs_1_, bf16[128,128]{1,0:T(8,128)(2,1)S(1)} %collective-permute-done.8.refs_2_), custom_call_target="tpu_custom_call" | custom-call | tf_op jit(solution)/shard_map/place/pallas_call | solution.py:462
  25.8 0.4 %collective-permute-done.9.rest_1_ = bf16[64,128]{1,0:T(8,128)(2,1)S(1)} collective-permute-done((bf16[64,128]{1,0:T(8,128)(2,1)S(1)}, bf16[64,128]{1,0:T(8,128)(2,1)S(1)}, u32[]{:S(2)}, u32[]{:S(2)}) %collective-permute-start.9) | collective-permute-done | bytes 16416 | tf_op jit(solution)/shard_map/ppermute | solution.py:515
  26.2 1.2 %collective-permute-done.10.rest_2_ = bf16[64,128]{1,0:T(8,128)(2,1)S(1)} collective-permute-done((bf16[64,128]{1,0:T(8,128)(2,1)S(1)}, bf16[64,128]{1,0:T(8,128)(2,1)S(1)}, u32[]{:S(2)}, u32[]{:S(2)}) %collective-permute-start.10) | collective-permute-done | bytes 16416 | tf_op jit(solution)/shard_map/ppermute | solution.py:515
  27.4 0.7 %collective-permute-done.11.rest_3_ = bf16[64,128]{1,0:T(8,128)(2,1)S(1)} collective-permute-done((bf16[64,128]{1,0:T(8,128)(2,1)S(1)}, bf16[64,128]{1,0:T(8,128)(2,1)S(1)}, u32[]{:S(2)}, u32[]{:S(2)}) %collective-permute-start.11) | collective-permute-done | bytes 16416 | tf_op jit(solution)/shard_map/ppermute | solution.py:515
  28.0 0.7 %col_sum.1 = (f32[16,128]{1,0:T(8,128)}, f32[16,128]{1,0:T(8,128)}, f32[32,64]{1,0:T(8,128)}, f32[16,16]{1,0:T(8,128)}) custom-call(bf16[64,128]{1,0:T(8,128)(2,1)S(1)} %get-tuple-element.121.rest_0_, bf16[64,128]{1,0:T(8,128)(2,1)S(1)} %collective-permute-done.9.rest_1_, bf16[64,128]{1,0:T(8,128)(2,1)S(1)} %collective-permute-done.10.rest_2_, ...), custom_call_target="tpu_custom_call" | custom-call | tf_op jit(solution)/shard_map/col_sum/pallas_call | solution.py:517
  (1 shorter events, 0.0 us)
Async XLA Ops:
  3.1 2.9 %collective-permute-start.2 = (bf16[2,128,128]{2,1,0:T(8,128)(2,1)S(1)}, bf16[2,128,128]{2,1,0:T(8,128)(2,1)S(1)}, u32[]{:S(2)}, u32[]{:S(2)}) collective-permute-start(bf16[2,128,128]{2,1,0:T(8,128)(2,1)S(1)} %get-tuple-element.89.refs_17_), channel_id=1, source_target_pairs={{0,4},{1,8},{2,16},{3,24},{4,0},{5,12},{6,20},{7,28},{8,1},{9,13},... | collective-permute-start | bytes 196616 | tf_op jit(solution)/shard_map/ppermute | solution.py:386
  3.6 1.4 %collective-permute-start.1 = (bf16[144,128]{1,0:T(8,128)(2,1)S(1)}, bf16[144,128]{1,0:T(8,128)(2,1)S(1)}, u32[]{:S(2)}, u32[]{:S(2)}) collective-permute-start(bf16[144,128]{1,0:T(8,128)(2,1)S(1)} %get-tuple-element.81), channel_id=1, source_target_pairs={{0,4},{4,0},{8,12},{12,8},{16,20},{20,16},{24,28},{28,24},{1,5},{5... | collective-permute-start | bytes 110600 | tf_op jit(solution)/shard_map/ppermute | solution.py:395
  3.7 1.3 %collective-permute-start = (bf16[128,128]{1,0:T(8,128)(2,1)S(1)}, bf16[128,128]{1,0:T(8,128)(2,1)S(1)}, u32[]{:S(2)}, u32[]{:S(2)}) collective-permute-start(bf16[128,128]{1,0:T(8,128)(2,1)S(1)} %get-tuple-element.80), channel_id=1, source_target_pairs={{0,4},{4,0},{8,12},{12,8},{16,20},{20,16},{24,28},{28,24},{1,5},{5... | collective-permute-start | bytes 98312 | tf_op jit(solution)/shard_map/ppermute | solution.py:395
  7.2 1.5 %collective-permute-start.3 = (bf16[4,208,128]{2,1,0:T(8,128)(2,1)S(1)}, bf16[4,208,128]{2,1,0:T(8,128)(2,1)S(1)}, u32[]{:S(2)}, u32[]{:S(2)}) collective-permute-start(bf16[4,208,128]{2,1,0:T(8,128)(2,1)S(1)} %get-tuple-element.91), channel_id=1, source_target_pairs={{0,4},{4,0},{8,12},{12,8},{16,20},{20,16},{24,28},{28,24},{1,5},{5... | collective-permute-start | bytes 638984 | tf_op jit(solution)/shard_map/ppermute | solution.py:483
  8.8 10.6 %collective-permute-start.4 = (bf16[208,128]{1,0:T(8,128)(2,1)S(1)}, bf16[208,128]{1,0:T(8,128)(2,1)S(1)}, u32[]{:S(2)}, u32[]{:S(2)}) collective-permute-start(bf16[208,128]{1,0:T(8,128)(2,1)S(1)} %get-tuple-element.103), channel_id=1, source_target_pairs={{0,12},{4,8},{8,20},{12,16},{16,28},{20,24},{24,4},{28,0},{1,13},{... | collective-permute-start | bytes 159752 | tf_op jit(solution)/shard_map/ppermute | solution.py:496
  15.8 5.2 %collective-permute-start.5 = (bf16[208,128]{1,0:T(8,128)(2,1)S(1)}, bf16[208,128]{1,0:T(8,128)(2,1)S(1)}, u32[]{:S(2)}, u32[]{:S(2)}) collective-permute-start(bf16[208,128]{1,0:T(8,128)(2,1)S(1)} %get-tuple-element.104), channel_id=1, source_target_pairs={{0,20},{4,16},{8,28},{12,24},{16,4},{20,0},{24,12},{28,8},{1,21},{... | collective-permute-start | bytes 159752 | tf_op jit(solution)/shard_map/ppermute | solution.py:496
  18.1 3.8 %collective-permute-start.6 = (bf16[208,128]{1,0:T(8,128)(2,1)S(1)}, bf16[208,128]{1,0:T(8,128)(2,1)S(1)}, u32[]{:S(2)}, u32[]{:S(2)}) collective-permute-start(bf16[208,128]{1,0:T(8,128)(2,1)S(1)} %get-tuple-element.105), channel_id=1, source_target_pairs={{0,28},{4,24},{8,4},{12,0},{16,12},{20,8},{24,20},{28,16},{1,29},{... | collective-permute-start | bytes 159752 | tf_op jit(solution)/shard_map/ppermute | solution.py:496
  18.1 1.2 %collective-permute-start.7 = (bf16[128,128]{1,0:T(8,128)(2,1)S(1)}, bf16[128,128]{1,0:T(8,128)(2,1)S(1)}, u32[]{:S(2)}, u32[]{:S(2)}) collective-permute-start(bf16[128,128]{1,0:T(8,128)(2,1)S(1)} %get-tuple-element.107), channel_id=1, source_target_pairs={{0,4},{4,0},{8,12},{12,8},{16,20},{20,16},{24,28},{28,24},{1,5},{5... | collective-permute-start | bytes 98312 | tf_op jit(solution)/shard_map/ppermute | solution.py:458
  18.2 1.2 %collective-permute-start.8 = (bf16[128,128]{1,0:T(8,128)(2,1)S(1)}, bf16[128,128]{1,0:T(8,128)(2,1)S(1)}, u32[]{:S(2)}, u32[]{:S(2)}) collective-permute-start(bf16[128,128]{1,0:T(8,128)(2,1)S(1)} %get-tuple-element.108), channel_id=1, source_target_pairs={{0,4},{4,0},{8,12},{12,8},{16,20},{20,16},{24,28},{28,24},{1,5},{5... | collective-permute-start | bytes 98312 | tf_op jit(solution)/shard_map/ppermute | solution.py:458
  22.0 4.2 %collective-permute-start.9 = (bf16[64,128]{1,0:T(8,128)(2,1)S(1)}, bf16[64,128]{1,0:T(8,128)(2,1)S(1)}, u32[]{:S(2)}, u32[]{:S(2)}) collective-permute-start(bf16[64,128]{1,0:T(8,128)(2,1)S(1)} %get-tuple-element.114), channel_id=1, source_target_pairs={{0,6},{1,7},{2,4},{3,5},{4,2},{5,3},{6,0},{7,1},{8,14},{9,15},{10,... | collective-permute-start | bytes 49160 | tf_op jit(solution)/shard_map/ppermute | solution.py:515
  22.4 5.0 %collective-permute-start.10 = (bf16[64,128]{1,0:T(8,128)(2,1)S(1)}, bf16[64,128]{1,0:T(8,128)(2,1)S(1)}, u32[]{:S(2)}, u32[]{:S(2)}) collective-permute-start(bf16[64,128]{1,0:T(8,128)(2,1)S(1)} %get-tuple-element.115), channel_id=1, source_target_pairs={{0,7},{1,6},{2,5},{3,4},{4,3},{5,2},{6,1},{7,0},{8,15},{9,14},{10,... | collective-permute-start | bytes 49160 | tf_op jit(solution)/shard_map/ppermute | solution.py:515
  24.7 3.4 %collective-permute-start.11 = (bf16[64,128]{1,0:T(8,128)(2,1)S(1)}, bf16[64,128]{1,0:T(8,128)(2,1)S(1)}, u32[]{:S(2)}, u32[]{:S(2)}) collective-permute-start(bf16[64,128]{1,0:T(8,128)(2,1)S(1)} %get-tuple-element.116), channel_id=1, source_target_pairs={{0,5},{1,4},{2,7},{3,6},{4,1},{5,0},{6,3},{7,2},{8,13},{9,12},{10,... | collective-permute-start | bytes 49160 | tf_op jit(solution)/shard_map/ppermute | solution.py:515

commit v14 on v11

--- a/solution.py
+++ b/solution.py
@@ -32,10 +32,6 @@
     centre = values - jnp.mean(values, axis=-1, keepdims=True)
     scale_inv = lax.rsqrt(jnp.mean(centre * centre, axis=-1, keepdims=True) + eps)
     return centre * scale_inv, scale_inv
-
-
-def sigmoid(v):
-    return 0.5 * jnp.tanh(0.5 * v) + 0.5
 
 
 def chunks_of(size, most):
@@ -96,11 +92,12 @@
     inputs = normalize(flat)[0].astype(bf16)
     for copy in copies[:2]:
         copy.wait()
-    for top, tall in chunks_of(q * side, 128):
-        for at, step in chunks_of(w_gate.shape[1], 256):
-            gate = nn(inputs[top : top + tall], w_gate[:, at : at + step])
+    for at, step in chunks_of(w_gate.shape[1], 256):
+        w_half = w_gate[:, at : at + step] * 0.5
+        for top, tall in chunks_of(q * side, 256):
+            half = nn(inputs[top : top + tall], w_half)
             upper = nn(inputs[top : top + tall], w_up[:, at : at + step])
-            hidden[top : top + tall, at : at + step] = (gate * sigmoid(gate) * upper).astype(bf16)
+            hidden[top : top + tall, at : at + step] = (half * (1.0 + jnp.tanh(half)) * upper).astype(bf16)
     for copy in copies[2:]:
         copy.wait()
     total = flat.astype(f32) + nn(hidden[...], w_out[...])
@@ -150,14 +147,15 @@
     total = flat.astype(f32)
     for at, step in chunks_of(w_gate.shape[1], 256):
         span = slice(at, at + step)
-        gate = nn(inputs, w_gate[:, span])
+        half = nn(inputs, w_gate[:, span] * 0.5)
         upper = nn(inputs, w_up[:, span])
-        sigma = sigmoid(gate)
-        swished = gate * sigma
+        curve = jnp.tanh(half)
+        raised = 1.0 + curve
+        swished = half * raised
         hidden_part = (swished * upper).astype(bf16)
         swish[:, span] = swished
         hidden[:, span] = hidden_part
-        slope[:, span] = upper * sigma * (1.0 + gate * (1.0 - sigma))
+        slope[:, span] = upper * (0.5 * raised) * (1.0 + half * (1.0 - curve))
         total = total + nn(hidden_part, w_out[span, :])
     upd = total.astype(bf16)
     updated_t[...] = upd.T

time: 28.7 us -> 28.7 us (level)
  no operation moved by 1% of the time
where the time goes in v14:
time: 28.7 us; the launch traced here: 28.6 us
  starting transfers between devices  14.3 us (50%)
  Pallas kernels  7.58 us (26%)
  waiting for transfers between devices  5.91 us (21%)
  between operations  0.71 us (2%)
    ppermute x3, starting transfers between devices, body(): lax.ppermute(hot[p], 'row', [(s, following(s // q, p, groups) * q + cross...  9.26 us
    ppermute x3, starting transfers between devices, body(): terms.append(lax.ppermute(hot[p], ('row', 'col'), pairs))  3.18 us
    ppermute x3, waiting for transfers between devices, body(): lax.ppermute(hot[p], 'row', [(s, following(s // q, p, groups) * q + cross...  2.42 us
    pallas_call x1, Pallas kernels, body(): pl.pallas_call(functools.partial(forward_kernel, q), out_shape=[shaped((q...  2.31 us
    ppermute x3, waiting for transfers between devices, body(): terms.append(lax.ppermute(hot[p], ('row', 'col'), pairs))  2.21 us
    pallas_call x2, Pallas kernels, body(): pl.pallas_call(functools.partial(prepare_kernel, q, p), out_shape=[shaped...  1.77 us
    pallas_call x1, Pallas kernels, body(): pl.pallas_call(functools.partial(backward_kernel, q, (nrow, ncol) if fits...  1.24 us
    ppermute x2, waiting for transfers between devices, returned(): lax.ppermute(x, 'row', core_pairs(nrow, q, n // 2 + 1))  0.86 us
  transfers between devices with their start and end apart: 12, of which 8 were waited for; matrix products, arithmetic and copies ran while one was open for 0% of the time, Pallas kernels for 11%

profile of v14, /device:TPU:0, one launch (start us, length us, event | category | flops | bytes accessed | tf_op | source)
XLA Modules:
  0.0 28.6 jit_solution(11520420556183369504)
XLA Ops:
  0.6 2.3 %forward.1 = (bf16[2,256,128]{2,1,0:T(8,128)(2,1)S(1)}, bf16[128,512]{1,0:T(8,128)(2,1)S(1)}, bf16[128,512]{1,0:T(8,128)(2,1)S(1)}, bf16[512,128]{1,0:T(8,128)(2...) custom-call(bf16[16,32,128]{2,1,0:T(8,128)(2,1)} %refs_0_.1, ...), custom_call_target="tpu_custom_call" | custom-call | tf_op jit(solution)/shard_map/forward/pallas_call | solution.py:358
  3.0 0.5 %collective-permute-start.2 = (bf16[2,128,128]{2,1,0:T(8,128)(2,1)S(1)}, bf16[2,128,128]{2,1,0:T(8,128)(2,1)S(1)}, u32[]{:S(2)}, u32[]{:S(2)}) collective-permute-start(bf16[2,128,128]{2,1,0:T(8,128)(2,1)S(1)} %get-tuple-element.89.refs_17_), channel_id=1, source_target_pairs={{0,4},{1,8},{2,16},{3,24},{4,0},{5,12},{6,20},{7,28},{8,1},{9,13},... | collective-permute-start | bytes 196616 | tf_op jit(solution)/shard_map/ppermute | solution.py:380
  3.5 0.1 collective-permute-start.1
  3.6 0.4 %collective-permute-start = (bf16[128,128]{1,0:T(8,128)(2,1)S(1)}, bf16[128,128]{1,0:T(8,128)(2,1)S(1)}, u32[]{:S(2)}, u32[]{:S(2)}) collective-permute-start(bf16[128,128]{1,0:T(8,128)(2,1)S(1)} %get-tuple-element.80), channel_id=1, source_target_pairs={{0,4},{4,0},{8,12},{12,8},{16,20},{20,16},{24,28},{28,24},{1,5},{5... | collective-permute-start | bytes 98312 | tf_op jit(solution)/shard_map/ppermute | solution.py:389
  4.0 0.9 %prepare.2 = (bf16[128,256]{1,0:T(8,128)(2,1)S(1)}, bf16[128,256]{1,0:T(8,128)(2,1)S(1)}, bf16[256,512]{1,0:T(8,128)(2,1)S(1)}, f32[256,512]{1,0:T(8,128)S(1)}, ...) custom-call(bf16[2,256,128]{2,1,0:T(8,128)(2,1)S(1)} %get-tuple-elem, ...), custom_call_target="tpu_custom_call" | custom-call | flops 100663296 | bytes 1048576 | tf_op jit(solution)/shard_map/prepare/pallas_call | solution.py:394
  4.9 0.0 collective-permute-done.refs_0_
  4.9 0.0 collective-permute-done.1.refs_1_
  4.9 0.9 %prepare.3 = (bf16[128,256]{1,0:T(8,128)(2,1)S(1)}, bf16[128,256]{1,0:T(8,128)(2,1)S(1)}, bf16[256,512]{1,0:T(8,128)(2,1)S(1)}, f32[256,512]{1,0:T(8,128)S(1)}, ...) custom-call(bf16[128,128]{1,0:T(8,128)(2,1)S(1)} %collective-permute, ...), custom_call_target="tpu_custom_call" | custom-call | tf_op jit(solution)/shard_map/prepare/pallas_call | solution.py:394
  5.8 0.0 collective-permute-done.2.refs_16_
  5.8 1.2 %backward.1 = (f32[512,128]{1,0:T(8,128)S(1)}, bf16[512,512]{1,0:T(8,128)(2,1)S(1)}, bf16[512,512]{1,0:T(8,128)(2,1)S(1)}, bf16[4,208,128]{2,1,0:T(8,128)(2,1)S(1)}, bf16[4,208,128]{2,1,0:T(8,128)(2,1)S(1)}) custom-call(bf16[128,256]{1,0:T(8,128)(2,1)S(1)} %get-tuple-element.73.refs_0_, bf16[128,256]{1,0:T(8,128)(2,1)S(1)} %get-tuple-element.74.refs_1_, ...), custom_call_target="tpu_custom_call" | custom-call | flops 268435456 | bytes 1048576 | tf_op jit(solution)/shard_map/backward/pallas_call | solution.py:426
  7.1 0.4 %collective-permute-start.3 = (bf16[4,208,128]{2,1,0:T(8,128)(2,1)S(1)}, bf16[4,208,128]{2,1,0:T(8,128)(2,1)S(1)}, u32[]{:S(2)}, u32[]{:S(2)}) collective-permute-start(bf16[4,208,128]{2,1,0:T(8,128)(2,1)S(1)} %get-tuple-element.91), channel_id=1, source_target_pairs={{0,4},{4,0},{8,12},{12,8},{16,20},{20,16},{24,28},{28,24},{1,5},{5... | collective-permute-start | bytes 638984 | tf_op jit(solution)/shard_map/ppermute | solution.py:477
  7.4 0.4 %d_inputs.3.rest_2_ = bf16[256,128]{1,0:T(8,128)(2,1)S(1)} custom-call(f32[512,128]{1,0:T(8,128)S(1)} %get-tuple-element.92.d_updated, bf16[512,512]{1,0:T(8,128)(2,1)S(1)} %get-tuple-element.93.d_gate, bf16[512,512]{1,0:T(8,128)(2,1)S(1)} %get-tuple-element.94.d_up, f32[256,128]{1,0:T(8,128)S(1)} %get-tuple-element.97.normed, ...), custom_call_target="tpu_custom_call" | custom-call | flops 67108864 | bytes 524288 | tf_op jit(solution)/shard_map/d_inputs/pallas_call | solution.py:439
  7.8 0.4 %d_inputs.2.refs_0_ = bf16[256,128]{1,0:T(8,128)(2,1)S(1)} custom-call(f32[512,128]{1,0:T(8,128)S(1)} %get-tuple-element.92.d_updated, bf16[512,512]{1,0:T(8,128)(2,1)S(1)} %get-tuple-element.93.d_gate, bf16[512,512]{1,0:T(8,128)(2,1)S(1)} %get-tuple-element.94.d_up, f32[256,128]{1,0:T(8,128)S(1)} %get-tuple-element.95.normed, ...), custom_call_target="tpu_custom_call" | custom-call | flops 67108864 | bytes 524288 | tf_op jit(solution)/shard_map/d_inputs/pallas_call | solution.py:439
  8.2 0.4 %collective-permute-done.3.rest_1_ = bf16[4,208,128]{2,1,0:T(8,128)(2,1)S(1)} collective-permute-done((bf16[4,208,128]{2,1,0:T(8,128)(2,1)S(1)}, bf16[4,208,128]{2,1,0:T(8,128)(2,1)S(1)}, u32[]{:S(2)}, u32[]{:S(2)}) %collective-permute-start.3) | collective-permute-done | bytes 213024 | tf_op jit(solution)/shard_map/ppermute | solution.py:477
  8.6 0.1 core_sum.1
  8.7 7.0 %collective-permute-start.4 = (bf16[208,128]{1,0:T(8,128)(2,1)S(1)}, bf16[208,128]{1,0:T(8,128)(2,1)S(1)}, u32[]{:S(2)}, u32[]{:S(2)}) collective-permute-start(bf16[208,128]{1,0:T(8,128)(2,1)S(1)} %get-tuple-element.103), channel_id=1, source_target_pairs={{0,12},{4,8},{8,20},{12,16},{16,28},{20,24},{24,4},{28,0},{1,13},{... | collective-permute-start | bytes 159752 | tf_op jit(solution)/shard_map/ppermute | solution.py:490
  15.6 2.3 %collective-permute-start.5 = (bf16[208,128]{1,0:T(8,128)(2,1)S(1)}, bf16[208,128]{1,0:T(8,128)(2,1)S(1)}, u32[]{:S(2)}, u32[]{:S(2)}) collective-permute-start(bf16[208,128]{1,0:T(8,128)(2,1)S(1)} %get-tuple-element.104), channel_id=1, source_target_pairs={{0,20},{4,16},{8,28},{12,24},{16,4},{20,0},{24,12},{28,8},{1,21},{... | collective-permute-start | bytes 159752 | tf_op jit(solution)/shard_map/ppermute | solution.py:490
  17.9 0.0 collective-permute-start.6
  17.9 0.2 collective-permute-start.7
  18.1 0.4 %collective-permute-start.8 = (bf16[128,128]{1,0:T(8,128)(2,1)S(1)}, bf16[128,128]{1,0:T(8,128)(2,1)S(1)}, u32[]{:S(2)}, u32[]{:S(2)}) collective-permute-start(bf16[128,128]{1,0:T(8,128)(2,1)S(1)} %get-tuple-element.108), channel_id=1, source_target_pairs={{0,4},{4,0},{8,12},{12,8},{16,20},{20,16},{24,28},{28,24},{1,5},{5... | collective-permute-start | bytes 98312 | tf_op jit(solution)/shard_map/ppermute | solution.py:452
  18.4 0.7 %collective-permute-done.7.refs_1_ = bf16[128,128]{1,0:T(8,128)(2,1)S(1)} collective-permute-done((bf16[128,128]{1,0:T(8,128)(2,1)S(1)}, bf16[128,128]{1,0:T(8,128)(2,1)S(1)}, u32[]{:S(2)}, u32[]{:S(2)}) %collective-permute-start.7) | collective-permute-done | bytes 32800 | tf_op jit(solution)/shard_map/ppermute | solution.py:452
  19.1 0.2 collective-permute-done.8.refs_2_
  19.3 0.0 collective-permute-done.4.rest_1_
  19.3 1.6 %collective-permute-done.5.rest_2_ = bf16[208,128]{1,0:T(8,128)(2,1)S(1)} collective-permute-done((bf16[208,128]{1,0:T(8,128)(2,1)S(1)}, bf16[208,128]{1,0:T(8,128)(2,1)S(1)}, u32[]{:S(2)}, u32[]{:S(2)}) %collective-permute-start.5) | collective-permute-done | bytes 53280 | tf_op jit(solution)/shard_map/ppermute | solution.py:490
  20.9 0.8 %collective-permute-done.6.rest_3_ = bf16[208,128]{1,0:T(8,128)(2,1)S(1)} collective-permute-done((bf16[208,128]{1,0:T(8,128)(2,1)S(1)}, bf16[208,128]{1,0:T(8,128)(2,1)S(1)}, u32[]{:S(2)}, u32[]{:S(2)}) %collective-permute-start.6) | collective-permute-done | bytes 53280 | tf_op jit(solution)/shard_map/ppermute | solution.py:490
  21.7 0.1 chip_sum.1
  21.8 0.5 %collective-permute-start.9 = (bf16[64,128]{1,0:T(8,128)(2,1)S(1)}, bf16[64,128]{1,0:T(8,128)(2,1)S(1)}, u32[]{:S(2)}, u32[]{:S(2)}) collective-permute-start(bf16[64,128]{1,0:T(8,128)(2,1)S(1)} %get-tuple-element.114), channel_id=1, source_target_pairs={{0,6},{1,7},{2,4},{3,5},{4,2},{5,3},{6,0},{7,1},{8,14},{9,15},{10,... | collective-permute-start | bytes 49160 | tf_op jit(solution)/shard_map/ppermute | solution.py:509
  22.3 2.3 %collective-permute-start.10 = (bf16[64,128]{1,0:T(8,128)(2,1)S(1)}, bf16[64,128]{1,0:T(8,128)(2,1)S(1)}, u32[]{:S(2)}, u32[]{:S(2)}) collective-permute-start(bf16[64,128]{1,0:T(8,128)(2,1)S(1)} %get-tuple-element.115), channel_id=1, source_target_pairs={{0,7},{1,6},{2,5},{3,4},{4,3},{5,2},{6,1},{7,0},{8,15},{9,14},{10,... | collective-permute-start | bytes 49160 | tf_op jit(solution)/shard_map/ppermute | solution.py:509
  24.5 0.5 %collective-permute-start.11 = (bf16[64,128]{1,0:T(8,128)(2,1)S(1)}, bf16[64,128]{1,0:T(8,128)(2,1)S(1)}, u32[]{:S(2)}, u32[]{:S(2)}) collective-permute-start(bf16[64,128]{1,0:T(8,128)(2,1)S(1)} %get-tuple-element.116), channel_id=1, source_target_pairs={{0,5},{1,4},{2,7},{3,6},{4,1},{5,0},{6,3},{7,2},{8,13},{9,12},{10,... | collective-permute-start | bytes 49160 | tf_op jit(solution)/shard_map/ppermute | solution.py:509
  25.0 0.7 %place.1 = bf16[16,2,16,128]{3,2,1,0:T(8,128)(2,1)} custom-call(bf16[256,128]{1,0:T(8,128)(2,1)S(1)} %d_inputs.2.refs_0_, bf16[128,128]{1,0:T(8,128)(2,1)S(1)} %collective-permute-done.7.refs_1_, bf16[128,128]{1,0:T(8,128)(2,1)S(1)} %collective-permute-done.8.refs_2_), custom_call_target="tpu_custom_call" | custom-call | tf_op jit(solution)/shard_map/place/pallas_call | solution.py:456
  25.7 0.4 %collective-permute-done.9.rest_1_ = bf16[64,128]{1,0:T(8,128)(2,1)S(1)} collective-permute-done((bf16[64,128]{1,0:T(8,128)(2,1)S(1)}, bf16[64,128]{1,0:T(8,128)(2,1)S(1)}, u32[]{:S(2)}, u32[]{:S(2)}) %collective-permute-start.9) | collective-permute-done | bytes 16416 | tf_op jit(solution)/shard_map/ppermute | solution.py:509
  26.0 1.2 %collective-permute-done.10.rest_2_ = bf16[64,128]{1,0:T(8,128)(2,1)S(1)} collective-permute-done((bf16[64,128]{1,0:T(8,128)(2,1)S(1)}, bf16[64,128]{1,0:T(8,128)(2,1)S(1)}, u32[]{:S(2)}, u32[]{:S(2)}) %collective-permute-start.10) | collective-permute-done | bytes 16416 | tf_op jit(solution)/shard_map/ppermute | solution.py:509
  27.2 0.6 %collective-permute-done.11.rest_3_ = bf16[64,128]{1,0:T(8,128)(2,1)S(1)} collective-permute-done((bf16[64,128]{1,0:T(8,128)(2,1)S(1)}, bf16[64,128]{1,0:T(8,128)(2,1)S(1)}, u32[]{:S(2)}, u32[]{:S(2)}) %collective-permute-start.11) | collective-permute-done | bytes 16416 | tf_op jit(solution)/shard_map/ppermute | solution.py:509
  27.9 0.7 %col_sum.1 = (f32[16,128]{1,0:T(8,128)}, f32[16,128]{1,0:T(8,128)}, f32[32,64]{1,0:T(8,128)}, f32[16,16]{1,0:T(8,128)}) custom-call(bf16[64,128]{1,0:T(8,128)(2,1)S(1)} %get-tuple-element.121.rest_0_, bf16[64,128]{1,0:T(8,128)(2,1)S(1)} %collective-permute-done.9.rest_1_, bf16[64,128]{1,0:T(8,128)(2,1)S(1)} %collective-permute-done.10.rest_2_, ...), custom_call_target="tpu_custom_call" | custom-call | tf_op jit(solution)/shard_map/col_sum/pallas_call | solution.py:511
  (1 shorter events, 0.0 us)
Async XLA Ops:
  3.0 2.9 %collective-permute-start.2 = (bf16[2,128,128]{2,1,0:T(8,128)(2,1)S(1)}, bf16[2,128,128]{2,1,0:T(8,128)(2,1)S(1)}, u32[]{:S(2)}, u32[]{:S(2)}) collective-permute-start(bf16[2,128,128]{2,1,0:T(8,128)(2,1)S(1)} %get-tuple-element.89.refs_17_), channel_id=1, source_target_pairs={{0,4},{1,8},{2,16},{3,24},{4,0},{5,12},{6,20},{7,28},{8,1},{9,13},... | collective-permute-start | bytes 196616 | tf_op jit(solution)/shard_map/ppermute | solution.py:380
  3.5 1.4 %collective-permute-start.1 = (bf16[144,128]{1,0:T(8,128)(2,1)S(1)}, bf16[144,128]{1,0:T(8,128)(2,1)S(1)}, u32[]{:S(2)}, u32[]{:S(2)}) collective-permute-start(bf16[144,128]{1,0:T(8,128)(2,1)S(1)} %get-tuple-element.81), channel_id=1, source_target_pairs={{0,4},{4,0},{8,12},{12,8},{16,20},{20,16},{24,28},{28,24},{1,5},{5... | collective-permute-start | bytes 110600 | tf_op jit(solution)/shard_map/ppermute | solution.py:389
  3.6 1.3 %collective-permute-start = (bf16[128,128]{1,0:T(8,128)(2,1)S(1)}, bf16[128,128]{1,0:T(8,128)(2,1)S(1)}, u32[]{:S(2)}, u32[]{:S(2)}) collective-permute-start(bf16[128,128]{1,0:T(8,128)(2,1)S(1)} %get-tuple-element.80), channel_id=1, source_target_pairs={{0,4},{4,0},{8,12},{12,8},{16,20},{20,16},{24,28},{28,24},{1,5},{5... | collective-permute-start | bytes 98312 | tf_op jit(solution)/shard_map/ppermute | solution.py:389
  7.1 1.5 %collective-permute-start.3 = (bf16[4,208,128]{2,1,0:T(8,128)(2,1)S(1)}, bf16[4,208,128]{2,1,0:T(8,128)(2,1)S(1)}, u32[]{:S(2)}, u32[]{:S(2)}) collective-permute-start(bf16[4,208,128]{2,1,0:T(8,128)(2,1)S(1)} %get-tuple-element.91), channel_id=1, source_target_pairs={{0,4},{4,0},{8,12},{12,8},{16,20},{20,16},{24,28},{28,24},{1,5},{5... | collective-permute-start | bytes 638984 | tf_op jit(solution)/shard_map/ppermute | solution.py:477
  8.7 10.6 %collective-permute-start.4 = (bf16[208,128]{1,0:T(8,128)(2,1)S(1)}, bf16[208,128]{1,0:T(8,128)(2,1)S(1)}, u32[]{:S(2)}, u32[]{:S(2)}) collective-permute-start(bf16[208,128]{1,0:T(8,128)(2,1)S(1)} %get-tuple-element.103), channel_id=1, source_target_pairs={{0,12},{4,8},{8,20},{12,16},{16,28},{20,24},{24,4},{28,0},{1,13},{... | collective-permute-start | bytes 159752 | tf_op jit(solution)/shard_map/ppermute | solution.py:490
  15.6 5.2 %collective-permute-start.5 = (bf16[208,128]{1,0:T(8,128)(2,1)S(1)}, bf16[208,128]{1,0:T(8,128)(2,1)S(1)}, u32[]{:S(2)}, u32[]{:S(2)}) collective-permute-start(bf16[208,128]{1,0:T(8,128)(2,1)S(1)} %get-tuple-element.104), channel_id=1, source_target_pairs={{0,20},{4,16},{8,28},{12,24},{16,4},{20,0},{24,12},{28,8},{1,21},{... | collective-permute-start | bytes 159752 | tf_op jit(solution)/shard_map/ppermute | solution.py:490
  17.9 3.8 %collective-permute-start.6 = (bf16[208,128]{1,0:T(8,128)(2,1)S(1)}, bf16[208,128]{1,0:T(8,128)(2,1)S(1)}, u32[]{:S(2)}, u32[]{:S(2)}) collective-permute-start(bf16[208,128]{1,0:T(8,128)(2,1)S(1)} %get-tuple-element.105), channel_id=1, source_target_pairs={{0,28},{4,24},{8,4},{12,0},{16,12},{20,8},{24,20},{28,16},{1,29},{... | collective-permute-start | bytes 159752 | tf_op jit(solution)/shard_map/ppermute | solution.py:490
  17.9 1.2 %collective-permute-start.7 = (bf16[128,128]{1,0:T(8,128)(2,1)S(1)}, bf16[128,128]{1,0:T(8,128)(2,1)S(1)}, u32[]{:S(2)}, u32[]{:S(2)}) collective-permute-start(bf16[128,128]{1,0:T(8,128)(2,1)S(1)} %get-tuple-element.107), channel_id=1, source_target_pairs={{0,4},{4,0},{8,12},{12,8},{16,20},{20,16},{24,28},{28,24},{1,5},{5... | collective-permute-start | bytes 98312 | tf_op jit(solution)/shard_map/ppermute | solution.py:452
  18.1 1.2 %collective-permute-start.8 = (bf16[128,128]{1,0:T(8,128)(2,1)S(1)}, bf16[128,128]{1,0:T(8,128)(2,1)S(1)}, u32[]{:S(2)}, u32[]{:S(2)}) collective-permute-start(bf16[128,128]{1,0:T(8,128)(2,1)S(1)} %get-tuple-element.108), channel_id=1, source_target_pairs={{0,4},{4,0},{8,12},{12,8},{16,20},{20,16},{24,28},{28,24},{1,5},{5... | collective-permute-start | bytes 98312 | tf_op jit(solution)/shard_map/ppermute | solution.py:452
  21.8 4.2 %collective-permute-start.9 = (bf16[64,128]{1,0:T(8,128)(2,1)S(1)}, bf16[64,128]{1,0:T(8,128)(2,1)S(1)}, u32[]{:S(2)}, u32[]{:S(2)}) collective-permute-start(bf16[64,128]{1,0:T(8,128)(2,1)S(1)} %get-tuple-element.114), channel_id=1, source_target_pairs={{0,6},{1,7},{2,4},{3,5},{4,2},{5,3},{6,0},{7,1},{8,14},{9,15},{10,... | collective-permute-start | bytes 49160 | tf_op jit(solution)/shard_map/ppermute | solution.py:509
  22.3 5.0 %collective-permute-start.10 = (bf16[64,128]{1,0:T(8,128)(2,1)S(1)}, bf16[64,128]{1,0:T(8,128)(2,1)S(1)}, u32[]{:S(2)}, u32[]{:S(2)}) collective-permute-start(bf16[64,128]{1,0:T(8,128)(2,1)S(1)} %get-tuple-element.115), channel_id=1, source_target_pairs={{0,7},{1,6},{2,5},{3,4},{4,3},{5,2},{6,1},{7,0},{8,15},{9,14},{10,... | collective-permute-start | bytes 49160 | tf_op jit(solution)/shard_map/ppermute | solution.py:509
  24.5 3.3 %collective-permute-start.11 = (bf16[64,128]{1,0:T(8,128)(2,1)S(1)}, bf16[64,128]{1,0:T(8,128)(2,1)S(1)}, u32[]{:S(2)}, u32[]{:S(2)}) collective-permute-start(bf16[64,128]{1,0:T(8,128)(2,1)S(1)} %get-tuple-element.116), channel_id=1, source_target_pairs={{0,5},{1,4},{2,7},{3,6},{4,1},{5,0},{6,3},{7,2},{8,13},{9,12},{10,... | collective-permute-start | bytes 49160 | tf_op jit(solution)/shard_map/ppermute | solution.py:509

commit v15 on v14

--- a/solution.py
+++ b/solution.py
@@ -32,6 +32,19 @@
     centre = values - jnp.mean(values, axis=-1, keepdims=True)
     scale_inv = lax.rsqrt(jnp.mean(centre * centre, axis=-1, keepdims=True) + eps)
     return centre * scale_inv, scale_inv
+
+
+def row_sums(values):
+    width = values.shape[1]
+    high = values.astype(bf16)
+    low = (values - high.astype(f32)).astype(bf16)
+    return nn(jnp.concatenate([high, low], axis=1), jnp.ones((2 * width, width), bf16))
+
+
+def normalize_rows(flat):
+    width = flat.shape[1]
+    centre = flat.astype(f32) - nn(flat, jnp.ones((width, width), bf16)) * (1.0 / width)
+    return centre * lax.rsqrt(row_sums(centre * centre) * (1.0 / width) + eps)
 
 
 def chunks_of(size, most):
@@ -89,7 +102,7 @@
     for copy in pieces:
         copy.wait()
     flat = pair[...].reshape(q * side, width)
-    inputs = normalize(flat)[0].astype(bf16)
+    inputs = normalize_rows(flat).astype(bf16)
     for copy in copies[:2]:
         copy.wait()
     for at, step in chunks_of(w_gate.shape[1], 256):
@@ -191,7 +204,7 @@
     mirror = jnp.concatenate([mirrored[p, :, u * bins : (u + 1) * bins] for p in range(q) for u in range(packs)], axis=0)
     summed = joined(logits, 0).astype(f32) + mirror.astype(f32)
     powers = jnp.exp(summed - jnp.max(summed, axis=-1, keepdims=True))
-    probs = powers / jnp.sum(powers, axis=-1, keepdims=True)
+    probs = powers / row_sums(powers)
     grad_sym = (probs - joined(onehot, 0)).astype(bf16)
     cotangent = (grad_sym.astype(f32) * 2.0).astype(bf16)
     d_upd = nn(cotangent, w_head[...])

time: 28.7 us -> 29 us (1.010)
  Pallas kernels: 7.58 us -> 7.91 us
where the time goes in v15:
time: 29 us; the launch traced here: 28.9 us
  starting transfers between devices  14.4 us (50%)
  Pallas kernels  7.91 us (27%)
  waiting for transfers between devices  5.9 us (20%)
  between operations  0.71 us (2%)
    ppermute x3, starting transfers between devices, body(): lax.ppermute(hot[p], 'row', [(s, following(s // q, p, groups) * q + cross...  9.27 us
    ppermute x3, starting transfers between devices, body(): terms.append(lax.ppermute(hot[p], ('row', 'col'), pairs))  3.18 us
    pallas_call x1, Pallas kernels, body(): pl.pallas_call(functools.partial(forward_kernel, q), out_shape=[shaped((q...  2.5 us
    ppermute x3, waiting for transfers between devices, body(): lax.ppermute(hot[p], 'row', [(s, following(s // q, p, groups) * q + cross...  2.42 us
    ppermute x3, waiting for transfers between devices, body(): terms.append(lax.ppermute(hot[p], ('row', 'col'), pairs))  2.22 us
    pallas_call x2, Pallas kernels, body(): pl.pallas_call(functools.partial(prepare_kernel, q, p), out_shape=[shaped...  1.77 us
    pallas_call x1, Pallas kernels, body(): pl.pallas_call(functools.partial(backward_kernel, q, (nrow, ncol) if fits...  1.37 us
    ppermute x2, waiting for transfers between devices, returned(): lax.ppermute(x, 'row', core_pairs(nrow, q, n // 2 + 1))  0.86 us
  transfers between devices with their start and end apart: 12, of which 8 were waited for; matrix products, arithmetic and copies ran while one was open for 0% of the time, Pallas kernels for 11%

profile of v15, /device:TPU:0, one launch (start us, length us, event | category | flops | bytes accessed | tf_op | source)
XLA Modules:
  0.0 28.9 jit_solution(3523733192437189777)
XLA Ops:
  0.6 2.5 %forward.1 = (bf16[2,256,128]{2,1,0:T(8,128)(2,1)S(1)}, bf16[128,512]{1,0:T(8,128)(2,1)S(1)}, bf16[128,512]{1,0:T(8,128)(2,1)S(1)}, bf16[512,128]{1,0:T(8,128)(2...) custom-call(bf16[16,32,128]{2,1,0:T(8,128)(2,1)} %refs_0_.1, ...), custom_call_target="tpu_custom_call" | custom-call | tf_op jit(solution)/shard_map/forward/pallas_call | solution.py:371
  3.1 0.5 %collective-permute-start.2 = (bf16[2,128,128]{2,1,0:T(8,128)(2,1)S(1)}, bf16[2,128,128]{2,1,0:T(8,128)(2,1)S(1)}, u32[]{:S(2)}, u32[]{:S(2)}) collective-permute-start(bf16[2,128,128]{2,1,0:T(8,128)(2,1)S(1)} %get-tuple-element.89.refs_17_), channel_id=1, source_target_pairs={{0,4},{1,8},{2,16},{3,24},{4,0},{5,12},{6,20},{7,28},{8,1},{9,13},... | collective-permute-start | bytes 196616 | tf_op jit(solution)/shard_map/ppermute | solution.py:393
  3.7 0.1 collective-permute-start.1
  3.8 0.4 %collective-permute-start = (bf16[128,128]{1,0:T(8,128)(2,1)S(1)}, bf16[128,128]{1,0:T(8,128)(2,1)S(1)}, u32[]{:S(2)}, u32[]{:S(2)}) collective-permute-start(bf16[128,128]{1,0:T(8,128)(2,1)S(1)} %get-tuple-element.80), channel_id=1, source_target_pairs={{0,4},{4,0},{8,12},{12,8},{16,20},{20,16},{24,28},{28,24},{1,5},{5... | collective-permute-start | bytes 98312 | tf_op jit(solution)/shard_map/ppermute | solution.py:402
  4.2 0.9 %prepare.2 = (bf16[128,256]{1,0:T(8,128)(2,1)S(1)}, bf16[128,256]{1,0:T(8,128)(2,1)S(1)}, bf16[256,512]{1,0:T(8,128)(2,1)S(1)}, f32[256,512]{1,0:T(8,128)S(1)}, ...) custom-call(bf16[2,256,128]{2,1,0:T(8,128)(2,1)S(1)} %get-tuple-elem, ...), custom_call_target="tpu_custom_call" | custom-call | flops 100663296 | bytes 1048576 | tf_op jit(solution)/shard_map/prepare/pallas_call | solution.py:407
  5.1 0.0 collective-permute-done.refs_0_
  5.1 0.0 collective-permute-done.1.refs_1_
  5.1 0.9 %prepare.3 = (bf16[128,256]{1,0:T(8,128)(2,1)S(1)}, bf16[128,256]{1,0:T(8,128)(2,1)S(1)}, bf16[256,512]{1,0:T(8,128)(2,1)S(1)}, f32[256,512]{1,0:T(8,128)S(1)}, ...) custom-call(bf16[128,128]{1,0:T(8,128)(2,1)S(1)} %collective-permute, ...), custom_call_target="tpu_custom_call" | custom-call | tf_op jit(solution)/shard_map/prepare/pallas_call | solution.py:407
  6.0 0.0 collective-permute-done.2.refs_16_
  6.0 1.4 %backward.1 = (f32[512,128]{1,0:T(8,128)S(1)}, bf16[512,512]{1,0:T(8,128)(2,1)S(1)}, bf16[512,512]{1,0:T(8,128)(2,1)S(1)}, bf16[4,208,128]{2,1,0:T(8,128)(2,1)S(1)}, bf16[4,208,128]{2,1,0:T(8,128)(2,1)S(1)}) custom-call(bf16[128,256]{1,0:T(8,128)(2,1)S(1)} %get-tuple-element.73.refs_0_, bf16[128,256]{1,0:T(8,128)(2,1)S(1)} %get-tuple-element.74.refs_1_, ...), custom_call_target="tpu_custom_call" | custom-call | flops 268435456 | bytes 1048576 | tf_op jit(solution)/shard_map/backward/pallas_call | solution.py:439
  7.4 0.4 %collective-permute-start.3 = (bf16[4,208,128]{2,1,0:T(8,128)(2,1)S(1)}, bf16[4,208,128]{2,1,0:T(8,128)(2,1)S(1)}, u32[]{:S(2)}, u32[]{:S(2)}) collective-permute-start(bf16[4,208,128]{2,1,0:T(8,128)(2,1)S(1)} %get-tuple-element.91), channel_id=1, source_target_pairs={{0,4},{4,0},{8,12},{12,8},{16,20},{20,16},{24,28},{28,24},{1,5},{5... | collective-permute-start | bytes 638984 | tf_op jit(solution)/shard_map/ppermute | solution.py:490
  7.8 0.4 %d_inputs.3.rest_2_ = bf16[256,128]{1,0:T(8,128)(2,1)S(1)} custom-call(f32[512,128]{1,0:T(8,128)S(1)} %get-tuple-element.92.d_updated, bf16[512,512]{1,0:T(8,128)(2,1)S(1)} %get-tuple-element.93.d_gate, bf16[512,512]{1,0:T(8,128)(2,1)S(1)} %get-tuple-element.94.d_up, f32[256,128]{1,0:T(8,128)S(1)} %get-tuple-element.97.normed, ...), custom_call_target="tpu_custom_call" | custom-call | flops 67108864 | bytes 524288 | tf_op jit(solution)/shard_map/d_inputs/pallas_call | solution.py:452
  8.1 0.4 %d_inputs.2.refs_0_ = bf16[256,128]{1,0:T(8,128)(2,1)S(1)} custom-call(f32[512,128]{1,0:T(8,128)S(1)} %get-tuple-element.92.d_updated, bf16[512,512]{1,0:T(8,128)(2,1)S(1)} %get-tuple-element.93.d_gate, bf16[512,512]{1,0:T(8,128)(2,1)S(1)} %get-tuple-element.94.d_up, f32[256,128]{1,0:T(8,128)S(1)} %get-tuple-element.95.normed, ...), custom_call_target="tpu_custom_call" | custom-call | flops 67108864 | bytes 524288 | tf_op jit(solution)/shard_map/d_inputs/pallas_call | solution.py:452
  8.5 0.4 %collective-permute-done.3.rest_1_ = bf16[4,208,128]{2,1,0:T(8,128)(2,1)S(1)} collective-permute-done((bf16[4,208,128]{2,1,0:T(8,128)(2,1)S(1)}, bf16[4,208,128]{2,1,0:T(8,128)(2,1)S(1)}, u32[]{:S(2)}, u32[]{:S(2)}) %collective-permute-start.3) | collective-permute-done | bytes 213024 | tf_op jit(solution)/shard_map/ppermute | solution.py:490
  8.9 0.1 core_sum.1
  9.0 7.0 %collective-permute-start.4 = (bf16[208,128]{1,0:T(8,128)(2,1)S(1)}, bf16[208,128]{1,0:T(8,128)(2,1)S(1)}, u32[]{:S(2)}, u32[]{:S(2)}) collective-permute-start(bf16[208,128]{1,0:T(8,128)(2,1)S(1)} %get-tuple-element.103), channel_id=1, source_target_pairs={{0,12},{4,8},{8,20},{12,16},{16,28},{20,24},{24,4},{28,0},{1,13},{... | collective-permute-start | bytes 159752 | tf_op jit(solution)/shard_map/ppermute | solution.py:503
  16.0 2.3 %collective-permute-start.5 = (bf16[208,128]{1,0:T(8,128)(2,1)S(1)}, bf16[208,128]{1,0:T(8,128)(2,1)S(1)}, u32[]{:S(2)}, u32[]{:S(2)}) collective-permute-start(bf16[208,128]{1,0:T(8,128)(2,1)S(1)} %get-tuple-element.104), channel_id=1, source_target_pairs={{0,20},{4,16},{8,28},{12,24},{16,4},{20,0},{24,12},{28,8},{1,21},{... | collective-permute-start | bytes 159752 | tf_op jit(solution)/shard_map/ppermute | solution.py:503
  18.3 0.0 collective-permute-start.6
  18.3 0.2 collective-permute-start.7
  18.4 0.4 %collective-permute-start.8 = (bf16[128,128]{1,0:T(8,128)(2,1)S(1)}, bf16[128,128]{1,0:T(8,128)(2,1)S(1)}, u32[]{:S(2)}, u32[]{:S(2)}) collective-permute-start(bf16[128,128]{1,0:T(8,128)(2,1)S(1)} %get-tuple-element.108), channel_id=1, source_target_pairs={{0,4},{4,0},{8,12},{12,8},{16,20},{20,16},{24,28},{28,24},{1,5},{5... | collective-permute-start | bytes 98312 | tf_op jit(solution)/shard_map/ppermute | solution.py:465
  18.8 0.7 %collective-permute-done.7.refs_1_ = bf16[128,128]{1,0:T(8,128)(2,1)S(1)} collective-permute-done((bf16[128,128]{1,0:T(8,128)(2,1)S(1)}, bf16[128,128]{1,0:T(8,128)(2,1)S(1)}, u32[]{:S(2)}, u32[]{:S(2)}) %collective-permute-start.7) | collective-permute-done | bytes 32800 | tf_op jit(solution)/shard_map/ppermute | solution.py:465
  19.5 0.2 collective-permute-done.8.refs_2_
  19.6 0.0 collective-permute-done.4.rest_1_
  19.6 1.6 %collective-permute-done.5.rest_2_ = bf16[208,128]{1,0:T(8,128)(2,1)S(1)} collective-permute-done((bf16[208,128]{1,0:T(8,128)(2,1)S(1)}, bf16[208,128]{1,0:T(8,128)(2,1)S(1)}, u32[]{:S(2)}, u32[]{:S(2)}) %collective-permute-start.5) | collective-permute-done | bytes 53280 | tf_op jit(solution)/shard_map/ppermute | solution.py:503
  21.2 0.8 %collective-permute-done.6.rest_3_ = bf16[208,128]{1,0:T(8,128)(2,1)S(1)} collective-permute-done((bf16[208,128]{1,0:T(8,128)(2,1)S(1)}, bf16[208,128]{1,0:T(8,128)(2,1)S(1)}, u32[]{:S(2)}, u32[]{:S(2)}) %collective-permute-start.6) | collective-permute-done | bytes 53280 | tf_op jit(solution)/shard_map/ppermute | solution.py:503
  22.1 0.1 chip_sum.1
  22.1 0.5 %collective-permute-start.9 = (bf16[64,128]{1,0:T(8,128)(2,1)S(1)}, bf16[64,128]{1,0:T(8,128)(2,1)S(1)}, u32[]{:S(2)}, u32[]{:S(2)}) collective-permute-start(bf16[64,128]{1,0:T(8,128)(2,1)S(1)} %get-tuple-element.114), channel_id=1, source_target_pairs={{0,6},{1,7},{2,4},{3,5},{4,2},{5,3},{6,0},{7,1},{8,14},{9,15},{10,... | collective-permute-start | bytes 49160 | tf_op jit(solution)/shard_map/ppermute | solution.py:522
  22.6 2.3 %collective-permute-start.10 = (bf16[64,128]{1,0:T(8,128)(2,1)S(1)}, bf16[64,128]{1,0:T(8,128)(2,1)S(1)}, u32[]{:S(2)}, u32[]{:S(2)}) collective-permute-start(bf16[64,128]{1,0:T(8,128)(2,1)S(1)} %get-tuple-element.115), channel_id=1, source_target_pairs={{0,7},{1,6},{2,5},{3,4},{4,3},{5,2},{6,1},{7,0},{8,15},{9,14},{10,... | collective-permute-start | bytes 49160 | tf_op jit(solution)/shard_map/ppermute | solution.py:522
  24.9 0.5 %collective-permute-start.11 = (bf16[64,128]{1,0:T(8,128)(2,1)S(1)}, bf16[64,128]{1,0:T(8,128)(2,1)S(1)}, u32[]{:S(2)}, u32[]{:S(2)}) collective-permute-start(bf16[64,128]{1,0:T(8,128)(2,1)S(1)} %get-tuple-element.116), channel_id=1, source_target_pairs={{0,5},{1,4},{2,7},{3,6},{4,1},{5,0},{6,3},{7,2},{8,13},{9,12},{10,... | collective-permute-start | bytes 49160 | tf_op jit(solution)/shard_map/ppermute | solution.py:522
  25.3 0.7 %place.1 = bf16[16,2,16,128]{3,2,1,0:T(8,128)(2,1)} custom-call(bf16[256,128]{1,0:T(8,128)(2,1)S(1)} %d_inputs.2.refs_0_, bf16[128,128]{1,0:T(8,128)(2,1)S(1)} %collective-permute-done.7.refs_1_, bf16[128,128]{1,0:T(8,128)(2,1)S(1)} %collective-permute-done.8.refs_2_), custom_call_target="tpu_custom_call" | custom-call | tf_op jit(solution)/shard_map/place/pallas_call | solution.py:469
  26.0 0.4 %collective-permute-done.9.rest_1_ = bf16[64,128]{1,0:T(8,128)(2,1)S(1)} collective-permute-done((bf16[64,128]{1,0:T(8,128)(2,1)S(1)}, bf16[64,128]{1,0:T(8,128)(2,1)S(1)}, u32[]{:S(2)}, u32[]{:S(2)}) %collective-permute-start.9) | collective-permute-done | bytes 16416 | tf_op jit(solution)/shard_map/ppermute | solution.py:522
  26.4 1.2 %collective-permute-done.10.rest_2_ = bf16[64,128]{1,0:T(8,128)(2,1)S(1)} collective-permute-done((bf16[64,128]{1,0:T(8,128)(2,1)S(1)}, bf16[64,128]{1,0:T(8,128)(2,1)S(1)}, u32[]{:S(2)}, u32[]{:S(2)}) %collective-permute-start.10) | collective-permute-done | bytes 16416 | tf_op jit(solution)/shard_map/ppermute | solution.py:522
  27.6 0.7 %collective-permute-done.11.rest_3_ = bf16[64,128]{1,0:T(8,128)(2,1)S(1)} collective-permute-done((bf16[64,128]{1,0:T(8,128)(2,1)S(1)}, bf16[64,128]{1,0:T(8,128)(2,1)S(1)}, u32[]{:S(2)}, u32[]{:S(2)}) %collective-permute-start.11) | collective-permute-done | bytes 16416 | tf_op jit(solution)/shard_map/ppermute | solution.py:522
  28.2 0.7 %col_sum.1 = (f32[16,128]{1,0:T(8,128)}, f32[16,128]{1,0:T(8,128)}, f32[32,64]{1,0:T(8,128)}, f32[16,16]{1,0:T(8,128)}) custom-call(bf16[64,128]{1,0:T(8,128)(2,1)S(1)} %get-tuple-element.121.rest_0_, bf16[64,128]{1,0:T(8,128)(2,1)S(1)} %collective-permute-done.9.rest_1_, bf16[64,128]{1,0:T(8,128)(2,1)S(1)} %collective-permute-done.10.rest_2_, ...), custom_call_target="tpu_custom_call" | custom-call | tf_op jit(solution)/shard_map/col_sum/pallas_call | solution.py:524
  (1 shorter events, 0.0 us)
Async XLA Ops:
  3.1 2.9 %collective-permute-start.2 = (bf16[2,128,128]{2,1,0:T(8,128)(2,1)S(1)}, bf16[2,128,128]{2,1,0:T(8,128)(2,1)S(1)}, u32[]{:S(2)}, u32[]{:S(2)}) collective-permute-start(bf16[2,128,128]{2,1,0:T(8,128)(2,1)S(1)} %get-tuple-element.89.refs_17_), channel_id=1, source_target_pairs={{0,4},{1,8},{2,16},{3,24},{4,0},{5,12},{6,20},{7,28},{8,1},{9,13},... | collective-permute-start | bytes 196616 | tf_op jit(solution)/shard_map/ppermute | solution.py:393
  3.7 1.4 %collective-permute-start.1 = (bf16[144,128]{1,0:T(8,128)(2,1)S(1)}, bf16[144,128]{1,0:T(8,128)(2,1)S(1)}, u32[]{:S(2)}, u32[]{:S(2)}) collective-permute-start(bf16[144,128]{1,0:T(8,128)(2,1)S(1)} %get-tuple-element.81), channel_id=1, source_target_pairs={{0,4},{4,0},{8,12},{12,8},{16,20},{20,16},{24,28},{28,24},{1,5},{5... | collective-permute-start | bytes 110600 | tf_op jit(solution)/shard_map/ppermute | solution.py:402
  3.8 1.3 %collective-permute-start = (bf16[128,128]{1,0:T(8,128)(2,1)S(1)}, bf16[128,128]{1,0:T(8,128)(2,1)S(1)}, u32[]{:S(2)}, u32[]{:S(2)}) collective-permute-start(bf16[128,128]{1,0:T(8,128)(2,1)S(1)} %get-tuple-element.80), channel_id=1, source_target_pairs={{0,4},{4,0},{8,12},{12,8},{16,20},{20,16},{24,28},{28,24},{1,5},{5... | collective-permute-start | bytes 98312 | tf_op jit(solution)/shard_map/ppermute | solution.py:402
  7.4 1.5 %collective-permute-start.3 = (bf16[4,208,128]{2,1,0:T(8,128)(2,1)S(1)}, bf16[4,208,128]{2,1,0:T(8,128)(2,1)S(1)}, u32[]{:S(2)}, u32[]{:S(2)}) collective-permute-start(bf16[4,208,128]{2,1,0:T(8,128)(2,1)S(1)} %get-tuple-element.91), channel_id=1, source_target_pairs={{0,4},{4,0},{8,12},{12,8},{16,20},{20,16},{24,28},{28,24},{1,5},{5... | collective-permute-start | bytes 638984 | tf_op jit(solution)/shard_map/ppermute | solution.py:490
  9.0 10.6 %collective-permute-start.4 = (bf16[208,128]{1,0:T(8,128)(2,1)S(1)}, bf16[208,128]{1,0:T(8,128)(2,1)S(1)}, u32[]{:S(2)}, u32[]{:S(2)}) collective-permute-start(bf16[208,128]{1,0:T(8,128)(2,1)S(1)} %get-tuple-element.103), channel_id=1, source_target_pairs={{0,12},{4,8},{8,20},{12,16},{16,28},{20,24},{24,4},{28,0},{1,13},{... | collective-permute-start | bytes 159752 | tf_op jit(solution)/shard_map/ppermute | solution.py:503
  16.0 5.2 %collective-permute-start.5 = (bf16[208,128]{1,0:T(8,128)(2,1)S(1)}, bf16[208,128]{1,0:T(8,128)(2,1)S(1)}, u32[]{:S(2)}, u32[]{:S(2)}) collective-permute-start(bf16[208,128]{1,0:T(8,128)(2,1)S(1)} %get-tuple-element.104), channel_id=1, source_target_pairs={{0,20},{4,16},{8,28},{12,24},{16,4},{20,0},{24,12},{28,8},{1,21},{... | collective-permute-start | bytes 159752 | tf_op jit(solution)/shard_map/ppermute | solution.py:503
  18.3 3.8 %collective-permute-start.6 = (bf16[208,128]{1,0:T(8,128)(2,1)S(1)}, bf16[208,128]{1,0:T(8,128)(2,1)S(1)}, u32[]{:S(2)}, u32[]{:S(2)}) collective-permute-start(bf16[208,128]{1,0:T(8,128)(2,1)S(1)} %get-tuple-element.105), channel_id=1, source_target_pairs={{0,28},{4,24},{8,4},{12,0},{16,12},{20,8},{24,20},{28,16},{1,29},{... | collective-permute-start | bytes 159752 | tf_op jit(solution)/shard_map/ppermute | solution.py:503
  18.3 1.2 %collective-permute-start.7 = (bf16[128,128]{1,0:T(8,128)(2,1)S(1)}, bf16[128,128]{1,0:T(8,128)(2,1)S(1)}, u32[]{:S(2)}, u32[]{:S(2)}) collective-permute-start(bf16[128,128]{1,0:T(8,128)(2,1)S(1)} %get-tuple-element.107), channel_id=1, source_target_pairs={{0,4},{4,0},{8,12},{12,8},{16,20},{20,16},{24,28},{28,24},{1,5},{5... | collective-permute-start | bytes 98312 | tf_op jit(solution)/shard_map/ppermute | solution.py:465
  18.4 1.2 %collective-permute-start.8 = (bf16[128,128]{1,0:T(8,128)(2,1)S(1)}, bf16[128,128]{1,0:T(8,128)(2,1)S(1)}, u32[]{:S(2)}, u32[]{:S(2)}) collective-permute-start(bf16[128,128]{1,0:T(8,128)(2,1)S(1)} %get-tuple-element.108), channel_id=1, source_target_pairs={{0,4},{4,0},{8,12},{12,8},{16,20},{20,16},{24,28},{28,24},{1,5},{5... | collective-permute-start | bytes 98312 | tf_op jit(solution)/shard_map/ppermute | solution.py:465
  22.1 4.2 %collective-permute-start.9 = (bf16[64,128]{1,0:T(8,128)(2,1)S(1)}, bf16[64,128]{1,0:T(8,128)(2,1)S(1)}, u32[]{:S(2)}, u32[]{:S(2)}) collective-permute-start(bf16[64,128]{1,0:T(8,128)(2,1)S(1)} %get-tuple-element.114), channel_id=1, source_target_pairs={{0,6},{1,7},{2,4},{3,5},{4,2},{5,3},{6,0},{7,1},{8,14},{9,15},{10,... | collective-permute-start | bytes 49160 | tf_op jit(solution)/shard_map/ppermute | solution.py:522
  22.6 5.0 %collective-permute-start.10 = (bf16[64,128]{1,0:T(8,128)(2,1)S(1)}, bf16[64,128]{1,0:T(8,128)(2,1)S(1)}, u32[]{:S(2)}, u32[]{:S(2)}) collective-permute-start(bf16[64,128]{1,0:T(8,128)(2,1)S(1)} %get-tuple-element.115), channel_id=1, source_target_pairs={{0,7},{1,6},{2,5},{3,4},{4,3},{5,2},{6,1},{7,0},{8,15},{9,14},{10,... | collective-permute-start | bytes 49160 | tf_op jit(solution)/shard_map/ppermute | solution.py:522
  24.9 3.4 %collective-permute-start.11 = (bf16[64,128]{1,0:T(8,128)(2,1)S(1)}, bf16[64,128]{1,0:T(8,128)(2,1)S(1)}, u32[]{:S(2)}, u32[]{:S(2)}) collective-permute-start(bf16[64,128]{1,0:T(8,128)(2,1)S(1)} %get-tuple-element.116), channel_id=1, source_target_pairs={{0,5},{1,4},{2,7},{3,6},{4,1},{5,0},{6,3},{7,2},{8,13},{9,12},{10,... | collective-permute-start | bytes 49160 | tf_op jit(solution)/shard_map/ppermute | solution.py:522

commit v16 on v14

--- a/solution.py
+++ b/solution.py
@@ -32,6 +32,16 @@
     centre = values - jnp.mean(values, axis=-1, keepdims=True)
     scale_inv = lax.rsqrt(jnp.mean(centre * centre, axis=-1, keepdims=True) + eps)
     return centre * scale_inv, scale_inv
+
+
+def exchange(side):
+    edge = 1
+    while edge * edge < side:
+        edge *= 2
+    shift = edge.bit_length() - 1
+    out_row = lax.broadcasted_iota(jnp.int32, (side, side), 0)
+    in_row = lax.broadcasted_iota(jnp.int32, (side, side), 1)
+    return jnp.where(in_row == (((out_row & (edge - 1)) << shift) | (out_row >> shift)), 1.0, 0.0).astype(bf16)
 
 
 def chunks_of(size, most):
@@ -80,11 +90,6 @@
     ]
     for copy in pieces + copies:
         copy.start()
-    shift = edge.bit_length() - 1
-    out_row = lax.broadcasted_iota(jnp.int32, (side, side), 0)
-    in_row = lax.broadcasted_iota(jnp.int32, (side, side), 1)
-    wanted = ((out_row & (edge - 1)) << shift) | (out_row >> shift)
-    swap = jnp.where(in_row == wanted, 1.0, 0.0).astype(bf16)
     own = lax.rem(lax.axis_index("row"), q)
     for copy in pieces:
         copy.wait()
@@ -94,7 +99,7 @@
         copy.wait()
     for at, step in chunks_of(w_gate.shape[1], 256):
         w_half = w_gate[:, at : at + step] * 0.5
-        for top, tall in chunks_of(q * side, 256):
+        for top, tall in chunks_of(q * side, 512):
             half = nn(inputs[top : top + tall], w_half)
             upper = nn(inputs[top : top + tall], w_up[:, at : at + step])
             hidden[top : top + tall, at : at + step] = (half * (1.0 + jnp.tanh(half)) * upper).astype(bf16)
@@ -105,10 +110,10 @@
     packs = lane_packs(bins, side)
     deep = side // packs
     for h in range(q):
-        piece = nn(swap, logit[h * side : (h + 1) * side])
+        piece = logit[h * side : (h + 1) * side]
         if packs > 1:
             piece = jnp.concatenate([piece[u * deep : (u + 1) * deep] for u in range(packs)], axis=1)
-        halves[h] = piece.astype(bf16)
+        halves[h] = piece
         mark = targets[:, h * edge : (h + 1) * edge].astype(f32)
         marks[h] = jnp.concatenate([mark, jnp.zeros((edge, width - edge), f32)], axis=1).astype(bf16)
     for p in range(q):
@@ -139,6 +144,7 @@
         flat, mark, refs = refs[0][own], refs[1][own], refs[2:]
     w_gate, w_up, w_out, w_head, inputs_t, updated_t, hidden, slope, swish, logits, onehot, normed, scale = refs
     width, bins = flat.shape[1], w_head.shape[0]
+    flat = nn(exchange(side), flat).astype(bf16)
     normal, scale_inv = normalize(flat)
     normed[...] = normal
     scale[...] = jnp.broadcast_to(scale_inv, normal.shape)
@@ -161,9 +167,9 @@
     updated_t[...] = upd.T
     logits[...] = nt(upd, w_head[...]).astype(bf16)
     shift = edge.bit_length() - 1
-    rows = lax.broadcasted_iota(jnp.int32, (side, edge), 0) >> shift
+    rows = lax.broadcasted_iota(jnp.int32, (side, edge), 0) & (edge - 1)
     pick = jnp.where(rows == lax.broadcasted_iota(jnp.int32, (side, edge), 1), 1.0, 0.0).astype(bf16)
-    columns = lax.broadcasted_iota(jnp.int32, (side, width), 0) & (edge - 1)
+    columns = lax.broadcasted_iota(jnp.int32, (side, width), 0) >> shift
     mask = columns == lax.broadcasted_iota(jnp.int32, (side, width), 1)
     lanes = lax.broadcasted_iota(jnp.int32, (side, bins), 1).astype(f32)
     picked = jnp.where(mask, nn(pick, mark), 0.0).astype(bf16)
@@ -268,7 +274,7 @@
         - jnp.mean(d_inputs, axis=-1, keepdims=True)
         - normal * jnp.mean(d_inputs * normal, axis=-1, keepdims=True)
     ) * scale[...]
-    result[...] = (d_updated[row] + d_norm).astype(bf16)
+    result[...] = nn(exchange(side), (d_updated[row] + d_norm).astype(bf16)).astype(bf16)
 
 
 def place_kernel(q, *refs):

time: 28.7 us -> 28.5 us (level)
  Pallas kernels: 7.58 us -> 8.38 us
  starting transfers between devices: 14.3 us -> 13.6 us
    pallas_call x2, Pallas kernels: 1.77 us -> 2.32 us  [body(): pl.pallas_call(functools.partial(prepare_kernel, q, p), out_shape=[shaped...]
    ppermute x3, starting transfers between devices: 9.26 us -> 8.73 us  [body(): lax.ppermute(hot[p], 'row', [(s, following(s // q, p, groups) * q + cross...]
    pallas_call x2, Pallas kernels: 0.75 us -> 1.19 us  [d_inputs(): pl.pallas_call(functools.partial(input_kernel, p), out_shape=shaped((side...]
  transfers between devices with their start and end apart: 12 -> 12, of which waited for: 8 -> 9; matrix products, arithmetic and copies ran while one was open for 0% -> 0% of each run, Pallas kernels for 11% -> 15%
where the time goes in v16:
time: 28.5 us; the launch traced here: 28.3 us
  starting transfers between devices  13.6 us (48%)
  Pallas kernels  8.38 us (29%)
  waiting for transfers between devices  5.63 us (20%)
  between operations  0.72 us (3%)
    ppermute x3, starting transfers between devices, body(): lax.ppermute(hot[p], 'row', [(s, following(s // q, p, groups) * q + cross...  8.73 us
    ppermute x3, starting transfers between devices, body(): terms.append(lax.ppermute(hot[p], ('row', 'col'), pairs))  3.18 us
    pallas_call x2, Pallas kernels, body(): pl.pallas_call(functools.partial(prepare_kernel, q, p), out_shape=[shaped...  2.32 us
    ppermute x3, waiting for transfers between devices, body(): lax.ppermute(hot[p], 'row', [(s, following(s // q, p, groups) * q + cross...  2.25 us
    ppermute x3, waiting for transfers between devices, body(): terms.append(lax.ppermute(hot[p], ('row', 'col'), pairs))  2.24 us
    pallas_call x1, Pallas kernels, body(): pl.pallas_call(functools.partial(forward_kernel, q), out_shape=[shaped((q...  2.13 us
    pallas_call x1, Pallas kernels, body(): pl.pallas_call(functools.partial(backward_kernel, q, (nrow, ncol) if fits...  1.23 us
    pallas_call x2, Pallas kernels, d_inputs(): pl.pallas_call(functools.partial(input_kernel, p), out_shape=shaped((side...  1.19 us
  transfers between devices with their start and end apart: 12, of which 9 were waited for; matrix products, arithmetic and copies ran while one was open for 0% of the time, Pallas kernels for 15%

profile of v16, /device:TPU:0, one launch (start us, length us, event | category | flops | bytes accessed | tf_op | source)
XLA Modules:
  0.0 28.3 jit_solution(14307100208443283981)
XLA Ops:
  0.6 2.1 %forward.1 = (bf16[2,256,128]{2,1,0:T(8,128)(2,1)S(1)}, bf16[128,512]{1,0:T(8,128)(2,1)S(1)}, bf16[128,512]{1,0:T(8,128)(2,1)S(1)}, bf16[512,128]{1,0:T(8,128)(2...) custom-call(bf16[16,32,128]{2,1,0:T(8,128)(2,1)} %refs_0_.1, ...), custom_call_target="tpu_custom_call" | custom-call | tf_op jit(solution)/shard_map/forward/pallas_call | solution.py:364
  2.8 0.5 %collective-permute-start.2 = (bf16[2,128,128]{2,1,0:T(8,128)(2,1)S(1)}, bf16[2,128,128]{2,1,0:T(8,128)(2,1)S(1)}, u32[]{:S(2)}, u32[]{:S(2)}) collective-permute-start(bf16[2,128,128]{2,1,0:T(8,128)(2,1)S(1)} %get-tuple-element.89.refs_17_), channel_id=1, source_target_pairs={{0,4},{1,8},{2,16},{3,24},{4,0},{5,12},{6,20},{7,28},{8,1},{9,13},... | collective-permute-start | bytes 196616 | tf_op jit(solution)/shard_map/ppermute | solution.py:386
  3.3 0.1 collective-permute-start.1
  3.4 0.4 %collective-permute-start = (bf16[128,128]{1,0:T(8,128)(2,1)S(1)}, bf16[128,128]{1,0:T(8,128)(2,1)S(1)}, u32[]{:S(2)}, u32[]{:S(2)}) collective-permute-start(bf16[128,128]{1,0:T(8,128)(2,1)S(1)} %get-tuple-element.80), channel_id=1, source_target_pairs={{0,4},{4,0},{8,12},{12,8},{16,20},{20,16},{24,28},{28,24},{1,5},{5... | collective-permute-start | bytes 98312 | tf_op jit(solution)/shard_map/ppermute | solution.py:395
  3.8 1.2 %prepare.2 = (bf16[128,256]{1,0:T(8,128)(2,1)S(1)}, bf16[128,256]{1,0:T(8,128)(2,1)S(1)}, bf16[256,512]{1,0:T(8,128)(2,1)S(1)}, f32[256,512]{1,0:T(8,128)S(1)}, ...) custom-call(bf16[2,256,128]{2,1,0:T(8,128)(2,1)S(1)} %get-tuple-elem, ...), custom_call_target="tpu_custom_call" | custom-call | flops 100663296 | bytes 1048576 | tf_op jit(solution)/shard_map/prepare/pallas_call | solution.py:400
  5.0 0.0 collective-permute-done.refs_0_
  5.0 0.0 collective-permute-done.1.refs_1_
  5.0 1.2 %prepare.3 = (bf16[128,256]{1,0:T(8,128)(2,1)S(1)}, bf16[128,256]{1,0:T(8,128)(2,1)S(1)}, bf16[256,512]{1,0:T(8,128)(2,1)S(1)}, f32[256,512]{1,0:T(8,128)S(1)}, ...) custom-call(bf16[128,128]{1,0:T(8,128)(2,1)S(1)} %collective-permute, ...), custom_call_target="tpu_custom_call" | custom-call | tf_op jit(solution)/shard_map/prepare/pallas_call | solution.py:400
  6.2 0.0 collective-permute-done.2.refs_16_
  6.2 1.2 %backward.1 = (f32[512,128]{1,0:T(8,128)S(1)}, bf16[512,512]{1,0:T(8,128)(2,1)S(1)}, bf16[512,512]{1,0:T(8,128)(2,1)S(1)}, bf16[4,208,128]{2,1,0:T(8,128)(2,1)S(1)}, bf16[4,208,128]{2,1,0:T(8,128)(2,1)S(1)}) custom-call(bf16[128,256]{1,0:T(8,128)(2,1)S(1)} %get-tuple-element.73.refs_0_, bf16[128,256]{1,0:T(8,128)(2,1)S(1)} %get-tuple-element.74.refs_1_, ...), custom_call_target="tpu_custom_call" | custom-call | flops 268435456 | bytes 1048576 | tf_op jit(solution)/shard_map/backward/pallas_call | solution.py:432
  7.4 0.2 collective-permute-start.3
  7.6 0.6 %d_inputs.3.rest_2_ = bf16[256,128]{1,0:T(8,128)(2,1)S(1)} custom-call(f32[512,128]{1,0:T(8,128)S(1)} %get-tuple-element.92.d_updated, bf16[512,512]{1,0:T(8,128)(2,1)S(1)} %get-tuple-element.93.d_gate, bf16[512,512]{1,0:T(8,128)(2,1)S(1)} %get-tuple-element.94.d_up, f32[256,128]{1,0:T(8,128)S(1)} %get-tuple-element.97.normed, ...), custom_call_target="tpu_custom_call" | custom-call | flops 67108864 | bytes 524288 | tf_op jit(solution)/shard_map/d_inputs/pallas_call | solution.py:445
  8.2 0.6 %d_inputs.2.refs_0_ = bf16[256,128]{1,0:T(8,128)(2,1)S(1)} custom-call(f32[512,128]{1,0:T(8,128)S(1)} %get-tuple-element.92.d_updated, bf16[512,512]{1,0:T(8,128)(2,1)S(1)} %get-tuple-element.93.d_gate, bf16[512,512]{1,0:T(8,128)(2,1)S(1)} %get-tuple-element.94.d_up, f32[256,128]{1,0:T(8,128)S(1)} %get-tuple-element.95.normed, ...), custom_call_target="tpu_custom_call" | custom-call | flops 67108864 | bytes 524288 | tf_op jit(solution)/shard_map/d_inputs/pallas_call | solution.py:445
  8.8 0.2 collective-permute-done.3.rest_1_
  8.9 0.1 core_sum.1
  9.0 6.6 %collective-permute-start.4 = (bf16[208,128]{1,0:T(8,128)(2,1)S(1)}, bf16[208,128]{1,0:T(8,128)(2,1)S(1)}, u32[]{:S(2)}, u32[]{:S(2)}) collective-permute-start(bf16[208,128]{1,0:T(8,128)(2,1)S(1)} %get-tuple-element.103), channel_id=1, source_target_pairs={{0,12},{4,8},{8,20},{12,16},{16,28},{20,24},{24,4},{28,0},{1,13},{... | collective-permute-start | bytes 159752 | tf_op jit(solution)/shard_map/ppermute | solution.py:496
  15.6 2.2 %collective-permute-start.5 = (bf16[208,128]{1,0:T(8,128)(2,1)S(1)}, bf16[208,128]{1,0:T(8,128)(2,1)S(1)}, u32[]{:S(2)}, u32[]{:S(2)}) collective-permute-start(bf16[208,128]{1,0:T(8,128)(2,1)S(1)} %get-tuple-element.104), channel_id=1, source_target_pairs={{0,20},{4,16},{8,28},{12,24},{16,4},{20,0},{24,12},{28,8},{1,21},{... | collective-permute-start | bytes 159752 | tf_op jit(solution)/shard_map/ppermute | solution.py:496
  17.7 0.0 collective-permute-start.6
  17.7 0.3 collective-permute-start.7
  18.0 0.2 collective-permute-start.8
  18.2 0.7 %collective-permute-done.7.refs_1_ = bf16[128,128]{1,0:T(8,128)(2,1)S(1)} collective-permute-done((bf16[128,128]{1,0:T(8,128)(2,1)S(1)}, bf16[128,128]{1,0:T(8,128)(2,1)S(1)}, u32[]{:S(2)}, u32[]{:S(2)}) %collective-permute-start.7) | collective-permute-done | bytes 32800 | tf_op jit(solution)/shard_map/ppermute | solution.py:458
  18.9 0.3 collective-permute-done.8.refs_2_
  19.2 0.2 collective-permute-done.4.rest_1_
  19.4 1.4 %collective-permute-done.5.rest_2_ = bf16[208,128]{1,0:T(8,128)(2,1)S(1)} collective-permute-done((bf16[208,128]{1,0:T(8,128)(2,1)S(1)}, bf16[208,128]{1,0:T(8,128)(2,1)S(1)}, u32[]{:S(2)}, u32[]{:S(2)}) %collective-permute-start.5) | collective-permute-done | bytes 53280 | tf_op jit(solution)/shard_map/ppermute | solution.py:496
  20.8 0.7 %collective-permute-done.6.rest_3_ = bf16[208,128]{1,0:T(8,128)(2,1)S(1)} collective-permute-done((bf16[208,128]{1,0:T(8,128)(2,1)S(1)}, bf16[208,128]{1,0:T(8,128)(2,1)S(1)}, u32[]{:S(2)}, u32[]{:S(2)}) %collective-permute-start.6) | collective-permute-done | bytes 53280 | tf_op jit(solution)/shard_map/ppermute | solution.py:496
  21.5 0.1 chip_sum.1
  21.6 0.5 %collective-permute-start.9 = (bf16[64,128]{1,0:T(8,128)(2,1)S(1)}, bf16[64,128]{1,0:T(8,128)(2,1)S(1)}, u32[]{:S(2)}, u32[]{:S(2)}) collective-permute-start(bf16[64,128]{1,0:T(8,128)(2,1)S(1)} %get-tuple-element.114), channel_id=1, source_target_pairs={{0,6},{1,7},{2,4},{3,5},{4,2},{5,3},{6,0},{7,1},{8,14},{9,15},{10,... | collective-permute-start | bytes 49160 | tf_op jit(solution)/shard_map/ppermute | solution.py:515
  22.1 2.3 %collective-permute-start.10 = (bf16[64,128]{1,0:T(8,128)(2,1)S(1)}, bf16[64,128]{1,0:T(8,128)(2,1)S(1)}, u32[]{:S(2)}, u32[]{:S(2)}) collective-permute-start(bf16[64,128]{1,0:T(8,128)(2,1)S(1)} %get-tuple-element.115), channel_id=1, source_target_pairs={{0,7},{1,6},{2,5},{3,4},{4,3},{5,2},{6,1},{7,0},{8,15},{9,14},{10,... | collective-permute-start | bytes 49160 | tf_op jit(solution)/shard_map/ppermute | solution.py:515
  24.3 0.4 %collective-permute-start.11 = (bf16[64,128]{1,0:T(8,128)(2,1)S(1)}, bf16[64,128]{1,0:T(8,128)(2,1)S(1)}, u32[]{:S(2)}, u32[]{:S(2)}) collective-permute-start(bf16[64,128]{1,0:T(8,128)(2,1)S(1)} %get-tuple-element.116), channel_id=1, source_target_pairs={{0,5},{1,4},{2,7},{3,6},{4,1},{5,0},{6,3},{7,2},{8,13},{9,12},{10,... | collective-permute-start | bytes 49160 | tf_op jit(solution)/shard_map/ppermute | solution.py:515
  24.7 0.7 %place.1 = bf16[16,2,16,128]{3,2,1,0:T(8,128)(2,1)} custom-call(bf16[256,128]{1,0:T(8,128)(2,1)S(1)} %d_inputs.2.refs_0_, bf16[128,128]{1,0:T(8,128)(2,1)S(1)} %collective-permute-done.7.refs_1_, bf16[128,128]{1,0:T(8,128)(2,1)S(1)} %collective-permute-done.8.refs_2_), custom_call_target="tpu_custom_call" | custom-call | tf_op jit(solution)/shard_map/place/pallas_call | solution.py:462
  25.4 0.4 %collective-permute-done.9.rest_1_ = bf16[64,128]{1,0:T(8,128)(2,1)S(1)} collective-permute-done((bf16[64,128]{1,0:T(8,128)(2,1)S(1)}, bf16[64,128]{1,0:T(8,128)(2,1)S(1)}, u32[]{:S(2)}, u32[]{:S(2)}) %collective-permute-start.9) | collective-permute-done | bytes 16416 | tf_op jit(solution)/shard_map/ppermute | solution.py:515
  25.8 1.2 %collective-permute-done.10.rest_2_ = bf16[64,128]{1,0:T(8,128)(2,1)S(1)} collective-permute-done((bf16[64,128]{1,0:T(8,128)(2,1)S(1)}, bf16[64,128]{1,0:T(8,128)(2,1)S(1)}, u32[]{:S(2)}, u32[]{:S(2)}) %collective-permute-start.10) | collective-permute-done | bytes 16416 | tf_op jit(solution)/shard_map/ppermute | solution.py:515
  27.0 0.6 %collective-permute-done.11.rest_3_ = bf16[64,128]{1,0:T(8,128)(2,1)S(1)} collective-permute-done((bf16[64,128]{1,0:T(8,128)(2,1)S(1)}, bf16[64,128]{1,0:T(8,128)(2,1)S(1)}, u32[]{:S(2)}, u32[]{:S(2)}) %collective-permute-start.11) | collective-permute-done | bytes 16416 | tf_op jit(solution)/shard_map/ppermute | solution.py:515
  27.7 0.7 %col_sum.1 = (f32[16,128]{1,0:T(8,128)}, f32[16,128]{1,0:T(8,128)}, f32[32,64]{1,0:T(8,128)}, f32[16,16]{1,0:T(8,128)}) custom-call(bf16[64,128]{1,0:T(8,128)(2,1)S(1)} %get-tuple-element.121.rest_0_, bf16[64,128]{1,0:T(8,128)(2,1)S(1)} %collective-permute-done.9.rest_1_, bf16[64,128]{1,0:T(8,128)(2,1)S(1)} %collective-permute-done.10.rest_2_, ...), custom_call_target="tpu_custom_call" | custom-call | tf_op jit(solution)/shard_map/col_sum/pallas_call | solution.py:517
  (1 shorter events, 0.0 us)
Async XLA Ops:
  2.8 3.4 %collective-permute-start.2 = (bf16[2,128,128]{2,1,0:T(8,128)(2,1)S(1)}, bf16[2,128,128]{2,1,0:T(8,128)(2,1)S(1)}, u32[]{:S(2)}, u32[]{:S(2)}) collective-permute-start(bf16[2,128,128]{2,1,0:T(8,128)(2,1)S(1)} %get-tuple-element.89.refs_17_), channel_id=1, source_target_pairs={{0,4},{1,8},{2,16},{3,24},{4,0},{5,12},{6,20},{7,28},{8,1},{9,13},... | collective-permute-start | bytes 196616 | tf_op jit(solution)/shard_map/ppermute | solution.py:386
  3.3 1.7 %collective-permute-start.1 = (bf16[144,128]{1,0:T(8,128)(2,1)S(1)}, bf16[144,128]{1,0:T(8,128)(2,1)S(1)}, u32[]{:S(2)}, u32[]{:S(2)}) collective-permute-start(bf16[144,128]{1,0:T(8,128)(2,1)S(1)} %get-tuple-element.81), channel_id=1, source_target_pairs={{0,4},{4,0},{8,12},{12,8},{16,20},{20,16},{24,28},{28,24},{1,5},{5... | collective-permute-start | bytes 110600 | tf_op jit(solution)/shard_map/ppermute | solution.py:395
  3.4 1.6 %collective-permute-start = (bf16[128,128]{1,0:T(8,128)(2,1)S(1)}, bf16[128,128]{1,0:T(8,128)(2,1)S(1)}, u32[]{:S(2)}, u32[]{:S(2)}) collective-permute-start(bf16[128,128]{1,0:T(8,128)(2,1)S(1)} %get-tuple-element.80), channel_id=1, source_target_pairs={{0,4},{4,0},{8,12},{12,8},{16,20},{20,16},{24,28},{28,24},{1,5},{5... | collective-permute-start | bytes 98312 | tf_op jit(solution)/shard_map/ppermute | solution.py:395
  7.4 1.5 %collective-permute-start.3 = (bf16[4,208,128]{2,1,0:T(8,128)(2,1)S(1)}, bf16[4,208,128]{2,1,0:T(8,128)(2,1)S(1)}, u32[]{:S(2)}, u32[]{:S(2)}) collective-permute-start(bf16[4,208,128]{2,1,0:T(8,128)(2,1)S(1)} %get-tuple-element.91), channel_id=1, source_target_pairs={{0,4},{4,0},{8,12},{12,8},{16,20},{20,16},{24,28},{28,24},{1,5},{5... | collective-permute-start | bytes 638984 | tf_op jit(solution)/shard_map/ppermute | solution.py:483
  9.0 10.4 %collective-permute-start.4 = (bf16[208,128]{1,0:T(8,128)(2,1)S(1)}, bf16[208,128]{1,0:T(8,128)(2,1)S(1)}, u32[]{:S(2)}, u32[]{:S(2)}) collective-permute-start(bf16[208,128]{1,0:T(8,128)(2,1)S(1)} %get-tuple-element.103), channel_id=1, source_target_pairs={{0,12},{4,8},{8,20},{12,16},{16,28},{20,24},{24,4},{28,0},{1,13},{... | collective-permute-start | bytes 159752 | tf_op jit(solution)/shard_map/ppermute | solution.py:496
  15.6 5.2 %collective-permute-start.5 = (bf16[208,128]{1,0:T(8,128)(2,1)S(1)}, bf16[208,128]{1,0:T(8,128)(2,1)S(1)}, u32[]{:S(2)}, u32[]{:S(2)}) collective-permute-start(bf16[208,128]{1,0:T(8,128)(2,1)S(1)} %get-tuple-element.104), channel_id=1, source_target_pairs={{0,20},{4,16},{8,28},{12,24},{16,4},{20,0},{24,12},{28,8},{1,21},{... | collective-permute-start | bytes 159752 | tf_op jit(solution)/shard_map/ppermute | solution.py:496
  17.7 3.7 %collective-permute-start.6 = (bf16[208,128]{1,0:T(8,128)(2,1)S(1)}, bf16[208,128]{1,0:T(8,128)(2,1)S(1)}, u32[]{:S(2)}, u32[]{:S(2)}) collective-permute-start(bf16[208,128]{1,0:T(8,128)(2,1)S(1)} %get-tuple-element.105), channel_id=1, source_target_pairs={{0,28},{4,24},{8,4},{12,0},{16,12},{20,8},{24,20},{28,16},{1,29},{... | collective-permute-start | bytes 159752 | tf_op jit(solution)/shard_map/ppermute | solution.py:496
  17.7 1.2 %collective-permute-start.7 = (bf16[128,128]{1,0:T(8,128)(2,1)S(1)}, bf16[128,128]{1,0:T(8,128)(2,1)S(1)}, u32[]{:S(2)}, u32[]{:S(2)}) collective-permute-start(bf16[128,128]{1,0:T(8,128)(2,1)S(1)} %get-tuple-element.107), channel_id=1, source_target_pairs={{0,4},{4,0},{8,12},{12,8},{16,20},{20,16},{24,28},{28,24},{1,5},{5... | collective-permute-start | bytes 98312 | tf_op jit(solution)/shard_map/ppermute | solution.py:458
  18.0 1.2 %collective-permute-start.8 = (bf16[128,128]{1,0:T(8,128)(2,1)S(1)}, bf16[128,128]{1,0:T(8,128)(2,1)S(1)}, u32[]{:S(2)}, u32[]{:S(2)}) collective-permute-start(bf16[128,128]{1,0:T(8,128)(2,1)S(1)} %get-tuple-element.108), channel_id=1, source_target_pairs={{0,4},{4,0},{8,12},{12,8},{16,20},{20,16},{24,28},{28,24},{1,5},{5... | collective-permute-start | bytes 98312 | tf_op jit(solution)/shard_map/ppermute | solution.py:458
  21.6 4.3 %collective-permute-start.9 = (bf16[64,128]{1,0:T(8,128)(2,1)S(1)}, bf16[64,128]{1,0:T(8,128)(2,1)S(1)}, u32[]{:S(2)}, u32[]{:S(2)}) collective-permute-start(bf16[64,128]{1,0:T(8,128)(2,1)S(1)} %get-tuple-element.114), channel_id=1, source_target_pairs={{0,6},{1,7},{2,4},{3,5},{4,2},{5,3},{6,0},{7,1},{8,14},{9,15},{10,... | collective-permute-start | bytes 49160 | tf_op jit(solution)/shard_map/ppermute | solution.py:515
  22.1 5.0 %collective-permute-start.10 = (bf16[64,128]{1,0:T(8,128)(2,1)S(1)}, bf16[64,128]{1,0:T(8,128)(2,1)S(1)}, u32[]{:S(2)}, u32[]{:S(2)}) collective-permute-start(bf16[64,128]{1,0:T(8,128)(2,1)S(1)} %get-tuple-element.115), channel_id=1, source_target_pairs={{0,7},{1,6},{2,5},{3,4},{4,3},{5,2},{6,1},{7,0},{8,15},{9,14},{10,... | collective-permute-start | bytes 49160 | tf_op jit(solution)/shard_map/ppermute | solution.py:515
  24.3 3.3 %collective-permute-start.11 = (bf16[64,128]{1,0:T(8,128)(2,1)S(1)}, bf16[64,128]{1,0:T(8,128)(2,1)S(1)}, u32[]{:S(2)}, u32[]{:S(2)}) collective-permute-start(bf16[64,128]{1,0:T(8,128)(2,1)S(1)} %get-tuple-element.116), channel_id=1, source_target_pairs={{0,5},{1,4},{2,7},{3,6},{4,1},{5,0},{6,3},{7,2},{8,13},{9,12},{10,... | collective-permute-start | bytes 49160 | tf_op jit(solution)/shard_map/ppermute | solution.py:515

commit v17 on v16

--- a/solution.py
+++ b/solution.py
@@ -274,17 +274,17 @@
         - jnp.mean(d_inputs, axis=-1, keepdims=True)
         - normal * jnp.mean(d_inputs * normal, axis=-1, keepdims=True)
     ) * scale[...]
-    result[...] = nn(exchange(side), (d_updated[row] + d_norm).astype(bf16)).astype(bf16)
+    result[...] = (d_updated[row] + d_norm).astype(bf16)
 
 
 def place_kernel(q, *refs):
     blocks, d_pair = refs[:-1], refs[-1]
     edge, _, _, width = d_pair.shape
     own = lax.rem(lax.axis_index("row"), q)
-    d_pair[:, own] = blocks[0][...].reshape(edge, edge, width)
-    for p in range(1, q):
-        for n, half in enumerate((slice(0, edge // 2), slice(edge // 2, edge))):
-            d_pair[half, partner(own, p, q)] = blocks[2 * p - 1 + n][...].reshape(edge // 2, edge, width)
+    back = exchange(edge * edge)
+    for p in range(q):
+        block = joined(blocks[2 * p - 1 : 2 * p + 1], 0) if p else blocks[0][...]
+        d_pair[:, partner(own, p, q)] = nn(back, block).astype(bf16).reshape(edge, edge, width)
 
 
 def core_sum_kernel(q, groups, *rest):

time: 28.5 us -> 28.5 us (level)
    ppermute x1, waiting for transfers between devices: 0.15 us -> 0.6 us  [body(): terms.append(lax.ppermute(hot[p], 'row', core_pairs(nrow, q, p)))]
    pallas_call x2, Pallas kernels: 1.19 us -> 0.75 us  [d_inputs(): pl.pallas_call(functools.partial(input_kernel, p), out_shape=shaped((side...]
  transfers between devices with their start and end apart: 12 -> 12, of which waited for: 9 -> 8; matrix products, arithmetic and copies ran while one was open for 0% -> 0% of each run, Pallas kernels for 15% -> 14%
where the time goes in v17:
time: 28.5 us; the launch traced here: 28.4 us
  starting transfers between devices  13.6 us (48%)
  Pallas kernels  8.15 us (29%)
  waiting for transfers between devices  5.89 us (21%)
  between operations  0.71 us (2%)
    ppermute x3, starting transfers between devices, body(): lax.ppermute(hot[p], 'row', [(s, following(s // q, p, groups) * q + cross...  8.73 us
    ppermute x3, starting transfers between devices, body(): terms.append(lax.ppermute(hot[p], ('row', 'col'), pairs))  3.17 us
    ppermute x3, waiting for transfers between devices, body(): lax.ppermute(hot[p], 'row', [(s, following(s // q, p, groups) * q + cross...  2.42 us
    pallas_call x2, Pallas kernels, body(): pl.pallas_call(functools.partial(prepare_kernel, q, p), out_shape=[shaped...  2.32 us
    pallas_call x1, Pallas kernels, body(): pl.pallas_call(functools.partial(forward_kernel, q), out_shape=[shaped((q...  2.13 us
    ppermute x3, waiting for transfers between devices, body(): terms.append(lax.ppermute(hot[p], ('row', 'col'), pairs))  2.01 us
    pallas_call x1, Pallas kernels, body(): pl.pallas_call(functools.partial(backward_kernel, q, (nrow, ncol) if fits...  1.23 us
    pallas_call x1, Pallas kernels, placed(): pl.pallas_call(functools.partial(place_kernel, q), out_shape=shaped((rows...  0.88 us
  transfers between devices with their start and end apart: 12, of which 8 were waited for; matrix products, arithmetic and copies ran while one was open for 0% of the time, Pallas kernels for 14%

profile of v17, /device:TPU:0, one launch (start us, length us, event | category | flops | bytes accessed | tf_op | source)
XLA Modules:
  0.0 28.4 jit_solution(7361177552064680909)
XLA Ops:
  0.6 2.1 %forward.1 = (bf16[2,256,128]{2,1,0:T(8,128)(2,1)S(1)}, bf16[128,512]{1,0:T(8,128)(2,1)S(1)}, bf16[128,512]{1,0:T(8,128)(2,1)S(1)}, bf16[512,128]{1,0:T(8,128)(2...) custom-call(bf16[16,32,128]{2,1,0:T(8,128)(2,1)} %refs_0_.1, ...), custom_call_target="tpu_custom_call" | custom-call | tf_op jit(solution)/shard_map/forward/pallas_call | solution.py:364
  2.8 0.5 %collective-permute-start.2 = (bf16[2,128,128]{2,1,0:T(8,128)(2,1)S(1)}, bf16[2,128,128]{2,1,0:T(8,128)(2,1)S(1)}, u32[]{:S(2)}, u32[]{:S(2)}) collective-permute-start(bf16[2,128,128]{2,1,0:T(8,128)(2,1)S(1)} %get-tuple-element.89.refs_17_), channel_id=1, source_target_pairs={{0,4},{1,8},{2,16},{3,24},{4,0},{5,12},{6,20},{7,28},{8,1},{9,13},... | collective-permute-start | bytes 196616 | tf_op jit(solution)/shard_map/ppermute | solution.py:386
  3.3 0.1 collective-permute-start.1
  3.4 0.4 %collective-permute-start = (bf16[128,128]{1,0:T(8,128)(2,1)S(1)}, bf16[128,128]{1,0:T(8,128)(2,1)S(1)}, u32[]{:S(2)}, u32[]{:S(2)}) collective-permute-start(bf16[128,128]{1,0:T(8,128)(2,1)S(1)} %get-tuple-element.80), channel_id=1, source_target_pairs={{0,4},{4,0},{8,12},{12,8},{16,20},{20,16},{24,28},{28,24},{1,5},{5... | collective-permute-start | bytes 98312 | tf_op jit(solution)/shard_map/ppermute | solution.py:395
  3.8 1.2 %prepare.2 = (bf16[128,256]{1,0:T(8,128)(2,1)S(1)}, bf16[128,256]{1,0:T(8,128)(2,1)S(1)}, bf16[256,512]{1,0:T(8,128)(2,1)S(1)}, f32[256,512]{1,0:T(8,128)S(1)}, ...) custom-call(bf16[2,256,128]{2,1,0:T(8,128)(2,1)S(1)} %get-tuple-elem, ...), custom_call_target="tpu_custom_call" | custom-call | flops 100663296 | bytes 1048576 | tf_op jit(solution)/shard_map/prepare/pallas_call | solution.py:400
  5.0 0.0 collective-permute-done.refs_0_
  5.0 0.0 collective-permute-done.1.refs_1_
  5.0 1.2 %prepare.3 = (bf16[128,256]{1,0:T(8,128)(2,1)S(1)}, bf16[128,256]{1,0:T(8,128)(2,1)S(1)}, bf16[256,512]{1,0:T(8,128)(2,1)S(1)}, f32[256,512]{1,0:T(8,128)S(1)}, ...) custom-call(bf16[128,128]{1,0:T(8,128)(2,1)S(1)} %collective-permute, ...), custom_call_target="tpu_custom_call" | custom-call | tf_op jit(solution)/shard_map/prepare/pallas_call | solution.py:400
  6.2 0.0 collective-permute-done.2.refs_16_
  6.2 1.2 %backward.1 = (f32[512,128]{1,0:T(8,128)S(1)}, bf16[512,512]{1,0:T(8,128)(2,1)S(1)}, bf16[512,512]{1,0:T(8,128)(2,1)S(1)}, bf16[4,208,128]{2,1,0:T(8,128)(2,1)S(1)}, bf16[4,208,128]{2,1,0:T(8,128)(2,1)S(1)}) custom-call(bf16[128,256]{1,0:T(8,128)(2,1)S(1)} %get-tuple-element.73.refs_0_, bf16[128,256]{1,0:T(8,128)(2,1)S(1)} %get-tuple-element.74.refs_1_, ...), custom_call_target="tpu_custom_call" | custom-call | flops 268435456 | bytes 1048576 | tf_op jit(solution)/shard_map/backward/pallas_call | solution.py:432
  7.4 0.2 collective-permute-start.3
  7.6 0.4 %d_inputs.3.rest_2_ = bf16[256,128]{1,0:T(8,128)(2,1)S(1)} custom-call(f32[512,128]{1,0:T(8,128)S(1)} %get-tuple-element.92.d_updated, bf16[512,512]{1,0:T(8,128)(2,1)S(1)} %get-tuple-element.93.d_gate, bf16[512,512]{1,0:T(8,128)(2,1)S(1)} %get-tuple-element.94.d_up, f32[256,128]{1,0:T(8,128)S(1)} %get-tuple-element.97.normed, ...), custom_call_target="tpu_custom_call" | custom-call | flops 67108864 | bytes 524288 | tf_op jit(solution)/shard_map/d_inputs/pallas_call | solution.py:445
  8.0 0.4 %d_inputs.2.refs_0_ = bf16[256,128]{1,0:T(8,128)(2,1)S(1)} custom-call(f32[512,128]{1,0:T(8,128)S(1)} %get-tuple-element.92.d_updated, bf16[512,512]{1,0:T(8,128)(2,1)S(1)} %get-tuple-element.93.d_gate, bf16[512,512]{1,0:T(8,128)(2,1)S(1)} %get-tuple-element.94.d_up, f32[256,128]{1,0:T(8,128)S(1)} %get-tuple-element.95.normed, ...), custom_call_target="tpu_custom_call" | custom-call | flops 67108864 | bytes 524288 | tf_op jit(solution)/shard_map/d_inputs/pallas_call | solution.py:445
  8.3 0.6 %collective-permute-done.3.rest_1_ = bf16[4,208,128]{2,1,0:T(8,128)(2,1)S(1)} collective-permute-done((bf16[4,208,128]{2,1,0:T(8,128)(2,1)S(1)}, bf16[4,208,128]{2,1,0:T(8,128)(2,1)S(1)}, u32[]{:S(2)}, u32[]{:S(2)}) %collective-permute-start.3) | collective-permute-done | bytes 213024 | tf_op jit(solution)/shard_map/ppermute | solution.py:483
  8.9 0.1 core_sum.1
  9.0 6.4 %collective-permute-start.4 = (bf16[208,128]{1,0:T(8,128)(2,1)S(1)}, bf16[208,128]{1,0:T(8,128)(2,1)S(1)}, u32[]{:S(2)}, u32[]{:S(2)}) collective-permute-start(bf16[208,128]{1,0:T(8,128)(2,1)S(1)} %get-tuple-element.103), channel_id=1, source_target_pairs={{0,12},{4,8},{8,20},{12,16},{16,28},{20,24},{24,4},{28,0},{1,13},{... | collective-permute-start | bytes 159752 | tf_op jit(solution)/shard_map/ppermute | solution.py:496
  15.4 2.3 %collective-permute-start.5 = (bf16[208,128]{1,0:T(8,128)(2,1)S(1)}, bf16[208,128]{1,0:T(8,128)(2,1)S(1)}, u32[]{:S(2)}, u32[]{:S(2)}) collective-permute-start(bf16[208,128]{1,0:T(8,128)(2,1)S(1)} %get-tuple-element.104), channel_id=1, source_target_pairs={{0,20},{4,16},{8,28},{12,24},{16,4},{20,0},{24,12},{28,8},{1,21},{... | collective-permute-start | bytes 159752 | tf_op jit(solution)/shard_map/ppermute | solution.py:496
  17.7 0.0 collective-permute-start.6
  17.7 0.2 collective-permute-start.7
  17.9 0.4 %collective-permute-start.8 = (bf16[128,128]{1,0:T(8,128)(2,1)S(1)}, bf16[128,128]{1,0:T(8,128)(2,1)S(1)}, u32[]{:S(2)}, u32[]{:S(2)}) collective-permute-start(bf16[128,128]{1,0:T(8,128)(2,1)S(1)} %get-tuple-element.108), channel_id=1, source_target_pairs={{0,4},{4,0},{8,12},{12,8},{16,20},{20,16},{24,28},{28,24},{1,5},{5... | collective-permute-start | bytes 98312 | tf_op jit(solution)/shard_map/ppermute | solution.py:458
  18.2 0.7 %collective-permute-done.7.refs_1_ = bf16[128,128]{1,0:T(8,128)(2,1)S(1)} collective-permute-done((bf16[128,128]{1,0:T(8,128)(2,1)S(1)}, bf16[128,128]{1,0:T(8,128)(2,1)S(1)}, u32[]{:S(2)}, u32[]{:S(2)}) %collective-permute-start.7) | collective-permute-done | bytes 32800 | tf_op jit(solution)/shard_map/ppermute | solution.py:458
  18.9 0.2 collective-permute-done.8.refs_2_
  19.1 0.0 collective-permute-done.4.rest_1_
  19.1 1.6 %collective-permute-done.5.rest_2_ = bf16[208,128]{1,0:T(8,128)(2,1)S(1)} collective-permute-done((bf16[208,128]{1,0:T(8,128)(2,1)S(1)}, bf16[208,128]{1,0:T(8,128)(2,1)S(1)}, u32[]{:S(2)}, u32[]{:S(2)}) %collective-permute-start.5) | collective-permute-done | bytes 53280 | tf_op jit(solution)/shard_map/ppermute | solution.py:496
  20.7 0.8 %collective-permute-done.6.rest_3_ = bf16[208,128]{1,0:T(8,128)(2,1)S(1)} collective-permute-done((bf16[208,128]{1,0:T(8,128)(2,1)S(1)}, bf16[208,128]{1,0:T(8,128)(2,1)S(1)}, u32[]{:S(2)}, u32[]{:S(2)}) %collective-permute-start.6) | collective-permute-done | bytes 53280 | tf_op jit(solution)/shard_map/ppermute | solution.py:496
  21.5 0.1 chip_sum.1
  21.6 0.4 %collective-permute-start.9 = (bf16[64,128]{1,0:T(8,128)(2,1)S(1)}, bf16[64,128]{1,0:T(8,128)(2,1)S(1)}, u32[]{:S(2)}, u32[]{:S(2)}) collective-permute-start(bf16[64,128]{1,0:T(8,128)(2,1)S(1)} %get-tuple-element.114), channel_id=1, source_target_pairs={{0,6},{1,7},{2,4},{3,5},{4,2},{5,3},{6,0},{7,1},{8,14},{9,15},{10,... | collective-permute-start | bytes 49160 | tf_op jit(solution)/shard_map/ppermute | solution.py:515
  22.1 2.3 %collective-permute-start.10 = (bf16[64,128]{1,0:T(8,128)(2,1)S(1)}, bf16[64,128]{1,0:T(8,128)(2,1)S(1)}, u32[]{:S(2)}, u32[]{:S(2)}) collective-permute-start(bf16[64,128]{1,0:T(8,128)(2,1)S(1)} %get-tuple-element.115), channel_id=1, source_target_pairs={{0,7},{1,6},{2,5},{3,4},{4,3},{5,2},{6,1},{7,0},{8,15},{9,14},{10,... | collective-permute-start | bytes 49160 | tf_op jit(solution)/shard_map/ppermute | solution.py:515
  24.3 0.5 %collective-permute-start.11 = (bf16[64,128]{1,0:T(8,128)(2,1)S(1)}, bf16[64,128]{1,0:T(8,128)(2,1)S(1)}, u32[]{:S(2)}, u32[]{:S(2)}) collective-permute-start(bf16[64,128]{1,0:T(8,128)(2,1)S(1)} %get-tuple-element.116), channel_id=1, source_target_pairs={{0,5},{1,4},{2,7},{3,6},{4,1},{5,0},{6,3},{7,2},{8,13},{9,12},{10,... | collective-permute-start | bytes 49160 | tf_op jit(solution)/shard_map/ppermute | solution.py:515
  24.8 0.9 %place.1 = bf16[16,2,16,128]{3,2,1,0:T(8,128)(2,1)} custom-call(bf16[256,128]{1,0:T(8,128)(2,1)S(1)} %d_inputs.2.refs_0_, bf16[128,128]{1,0:T(8,128)(2,1)S(1)} %collective-permute-done.7.refs_1_, bf16[128,128]{1,0:T(8,128)(2,1)S(1)} %collective-permute-done.8.refs_2_), custom_call_target="tpu_custom_call" | custom-call | tf_op jit(solution)/shard_map/place/pallas_call | solution.py:462
  25.7 0.2 collective-permute-done.9.rest_1_
  25.8 1.2 %collective-permute-done.10.rest_2_ = bf16[64,128]{1,0:T(8,128)(2,1)S(1)} collective-permute-done((bf16[64,128]{1,0:T(8,128)(2,1)S(1)}, bf16[64,128]{1,0:T(8,128)(2,1)S(1)}, u32[]{:S(2)}, u32[]{:S(2)}) %collective-permute-start.10) | collective-permute-done | bytes 16416 | tf_op jit(solution)/shard_map/ppermute | solution.py:515
  27.0 0.6 %collective-permute-done.11.rest_3_ = bf16[64,128]{1,0:T(8,128)(2,1)S(1)} collective-permute-done((bf16[64,128]{1,0:T(8,128)(2,1)S(1)}, bf16[64,128]{1,0:T(8,128)(2,1)S(1)}, u32[]{:S(2)}, u32[]{:S(2)}) %collective-permute-start.11) | collective-permute-done | bytes 16416 | tf_op jit(solution)/shard_map/ppermute | solution.py:515
  27.7 0.7 %col_sum.1 = (f32[16,128]{1,0:T(8,128)}, f32[16,128]{1,0:T(8,128)}, f32[32,64]{1,0:T(8,128)}, f32[16,16]{1,0:T(8,128)}) custom-call(bf16[64,128]{1,0:T(8,128)(2,1)S(1)} %get-tuple-element.121.rest_0_, bf16[64,128]{1,0:T(8,128)(2,1)S(1)} %collective-permute-done.9.rest_1_, bf16[64,128]{1,0:T(8,128)(2,1)S(1)} %collective-permute-done.10.rest_2_, ...), custom_call_target="tpu_custom_call" | custom-call | tf_op jit(solution)/shard_map/col_sum/pallas_call | solution.py:517
  (1 shorter events, 0.0 us)
Async XLA Ops:
  2.8 3.4 %collective-permute-start.2 = (bf16[2,128,128]{2,1,0:T(8,128)(2,1)S(1)}, bf16[2,128,128]{2,1,0:T(8,128)(2,1)S(1)}, u32[]{:S(2)}, u32[]{:S(2)}) collective-permute-start(bf16[2,128,128]{2,1,0:T(8,128)(2,1)S(1)} %get-tuple-element.89.refs_17_), channel_id=1, source_target_pairs={{0,4},{1,8},{2,16},{3,24},{4,0},{5,12},{6,20},{7,28},{8,1},{9,13},... | collective-permute-start | bytes 196616 | tf_op jit(solution)/shard_map/ppermute | solution.py:386
  3.3 1.7 %collective-permute-start.1 = (bf16[144,128]{1,0:T(8,128)(2,1)S(1)}, bf16[144,128]{1,0:T(8,128)(2,1)S(1)}, u32[]{:S(2)}, u32[]{:S(2)}) collective-permute-start(bf16[144,128]{1,0:T(8,128)(2,1)S(1)} %get-tuple-element.81), channel_id=1, source_target_pairs={{0,4},{4,0},{8,12},{12,8},{16,20},{20,16},{24,28},{28,24},{1,5},{5... | collective-permute-start | bytes 110600 | tf_op jit(solution)/shard_map/ppermute | solution.py:395
  3.4 1.6 %collective-permute-start = (bf16[128,128]{1,0:T(8,128)(2,1)S(1)}, bf16[128,128]{1,0:T(8,128)(2,1)S(1)}, u32[]{:S(2)}, u32[]{:S(2)}) collective-permute-start(bf16[128,128]{1,0:T(8,128)(2,1)S(1)} %get-tuple-element.80), channel_id=1, source_target_pairs={{0,4},{4,0},{8,12},{12,8},{16,20},{20,16},{24,28},{28,24},{1,5},{5... | collective-permute-start | bytes 98312 | tf_op jit(solution)/shard_map/ppermute | solution.py:395
  7.4 1.5 %collective-permute-start.3 = (bf16[4,208,128]{2,1,0:T(8,128)(2,1)S(1)}, bf16[4,208,128]{2,1,0:T(8,128)(2,1)S(1)}, u32[]{:S(2)}, u32[]{:S(2)}) collective-permute-start(bf16[4,208,128]{2,1,0:T(8,128)(2,1)S(1)} %get-tuple-element.91), channel_id=1, source_target_pairs={{0,4},{4,0},{8,12},{12,8},{16,20},{20,16},{24,28},{28,24},{1,5},{5... | collective-permute-start | bytes 638984 | tf_op jit(solution)/shard_map/ppermute | solution.py:483
  9.0 10.1 %collective-permute-start.4 = (bf16[208,128]{1,0:T(8,128)(2,1)S(1)}, bf16[208,128]{1,0:T(8,128)(2,1)S(1)}, u32[]{:S(2)}, u32[]{:S(2)}) collective-permute-start(bf16[208,128]{1,0:T(8,128)(2,1)S(1)} %get-tuple-element.103), channel_id=1, source_target_pairs={{0,12},{4,8},{8,20},{12,16},{16,28},{20,24},{24,4},{28,0},{1,13},{... | collective-permute-start | bytes 159752 | tf_op jit(solution)/shard_map/ppermute | solution.py:496
  15.4 5.3 %collective-permute-start.5 = (bf16[208,128]{1,0:T(8,128)(2,1)S(1)}, bf16[208,128]{1,0:T(8,128)(2,1)S(1)}, u32[]{:S(2)}, u32[]{:S(2)}) collective-permute-start(bf16[208,128]{1,0:T(8,128)(2,1)S(1)} %get-tuple-element.104), channel_id=1, source_target_pairs={{0,20},{4,16},{8,28},{12,24},{16,4},{20,0},{24,12},{28,8},{1,21},{... | collective-permute-start | bytes 159752 | tf_op jit(solution)/shard_map/ppermute | solution.py:496
  17.7 3.8 %collective-permute-start.6 = (bf16[208,128]{1,0:T(8,128)(2,1)S(1)}, bf16[208,128]{1,0:T(8,128)(2,1)S(1)}, u32[]{:S(2)}, u32[]{:S(2)}) collective-permute-start(bf16[208,128]{1,0:T(8,128)(2,1)S(1)} %get-tuple-element.105), channel_id=1, source_target_pairs={{0,28},{4,24},{8,4},{12,0},{16,12},{20,8},{24,20},{28,16},{1,29},{... | collective-permute-start | bytes 159752 | tf_op jit(solution)/shard_map/ppermute | solution.py:496
  17.7 1.2 %collective-permute-start.7 = (bf16[128,128]{1,0:T(8,128)(2,1)S(1)}, bf16[128,128]{1,0:T(8,128)(2,1)S(1)}, u32[]{:S(2)}, u32[]{:S(2)}) collective-permute-start(bf16[128,128]{1,0:T(8,128)(2,1)S(1)} %get-tuple-element.107), channel_id=1, source_target_pairs={{0,4},{4,0},{8,12},{12,8},{16,20},{20,16},{24,28},{28,24},{1,5},{5... | collective-permute-start | bytes 98312 | tf_op jit(solution)/shard_map/ppermute | solution.py:458
  17.9 1.2 %collective-permute-start.8 = (bf16[128,128]{1,0:T(8,128)(2,1)S(1)}, bf16[128,128]{1,0:T(8,128)(2,1)S(1)}, u32[]{:S(2)}, u32[]{:S(2)}) collective-permute-start(bf16[128,128]{1,0:T(8,128)(2,1)S(1)} %get-tuple-element.108), channel_id=1, source_target_pairs={{0,4},{4,0},{8,12},{12,8},{16,20},{20,16},{24,28},{28,24},{1,5},{5... | collective-permute-start | bytes 98312 | tf_op jit(solution)/shard_map/ppermute | solution.py:458
  21.6 4.2 %collective-permute-start.9 = (bf16[64,128]{1,0:T(8,128)(2,1)S(1)}, bf16[64,128]{1,0:T(8,128)(2,1)S(1)}, u32[]{:S(2)}, u32[]{:S(2)}) collective-permute-start(bf16[64,128]{1,0:T(8,128)(2,1)S(1)} %get-tuple-element.114), channel_id=1, source_target_pairs={{0,6},{1,7},{2,4},{3,5},{4,2},{5,3},{6,0},{7,1},{8,14},{9,15},{10,... | collective-permute-start | bytes 49160 | tf_op jit(solution)/shard_map/ppermute | solution.py:515
  22.1 5.0 %collective-permute-start.10 = (bf16[64,128]{1,0:T(8,128)(2,1)S(1)}, bf16[64,128]{1,0:T(8,128)(2,1)S(1)}, u32[]{:S(2)}, u32[]{:S(2)}) collective-permute-start(bf16[64,128]{1,0:T(8,128)(2,1)S(1)} %get-tuple-element.115), channel_id=1, source_target_pairs={{0,7},{1,6},{2,5},{3,4},{4,3},{5,2},{6,1},{7,0},{8,15},{9,14},{10,... | collective-permute-start | bytes 49160 | tf_op jit(solution)/shard_map/ppermute | solution.py:515
  24.3 3.4 %collective-permute-start.11 = (bf16[64,128]{1,0:T(8,128)(2,1)S(1)}, bf16[64,128]{1,0:T(8,128)(2,1)S(1)}, u32[]{:S(2)}, u32[]{:S(2)}) collective-permute-start(bf16[64,128]{1,0:T(8,128)(2,1)S(1)} %get-tuple-element.116), channel_id=1, source_target_pairs={{0,5},{1,4},{2,7},{3,6},{4,1},{5,0},{6,3},{7,2},{8,13},{9,12},{10,... | collective-permute-start | bytes 49160 | tf_op jit(solution)/shard_map/ppermute | solution.py:515
